TPU v7x, 32 devices: a whole 2x2x4 slice. The times are simulated.
32 devices in a mesh: section: 2 (over core), dp: 4 (over z), mp: 4 (over y, x).
Axes of the slice: x: 2, y: 2, z: 4, core: 2. Of those that a mesh axis runs over, the one named last changes fastest.
Arguments:
- tokens: bfloat16 [512, 12288], P('mp', 'dp'), may hold values from -600 to 600
- weights: bfloat16 [2, 12288, 24576], P('section', 'dp', 'mp'), may hold values from -0.078125 to 0.078125
- gain: float32 [12288], P('dp'), may hold values from 0.1 to 1.9
- cotangent: bfloat16 [512, 12288], P('mp', 'dp'), may hold values from -6 to 6
Outputs:
- section_results: bfloat16 [2, 512, 12288], P('section', 'mp', 'dp')
- weight_grads: bfloat16 [2, 12288, 24576], P('section', 'dp', 'mp')
All inputs are finite; a program needn't handle non-finite values.
Results may differ from a plain program's by a relative error of at most 0.035.
Values may be sent and summed in bfloat16 or wider, within the bound.
No kernel may reach another device: no remote copies, remote signals or barrier semaphores. Data moves between devices by JAX's collectives and lax.ppermute only.
A program may use at most 192 MiB of HBM per device.

v0:
```python
import jax
import jax.numpy as jnp
from jax import lax
from jax.sharding import PartitionSpec as P

D = 12288


epsilon = 1e-05


def from_behind(value, axis, by):
    peers = lax.axis_size(axis)
    pairs = [(i, i + by) for i in range(peers) if 0 <= i + by < peers]
    return lax.ppermute(value, axis, pairs)


def gelu_tanh(inputs):
    return jax.nn.gelu(inputs, approximate=True)


def gelu_back(preact, grad_hidden):
    return jax.vjp(gelu_tanh, preact)[1](grad_hidden.astype(jnp.float32))[0]


def contract_last(left, right):
    return lax.dot_general(
        left, right, (((1,), (1,)), ((), ())), preferred_element_type=jnp.float32
    )


def contract_first(left, right):
    return lax.dot_general(
        left, right, (((0,), (0,)), ((), ())), preferred_element_type=jnp.float32
    )


def only_when(flag, compute, shape):
    return lax.cond(flag, compute, lambda: jnp.zeros(shape, jnp.float32))


def local(tokens, weights, gain, cotangent):
    section_index = lax.axis_index("section")
    first_section = section_index == 0
    second_section = jnp.logical_not(first_section)
    weight = weights[0]
    local_rows = tokens.shape[0]
    width_local = weight.shape[0]
    hidden_local = weight.shape[1]
    values = tokens.astype(jnp.float32)
    row_total, row_squares = lax.psum((jnp.sum(values, 1), jnp.sum(values * values, 1)), "dp")
    average = row_total / D
    inverse_std = lax.rsqrt(row_squares / D - average * average + epsilon)
    centred = (values - average[:, None]) * inverse_std[:, None]
    normed = (centred * gain).astype(jnp.bfloat16)
    gathered = lax.all_gather(normed, "mp", axis=0, tiled=True)
    all_rows = gathered.shape[0]

    def compute():
        return jnp.dot(gathered, weight, preferred_element_type=jnp.float32)

    preact = lax.psum(
        only_when(first_section, compute, (all_rows, hidden_local)).astype(jnp.bfloat16), "dp"
    ).astype(jnp.float32)
    hidden = gelu_tanh(preact).astype(jnp.bfloat16)
    arrived = from_behind(hidden, "section", 1)

    def compute():
        return contract_last(arrived, weight)

    output = lax.psum_scatter(
        only_when(second_section, compute, (local_rows * lax.axis_size("mp"), width_local)).astype(
            jnp.bfloat16
        ),
        "mp",
        scatter_dimension=0,
        tiled=True,
    )
    cotangent_all = lax.all_gather(cotangent, "mp", axis=0, tiled=True)
    grad_down = only_when(
        second_section, lambda: contract_first(cotangent_all, arrived), (width_local, hidden_local)
    ).astype(jnp.bfloat16)

    def compute():
        return jnp.dot(cotangent_all, weight, preferred_element_type=jnp.float32)

    grad_hidden = lax.psum(
        only_when(second_section, compute, (all_rows, hidden_local)).astype(jnp.bfloat16), "dp"
    )
    returned = from_behind(grad_hidden, "section", -1)
    grad_preact = gelu_back(preact, returned).astype(jnp.bfloat16)
    grad_up = only_when(
        first_section, lambda: contract_first(gathered, grad_preact), (width_local, hidden_local)
    ).astype(jnp.bfloat16)

    def compute():
        return contract_last(grad_preact, weight)

    grad_normed = lax.psum_scatter(
        only_when(first_section, compute, (local_rows * lax.axis_size("mp"), width_local)).astype(
            jnp.bfloat16
        ),
        "mp",
        scatter_dimension=0,
        tiled=True,
    )
    section_results = jnp.where(first_section, grad_normed, output)[None]
    weight_grads = jnp.where(first_section, grad_up, grad_down)[None]
    return (section_results, weight_grads)


def solution(mesh):
    placed = (P("mp", "dp"), P("section", "dp", "mp"), P("dp"), P("mp", "dp"))
    return jax.shard_map(
        local,
        mesh=mesh,
        in_specs=placed,
        out_specs=(P("section", "mp", "dp"), P("section", "dp", "mp")),
        check_vma=False,
    )
```

profile of v0, /device:TPU:0, one launch (start us, length us, event | category | flops | bytes accessed | tf_op | source)
XLA Modules:
  0.0 722.9 jit_solution(4092760394996489886)
XLA Ops:
  7.2 0.0 all-gather.5.cloned.1.call-start
  7.2 1.4 convert_reduce_fusion
  8.6 13.5 %all-reduce = (f32[128]{0:T(128)S(1)}, f32[128]{0:T(128)S(1)}) all-reduce(f32[128]{0:T(128)S(1)} %get-tuple-element.59, f32[128]{0:T(128)S(1)} %get-tuple-element.58), channel_id=1, replica_groups=mesh['section'=2,'dp'=4,'mp'=4] {'dp'}, use_global_device_ids=true, to_apply=%region_6.0 | all-reduce | flops 256 | bytes 2048 | tf_op jit(solution)/shard_map/psum | solution.py:51
  22.1 2.3 fusion.13
  24.4 0.0 all-gather.5.cloned.1.call-update
  24.5 0.0 all-gather.3.cloned.1.call-start
  24.5 0.7 all-gather.3.cloned.1.call-update
  25.2 0.0 all-reduce.4.cloned.1.call-start
  25.3 41.5 %all-gather.5.cloned.1.call-done = bf16[512,3072]{1,0:T(8,128)(2,1)} async-done(((bf16[128,3072]{1,0:T(8,128)(2,1)}), bf16[512,3072]{1,0:T(8,128)(2,1)}) %all-gather.5.cloned.1.call-update) | async-done | bytes 3145744 | tf_op jit(solution)/shard_map/all_gather | solution.py:56
  66.8 26.8 %conditional.7 = (bf16[512,6144]{1,0:T(8,128)(2,1)}) conditional(s32[]{:T(128)} %convert_element_type.52, () %tuple.51, (bf16[512,3072]{1,0:T(8,128)(2,1)}, bf16[3072,6144]{1,0:T(8,128)(2,1)}) %tuple.87), branch_computations={%region_7.0_spmd, %region_8.0_spmd} | conditional | flops 19327352832 | bytes 47185928 | solution.py:39
  66.8 26.8 %fusion.16 = bf16[512,6144]{1,0:T(8,128)(2,1)} fusion(bf16[512,3072]{1,0:T(8,128)(2,1)} %get-tuple-element.43, bf16[3072,6144]{1,0:T(8,128)(2,1)} %get-tuple-element.44), kind=kOutput, calls=%fused_computation.31 | convolution fusion | flops 19327352832 | bytes 47185920 | tf_op jit(solution)/shard_map/cond/branch_1_fun/dot_general | solution.py:60
  93.6 19.1 %all-gather.3.cloned.1.call-done = bf16[512,3072]{1,0:T(8,128)(2,1)} async-done(((bf16[128,3072]{1,0:T(8,128)(2,1)}), bf16[512,3072]{1,0:T(8,128)(2,1)}) %all-gather.3.cloned.1.call-update) | async-done | bytes 3145744 | tf_op jit(solution)/shard_map/all_gather | solution.py:79
  112.7 3.5 conditional.6
  112.7 3.5 broadcast.32
  116.1 0.0 all-reduce.4.cloned.1.call-update
  116.2 0.0 reduce-scatter.3.cloned.1.call-start
  116.2 449.7 %all-reduce.4.cloned.1.call-done = (bf16[512,6144]{1,0:T(8,128)(2,1)}, bf16[512,6144]{1,0:T(8,128)(2,1)}) async-done(((bf16[512,6144]{1,0:T(8,128)(2,1)}, bf16[512,6144]{1,0:T(8,128)(2,1)}), (bf16[512,6144]{1,0:T(8,128)(2,1)}, bf16[512,6144]{1,0:T(8,128)(2,1)})) %all-reduce.4.cloned.1.call-update) | async-done | bytes 12582928 | tf_op jit(solution)/shard_map/psum | solution.py:87
  565.9 1.5 collective-permute-start
  567.4 10.8 %collective-permute-done = bf16[512,6144]{1,0:T(8,128)(2,1)S(1)} collective-permute-done((bf16[512,6144]{1,0:T(8,128)(2,1)}, bf16[512,6144]{1,0:T(8,128)(2,1)S(1)}, u32[]{:S(2)}, u32[]{:S(2)}) %collective-permute-start) | collective-permute-done | bytes 6291488 | tf_op jit(solution)/shard_map/ppermute | solution.py:15
  578.2 13.6 %fusion.10 = (bf16[512,6144]{1,0:T(8,128)(2,1)}, bf16[512,6144]{1,0:T(8,128)(2,1)}) fusion(bf16[512,6144]{1,0:T(8,128)(2,1)} %get-tuple-element.63, bf16[512,6144]{1,0:T(8,128)(2,1)S(1)} %collective-permute-done), kind=kLoop, calls=%fused_computation.19 | loop fusion | flops 75497472 | bytes 25165824 | tf_op jit(solution)/shard_map/convert_element_type | solution.py:65
  591.8 4.7 collective-permute-start.1
  596.5 25.8 %conditional.8 = (bf16[512,3072]{1,0:T(8,128)(2,1)S(1)}) conditional(s32[]{:T(128)} %convert_element_type.52, () %tuple.48, (bf16[512,6144]{1,0:T(8,128)(2,1)}, bf16[3072,6144]{1,0:T(8,128)(2,1)}) %tuple.89), branch_computations={%region_10.0_spmd, %region_11.0_spmd} | conditional | flops 19327352832 | bytes 47185928 | solution.py:39
  596.5 25.8 %fusion.17 = bf16[512,3072]{1,0:T(8,128)(2,1)S(1)} fusion(bf16[512,6144]{1,0:T(8,128)(2,1)} %get-tuple-element.48, bf16[3072,6144]{1,0:T(8,128)(2,1)} %get-tuple-element.49), kind=kOutput, calls=%fused_computation.32 | convolution fusion | flops 19327352832 | bytes 47185920 | tf_op jit(solution)/shard_map/cond/branch_1_fun/dot_general | solution.py:27
  622.3 0.0 copy-start
  622.3 1.6 copy-done
  623.9 0.0 reduce-scatter.3.cloned.1.call-update
  623.9 0.0 reduce-scatter.5.cloned.1.call-start
  624.0 28.4 %conditional.10 = (bf16[3072,6144]{1,0:T(8,128)(2,1)}) conditional(s32[]{:T(128)} %convert_element_type.52, () %tuple.56, (bf16[512,3072]{1,0:T(8,128)(2,1)}, bf16[512,6144]{1,0:T(8,128)(2,1)}) %tuple.57), branch_computations={%region_16.0_spmd, %region_17.0_spmd} | conditional | flops 19346227200 | bytes 47185928 | solution.py:39
  624.2 28.2 %convolution_convert_fusion = bf16[3072,6144]{1,0:T(8,128)(2,1)} fusion(bf16[512,3072]{1,0:T(8,128)(2,1)} %get-tuple-element.52, bf16[512,6144]{1,0:T(8,128)(2,1)} %get-tuple-element.53), kind=kOutput, calls=%fused_computation | convolution fusion | flops 19346227200 | bytes 47185920 | tf_op jit(solution)/shard_map/cond/branch_1_fun/dot_general | solution.py:33
  652.4 0.0 collective-permute-done.1
  652.4 0.4 conditional.9
  652.4 0.4 broadcast.35
  652.8 0.0 copy-start.1
  652.8 1.6 copy-done.1
  654.4 0.0 reduce-scatter.5.cloned.1.call-update
  654.5 12.7 %conditional.11 = (bf16[3072,6144]{1,0:T(8,128)(2,1)}) conditional(s32[]{:T(128)} %convert_element_type.53, () %tuple.58, (bf16[512,3072]{1,0:T(8,128)(2,1)}, bf16[512,6144]{1,0:T(8,128)(2,1)}) %tuple.59), branch_computations={%region_18.0_spmd, %region_19.0_spmd} | conditional | flops 19346227200 | bytes 47185928 | solution.py:39
  654.5 12.5 %broadcast.37 = bf16[3072,6144]{1,0:T(8,128)(2,1)} broadcast(bf16[]{:T(256)} %constant.8.clone), dimensions={} | broadcast | bytes 37748736 | tf_op jit(solution)/shard_map/broadcast.9
  667.2 26.0 %select_bitcast_fusion = bf16[1,3072,6144]{2,1,0:T(8,128)(2,1)} fusion(bf16[3072,6144]{1,0:T(8,128)(2,1)} %get-tuple-element.74, bf16[3072,6144]{1,0:T(8,128)(2,1)} %get-tuple-element.75, pred[]{:T(512)S(6)} %eq.3), kind=kLoop, calls=%fused_computation.2 | loop fusion | flops 18874368 | bytes 113246208 | tf_op jit(solution)/shard_map/broadcast_in_dim | solution.py:108
  693.2 0.0 reduce-scatter.3.cloned.1.call-done
  693.2 20.6 %reduce-scatter.5.cloned.1.call-done = bf16[128,3072]{1,0:T(8,128)(2,1)} async-done(((bf16[512,3072]{1,0:T(8,128)(2,1)}), bf16[128,3072]{1,0:T(8,128)(2,1)}) %reduce-scatter.5.cloned.1.call-update) | async-done | bytes 786448 | tf_op jit(solution)/shard_map/reduce_scatter | solution.py:71
  713.8 2.1 select_bitcast_fusion.1
  (1 shorter events, 0.0 us)
Async XLA Ops:
  7.2 59.6 %all-gather.5.cloned.1.call-start = ((), (), s32[]{:S(2)}) async-start(), calls=%async_computation.3 | async-start | bytes 3932160 | tf_op jit(solution)/shard_map/all_gather | solution.py:56
  24.5 88.2 %all-gather.3.cloned.1.call-start = ((), (), s32[]{:S(2)}) async-start(), calls=%async_computation.2 | async-start | bytes 3932160 | tf_op jit(solution)/shard_map/all_gather | solution.py:79
  25.2 540.7 %all-reduce.4.cloned.1.call-start = ((), (), s32[]{:S(2)}) async-start(), calls=%async_computation.6 | async-start | bytes 25165824 | tf_op jit(solution)/shard_map/psum | solution.py:87
  116.2 577.1 %reduce-scatter.3.cloned.1.call-start = ((), (), s32[]{:S(2)}) async-start(), calls=%async_computation.4 | async-start | bytes 3932160 | tf_op jit(solution)/shard_map/reduce_scatter | solution.py:99
  565.9 12.3 %collective-permute-start = (bf16[512,6144]{1,0:T(8,128)(2,1)}, bf16[512,6144]{1,0:T(8,128)(2,1)S(1)}, u32[]{:S(2)}, u32[]{:S(2)}) collective-permute-start(bf16[512,6144]{1,0:T(8,128)(2,1)} %get-tuple-element.62), channel_id=1, source_target_pairs={{16,0},{17,1},{18,2},{19,3},{20,4},{21,5},{22,6},{23,7},{24,8},{25... | collective-permute-start | bytes 18874376 | tf_op jit(solution)/shard_map/ppermute | solution.py:15
  591.8 60.7 %collective-permute-start.1 = (bf16[512,6144]{1,0:T(8,128)(2,1)}, bf16[512,6144]{1,0:T(8,128)(2,1)}, u32[]{:S(2)}, u32[]{:S(2)}) collective-permute-start(bf16[512,6144]{1,0:T(8,128)(2,1)} %get-tuple-element.64), channel_id=1, source_target_pairs={{0,16},{1,17},{2,18},{3,19},{4,20},{5,21},{6,22},{7,23},{8,24},{9,... | collective-permute-start | bytes 18874376 | tf_op jit(solution)/shard_map/ppermute | solution.py:15
  622.3 1.6 copy-start
  623.9 89.9 %reduce-scatter.5.cloned.1.call-start = ((), (), s32[]{:S(2)}) async-start(), calls=%async_computation.5 | async-start | bytes 3932160 | tf_op jit(solution)/shard_map/reduce_scatter | solution.py:71
  652.8 1.6 copy-start.1
Sparse Core Ops, SparseCore 0:
  24.6 42.1 all-gather.4
  68.6 43.9 all-gather.2
  116.3 449.6 all-reduce.3
  624.1 42.8 reduce-scatter.2
  669.8 43.9 reduce-scatter.4
where the time goes:
time: 731 us; the launch traced here: 723 us
  waiting for transfers between devices  542 us (74%)
  matrix products  80.8 us (11%)
  other arithmetic  45.5 us (6%)
  local copies, waits for them, and re-layouts  19.6 us (3%)
  between operations  14.3 us (2%)
  blocking collectives  13.5 us (2%)
    psum x1, waiting for transfers between devices, local(): lax.psum(only_when(second_section, compute, (all_rows, hidden_local)).ast...  450 us
    all_gather x1, waiting for transfers between devices, local(): gathered = lax.all_gather(normed, 'mp', axis=0, tiled=True)  41.5 us
    dot_general x1, matrix products, contract_first(): lax.dot_general(left, right, (((0,), (0,)), ((), ())), preferred_element_...  28.2 us
    dot_general x1, matrix products, compute(): return jnp.dot(gathered, weight, preferred_element_type=jnp.float32)  26.8 us
    broadcast_in_dim x1, other arithmetic, local(): weight_grads = jnp.where(first_section, grad_up, grad_down)[None]  26 us
    dot_general x1, matrix products, contract_last(): lax.dot_general(left, right, (((1,), (1,)), ((), ())), preferred_element_...  25.8 us
    reduce_scatter x1, waiting for transfers between devices, local(): lax.psum_scatter(only_when(second_section, compute, (local_rows * lax.axi...  20.6 us
    all_gather x1, waiting for transfers between devices, local(): cotangent_all = lax.all_gather(cotangent, 'mp', axis=0, tiled=True)  19.1 us
  transfers between devices with their start and end apart: 7, of which 5 were waited for; matrix products, arithmetic and copies ran while one was open for 17% of the time, Pallas kernels for 0%

commit v1 on v0

v1 whole, which is shorter than its diff:
```python
import jax
import jax.numpy as jnp
from jax import lax
from jax.sharding import PartitionSpec as P

D = 12288


epsilon = 1e-05


def gelu_tanh(inputs):
    return jax.nn.gelu(inputs, approximate=True)


def gelu_back(preact, grad_hidden):
    return jax.vjp(gelu_tanh, preact)[1](grad_hidden.astype(jnp.float32))[0]


def dot_f32(left, right, dims):
    return lax.dot_general(left, right, (dims, ((), ())), preferred_element_type=jnp.float32)


def from_peer(value, by):
    peers = lax.axis_size("mp")
    return lax.ppermute(value, "mp", [(i, i ^ by) for i in range(peers)])


def across_sections(value):
    return lax.ppermute(value, "section", [(0, 1), (1, 0)])


def add_bf16(left, right):
    return (left.astype(jnp.float32) + right.astype(jnp.float32)).astype(jnp.bfloat16)


def line_sum(part, activate):
    peers = lax.axis_size("dp")
    half = peers // 2
    index = lax.axis_index("dp")
    for hop in range(half - 1):
        arrived = lax.ppermute(part, "dp", [(hop, hop + 1), (peers - 1 - hop, peers - 2 - hop)])
        part = add_bf16(part, arrived)
    arrived = lax.ppermute(part, "dp", [(half - 1, half), (half, half - 1)])
    result = activate(add_bf16(part, arrived))
    for hop in reversed(range(half - 1)):
        arrived = lax.ppermute(result, "dp", [(hop + 1, hop), (peers - 2 - hop, peers - 1 - hop)])
        receives = jnp.logical_or(index == hop, index == peers - 1 - hop)
        result = jnp.where(receives, arrived, result)
    return result


def local(tokens, weights, gain, cotangent):
    first = lax.axis_index("section") == 0
    weight = weights[0]
    peers = lax.axis_size("mp")
    rows = tokens.shape[0]
    hidden_local = weight.shape[1]

    raw = jnp.where(first, tokens, cotangent)
    gathered = [raw] + [from_peer(raw, by) for by in range(1, peers)]

    values = tokens.astype(jnp.float32)
    sums = lax.psum(jnp.stack([jnp.sum(values, 1), jnp.sum(values * values, 1)]), "dp")
    average = sums[0] / D
    inverse_std = lax.rsqrt(sums[1] / D - average * average + epsilon)
    stats = jnp.stack([average, inverse_std])

    def prepared(block, scale):
        centred = (block.astype(jnp.float32) - scale[0][:, None]) * scale[1][:, None]
        return jnp.where(first, (centred * gain).astype(jnp.bfloat16), block)

    own = prepared(raw, stats)
    others = jnp.concatenate(
        [prepared(gathered[by], from_peer(stats, by)) for by in range(1, peers)], 0
    )

    def activate(total):
        other = across_sections(total)
        preact = jnp.where(first, total, other).astype(jnp.float32)
        grad_hidden = jnp.where(first, other, total)
        return jnp.where(first, gelu_back(preact, grad_hidden), gelu_tanh(preact)).astype(
            jnp.bfloat16
        )

    def chunk(block, start, stop):
        part = dot_f32(block, weight[:, start:stop], ((1,), (0,))).astype(jnp.bfloat16)
        return line_sum(part, activate)

    unit = hidden_local // 6
    own_hidden = [chunk(own, 0, 2 * unit)]
    others_hidden = [chunk(others, i * unit, (i + 1) * unit) for i in range(6)]
    own_hidden += [chunk(own, 2 * unit, 4 * unit)]
    own_hidden += [chunk(own, i * unit, (i + 1) * unit) for i in (4, 5)]
    others_hidden = jnp.concatenate(others_hidden, 1)
    own_hidden = jnp.concatenate(own_hidden, 1)

    partial = dot_f32(others_hidden, weight, ((1,), (1,))).astype(jnp.bfloat16)
    arrived = [
        from_peer(partial[(by - 1) * rows : by * rows], by) for by in range(1, peers)
    ]
    result = dot_f32(own_hidden, weight, ((1,), (1,))).astype(jnp.bfloat16).astype(jnp.float32)
    for block in arrived:
        result = result + block.astype(jnp.float32)
    section_results = result.astype(jnp.bfloat16)[None]

    weight_grads = dot_f32(
        jnp.concatenate([own, others], 0),
        jnp.concatenate([own_hidden, others_hidden], 0),
        ((0,), (0,)),
    ).astype(jnp.bfloat16)[None]
    return (section_results, weight_grads)


def solution(mesh):
    placed = (P("mp", "dp"), P("section", "dp", "mp"), P("dp"), P("mp", "dp"))
    return jax.shard_map(
        local,
        mesh=mesh,
        in_specs=placed,
        out_specs=(P("section", "mp", "dp"), P("section", "dp", "mp")),
        check_vma=False,
    )
```

time: 731 us -> 503 us (0.69)
  waiting for transfers between devices: 542 us -> 250 us
  starting transfers between devices: 6.35 us -> 72.1 us
  matrix products: 80.8 us -> 125 us
  local copies, waits for them, and re-layouts: 19.6 us -> 1.42 us
  other arithmetic: 45.5 us -> 31.3 us
  between operations: 14.3 us -> 2.03 us
    psum x1 -> x0, waiting for transfers between devices: 450 us -> none  [local(): lax.psum(only_when(second_section, compute, (all_rows, hidden_local)).ast...]
    ppermute x2 -> x49, waiting for transfers between devices: 10.8 us -> 250 us  [the longest x10 150 us: line_sum(): lax.ppermute(result, 'dp', [(hop + 1, hop), (peers - 2 - hop, peers - 1 -...]
    ppermute x2 -> x49, starting transfers between devices: 6.15 us -> 72.1 us  [the longest x10 38.4 us: line_sum(): lax.ppermute(part, 'dp', [(hop, hop + 1), (peers - 1 - hop, peers - 2 - h...]
    all_gather x2 -> x0, waiting for transfers between devices: 60.6 us -> none  [the longest x1 41.5 us: local(): gathered = lax.all_gather(normed, 'mp', axis=0, tiled=True)]
    dot_general x3 -> x13, matrix products: 80.8 us -> 125 us  [dot_f32(): lax.dot_general(left, right, (dims, ((), ())), preferred_element_type=jnp...]
    broadcast_in_dim x2 -> x0, other arithmetic: 28.1 us -> none  [the longest x1 26 us: local(): weight_grads = jnp.where(first_section, grad_up, grad_down)[None]]
    reduce_scatter x2 -> x0, waiting for transfers between devices: 20.6 us -> none  [the longest x1 20.6 us: local(): lax.psum_scatter(only_when(second_section, compute, (local_rows * lax.axi...]
    another operation x3 -> x0, local copies, waits for them, and re-layouts: 16.3 us -> none
  transfers between devices with their start and end apart: 7 -> 49, of which waited for: 5 -> 14; matrix products, arithmetic and copies ran while one was open for 17% -> 22% of each run, Pallas kernels for 0% -> 0%
where the time goes in v1:
time: 503 us; the launch traced here: 495 us
  waiting for transfers between devices  250 us (50%)
  matrix products  125 us (25%)
  starting transfers between devices  72.1 us (14%)
  other arithmetic  31.3 us (6%)
  blocking collectives  13.5 us (3%)
    ppermute x10, waiting for transfers between devices, line_sum(): lax.ppermute(result, 'dp', [(hop + 1, hop), (peers - 2 - hop, peers - 1 -...  150 us
    dot_general x13, matrix products, dot_f32(): lax.dot_general(left, right, (dims, ((), ())), preferred_element_type=jnp...  125 us
    ppermute x10, waiting for transfers between devices, line_sum(): lax.ppermute(part, 'dp', [(hop, hop + 1), (peers - 1 - hop, peers - 2 - h...  94.2 us
    ppermute x10, starting transfers between devices, line_sum(): lax.ppermute(part, 'dp', [(hop, hop + 1), (peers - 1 - hop, peers - 2 - h...  38.4 us
    ppermute x10, starting transfers between devices, line_sum(): lax.ppermute(result, 'dp', [(hop + 1, hop), (peers - 2 - hop, peers - 1 -...  13.6 us
    psum x1, blocking collectives, local(): lax.psum(jnp.stack([jnp.sum(values, 1), jnp.sum(values * values, 1)]), 'dp')  13.5 us
    convert_element_type x10, other arithmetic, activate(): jnp.where(first, gelu_back(preact, grad_hidden), gelu_tanh(preact))  10.9 us
    ppermute x9, starting transfers between devices, from_peer(): return lax.ppermute(value, 'mp', [(i, i ^ by) for i in range(peers)])  10.6 us
  transfers between devices with their start and end apart: 49, of which 14 were waited for; matrix products, arithmetic and copies ran while one was open for 22% of the time, Pallas kernels for 0%

profile of v1, /device:TPU:0, one launch (start us, length us, event | category | flops | bytes accessed | tf_op | source)
XLA Modules:
  0.0 494.9 jit_solution(47299028618461951)
XLA Ops:
  0.6 1.4 convert_reduce_fusion
  2.1 13.5 %psum.7 = f32[2,128]{1,0:T(2,128)S(1)} all-reduce(f32[2,128]{1,0:T(2,128)S(1)} %pad_maximum_fusion.1), channel_id=1, replica_groups=mesh['section'=2,'dp'=4,'mp'=4] {'dp'}, use_global_device_ids=true, to_apply=%region_2.3 | all-reduce | flops 256 | bytes 2048 | tf_op jit(solution)/shard_map/psum | solution.py:64
  15.6 1.6 fusion.148
  17.2 1.6 collective-permute-start.16
  18.7 1.5 collective-permute-start.18
  21.3 2.4 collective-permute-start.21
  23.7 6.4 %fusion.42 = bf16[128,2048]{1,0:T(8,128)(2,1)S(1)} fusion(bf16[128,3072]{1,0:T(8,128)(2,1)S(1)} %get-tuple-element.4, bf16[3072,6144]{1,0:T(8,128)(2,1)} %bitcast.39), kind=kOutput, calls=%fused_computation.75 | convolution fusion | flops 1610874880 | bytes 13893632 | tf_op jit(solution)/shard_map/dot_general | solution.py:21
  30.2 6.4 %fusion.45 = bf16[128,2048]{1,0:T(8,128)(2,1)S(1)} fusion(bf16[128,3072]{1,0:T(8,128)(2,1)S(1)} %get-tuple-element.4, bf16[3072,6144]{1,0:T(8,128)(2,1)} %bitcast.40), kind=kOutput, calls=%fused_computation.76 | convolution fusion | flops 1610874880 | bytes 13893632 | tf_op jit(solution)/shard_map/dot_general | solution.py:21
  36.6 4.5 fusion.142
  41.1 4.5 fusion.145
  45.7 1.3 collective-permute-start.8
  47.0 1.3 collective-permute-start.12
  48.3 5.4 %collective-permute-done.8 = bf16[128,1024]{1,0:T(8,128)(2,1)S(1)} collective-permute-done((bf16[128,1024]{1,0:T(8,128)(2,1)}, bf16[128,1024]{1,0:T(8,128)(2,1)S(1)}, u32[]{:S(2)}, u32[]{:S(2)}) %collective-permute-start.8) | collective-permute-done | bytes 262176 | tf_op jit(solution)/shard_map/ppermute | solution.py:42
  53.7 4.3 collective-permute-start
  62.4 13.0 %collective-permute-start.4 = (bf16[128,2048]{1,0:T(8,128)(2,1)S(1)}, bf16[128,2048]{1,0:T(8,128)(2,1)S(1)}, u32[]{:S(2)}, u32[]{:S(2)}) collective-permute-start(bf16[128,2048]{1,0:T(8,128)(2,1)S(1)} %fusion.45), channel_id=1, source_target_pairs={{0,4},{12,8},{1,5},{13,9},{2,6},{14,10},{3,7},{15,11},{16,20},{28,... | collective-permute-start | bytes 1572872 | tf_op jit(solution)/shard_map/ppermute | solution.py:42
  75.7 6.3 %collective-permute-done.4 = bf16[128,2048]{1,0:T(8,128)(2,1)S(1)} collective-permute-done((bf16[128,2048]{1,0:T(8,128)(2,1)S(1)}, bf16[128,2048]{1,0:T(8,128)(2,1)S(1)}, u32[]{:S(2)}, u32[]{:S(2)}) %collective-permute-start.4) | collective-permute-done | bytes 524320 | tf_op jit(solution)/shard_map/ppermute | solution.py:42
  84.7 1.3 collective-permute-start.11
  86.0 1.8 collective-permute-start.15
  87.8 1.2 fusion.149
  89.1 6.3 %fusion.127 = bf16[384,1024]{1,0:T(8,128)(2,1)S(1)} fusion(bf16[3072,6144]{1,0:T(8,128)(2,1)} %bitcast.43, bf16[128,3072]{1,0:T(8,128)(2,1)S(1)} %get-tuple-element.11, bf16[128,3072]{1,0:T(8,128)(2,1)S(1)} %get-tuple-element.10, bf16[128,3072]{1,0:T(8,128)(2,1)S(1)} %get-tuple-element.9), kind=kOutput, calls=%fused_computation.189 | convolution fusion | flops 2423390208 | bytes 9437184 | tf_op jit(solution)/shard_map/dot_general | solution.py:21
  95.4 5.4 %fusion.124 = bf16[384,1024]{1,0:T(8,128)(2,1)S(1)} fusion(bf16[3072,6144]{1,0:T(8,128)(2,1)} %bitcast.44, bf16[128,3072]{1,0:T(8,128)(2,1)S(1)} %get-tuple-element.11, bf16[128,3072]{1,0:T(8,128)(2,1)S(1)} %get-tuple-element.10, bf16[128,3072]{1,0:T(8,128)(2,1)S(1)} %get-tuple-element.9), kind=kOutput, calls=%fused_computation.188 | convolution fusion | flops 2423390208 | bytes 9437184 | tf_op jit(solution)/shard_map/dot_general | solution.py:21
  100.8 5.5 %fusion.139 = bf16[384,1024]{1,0:T(8,128)(2,1)S(1)} fusion(bf16[3072,6144]{1,0:T(8,128)(2,1)} %bitcast.45, bf16[128,3072]{1,0:T(8,128)(2,1)S(1)} %get-tuple-element.11, bf16[128,3072]{1,0:T(8,128)(2,1)S(1)} %get-tuple-element.10, bf16[128,3072]{1,0:T(8,128)(2,1)S(1)} %get-tuple-element.9), kind=kOutput, calls=%fused_computation.193 | convolution fusion | flops 2423390208 | bytes 9437184 | tf_op jit(solution)/shard_map/dot_general | solution.py:21
  106.3 5.4 %fusion.136 = bf16[384,1024]{1,0:T(8,128)(2,1)S(1)} fusion(bf16[3072,6144]{1,0:T(8,128)(2,1)} %bitcast.46, bf16[128,3072]{1,0:T(8,128)(2,1)S(1)} %get-tuple-element.11, bf16[128,3072]{1,0:T(8,128)(2,1)S(1)} %get-tuple-element.10, bf16[128,3072]{1,0:T(8,128)(2,1)S(1)} %get-tuple-element.9), kind=kOutput, calls=%fused_computation.192 | convolution fusion | flops 2423390208 | bytes 9437184 | tf_op jit(solution)/shard_map/dot_general | solution.py:21
  111.8 5.4 %fusion.133 = bf16[384,1024]{1,0:T(8,128)(2,1)S(1)} fusion(bf16[3072,6144]{1,0:T(8,128)(2,1)} %bitcast.47, bf16[128,3072]{1,0:T(8,128)(2,1)S(1)} %get-tuple-element.11, bf16[128,3072]{1,0:T(8,128)(2,1)S(1)} %get-tuple-element.10, bf16[128,3072]{1,0:T(8,128)(2,1)S(1)} %get-tuple-element.9), kind=kOutput, calls=%fused_computation.191 | convolution fusion | flops 2423390208 | bytes 9437184 | tf_op jit(solution)/shard_map/dot_general | solution.py:21
  117.2 5.6 %fusion.130 = bf16[384,1024]{1,0:T(8,128)(2,1)S(1)} fusion(bf16[3072,6144]{1,0:T(8,128)(2,1)} %bitcast.48, bf16[128,3072]{1,0:T(8,128)(2,1)S(1)} %get-tuple-element.11, bf16[128,3072]{1,0:T(8,128)(2,1)S(1)} %get-tuple-element.10, bf16[128,3072]{1,0:T(8,128)(2,1)S(1)} %get-tuple-element.9), kind=kOutput, calls=%fused_computation.190 | convolution fusion | flops 2423390208 | bytes 9437184 | tf_op jit(solution)/shard_map/dot_general | solution.py:21
  122.8 8.7 %collective-permute-start.42 = (bf16[384,1024]{1,0:T(8,128)(2,1)S(1)}, bf16[384,1024]{1,0:T(8,128)(2,1)S(1)}, u32[]{:S(2)}, u32[]{:S(2)}) collective-permute-start(bf16[384,1024]{1,0:T(8,128)(2,1)S(1)} %fusion.127), channel_id=1, source_target_pairs={{0,4},{12,8},{1,5},{13,9},{2,6},{14,10},{3,7},{15,11},{16,20},{28,... | collective-permute-start | bytes 2359304 | tf_op jit(solution)/shard_map/ppermute | solution.py:42
  131.6 1.3 collective-permute-start.38
  133.3 1.3 collective-permute-start.34
  136.0 1.3 collective-permute-start.30
  138.2 1.3 collective-permute-start.26
  140.5 8.9 %collective-permute-done.42 = bf16[384,1024]{1,0:T(8,128)(2,1)S(1)} collective-permute-done((bf16[384,1024]{1,0:T(8,128)(2,1)S(1)}, bf16[384,1024]{1,0:T(8,128)(2,1)S(1)}, u32[]{:S(2)}, u32[]{:S(2)}) %collective-permute-start.42) | collective-permute-done | bytes 786464 | tf_op jit(solution)/shard_map/ppermute | solution.py:42
  149.4 4.4 collective-permute-start.22
  154.2 12.1 %collective-permute-done.38 = bf16[384,1024]{1,0:T(8,128)(2,1)S(1)} collective-permute-done((bf16[384,1024]{1,0:T(8,128)(2,1)S(1)}, bf16[384,1024]{1,0:T(8,128)(2,1)S(1)}, u32[]{:S(2)}, u32[]{:S(2)}) %collective-permute-start.38) | collective-permute-done | bytes 786464 | tf_op jit(solution)/shard_map/ppermute | solution.py:42
  166.3 1.3 collective-permute-start.3
  167.9 15.3 %collective-permute-done.34 = bf16[384,1024]{1,0:T(8,128)(2,1)S(1)} collective-permute-done((bf16[384,1024]{1,0:T(8,128)(2,1)S(1)}, bf16[384,1024]{1,0:T(8,128)(2,1)S(1)}, u32[]{:S(2)}, u32[]{:S(2)}) %collective-permute-start.34) | collective-permute-done | bytes 786464 | tf_op jit(solution)/shard_map/ppermute | solution.py:42
  183.1 1.3 collective-permute-start.7
  184.7 15.3 %collective-permute-done.30 = bf16[384,1024]{1,0:T(8,128)(2,1)S(1)} collective-permute-done((bf16[384,1024]{1,0:T(8,128)(2,1)S(1)}, bf16[384,1024]{1,0:T(8,128)(2,1)S(1)}, u32[]{:S(2)}, u32[]{:S(2)}) %collective-permute-start.30) | collective-permute-done | bytes 786464 | tf_op jit(solution)/shard_map/ppermute | solution.py:42
  201.0 15.8 %collective-permute-done.26 = bf16[384,1024]{1,0:T(8,128)(2,1)S(1)} collective-permute-done((bf16[384,1024]{1,0:T(8,128)(2,1)S(1)}, bf16[384,1024]{1,0:T(8,128)(2,1)S(1)}, u32[]{:S(2)}, u32[]{:S(2)}) %collective-permute-start.26) | collective-permute-done | bytes 786464 | tf_op jit(solution)/shard_map/ppermute | solution.py:42
  217.8 14.8 %collective-permute-done.22 = bf16[384,1024]{1,0:T(8,128)(2,1)S(1)} collective-permute-done((bf16[384,1024]{1,0:T(8,128)(2,1)S(1)}, bf16[384,1024]{1,0:T(8,128)(2,1)S(1)}, u32[]{:S(2)}, u32[]{:S(2)}) %collective-permute-start.22) | collective-permute-done | bytes 786464 | tf_op jit(solution)/shard_map/ppermute | solution.py:42
  241.4 1.4 fusion.78
  242.7 1.5 collective-permute-start.45
  244.3 1.4 fusion.74
  245.6 1.3 collective-permute-start.41
  246.9 1.4 fusion.62
  248.3 1.3 collective-permute-start.29
  249.6 1.4 fusion.58
  251.0 1.3 collective-permute-start.25
  252.3 1.4 fusion.66
  253.6 1.3 collective-permute-start.33
  254.9 1.4 fusion.70
  256.3 122.3 %collective-permute-done.25 = bf16[384,1024]{1,0:T(8,128)(2,1)S(1)} collective-permute-done((bf16[384,1024]{1,0:T(8,128)(2,1)S(1)}, bf16[384,1024]{1,0:T(8,128)(2,1)S(1)}, u32[]{:S(2)}, u32[]{:S(2)}) %collective-permute-start.25) | collective-permute-done | bytes 786464 | tf_op jit(solution)/shard_map/ppermute | solution.py:47
  378.6 1.3 collective-permute-start.37
  379.8 1.3 select_dynamic-update-slice_fusion.5
  381.1 1.3 select_dynamic-update-slice_fusion.4
  382.4 13.0 %collective-permute-done.33 = bf16[384,1024]{1,0:T(8,128)(2,1)S(1)} collective-permute-done((bf16[384,1024]{1,0:T(8,128)(2,1)S(1)}, bf16[384,1024]{1,0:T(8,128)(2,1)S(1)}, u32[]{:S(2)}, u32[]{:S(2)}) %collective-permute-start.33) | collective-permute-done | bytes 786464 | tf_op jit(solution)/shard_map/ppermute | solution.py:47
  396.6 15.0 %collective-permute-done.37 = bf16[384,1024]{1,0:T(8,128)(2,1)S(1)} collective-permute-done((bf16[384,1024]{1,0:T(8,128)(2,1)S(1)}, bf16[384,1024]{1,0:T(8,128)(2,1)S(1)}, u32[]{:S(2)}, u32[]{:S(2)}) %collective-permute-start.37) | collective-permute-done | bytes 786464 | tf_op jit(solution)/shard_map/ppermute | solution.py:47
  412.9 1.3 select_dynamic-update-slice_fusion.1
  414.1 1.2 select_dynamic-update-slice_fusion
  415.4 21.4 %convolution_convert_fusion = bf16[384,3072]{1,0:T(8,128)(2,1)S(1)} fusion(bf16[384,6144]{1,0:T(8,128)(2,1)} %select_dynamic-update-slice_fusion, bf16[1,3072,6144]{2,1,0:T(8,128)(2,1)} %param.5), kind=kOutput, calls=%fused_computation.30 | convolution fusion | flops 14496694272 | bytes 44826624 | tf_op jit(solution)/shard_map/dot_general | solution.py:21
  436.7 1.4 fusion.201
  439.1 2.5 collective-permute-start.48
  441.6 28.1 %convert_bitcast_fusion = bf16[1,3072,6144]{2,1,0:T(8,128)(2,1)} fusion(bf16[384,6144]{1,0:T(8,128)(2,1)} %select_dynamic-update-slice_fusion, bf16[128,1024]{1,0:T(8,128)(2,1)} %broadcast_select_fusion.3, bf16[128,1024]{1,0:T(8,128)(2,1)S(1)} %broadcast_select_fusion.4, bf16[128,2048]{1,0:T(8,128)(2,1)} %broadcast_select_fusion.1, ...), kind=kOutput, calls=%fused_computation | convolution fusion | flops 19390267392 | bytes 47185920 | tf_op jit(solution)/shard_map/dot_general | solution.py:21
  469.7 4.7 collective-permute-done.47
  474.5 19.9 %fusion.34 = bf16[1,128,3072]{2,1,0:T(8,128)(2,1)} fusion(bf16[128,1024]{1,0:T(8,128)(2,1)S(1)} %copy-done.6, bf16[128,1024]{1,0:T(8,128)(2,1)S(1)} %broadcast_select_fusion.4, bf16[128,2048]{1,0:T(8,128)(2,1)S(1)} %copy-done.5, bf16[128,2048]{1,0:T(8,128)(2,1)S(1)} %copy-done.4, bf16[128,3072]{1,0:T(8,128)(2,1)} %collective-permute-done.48, ...), kind=kOutput, calls=%fused_computation.37 | convolution fusion | flops 4841668608 | bytes 42467328 | tf_op jit(solution)/shard_map/dot_general | solution.py:21
  (115 shorter events, 26.8 us)
Async XLA Ops:
  17.2 24.0 %copy-start = (bf16[128,3072]{1,0:T(8,128)(2,1)}, bf16[128,3072]{1,0:T(8,128)(2,1)S(1)}, u32[]{:S(2)}) copy-start(bf16[128,3072]{1,0:T(8,128)(2,1)S(1)} %get-tuple-element.4) | copy-start | bytes 2359300
  17.2 67.5 %collective-permute-start.16 = (bf16[128,3072]{1,0:T(8,128)(2,1)S(1)}, bf16[128,3072]{1,0:T(8,128)(2,1)S(1)}, u32[]{:S(2)}, u32[]{:S(2)}) collective-permute-start(bf16[128,3072]{1,0:T(8,128)(2,1)S(1)} %get-tuple-element.5), channel_id=1, source_target_pairs={{0,1},{1,0},{2,3},{3,2},{4,5},{5,4},{6,7},{7,6},{8,9},{9,8},{10,11... | collective-permute-start | bytes 2359304 | tf_op jit(solution)/shard_map/ppermute | solution.py:26
  18.7 67.3 %collective-permute-start.18 = (bf16[128,3072]{1,0:T(8,128)(2,1)S(1)}, bf16[128,3072]{1,0:T(8,128)(2,1)S(1)}, u32[]{:S(2)}, u32[]{:S(2)}) collective-permute-start(bf16[128,3072]{1,0:T(8,128)(2,1)S(1)} %get-tuple-element.5), channel_id=1, source_target_pairs={{0,2},{1,3},{2,0},{3,1},{4,6},{5,7},{6,4},{7,5},{8,10},{9,11},{10,... | collective-permute-start | bytes 2359304 | tf_op jit(solution)/shard_map/ppermute | solution.py:26
  20.3 25.4 %collective-permute-start.17 = (f32[2,128]{1,0:T(2,128)S(1)}, f32[2,128]{1,0:T(2,128)S(1)}, u32[]{:S(2)}, u32[]{:S(2)}) collective-permute-start(f32[2,128]{1,0:T(2,128)S(1)} %pad_maximum_fusion.2), channel_id=1, source_target_pairs={{0,1},{1,0},{2,3},{3,2},{4,5},{5,4},{6,7},{7,6},{8,9},{9,8},{10,11... | collective-permute-start | bytes 3080 | tf_op jit(solution)/shard_map/ppermute | solution.py:26
  20.8 26.2 %collective-permute-start.19 = (f32[2,128]{1,0:T(2,128)S(1)}, f32[2,128]{1,0:T(2,128)S(1)}, u32[]{:S(2)}, u32[]{:S(2)}) collective-permute-start(f32[2,128]{1,0:T(2,128)S(1)} %pad_maximum_fusion.2), channel_id=1, source_target_pairs={{0,2},{1,3},{2,0},{3,1},{4,6},{5,7},{6,4},{7,5},{8,10},{9,11},{10,... | collective-permute-start | bytes 3080 | tf_op jit(solution)/shard_map/ppermute | solution.py:26
  21.3 39.7 %collective-permute-start.21 = (f32[2,128]{1,0:T(2,128)S(1)}, f32[2,128]{1,0:T(2,128)S(1)}, u32[]{:S(2)}, u32[]{:S(2)}) collective-permute-start(f32[2,128]{1,0:T(2,128)S(1)} %pad_maximum_fusion.2), channel_id=1, source_target_pairs={{0,3},{1,2},{2,1},{3,0},{4,7},{5,6},{6,5},{7,4},{8,11},{9,10},{10,... | collective-permute-start | bytes 3080 | tf_op jit(solution)/shard_map/ppermute | solution.py:26
  45.7 8.0 %collective-permute-start.8 = (bf16[128,1024]{1,0:T(8,128)(2,1)}, bf16[128,1024]{1,0:T(8,128)(2,1)S(1)}, u32[]{:S(2)}, u32[]{:S(2)}) collective-permute-start(bf16[128,1024]{1,0:T(8,128)(2,1)} %fusion.142), channel_id=1, source_target_pairs={{0,4},{12,8},{1,5},{13,9},{2,6},{14,10},{3,7},{15,11},{16,20},{28,... | collective-permute-start | bytes 786440 | tf_op jit(solution)/shard_map/ppermute | solution.py:42
  47.0 12.3 %collective-permute-start.12 = (bf16[128,1024]{1,0:T(8,128)(2,1)}, bf16[128,1024]{1,0:T(8,128)(2,1)S(1)}, u32[]{:S(2)}, u32[]{:S(2)}) collective-permute-start(bf16[128,1024]{1,0:T(8,128)(2,1)} %fusion.145), channel_id=1, source_target_pairs={{0,4},{12,8},{1,5},{13,9},{2,6},{14,10},{3,7},{15,11},{16,20},{28,... | collective-permute-start | bytes 786440 | tf_op jit(solution)/shard_map/ppermute | solution.py:42
  53.7 21.7 %collective-permute-start = (bf16[128,2048]{1,0:T(8,128)(2,1)S(1)}, bf16[128,2048]{1,0:T(8,128)(2,1)S(1)}, u32[]{:S(2)}, u32[]{:S(2)}) collective-permute-start(bf16[128,2048]{1,0:T(8,128)(2,1)S(1)} %fusion.42), channel_id=1, source_target_pairs={{0,4},{12,8},{1,5},{13,9},{2,6},{14,10},{3,7},{15,11},{16,20},{28,... | collective-permute-start | bytes 1572872 | tf_op jit(solution)/shard_map/ppermute | solution.py:42
  59.3 2.4 collective-permute-start.9
  61.0 1.3 collective-permute-start.13
  61.7 26.1 %collective-permute-start.20 = (bf16[128,3072]{1,0:T(8,128)(2,1)S(1)}, bf16[128,3072]{1,0:T(8,128)(2,1)S(1)}, u32[]{:S(2)}, u32[]{:S(2)}) collective-permute-start(bf16[128,3072]{1,0:T(8,128)(2,1)S(1)} %get-tuple-element.5), channel_id=1, source_target_pairs={{0,3},{1,2},{2,1},{3,0},{4,7},{5,6},{6,5},{7,4},{8,11},{9,10},{10,... | collective-permute-start | bytes 2359304 | tf_op jit(solution)/shard_map/ppermute | solution.py:26
  62.4 19.6 %collective-permute-start.4 = (bf16[128,2048]{1,0:T(8,128)(2,1)S(1)}, bf16[128,2048]{1,0:T(8,128)(2,1)S(1)}, u32[]{:S(2)}, u32[]{:S(2)}) collective-permute-start(bf16[128,2048]{1,0:T(8,128)(2,1)S(1)} %fusion.45), channel_id=1, source_target_pairs={{0,4},{12,8},{1,5},{13,9},{2,6},{14,10},{3,7},{15,11},{16,20},{28,... | collective-permute-start | bytes 1572872 | tf_op jit(solution)/shard_map/ppermute | solution.py:42
  75.4 6.7 %collective-permute-start.10 = (bf16[128,1024]{1,0:T(8,128)(2,1)S(1)}, bf16[128,1024]{1,0:T(8,128)(2,1)S(1)}, u32[]{:S(2)}, u32[]{:S(2)}) collective-permute-start(bf16[128,1024]{1,0:T(8,128)(2,1)S(1)} %add_convert_fusion.18), channel_id=1, source_target_pairs={{0,16},{16,0},{1,17},{17,1},{2,18},{18,2},{3,19},{19,3},{4,20},{20... | collective-permute-start | bytes 786440 | tf_op jit(solution)/shard_map/ppermute | solution.py:30
  75.6 12.2 %copy-start.7 = (f32[3072]{0:T(1024)S(1)}, f32[3072]{0:T(1024)}, u32[]{:S(2)}) copy-start(f32[3072]{0:T(1024)} %param.6) | copy-start | bytes 36868
  82.0 1.5 collective-permute-start.14
  82.1 49.4 %collective-permute-start.1 = (bf16[128,2048]{1,0:T(8,128)(2,1)S(1)}, bf16[128,2048]{1,0:T(8,128)(2,1)S(1)}, u32[]{:S(2)}, u32[]{:S(2)}) collective-permute-start(bf16[128,2048]{1,0:T(8,128)(2,1)S(1)} %add_convert_fusion.15), channel_id=1, source_target_pairs={{4,8},{8,4},{5,9},{9,5},{6,10},{10,6},{7,11},{11,7},{20,24},{24,20... | collective-permute-start | bytes 1572872 | tf_op jit(solution)/shard_map/ppermute | solution.py:44
  83.5 49.5 %collective-permute-start.5 = (bf16[128,2048]{1,0:T(8,128)(2,1)S(1)}, bf16[128,2048]{1,0:T(8,128)(2,1)S(1)}, u32[]{:S(2)}, u32[]{:S(2)}) collective-permute-start(bf16[128,2048]{1,0:T(8,128)(2,1)S(1)} %add_convert_fusion.13), channel_id=1, source_target_pairs={{4,8},{8,4},{5,9},{9,5},{6,10},{10,6},{7,11},{11,7},{20,24},{24,20... | collective-permute-start | bytes 1572872 | tf_op jit(solution)/shard_map/ppermute | solution.py:44
  84.7 48.6 %collective-permute-start.11 = (bf16[128,1024]{1,0:T(8,128)(2,1)S(1)}, bf16[128,1024]{1,0:T(8,128)(2,1)S(1)}, u32[]{:S(2)}, u32[]{:S(2)}) collective-permute-start(bf16[128,1024]{1,0:T(8,128)(2,1)S(1)} %fusion.177), channel_id=1, source_target_pairs={{4,0},{8,12},{5,1},{9,13},{6,2},{10,14},{7,3},{11,15},{20,16},{24,... | collective-permute-start | bytes 786440 | tf_op jit(solution)/shard_map/ppermute | solution.py:47
  86.0 48.7 %collective-permute-start.15 = (bf16[128,1024]{1,0:T(8,128)(2,1)S(1)}, bf16[128,1024]{1,0:T(8,128)(2,1)S(1)}, u32[]{:S(2)}, u32[]{:S(2)}) collective-permute-start(bf16[128,1024]{1,0:T(8,128)(2,1)S(1)} %fusion.181), channel_id=1, source_target_pairs={{4,0},{8,12},{5,1},{9,13},{6,2},{10,14},{7,3},{11,15},{20,16},{24,... | collective-permute-start | bytes 786440 | tf_op jit(solution)/shard_map/ppermute | solution.py:47
  89.1 28.1 %copy-start.1 = (bf16[128,3072]{1,0:T(8,128)(2,1)}, bf16[128,3072]{1,0:T(8,128)(2,1)S(1)}, u32[]{:S(2)}) copy-start(bf16[128,3072]{1,0:T(8,128)(2,1)S(1)} %get-tuple-element.9) | copy-start | bytes 2359300
  89.1 28.1 %copy-start.2 = (bf16[128,3072]{1,0:T(8,128)(2,1)}, bf16[128,3072]{1,0:T(8,128)(2,1)S(1)}, u32[]{:S(2)}) copy-start(bf16[128,3072]{1,0:T(8,128)(2,1)S(1)} %get-tuple-element.10) | copy-start | bytes 2359300
  89.1 28.1 %copy-start.3 = (bf16[128,3072]{1,0:T(8,128)(2,1)}, bf16[128,3072]{1,0:T(8,128)(2,1)S(1)}, u32[]{:S(2)}) copy-start(bf16[128,3072]{1,0:T(8,128)(2,1)S(1)} %get-tuple-element.11) | copy-start | bytes 2359300
  122.8 26.6 %collective-permute-start.42 = (bf16[384,1024]{1,0:T(8,128)(2,1)S(1)}, bf16[384,1024]{1,0:T(8,128)(2,1)S(1)}, u32[]{:S(2)}, u32[]{:S(2)}) collective-permute-start(bf16[384,1024]{1,0:T(8,128)(2,1)S(1)} %fusion.127), channel_id=1, source_target_pairs={{0,4},{12,8},{1,5},{13,9},{2,6},{14,10},{3,7},{15,11},{16,20},{28,... | collective-permute-start | bytes 2359304 | tf_op jit(solution)/shard_map/ppermute | solution.py:42
  131.6 34.7 %collective-permute-start.38 = (bf16[384,1024]{1,0:T(8,128)(2,1)S(1)}, bf16[384,1024]{1,0:T(8,128)(2,1)S(1)}, u32[]{:S(2)}, u32[]{:S(2)}) collective-permute-start(bf16[384,1024]{1,0:T(8,128)(2,1)S(1)} %fusion.124), channel_id=1, source_target_pairs={{0,4},{12,8},{1,5},{13,9},{2,6},{14,10},{3,7},{15,11},{16,20},{28,... | collective-permute-start | bytes 2359304 | tf_op jit(solution)/shard_map/ppermute | solution.py:42
  133.1 2.9 collective-permute-start.2
  133.3 49.8 %collective-permute-start.34 = (bf16[384,1024]{1,0:T(8,128)(2,1)S(1)}, bf16[384,1024]{1,0:T(8,128)(2,1)S(1)}, u32[]{:S(2)}, u32[]{:S(2)}) collective-permute-start(bf16[384,1024]{1,0:T(8,128)(2,1)S(1)} %fusion.139), channel_id=1, source_target_pairs={{0,4},{12,8},{1,5},{13,9},{2,6},{14,10},{3,7},{15,11},{16,20},{28,... | collective-permute-start | bytes 2359304 | tf_op jit(solution)/shard_map/ppermute | solution.py:42
  134.7 3.5 collective-permute-start.6
  136.0 64.0 %collective-permute-start.30 = (bf16[384,1024]{1,0:T(8,128)(2,1)S(1)}, bf16[384,1024]{1,0:T(8,128)(2,1)S(1)}, u32[]{:S(2)}, u32[]{:S(2)}) collective-permute-start(bf16[384,1024]{1,0:T(8,128)(2,1)S(1)} %fusion.136), channel_id=1, source_target_pairs={{0,4},{12,8},{1,5},{13,9},{2,6},{14,10},{3,7},{15,11},{16,20},{28,... | collective-permute-start | bytes 2359304 | tf_op jit(solution)/shard_map/ppermute | solution.py:42
  138.2 78.6 %collective-permute-start.26 = (bf16[384,1024]{1,0:T(8,128)(2,1)S(1)}, bf16[384,1024]{1,0:T(8,128)(2,1)S(1)}, u32[]{:S(2)}, u32[]{:S(2)}) collective-permute-start(bf16[384,1024]{1,0:T(8,128)(2,1)S(1)} %fusion.133), channel_id=1, source_target_pairs={{0,4},{12,8},{1,5},{13,9},{2,6},{14,10},{3,7},{15,11},{16,20},{28,... | collective-permute-start | bytes 2359304 | tf_op jit(solution)/shard_map/ppermute | solution.py:42
  149.4 83.2 %collective-permute-start.22 = (bf16[384,1024]{1,0:T(8,128)(2,1)S(1)}, bf16[384,1024]{1,0:T(8,128)(2,1)S(1)}, u32[]{:S(2)}, u32[]{:S(2)}) collective-permute-start(bf16[384,1024]{1,0:T(8,128)(2,1)S(1)} %fusion.130), channel_id=1, source_target_pairs={{0,4},{12,8},{1,5},{13,9},{2,6},{14,10},{3,7},{15,11},{16,20},{28,... | collective-permute-start | bytes 2359304 | tf_op jit(solution)/shard_map/ppermute | solution.py:42
  166.3 67.4 %collective-permute-start.3 = (bf16[128,2048]{1,0:T(8,128)(2,1)S(1)}, bf16[128,2048]{1,0:T(8,128)(2,1)S(1)}, u32[]{:S(2)}, u32[]{:S(2)}) collective-permute-start(bf16[128,2048]{1,0:T(8,128)(2,1)S(1)} %fusion.155), channel_id=1, source_target_pairs={{4,0},{8,12},{5,1},{9,13},{6,2},{10,14},{7,3},{11,15},{20,16},{24,... | collective-permute-start | bytes 1572872 | tf_op jit(solution)/shard_map/ppermute | solution.py:47
  183.1 52.2 %collective-permute-start.7 = (bf16[128,2048]{1,0:T(8,128)(2,1)S(1)}, bf16[128,2048]{1,0:T(8,128)(2,1)S(1)}, u32[]{:S(2)}, u32[]{:S(2)}) collective-permute-start(bf16[128,2048]{1,0:T(8,128)(2,1)S(1)} %fusion.159), channel_id=1, source_target_pairs={{4,0},{8,12},{5,1},{9,13},{6,2},{10,14},{7,3},{11,15},{20,16},{24,... | collective-permute-start | bytes 1572872 | tf_op jit(solution)/shard_map/ppermute | solution.py:47
  200.0 36.9 %collective-permute-start.43 = (bf16[384,1024]{1,0:T(8,128)(2,1)S(1)}, bf16[384,1024]{1,0:T(8,128)(2,1)S(1)}, u32[]{:S(2)}, u32[]{:S(2)}) collective-permute-start(bf16[384,1024]{1,0:T(8,128)(2,1)S(1)} %add_convert_fusion.1), channel_id=1, source_target_pairs={{4,8},{8,4},{5,9},{9,5},{6,10},{10,6},{7,11},{11,7},{20,24},{24,20... | collective-permute-start | bytes 2359304 | tf_op jit(solution)/shard_map/ppermute | solution.py:44
  216.8 21.0 %collective-permute-start.39 = (bf16[384,1024]{1,0:T(8,128)(2,1)S(1)}, bf16[384,1024]{1,0:T(8,128)(2,1)S(1)}, u32[]{:S(2)}, u32[]{:S(2)}) collective-permute-start(bf16[384,1024]{1,0:T(8,128)(2,1)S(1)} %add_convert_fusion.3), channel_id=1, source_target_pairs={{4,8},{8,4},{5,9},{9,5},{6,10},{10,6},{7,11},{11,7},{20,24},{24,20... | collective-permute-start | bytes 2359304 | tf_op jit(solution)/shard_map/ppermute | solution.py:44
  232.7 5.6 %collective-permute-start.35 = (bf16[384,1024]{1,0:T(8,128)(2,1)S(1)}, bf16[384,1024]{1,0:T(8,128)(2,1)S(1)}, u32[]{:S(2)}, u32[]{:S(2)}) collective-permute-start(bf16[384,1024]{1,0:T(8,128)(2,1)S(1)} %add_convert_fusion.5), channel_id=1, source_target_pairs={{4,8},{8,4},{5,9},{9,5},{6,10},{10,6},{7,11},{11,7},{20,24},{24,20... | collective-permute-start | bytes 2359304 | tf_op jit(solution)/shard_map/ppermute | solution.py:44
  233.7 5.4 %collective-permute-start.31 = (bf16[384,1024]{1,0:T(8,128)(2,1)S(1)}, bf16[384,1024]{1,0:T(8,128)(2,1)S(1)}, u32[]{:S(2)}, u32[]{:S(2)}) collective-permute-start(bf16[384,1024]{1,0:T(8,128)(2,1)S(1)} %add_convert_fusion.7), channel_id=1, source_target_pairs={{4,8},{8,4},{5,9},{9,5},{6,10},{10,6},{7,11},{11,7},{20,24},{24,20... | collective-permute-start | bytes 2359304 | tf_op jit(solution)/shard_map/ppermute | solution.py:44
  235.3 4.3 collective-permute-start.27
  236.8 3.6 collective-permute-start.23
  237.9 3.0 collective-permute-start.44
  238.3 4.5 collective-permute-start.40
  239.1 14.5 %collective-permute-start.36 = (bf16[384,1024]{1,0:T(8,128)(2,1)S(1)}, bf16[384,1024]{1,0:T(8,128)(2,1)S(1)}, u32[]{:S(2)}, u32[]{:S(2)}) collective-permute-start(bf16[384,1024]{1,0:T(8,128)(2,1)S(1)} %add_convert_fusion.4), channel_id=1, source_target_pairs={{0,16},{16,0},{1,17},{17,1},{2,18},{18,2},{3,19},{19,3},{4,20},{20... | collective-permute-start | bytes 2359304 | tf_op jit(solution)/shard_map/ppermute | solution.py:30
  239.5 11.4 %collective-permute-start.32 = (bf16[384,1024]{1,0:T(8,128)(2,1)S(1)}, bf16[384,1024]{1,0:T(8,128)(2,1)S(1)}, u32[]{:S(2)}, u32[]{:S(2)}) collective-permute-start(bf16[384,1024]{1,0:T(8,128)(2,1)S(1)} %add_convert_fusion.6), channel_id=1, source_target_pairs={{0,16},{16,0},{1,17},{17,1},{2,18},{18,2},{3,19},{19,3},{4,20},{20... | collective-permute-start | bytes 2359304 | tf_op jit(solution)/shard_map/ppermute | solution.py:30
  240.4 5.2 %collective-permute-start.28 = (bf16[384,1024]{1,0:T(8,128)(2,1)S(1)}, bf16[384,1024]{1,0:T(8,128)(2,1)S(1)}, u32[]{:S(2)}, u32[]{:S(2)}) collective-permute-start(bf16[384,1024]{1,0:T(8,128)(2,1)S(1)} %add_convert_fusion.8), channel_id=1, source_target_pairs={{0,16},{16,0},{1,17},{17,1},{2,18},{18,2},{3,19},{19,3},{4,20},{20... | collective-permute-start | bytes 2359304 | tf_op jit(solution)/shard_map/ppermute | solution.py:30
  240.8 7.5 %collective-permute-start.24 = (bf16[384,1024]{1,0:T(8,128)(2,1)S(1)}, bf16[384,1024]{1,0:T(8,128)(2,1)S(1)}, u32[]{:S(2)}, u32[]{:S(2)}) collective-permute-start(bf16[384,1024]{1,0:T(8,128)(2,1)S(1)} %add_convert_fusion.10), channel_id=1, source_target_pairs={{0,16},{16,0},{1,17},{17,1},{2,18},{18,2},{3,19},{19,3},{4,20},{20... | collective-permute-start | bytes 2359304 | tf_op jit(solution)/shard_map/ppermute | solution.py:30
  242.7 171.4 %collective-permute-start.45 = (bf16[384,1024]{1,0:T(8,128)(2,1)S(1)}, bf16[384,1024]{1,0:T(8,128)(2,1)S(1)}, u32[]{:S(2)}, u32[]{:S(2)}) collective-permute-start(bf16[384,1024]{1,0:T(8,128)(2,1)S(1)} %fusion.78), channel_id=1, source_target_pairs={{4,0},{8,12},{5,1},{9,13},{6,2},{10,14},{7,3},{11,15},{20,16},{24,... | collective-permute-start | bytes 2359304 | tf_op jit(solution)/shard_map/ppermute | solution.py:47
  245.6 167.2 %collective-permute-start.41 = (bf16[384,1024]{1,0:T(8,128)(2,1)S(1)}, bf16[384,1024]{1,0:T(8,128)(2,1)S(1)}, u32[]{:S(2)}, u32[]{:S(2)}) collective-permute-start(bf16[384,1024]{1,0:T(8,128)(2,1)S(1)} %fusion.74), channel_id=1, source_target_pairs={{4,0},{8,12},{5,1},{9,13},{6,2},{10,14},{7,3},{11,15},{20,16},{24,... | collective-permute-start | bytes 2359304 | tf_op jit(solution)/shard_map/ppermute | solution.py:47
  248.3 132.8 %collective-permute-start.29 = (bf16[384,1024]{1,0:T(8,128)(2,1)S(1)}, bf16[384,1024]{1,0:T(8,128)(2,1)S(1)}, u32[]{:S(2)}, u32[]{:S(2)}) collective-permute-start(bf16[384,1024]{1,0:T(8,128)(2,1)S(1)} %fusion.62), channel_id=1, source_target_pairs={{4,0},{8,12},{5,1},{9,13},{6,2},{10,14},{7,3},{11,15},{20,16},{24,... | collective-permute-start | bytes 2359304 | tf_op jit(solution)/shard_map/ppermute | solution.py:47
  251.0 127.6 %collective-permute-start.25 = (bf16[384,1024]{1,0:T(8,128)(2,1)S(1)}, bf16[384,1024]{1,0:T(8,128)(2,1)S(1)}, u32[]{:S(2)}, u32[]{:S(2)}) collective-permute-start(bf16[384,1024]{1,0:T(8,128)(2,1)S(1)} %fusion.58), channel_id=1, source_target_pairs={{4,0},{8,12},{5,1},{9,13},{6,2},{10,14},{7,3},{11,15},{20,16},{24,... | collective-permute-start | bytes 2359304 | tf_op jit(solution)/shard_map/ppermute | solution.py:47
  253.6 141.8 %collective-permute-start.33 = (bf16[384,1024]{1,0:T(8,128)(2,1)S(1)}, bf16[384,1024]{1,0:T(8,128)(2,1)S(1)}, u32[]{:S(2)}, u32[]{:S(2)}) collective-permute-start(bf16[384,1024]{1,0:T(8,128)(2,1)S(1)} %fusion.66), channel_id=1, source_target_pairs={{4,0},{8,12},{5,1},{9,13},{6,2},{10,14},{7,3},{11,15},{20,16},{24,... | collective-permute-start | bytes 2359304 | tf_op jit(solution)/shard_map/ppermute | solution.py:47
  378.6 33.1 %collective-permute-start.37 = (bf16[384,1024]{1,0:T(8,128)(2,1)S(1)}, bf16[384,1024]{1,0:T(8,128)(2,1)S(1)}, u32[]{:S(2)}, u32[]{:S(2)}) collective-permute-start(bf16[384,1024]{1,0:T(8,128)(2,1)S(1)} %fusion.70), channel_id=1, source_target_pairs={{4,0},{8,12},{5,1},{9,13},{6,2},{10,14},{7,3},{11,15},{20,16},{24,... | collective-permute-start | bytes 2359304 | tf_op jit(solution)/shard_map/ppermute | solution.py:47
  438.1 31.6 %collective-permute-start.46 = (bf16[128,3072]{1,0:T(8,128)(2,1)}, bf16[128,3072]{1,0:T(8,128)(2,1)S(1)}, u32[]{:S(2)}, u32[]{:S(2)}) collective-permute-start(bf16[128,3072]{1,0:T(8,128)(2,1)} %get-tuple-element.6), channel_id=1, source_target_pairs={{0,1},{1,0},{2,3},{3,2},{4,5},{5,4},{6,7},{7,6},{8,9},{9,8},{10,11... | collective-permute-start | bytes 2359304 | tf_op jit(solution)/shard_map/ppermute | solution.py:26
  438.6 35.8 %collective-permute-start.47 = (bf16[128,3072]{1,0:T(8,128)(2,1)}, bf16[128,3072]{1,0:T(8,128)(2,1)}, u32[]{:S(2)}, u32[]{:S(2)}) collective-permute-start(bf16[128,3072]{1,0:T(8,128)(2,1)} %get-tuple-element.8), channel_id=1, source_target_pairs={{0,2},{1,3},{2,0},{3,1},{4,6},{5,7},{6,4},{7,5},{8,10},{9,11},{10,... | collective-permute-start | bytes 2359304 | tf_op jit(solution)/shard_map/ppermute | solution.py:26
  439.1 35.3 %copy-start.4 = (bf16[128,2048]{1,0:T(8,128)(2,1)S(1)}, bf16[128,2048]{1,0:T(8,128)(2,1)}, u32[]{:S(2)}) copy-start(bf16[128,2048]{1,0:T(8,128)(2,1)} %broadcast_select_fusion.2) | copy-start | bytes 1572868
  439.1 35.3 %copy-start.5 = (bf16[128,2048]{1,0:T(8,128)(2,1)S(1)}, bf16[128,2048]{1,0:T(8,128)(2,1)}, u32[]{:S(2)}) copy-start(bf16[128,2048]{1,0:T(8,128)(2,1)} %broadcast_select_fusion.1) | copy-start | bytes 1572868
  439.1 35.3 %copy-start.6 = (bf16[128,1024]{1,0:T(8,128)(2,1)S(1)}, bf16[128,1024]{1,0:T(8,128)(2,1)}, u32[]{:S(2)}) copy-start(bf16[128,1024]{1,0:T(8,128)(2,1)} %broadcast_select_fusion.3) | copy-start | bytes 786436
  439.1 35.3 %collective-permute-start.48 = (bf16[128,3072]{1,0:T(8,128)(2,1)S(1)}, bf16[128,3072]{1,0:T(8,128)(2,1)}, u32[]{:S(2)}, u32[]{:S(2)}) collective-permute-start(bf16[128,3072]{1,0:T(8,128)(2,1)S(1)} %get-tuple-element.7), channel_id=1, source_target_pairs={{0,3},{1,2},{2,1},{3,0},{4,7},{5,6},{6,5},{7,4},{8,11},{9,10},{10,... | collective-permute-start | bytes 2359304 | tf_op jit(solution)/shard_map/ppermute | solution.py:26

commit v2 on v1

v2 whole, which is shorter than its diff:
```python
import jax
import jax.numpy as jnp
from jax import lax
from jax.experimental import pallas as pl
from jax.experimental.pallas import tpu as pltpu
from jax.sharding import PartitionSpec as P

D = 12288
VMEM = 40 * 1024 * 1024
FAR, NEAR = 0, 1


epsilon = 1e-05


def dot_f32(left, right, contract):
    return lax.dot_general(
        left, right, ((contract[:1], contract[1:]), ((), ())), preferred_element_type=jnp.float32
    )


def tile_of(extent, limit):
    return max(t for t in range(128, limit + 1, 128) if extent % t == 0)


def call(kernel, name, grid, scalars, operands, in_specs, out_specs, out_shape, scratch=(), aliases={}):
    return pl.pallas_call(
        kernel,
        grid_spec=pltpu.PrefetchScalarGridSpec(
            num_scalar_prefetch=len(scalars),
            grid=grid,
            in_specs=in_specs,
            out_specs=out_specs,
            scratch_shapes=list(scratch),
        ),
        out_shape=out_shape,
        input_output_aliases=aliases,
        compiler_params=pltpu.CompilerParams(vmem_limit_bytes=VMEM),
        name=name,
    )(*scalars, *operands)


def normalize(first, blocks, scale, gain, group, into):
    rows, width = blocks[0].shape
    count = rows * len(blocks)
    tile = tile_of(width, 768)

    def kernel(first_ref, scale_ref, gain_ref, *refs):
        out = refs[-1]
        for i, ref in enumerate(refs[: len(blocks)]):
            own = pl.ds(i * rows, rows)
            value = ref[...].astype(jnp.float32)
            centred = (value - scale_ref[own, 0:1]) * scale_ref[own, 1:2]
            normed = (centred * gain_ref[...]).astype(jnp.bfloat16)
            out[own, :] = jnp.where(first_ref[0] == 1, normed, ref[...])

    column = lambda i, _: (0, i)
    extra = [] if into is None else [into]
    return call(
        kernel,
        "normalize",
        (width // tile,),
        [first],
        [scale, gain.reshape(1, width), *blocks, *extra],
        [pl.BlockSpec((count, 2), lambda i, _: (0, 0)), pl.BlockSpec((1, tile), column)]
        + [pl.BlockSpec((rows, tile), column)] * len(blocks)
        + [pl.BlockSpec(memory_space=pl.ANY)] * len(extra),
        pl.BlockSpec((count, tile), lambda i, _: (group, i)),
        jax.ShapeDtypeStruct((2 * count, width), jnp.bfloat16),
        aliases={3 + len(blocks): 0} if extra else {},
    )


def up_product(section, rows, weight, part, parts, groups):
    pieces = len(groups)
    count, width = rows.shape[0] // 2 * pieces, rows.shape[1]
    at = groups[0]
    columns = weight.shape[1] // parts
    tile = tile_of(columns // 2, 768)
    steps = columns // tile
    mine = steps // 2
    piece = count // pieces

    def kernel(section_ref, rows_ref, weight_ref, *results):
        product = dot_f32(rows_ref[...], weight_ref[...], (1, 0)).astype(jnp.bfloat16)

        def store(refs):
            for i, result in enumerate(refs):
                result[...] = product[i * piece : (i + 1) * piece]

        pl.when(pl.program_id(0) < mine)(lambda: store(results[:pieces]))
        pl.when(pl.program_id(0) >= mine)(lambda: store(results[pieces:]))

    column = lambda i, s: (0, part * steps + lax.rem(i + s[0] * mine, steps))
    return call(
        kernel,
        "up_product",
        (steps,),
        [section],
        [rows, weight],
        [pl.BlockSpec((count, width), lambda i, s: (at, 0)), pl.BlockSpec((width, tile), column)],
        [pl.BlockSpec((piece, tile), lambda i, s: (0, jnp.minimum(i, mine - 1)))] * pieces
        + [pl.BlockSpec((piece, tile), lambda i, s: (0, jnp.maximum(i - mine, 0)))] * pieces,
        [jax.ShapeDtypeStruct((piece, columns // 2), jnp.bfloat16)] * (2 * pieces),
    )


def elementwise(body, name, scalars, operands, out_rows):
    columns = operands[0].shape[1]
    tile = tile_of(columns, 256)
    column = lambda i, *_: (0, i)

    def kernel(*refs):
        scalar_refs = refs[: len(scalars)]
        ins = refs[len(scalars) : len(scalars) + len(operands)]
        outs = refs[len(scalars) + len(operands) :]
        for out, value in zip(outs, body(scalar_refs, ins)):
            out[...] = value

    return call(
        kernel,
        name,
        (columns // tile,),
        scalars,
        operands,
        [pl.BlockSpec((o.shape[0], tile), column) for o in operands],
        [pl.BlockSpec((r, tile), column) for r in out_rows],
        [jax.ShapeDtypeStruct((r, columns), jnp.bfloat16) for r in out_rows],
    )


def stacked(mine, arrived):
    rows = mine.shape[0]
    body = lambda _, ins: (jnp.concatenate([ins[0][...], ins[1][...]], 0),)
    return elementwise(body, "stacked", [], [mine, arrived], [2 * rows])[0]


def added(value, arrived):
    def body(_, ins):
        total = ins[0][...].astype(jnp.float32) + ins[1][...].astype(jnp.float32)
        return (total.astype(jnp.bfloat16),)

    return elementwise(body, "added", [], [value, arrived], [value.shape[0]])[0]


def activated(first, value, arrived):
    rows = value.shape[0] // 2

    def body(scalars, ins):
        is_first = scalars[0][0] == 1
        total = ins[0][...].astype(jnp.float32) + ins[1][...].astype(jnp.float32)
        above, below = total[:rows], total[rows:]
        v = jnp.where(is_first, above, below)
        grad = jnp.where(is_first, below, above)
        c = 0.7978845608028654
        t = jnp.tanh(c * (v + 0.044715 * (v * v * v)))
        hidden = (0.5 * v * (1.0 + t)).astype(jnp.bfloat16)
        slope = 0.5 * (1.0 + t) + 0.5 * v * (1.0 - t * t) * (c * (1.0 + 3.0 * 0.044715 * (v * v)))
        grad_preact = (grad * slope).astype(jnp.bfloat16)
        kept = jnp.where(is_first, grad_preact, hidden)
        sent = jnp.where(is_first, hidden, grad_preact)
        return (jnp.concatenate([kept, sent], 0),)

    return elementwise(body, "activated", [first], [value, arrived], [2 * rows])[0]


def chosen(receives, value, arrived, halves):
    rows = value.shape[0]

    def body(scalars, ins):
        result = jnp.where(scalars[0][0] == 1, ins[1][...], ins[0][...])
        return (result[: rows // 2], result[rows // 2 :]) if halves else (result,)

    out_rows = [rows // 2] * 2 if halves else [rows]
    return elementwise(body, "chosen", [receives], [value, arrived], out_rows)


def down_product(section, kept, came, weight, part, parts, before, before_row, kinds):
    counts = [k.shape[0] for k in kept]
    count, half = sum(counts), kept[0].shape[1]
    width = weight.shape[0]
    tile = tile_of(width, 256)
    piece = count // len(kinds)
    n = len(kept)

    def kernel(section_ref, *refs):
        weight_mine, weight_theirs = refs[2 * n : 2 * n + 2]
        results = refs[2 * n + 2 + (before is not None) : -2]
        held_mine, held_theirs = refs[-2:]

        @pl.when(pl.program_id(0) == 0)
        def _():
            at = 0
            for i, rows in enumerate(counts):
                held_mine[at : at + rows, :] = refs[i][...]
                held_theirs[at : at + rows, :] = refs[n + i][...]
                at += rows

        product = dot_f32(held_mine[...], weight_mine[...], (1, 1))
        product = product + dot_f32(held_theirs[...], weight_theirs[...], (1, 1))
        if before is not None:
            product = product + refs[2 * n + 2][...]
        for i, result in enumerate(results):
            result[...] = product[i * piece : (i + 1) * piece].astype(result.dtype)

    whole = [pl.BlockSpec((rows, half), lambda i, s: (0, 0)) for rows in counts]
    extra = [] if before is None else [before]
    return call(
        kernel,
        "down_product",
        (width // tile,),
        [section],
        [*kept, *came, weight, weight, *extra],
        whole
        + whole
        + [
            pl.BlockSpec((tile, half), lambda i, s: (i, 2 * part + s[0])),
            pl.BlockSpec((tile, half), lambda i, s: (i, 2 * part + 1 - s[0])),
        ]
        + [pl.BlockSpec((count, tile), lambda i, s: (before_row, i))] * len(extra),
        [pl.BlockSpec((piece, tile), lambda i, s: (0, i))] * len(kinds),
        [jax.ShapeDtypeStruct((piece, width), kind) for kind in kinds],
        [pltpu.VMEM((count, half), jnp.bfloat16)] * 2,
    )


def weight_gradient(section, turned, kept, came, part, parts, into):
    width, count = turned.shape
    counts = [k.shape[0] for k in kept]
    half = kept[0].shape[1]
    tile = tile_of(width, 512)
    n = len(kept)

    def kernel(section_ref, turned_ref, *refs):
        out, held = refs[-2:]

        def hold(blocks):
            at = 0
            for rows, block in zip(counts, blocks):
                held[at : at + rows, :] = block[...]
                at += rows

        start = pl.program_id(1) == 0
        pl.when(jnp.logical_and(start, pl.program_id(0) == 0))(lambda: hold(refs[:n]))
        pl.when(jnp.logical_and(start, pl.program_id(0) == 1))(lambda: hold(refs[n : 2 * n]))
        out[...] = dot_f32(turned_ref[...], held[...], (1, 0)).astype(jnp.bfloat16)

    whole = [pl.BlockSpec((rows, half), lambda j, i, s: (0, 0)) for rows in counts]
    extra = [] if into is None else [into]
    return call(
        kernel,
        "weight_gradient",
        (2, width // tile),
        [section],
        [turned, *kept, *came, *extra],
        [pl.BlockSpec((tile, count), lambda j, i, s: (i, 0))]
        + whole
        + whole
        + [pl.BlockSpec(memory_space=pl.ANY)] * len(extra),
        pl.BlockSpec((tile, half), lambda j, i, s: (i, 2 * part + lax.rem(j + s[0], 2))),
        jax.ShapeDtypeStruct((width, 2 * half * parts), jnp.bfloat16),
        [pltpu.VMEM((count, half), jnp.bfloat16)],
        {2 + 2 * n: 0} if extra else {},
    )


def from_peer(value, by):
    peers = lax.axis_size("mp")
    return lax.ppermute(value, "mp", [(i, i ^ by) for i in range(peers)])


def across_sections(value):
    return lax.ppermute(value, "section", [(0, 1), (1, 0)])


def local(tokens, weights, gain, cotangent):
    section = lax.axis_index("section").astype(jnp.int32).reshape(1)
    first = 1 - section
    weight = weights[0]
    peers = lax.axis_size("mp")
    line = lax.axis_size("dp")
    half = line // 2
    place = lax.axis_index("dp")
    rows = tokens.shape[0]
    each = peers // 4
    parts = 4 if weight.shape[1] % 1024 == 0 else 3

    last = []

    def run(work, anchor, *others):
        if last:
            held = last[-1]
            anchor, held["value"] = lax.optimization_barrier((anchor, held["value"]))
        held = {"value": work(anchor, *others)}
        last.append(held)
        return held

    raw = run(lambda a, b: jnp.where(first[0] == 1, a, b), tokens, cotangent)["value"]
    gathered = {by: from_peer(raw, by) for by in range(1, peers)}
    gathered[0] = raw

    values = tokens.astype(jnp.float32)
    sums = jnp.stack([jnp.sum(values, 1), jnp.sum(values * values, 1)], 1)
    mine = jnp.arange(peers)[:, None, None] == lax.axis_index("mp")
    sums = lax.psum(jnp.where(mine, sums[None], 0.0), ("dp", "mp"))
    average = sums[:, :, 0] / D
    inverse_std = lax.rsqrt(sums[:, :, 1] / D - average * average + epsilon)
    scale = jnp.stack([average, inverse_std], 2)

    far = list(range(2 * each, 4 * each))
    near = list(range(each, 2 * each)) + list(range(each))

    def prepare(members, group, into):
        mp = lax.axis_index("mp")
        scales = jnp.concatenate([lax.dynamic_index_in_dim(scale, mp ^ by, 0, False) for by in members], 0)
        return run(
            lambda s: normalize(first, [gathered[by] for by in members], s, gain, group, into), scales
        )["value"]

    chunks = {}

    def multiply(value, part, groups):
        products = run(lambda s: up_product(s, value, weight, part, parts, groups), section)
        for i, group in enumerate(groups):
            chunks[part, group] = {"products": products, "mine": i, "theirs": len(groups) + i}

    def stack(chunk):
        products = chunk["products"]
        arrived = across_sections(products["value"][chunk["theirs"]])
        chunk["sum"] = run(stacked, products["value"][chunk["mine"]], arrived)

    def inward(chunk):
        for hop in range(half - 1):
            value = chunk["sum"]["value"]
            arrived = lax.ppermute(value, "dp", [(hop, hop + 1), (line - 1 - hop, line - 2 - hop)])
            chunk["sum"] = run(added, value, arrived)

    def middle(chunk):
        value = chunk["sum"]["value"]
        arrived = lax.ppermute(value, "dp", [(half - 1, half), (half, half - 1)])
        chunk["result"] = run(lambda a, b: activated(first, a, b), value, arrived)

    def outward(chunk):
        for hop in reversed(range(half - 1)):
            value = chunk["result"]["value"]
            arrived = lax.ppermute(value, "dp", [(hop + 1, hop), (line - 2 - hop, line - 1 - hop)])
            receives = jnp.logical_or(place == hop, place == line - 1 - hop).astype(jnp.int32).reshape(1)
            if hop:
                chunk["result"] = run(lambda a, b: chosen(receives, a, b, False)[0], value, arrived)
            else:
                chunk["halves"] = run(lambda a, b: chosen(receives, a, b, True), value, arrived)

    def hidden(part, groups):
        kept = [chunks[part, g]["halves"]["value"][0] for g in groups]
        for g in groups:
            if "came" not in chunks[part, g]:
                chunks[part, g]["came"] = across_sections(chunks[part, g]["halves"]["value"][1])
        return kept, [chunks[part, g]["came"] for g in groups]

    both = (FAR, NEAR)
    order = [(part, g) for part in range(parts - 1) for g in (NEAR, FAR)]
    order += [(parts - 1, g) for g in (FAR, NEAR)]
    count = len(order)
    held = {"partial": None, "gradient": None}

    def tick(t):
        if 0 <= t - 1 < count:
            middle(chunks[order[t - 1]])
        if 0 <= t - 2 < count:
            outward(chunks[order[t - 2]])
        if 2 <= t + 2 < count:
            stack(chunks[order[t + 2]])

    def go_down(part):
        kept, came = hidden(part, both)
        before = None if held["partial"] is None else held["partial"]["value"][0]
        held["partial"] = run(
            lambda k: down_product(section, [k] + kept[1:], came, weight, part, parts, before, 0, [jnp.float32]),
            kept[0],
        )

    def go_gradient(part):
        kept, came = hidden(part, both)
        into = None if held["gradient"] is None else held["gradient"]["value"]
        held["gradient"] = run(
            lambda k: weight_gradient(section, turned, [k] + kept[1:], came, part, parts, into), kept[0]
        )

    def go_last(group, kinds):
        kept, came = hidden(parts - 1, [group])
        before = held["partial"]["value"][0]
        return run(
            lambda k: down_product(section, [k], came, weight, parts - 1, parts, before, group, kinds), kept[0]
        )

    x_near = prepare(near, NEAR, None)
    multiply(x_near, 0, [NEAR])
    stack(chunks[order[0]])
    x_all = prepare(far, FAR, x_near)
    multiply(x_all, 0, [FAR])
    stack(chunks[order[1]])
    for t in range(count + 2):
        if 0 <= t < count:
            inward(chunks[order[t]])
        if t == 0:
            multiply(x_all, 1, both)
        tick(t)
        if t == 0:
            turned = run(lambda a: a.T, x_all)["value"]
        part, odd = t // 2 + 2, t % 2 == 1
        if odd and part < parts:
            multiply(x_all, part, both)
        done, late = (t - 3) // 2, t % 2 == 1
        if t >= 3 and done < parts - 1:
            if late:
                go_down(done)
            else:
                go_gradient(done)
        if t == count:
            sent_far = go_last(FAR, [jnp.bfloat16] * 2)
    sent_near = go_last(NEAR, [jnp.bfloat16, jnp.float32])
    go_gradient(parts - 1)

    own = sent_near["value"][1]
    blocks = {0: own.astype(jnp.bfloat16), 1: sent_near["value"][0]}
    blocks[2], blocks[3] = sent_far["value"]
    result = own[:rows]
    for by in range(1, peers):
        at = (by % each) * rows
        result = result + from_peer(blocks[by // each][at : at + rows], by).astype(jnp.float32)
    return (result.astype(jnp.bfloat16)[None], held["gradient"]["value"][None])


def solution(mesh):
    placed = (P("mp", "dp"), P("section", "dp", "mp"), P("dp"), P("mp", "dp"))
    return jax.shard_map(
        local,
        mesh=mesh,
        in_specs=placed,
        out_specs=(P("section", "mp", "dp"), P("section", "dp", "mp")),
        check_vma=False,
    )
```

time: 503 us -> 361 us (0.72); the launches traced: 495 us -> 359 us
  waiting for transfers between devices: 250 us -> 35.5 us
  Pallas kernels: 0 us -> 172 us
  matrix products: 125 us -> 0 us
  blocking collectives: 13.5 us -> 65.5 us
  other arithmetic: 31.3 us -> 4.98 us
  local copies, waits for them, and re-layouts: 1.42 us -> 7.68 us
    ppermute x30 -> x24, waiting for transfers between devices: 245 us -> 14.8 us  [the longest x8 11.3 us: outward(): lax.ppermute(value, 'dp', [(hop + 1, hop), (line - 2 - hop, line - 1 - ho...]
    pallas_call x0 -> x48, Pallas kernels: none -> 172 us  [call(): pl.pallas_call(kernel, grid_spec=pltpu.PrefetchScalarGridSpec(num_scalar_...]
    dot_general x13 -> x0, matrix products: 125 us -> none  [dot_f32(): lax.dot_general(left, right, (dims, ((), ())), preferred_element_type=jnp...]
    psum x1, blocking collectives: 13.5 us -> 65.5 us  [local(): sums = lax.psum(jnp.where(mine, sums[None], 0.0), ('dp', 'mp'))]
    convert_element_type x30 -> x0, other arithmetic: 17.2 us -> none  [the longest x10 10.9 us: activate(): jnp.where(first, gelu_back(preact, grad_hidden), gelu_tanh(preact))]
    ppermute x9 -> x6, waiting for transfers between devices: 4.73 us -> 13.3 us  [from_peer(): return lax.ppermute(value, 'mp', [(i, i ^ by) for i in range(peers)])]
    ppermute x10 -> x16, waiting for transfers between devices: 0.25 us -> 7.42 us  [across_sections(): return lax.ppermute(value, 'section', [(0, 1), (1, 0)])]
    unnamed x5 -> x0, other arithmetic: 6.2 us -> none
  transfers between devices with their start and end apart: 49 -> 46, of which waited for: 14 -> 13; matrix products, arithmetic and copies ran while one was open for 22% -> 1% of each run, Pallas kernels for 0% -> 48%
where the time goes in v2:
time: 361 us; the launch traced here: 359 us
  Pallas kernels  172 us (48%)
  starting transfers between devices  71.2 us (20%)
  blocking collectives  65.5 us (18%)
  waiting for transfers between devices  35.5 us (10%)
  local copies, waits for them, and re-layouts  7.68 us (2%)
  other arithmetic  4.98 us (1%)
    pallas_call x48, Pallas kernels, call(): pl.pallas_call(kernel, grid_spec=pltpu.PrefetchScalarGridSpec(num_scalar_...  172 us
    psum x1, blocking collectives, local(): sums = lax.psum(jnp.where(mine, sums[None], 0.0), ('dp', 'mp'))  65.5 us
    ppermute x8, starting transfers between devices, inward(): lax.ppermute(value, 'dp', [(hop, hop + 1), (line - 1 - hop, line - 2 - ho...  43.5 us
    ppermute x6, waiting for transfers between devices, from_peer(): return lax.ppermute(value, 'mp', [(i, i ^ by) for i in range(peers)])  13.3 us
    ppermute x8, waiting for transfers between devices, outward(): lax.ppermute(value, 'dp', [(hop + 1, hop), (line - 2 - hop, line - 1 - ho...  11.3 us
    ppermute x8, starting transfers between devices, outward(): lax.ppermute(value, 'dp', [(hop + 1, hop), (line - 2 - hop, line - 1 - ho...  10.7 us
    ppermute x8, starting transfers between devices, middle(): arrived = lax.ppermute(value, 'dp', [(half - 1, half), (half, half - 1)])  7.48 us
    ppermute x16, waiting for transfers between devices, across_sections(): return lax.ppermute(value, 'section', [(0, 1), (1, 0)])  7.42 us
  transfers between devices with their start and end apart: 46, of which 13 were waited for; matrix products, arithmetic and copies ran while one was open for 1% of the time, Pallas kernels for 48%

profile of v2, /device:TPU:0, one launch (start us, length us, event | category | flops | bytes accessed | tf_op | source)
XLA Modules:
  0.0 358.7 jit_solution(13207957952083351959)
XLA Ops:
  0.6 2.1 broadcast_select_fusion.refs_1_
  2.8 2.9 collective-permute-start
  5.7 1.5 collective-permute-start.2
  7.2 1.4 convert_reduce_fusion
  8.8 65.5 %psum.7 = f32[4,128,2]{1,0,2:T(4,128)S(1)} all-reduce(f32[4,128,2]{1,0,2:T(4,128)S(1)} %broadcast_select_fusion.1), channel_id=1, replica_groups=mesh['section'=2,'dp'=4,'mp'=4] {'dp','mp'}, use_global_device_ids=true, to_apply=%region_2.3 | all-reduce | flops 1024 | bytes 8192 | tf_op jit(solution)/shard_map/psum | solution.py:305
  76.5 2.7 normalize.2.rows_ref.refs_2_
  79.2 5.3 %up_product.5 = (bf16[256,768]{1,0:T(8,128)(2,1)S(1)}, bf16[256,768]{1,0:T(8,128)(2,1)S(1)}) custom-call(s32[1]{0:T(128)} %bitcast.1.section_ref, bf16[512,3072]{1,0:T(8,128)(2,1)S(1)} %normalize.2.rows_ref.refs_2_, bf16[3072,6144]{1,0:T(8,128)(2,1)} %bitcast.21), custom_call_target="tpu_custom_call" | custom-call | tf_op jit(solution)/shard_map/up_product/pallas_call | solution.py:27
  84.6 1.7 collective-permute-done.1.refs_1_
  86.3 1.5 stacked.8.refs_0_
  87.7 2.2 collective-permute-start.5
  90.1 2.9 normalize.3.rows_ref
  93.0 5.3 %up_product.6 = (bf16[256,768]{1,0:T(8,128)(2,1)S(1)}, bf16[256,768]{1,0:T(8,128)(2,1)S(1)}) custom-call(s32[1]{0:T(128)} %bitcast.1.section_ref, bf16[512,3072]{1,0:T(8,128)(2,1)S(1)} %normalize.3.rows_ref, bf16[3072,6144]{1,0:T(8,128)(2,1)} %bitcast.22), custom_call_target="tpu_custom_call" | custom-call | tf_op jit(solution)/shard_map/up_product/pallas_call | solution.py:27
  98.5 1.6 collective-permute-done.4.refs_1_
  100.0 1.5 stacked.9.refs_0_
  101.5 2.2 collective-permute-start.7
  103.7 3.5 collective-permute-done.5.refs_1_
  107.2 3.2 added.8.refs_1_
  110.4 7.7 %up_product.7 = (bf16[256,768]{1,0:T(8,128)(2,1)S(1)}, bf16[256,768]{1,0:T(8,128)(2,1)S(1)}, bf16[256,768]{1,0:T(8,128)(2,1)S(1)}, bf16[256,768]{1,0:T(8,128)(2,1)S(1)}) custom-call(s32[1]{0:T(128)} %bitcast.1.section_ref, bf16[512,3072]{1,0:T(8,128)(2,1)S(1)} %normalize.3.rows_ref, bf16[3072,6144]{1,0:T(8,128)(2,1)} %bitcast.23), custom_call_target="tpu_custom_call" | custom-call | tf_op jit(solution)/shard_map/up_product/pallas_call | solution.py:27
  118.8 1.5 collective-permute-start.8
  121.7 2.8 copy.14
  124.5 4.6 %collective-permute-start.10 = (bf16[512,768]{1,0:T(8,128)(2,1)}, bf16[512,768]{1,0:T(8,128)(2,1)S(1)}, u32[]{:S(2)}, u32[]{:S(2)}) collective-permute-start(bf16[512,768]{1,0:T(8,128)(2,1)} %copy-done.1), channel_id=1, source_target_pairs={{0,4},{12,8},{1,5},{13,9},{2,6},{14,10},{3,7},{15,11},{16,20},{28,... | collective-permute-start | bytes 2359304 | tf_op jit(solution)/shard_map/ppermute | solution.py:335
  129.1 2.3 added.9.refs_1_
  132.4 3.4 activated.8.refs_1_
  135.8 1.3 collective-permute-start.12
  137.1 1.5 stacked.11.refs_0_
  138.7 15.2 %collective-permute-start.14 = (bf16[512,768]{1,0:T(8,128)(2,1)}, bf16[512,768]{1,0:T(8,128)(2,1)}, u32[]{:S(2)}, u32[]{:S(2)}) collective-permute-start(bf16[512,768]{1,0:T(8,128)(2,1)} %stacked.11.refs_0_), channel_id=1, source_target_pairs={{0,4},{12,8},{1,5},{13,9},{2,6},{14,10},{3,7},{15,11},{16,20},{28,... | collective-permute-start | bytes 2359304 | tf_op jit(solution)/shard_map/ppermute | solution.py:335
  153.9 8.5 %up_product.8 = (bf16[256,768]{1,0:T(8,128)(2,1)S(1)}, bf16[256,768]{1,0:T(8,128)(2,1)S(1)}, bf16[256,768]{1,0:T(8,128)(2,1)S(1)}, bf16[256,768]{1,0:T(8,128)(2,1)}) custom-call(s32[1]{0:T(128)} %bitcast.1.section_ref, bf16[512,3072]{1,0:T(8,128)(2,1)S(1)} %normalize.3.rows_ref, bf16[3072,6144]{1,0:T(8,128)(2,1)} %bitcast.24), custom_call_target="tpu_custom_call" | custom-call | tf_op jit(solution)/shard_map/up_product/pallas_call | solution.py:27
  162.4 1.7 added.10.refs_1_
  164.1 1.5 collective-permute-start.15
  165.7 2.1 activated.9.refs_1_
  167.8 1.3 collective-permute-start.16
  169.2 2.3 chosen.8
  172.5 1.9 stacked.12.refs_0_
  174.4 5.4 %collective-permute-start.20 = (bf16[512,768]{1,0:T(8,128)(2,1)S(1)}, bf16[512,768]{1,0:T(8,128)(2,1)S(1)}, u32[]{:S(2)}, u32[]{:S(2)}) collective-permute-start(bf16[512,768]{1,0:T(8,128)(2,1)S(1)} %stacked.12.refs_0_), channel_id=1, source_target_pairs={{0,4},{12,8},{1,5},{13,9},{2,6},{14,10},{3,7},{15,11},{16,20},{28,... | collective-permute-start | bytes 2359304 | tf_op jit(solution)/shard_map/ppermute | solution.py:335
  180.1 2.3 added.11.refs_1_
  183.5 2.7 activated.10.refs_1_
  186.1 2.4 collective-permute-done.16.refs_2_
  188.5 2.2 chosen.9
  190.8 1.5 collective-permute-start.22
  192.5 8.5 %up_product.9 = (bf16[256,768]{1,0:T(8,128)(2,1)S(1)}, bf16[256,768]{1,0:T(8,128)(2,1)S(1)}, bf16[256,768]{1,0:T(8,128)(2,1)S(1)}, bf16[256,768]{1,0:T(8,128)(2,1)}) custom-call(s32[1]{0:T(128)} %bitcast.1.section_ref, bf16[512,3072]{1,0:T(8,128)(2,1)S(1)} %normalize.3.rows_ref, bf16[3072,6144]{1,0:T(8,128)(2,1)} %bitcast.25), custom_call_target="tpu_custom_call" | custom-call | tf_op jit(solution)/shard_map/up_product/pallas_call | solution.py:27
  201.0 4.6 %collective-permute-start.24 = (bf16[512,768]{1,0:T(8,128)(2,1)S(1)}, bf16[512,768]{1,0:T(8,128)(2,1)S(1)}, u32[]{:S(2)}, u32[]{:S(2)}) collective-permute-start(bf16[512,768]{1,0:T(8,128)(2,1)S(1)} %stacked.13.refs_0_), channel_id=1, source_target_pairs={{0,4},{12,8},{1,5},{13,9},{2,6},{14,10},{3,7},{15,11},{16,20},{28,... | collective-permute-start | bytes 2359304 | tf_op jit(solution)/shard_map/ppermute | solution.py:335
  205.7 11.6 %down_product.5.refs_6_ = f32[512,3072]{1,0:T(8,128)S(1)} custom-call(s32[1]{0:T(128)} %bitcast.1.section_ref, bf16[256,768]{1,0:T(8,128)(2,1)S(1)} %get-tuple-element.220.refs_0_, bf16[256,768]{1,0:T(8,128)(2,1)S(1)} %get-tuple-element.206.refs_1_, bf16[256,768]{1,0:T(8,128)(2,1)S(1)} %collective-permute-done.18.refs_2_, ...), custom_call_target="tpu_custom_call" | custom-call | tf_op jit(solution)/shard_map/down_product/pallas_call | solution.py:27
  219.6 1.3 collective-permute-start.26
  223.0 9.5 %weight_gradient.4.refs_4_ = bf16[3072,6144]{1,0:T(8,128)(2,1)} custom-call(s32[1]{0:T(128)} %bitcast.1.section_ref, bf16[3072,512]{1,0:T(8,128)(2,1)S(1)} %bitcast.15, bf16[256,768]{1,0:T(8,128)(2,1)S(1)} %get-tuple-element.220.refs_0_, bf16[256,768]{1,0:T(8,128)(2,1)S(1)} %get-tuple-element.206.refs_1_, ...), custom_call_target="tpu_custom_call" | custom-call | tf_op jit(solution)/shard_map/weight_gradient/pallas_call | solution.py:27
  232.5 4.6 %collective-permute-start.30 = (bf16[512,768]{1,0:T(8,128)(2,1)S(1)}, bf16[512,768]{1,0:T(8,128)(2,1)S(1)}, u32[]{:S(2)}, u32[]{:S(2)}) collective-permute-start(bf16[512,768]{1,0:T(8,128)(2,1)S(1)} %stacked.14.refs_0_), channel_id=1, source_target_pairs={{0,4},{12,8},{1,5},{13,9},{2,6},{14,10},{3,7},{15,11},{16,20},{28,... | collective-permute-start | bytes 2359304 | tf_op jit(solution)/shard_map/ppermute | solution.py:335
  239.4 1.5 collective-permute-done.26.refs_2_
  241.3 1.3 collective-permute-start.32
  242.9 4.6 %collective-permute-start.33 = (bf16[512,768]{1,0:T(8,128)(2,1)S(1)}, bf16[512,768]{1,0:T(8,128)(2,1)S(1)}, u32[]{:S(2)}, u32[]{:S(2)}) collective-permute-start(bf16[512,768]{1,0:T(8,128)(2,1)S(1)} %stacked.15.refs_0_), channel_id=1, source_target_pairs={{0,4},{12,8},{1,5},{13,9},{2,6},{14,10},{3,7},{15,11},{16,20},{28,... | collective-permute-start | bytes 2359304 | tf_op jit(solution)/shard_map/ppermute | solution.py:335
  247.5 11.8 %down_product.6.refs_6_ = f32[512,3072]{1,0:T(8,128)S(1)} custom-call(s32[1]{0:T(128)} %bitcast.1.section_ref, bf16[256,768]{1,0:T(8,128)(2,1)S(1)} %get-tuple-element.246.refs_0_, bf16[256,768]{1,0:T(8,128)(2,1)S(1)} %get-tuple-element.234.refs_1_, bf16[256,768]{1,0:T(8,128)(2,1)S(1)} %collective-permute-done.28.refs_2_, ...), custom_call_target="tpu_custom_call" | custom-call | tf_op jit(solution)/shard_map/down_product/pallas_call | solution.py:27
  261.5 1.3 collective-permute-start.35
  263.5 9.5 %weight_gradient.5.refs_4_ = bf16[3072,6144]{1,0:T(8,128)(2,1)} custom-call(s32[1]{0:T(128)} %bitcast.1.section_ref, bf16[3072,512]{1,0:T(8,128)(2,1)S(1)} %bitcast.16, bf16[256,768]{1,0:T(8,128)(2,1)S(1)} %get-tuple-element.246.refs_0_, bf16[256,768]{1,0:T(8,128)(2,1)S(1)} %get-tuple-element.234.refs_1_, ...), custom_call_target="tpu_custom_call", output_to_operand_aliasing={{}: (6, {})} | custom-call | tf_op jit(solution)/shard_map/weight_gradient/pallas_call | solution.py:27
  275.2 1.3 collective-permute-start.39
  276.5 6.3 %collective-permute-done.35.refs_2_ = bf16[512,768]{1,0:T(8,128)(2,1)S(1)} collective-permute-done((bf16[512,768]{1,0:T(8,128)(2,1)S(1)}, bf16[512,768]{1,0:T(8,128)(2,1)S(1)}, u32[]{:S(2)}, u32[]{:S(2)}) %collective-permute-start.35) | collective-permute-done | bytes 786464 | tf_op jit(solution)/shard_map/ppermute | solution.py:346
  283.2 1.7 collective-permute-done.36.refs_2_
  284.9 11.7 %down_product.7.refs_4_ = f32[512,3072]{1,0:T(8,128)S(1)} custom-call(s32[1]{0:T(128)} %bitcast.1.section_ref, bf16[256,768]{1,0:T(8,128)(2,1)S(1)} %get-tuple-element.266.refs_0_, bf16[256,768]{1,0:T(8,128)(2,1)S(1)} %get-tuple-element.257.refs_1_, bf16[256,768]{1,0:T(8,128)(2,1)S(1)} %collective-permute-done.36.refs_2_, ...), custom_call_target="tpu_custom_call" | custom-call | tf_op jit(solution)/shard_map/down_product/pallas_call | solution.py:27
  297.7 1.5 collective-permute-start.41
  300.4 9.5 %weight_gradient.6.refs_4_ = bf16[3072,6144]{1,0:T(8,128)(2,1)} custom-call(s32[1]{0:T(128)} %bitcast.1.section_ref, bf16[3072,512]{1,0:T(8,128)(2,1)S(1)} %bitcast.17, bf16[256,768]{1,0:T(8,128)(2,1)S(1)} %get-tuple-element.266.refs_0_, bf16[256,768]{1,0:T(8,128)(2,1)S(1)} %get-tuple-element.257.refs_1_, ...), custom_call_target="tpu_custom_call", output_to_operand_aliasing={{}: (6, {})} | custom-call | tf_op jit(solution)/shard_map/weight_gradient/pallas_call | solution.py:27
  309.9 10.1 %down_product.8 = (bf16[128,3072]{1,0:T(8,128)(2,1)S(1)}, bf16[128,3072]{1,0:T(8,128)(2,1)S(1)}) custom-call(s32[1]{0:T(128)} %bitcast.1.section_ref, bf16[256,768]{1,0:T(8,128)(2,1)S(1)} %get-tuple-element.283.refs_0_, bf16[256,768]{1,0:T(8,128)(2,1)S(1)} %collective-permute-done.40.refs_1_.refs_2_, bf16[3072,6144]{1,0:T(8,128)(2,1)} %bitcast.32, ...), custom_call_target="tpu_custom_call" | custom-call | tf_op jit(solution)/shard_map/down_product/pallas_call | solution.py:27
  320.9 1.3 collective-permute-done.42.refs_1_.refs_3_
  322.2 10.2 %down_product.9 = (bf16[128,3072]{1,0:T(8,128)(2,1)S(1)}, f32[128,3072]{1,0:T(8,128)S(1)}) custom-call(s32[1]{0:T(128)} %bitcast.1.section_ref, bf16[256,768]{1,0:T(8,128)(2,1)S(1)} %get-tuple-element.284.refs_0_.refs_1_, bf16[256,768]{1,0:T(8,128)(2,1)S(1)} %collective-permute-done.42.refs_1_.refs_3_, bf16[3072,6144]{1,0:T(8,128)(2,1)} %bitcast.34, ...), custom_call_target="tpu_custom_call" | custom-call | tf_op jit(solution)/shard_map/down_product/pallas_call | solution.py:27
  332.4 2.2 collective-permute-start.43
  334.6 9.4 %weight_gradient.7 = bf16[3072,6144]{1,0:T(8,128)(2,1)} custom-call(s32[1]{0:T(128)} %bitcast.1.section_ref, bf16[3072,512]{1,0:T(8,128)(2,1)S(1)} %bitcast.18, bf16[256,768]{1,0:T(8,128)(2,1)S(1)} %get-tuple-element.283.refs_0_, bf16[256,768]{1,0:T(8,128)(2,1)S(1)} %get-tuple-element.284.refs_0_.refs_1_, ...), custom_call_target="tpu_custom_call", output_to_operand_aliasing={{}: (6, {})} | custom-call | tf_op jit(solution)/shard_map/weight_gradient/pallas_call | solution.py:27
  344.1 13.3 %collective-permute-done.44 = bf16[128,3072]{1,0:T(8,128)(2,1)S(1)} collective-permute-done((bf16[128,3072]{1,0:T(8,128)(2,1)S(1)}, bf16[128,3072]{1,0:T(8,128)(2,1)S(1)}, u32[]{:S(2)}, u32[]{:S(2)}) %collective-permute-start.44) | collective-permute-done | bytes 786464 | tf_op jit(solution)/shard_map/ppermute | solution.py:269
  357.4 1.3 fusion.1
  (112 shorter events, 24.2 us)
Async XLA Ops:
  0.6 74.7 %copy-start.7 = (f32[3072]{0:T(1024)S(1)}, f32[3072]{0:T(1024)}, u32[]{:S(2)}) copy-start(f32[3072]{0:T(1024)} %param.6) | copy-start | bytes 36868
  2.8 71.7 %collective-permute-start = (bf16[128,3072]{1,0:T(8,128)(2,1)}, bf16[128,3072]{1,0:T(8,128)(2,1)S(1)}, u32[]{:S(2)}, u32[]{:S(2)}) collective-permute-start(bf16[128,3072]{1,0:T(8,128)(2,1)} %broadcast_select_fusion.refs_1_), channel_id=1, source_target_pairs={{0,1},{1,0},{2,3},{3,2},{4,5},{5,4},{6,7},{7,6},{8,9},{9,8},{10,11... | collective-permute-start | bytes 2359304 | tf_op jit(solution)/shard_map/ppermute | solution.py:269
  5.7 84.4 %collective-permute-start.2 = (bf16[128,3072]{1,0:T(8,128)(2,1)}, bf16[128,3072]{1,0:T(8,128)(2,1)}, u32[]{:S(2)}, u32[]{:S(2)}) collective-permute-start(bf16[128,3072]{1,0:T(8,128)(2,1)} %broadcast_select_fusion.refs_1_), channel_id=1, source_target_pairs={{0,2},{1,3},{2,0},{3,1},{4,6},{5,7},{6,4},{7,5},{8,10},{9,11},{10,... | collective-permute-start | bytes 2359304 | tf_op jit(solution)/shard_map/ppermute | solution.py:269
  7.2 82.9 %collective-permute-start.3 = (bf16[128,3072]{1,0:T(8,128)(2,1)}, bf16[128,3072]{1,0:T(8,128)(2,1)}, u32[]{:S(2)}, u32[]{:S(2)}) collective-permute-start(bf16[128,3072]{1,0:T(8,128)(2,1)} %broadcast_select_fusion.refs_1_), channel_id=1, source_target_pairs={{0,3},{1,2},{2,1},{3,0},{4,7},{5,6},{6,5},{7,4},{8,11},{9,10},{10,... | collective-permute-start | bytes 2359304 | tf_op jit(solution)/shard_map/ppermute | solution.py:269
  74.4 0.9 copy-start.3
  75.3 1.1 copy-start.4
  84.5 1.8 collective-permute-start.1
  87.7 19.4 %collective-permute-start.5 = (bf16[512,768]{1,0:T(8,128)(2,1)}, bf16[512,768]{1,0:T(8,128)(2,1)}, u32[]{:S(2)}, u32[]{:S(2)}) collective-permute-start(bf16[512,768]{1,0:T(8,128)(2,1)} %stacked.8.refs_0_), channel_id=1, source_target_pairs={{0,4},{12,8},{1,5},{13,9},{2,6},{14,10},{3,7},{15,11},{16,20},{28,... | collective-permute-start | bytes 2359304 | tf_op jit(solution)/shard_map/ppermute | solution.py:335
  98.3 1.8 collective-permute-start.4
  101.5 27.6 %collective-permute-start.7 = (bf16[512,768]{1,0:T(8,128)(2,1)}, bf16[512,768]{1,0:T(8,128)(2,1)}, u32[]{:S(2)}, u32[]{:S(2)}) collective-permute-start(bf16[512,768]{1,0:T(8,128)(2,1)} %stacked.9.refs_0_), channel_id=1, source_target_pairs={{0,4},{12,8},{1,5},{13,9},{2,6},{14,10},{3,7},{15,11},{16,20},{28,... | collective-permute-start | bytes 2359304 | tf_op jit(solution)/shard_map/ppermute | solution.py:335
  118.1 0.7 copy-start.10
  118.8 1.7 collective-permute-start.6
  118.8 13.6 %collective-permute-start.8 = (bf16[512,768]{1,0:T(8,128)(2,1)}, bf16[512,768]{1,0:T(8,128)(2,1)}, u32[]{:S(2)}, u32[]{:S(2)}) collective-permute-start(bf16[512,768]{1,0:T(8,128)(2,1)} %added.8.refs_1_), channel_id=1, source_target_pairs={{4,8},{8,4},{5,9},{9,5},{6,10},{10,6},{7,11},{11,7},{20,24},{24,20... | collective-permute-start | bytes 2359304 | tf_op jit(solution)/shard_map/ppermute | solution.py:340
  120.8 0.9 copy-start.1
  124.5 37.9 %collective-permute-start.10 = (bf16[512,768]{1,0:T(8,128)(2,1)}, bf16[512,768]{1,0:T(8,128)(2,1)S(1)}, u32[]{:S(2)}, u32[]{:S(2)}) collective-permute-start(bf16[512,768]{1,0:T(8,128)(2,1)} %copy-done.1), channel_id=1, source_target_pairs={{0,4},{12,8},{1,5},{13,9},{2,6},{14,10},{3,7},{15,11},{16,20},{28,... | collective-permute-start | bytes 2359304 | tf_op jit(solution)/shard_map/ppermute | solution.py:335
  131.4 34.3 %collective-permute-start.11 = (bf16[512,768]{1,0:T(8,128)(2,1)S(1)}, bf16[512,768]{1,0:T(8,128)(2,1)S(1)}, u32[]{:S(2)}, u32[]{:S(2)}) collective-permute-start(bf16[512,768]{1,0:T(8,128)(2,1)S(1)} %added.9.refs_1_), channel_id=1, source_target_pairs={{4,8},{8,4},{5,9},{9,5},{6,10},{10,6},{7,11},{11,7},{20,24},{24,20... | collective-permute-start | bytes 2359304 | tf_op jit(solution)/shard_map/ppermute | solution.py:340
  132.1 5.0 %collective-permute-start.9 = (bf16[256,768]{1,0:T(8,128)(2,1)}, bf16[256,768]{1,0:T(8,128)(2,1)S(1)}, u32[]{:S(2)}, u32[]{:S(2)}) collective-permute-start(bf16[256,768]{1,0:T(8,128)(2,1)} %copy-done.10), channel_id=1, source_target_pairs={{0,16},{16,0},{1,17},{17,1},{2,18},{18,2},{3,19},{19,3},{4,20},{20... | collective-permute-start | bytes 1179656 | tf_op jit(solution)/shard_map/ppermute | solution.py:273
  135.8 33.3 %collective-permute-start.12 = (bf16[512,768]{1,0:T(8,128)(2,1)}, bf16[512,768]{1,0:T(8,128)(2,1)}, u32[]{:S(2)}, u32[]{:S(2)}) collective-permute-start(bf16[512,768]{1,0:T(8,128)(2,1)} %activated.8.refs_1_), channel_id=1, source_target_pairs={{4,0},{8,12},{5,1},{9,13},{6,2},{10,14},{7,3},{11,15},{20,16},{24,... | collective-permute-start | bytes 2359304 | tf_op jit(solution)/shard_map/ppermute | solution.py:346
  138.7 23.7 %copy-start.2 = (bf16[512,768]{1,0:T(8,128)(2,1)S(1)}, bf16[512,768]{1,0:T(8,128)(2,1)}, u32[]{:S(2)}) copy-start(bf16[512,768]{1,0:T(8,128)(2,1)} %copy-done.1) | copy-start | bytes 2359300
  138.7 41.4 %collective-permute-start.14 = (bf16[512,768]{1,0:T(8,128)(2,1)}, bf16[512,768]{1,0:T(8,128)(2,1)}, u32[]{:S(2)}, u32[]{:S(2)}) collective-permute-start(bf16[512,768]{1,0:T(8,128)(2,1)} %stacked.11.refs_0_), channel_id=1, source_target_pairs={{0,4},{12,8},{1,5},{13,9},{2,6},{14,10},{3,7},{15,11},{16,20},{28,... | collective-permute-start | bytes 2359304 | tf_op jit(solution)/shard_map/ppermute | solution.py:335
  162.4 5.4 %copy-start.5 = (bf16[256,768]{1,0:T(8,128)(2,1)}, bf16[256,768]{1,0:T(8,128)(2,1)S(1)}, u32[]{:S(2)}) copy-start(bf16[256,768]{1,0:T(8,128)(2,1)S(1)} %get-tuple-element.186.refs_0_) | copy-start | bytes 1179652
  162.4 6.7 %copy-start.8 = (bf16[256,768]{1,0:T(8,128)(2,1)}, bf16[256,768]{1,0:T(8,128)(2,1)S(1)}, u32[]{:S(2)}) copy-start(bf16[256,768]{1,0:T(8,128)(2,1)S(1)} %get-tuple-element.199) | copy-start | bytes 1179652
  164.1 19.0 %collective-permute-start.15 = (bf16[512,768]{1,0:T(8,128)(2,1)}, bf16[512,768]{1,0:T(8,128)(2,1)}, u32[]{:S(2)}, u32[]{:S(2)}) collective-permute-start(bf16[512,768]{1,0:T(8,128)(2,1)} %added.10.refs_1_), channel_id=1, source_target_pairs={{4,8},{8,4},{5,9},{9,5},{6,10},{10,6},{7,11},{11,7},{20,24},{24,20... | collective-permute-start | bytes 2359304 | tf_op jit(solution)/shard_map/ppermute | solution.py:340
  167.8 20.7 %collective-permute-start.16 = (bf16[512,768]{1,0:T(8,128)(2,1)}, bf16[512,768]{1,0:T(8,128)(2,1)}, u32[]{:S(2)}, u32[]{:S(2)}) collective-permute-start(bf16[512,768]{1,0:T(8,128)(2,1)} %activated.9.refs_1_), channel_id=1, source_target_pairs={{4,0},{8,12},{5,1},{9,13},{6,2},{10,14},{7,3},{11,15},{20,16},{24,... | collective-permute-start | bytes 2359304 | tf_op jit(solution)/shard_map/ppermute | solution.py:346
  169.1 2.4 collective-permute-start.13
  169.2 10.6 %copy-start.9 = (bf16[256,768]{1,0:T(8,128)(2,1)S(1)}, bf16[256,768]{1,0:T(8,128)(2,1)}, u32[]{:S(2)}) copy-start(bf16[256,768]{1,0:T(8,128)(2,1)} %copy-done.8) | copy-start | bytes 1179652
  171.5 1.0 copy-start.6
  174.4 42.9 %collective-permute-start.20 = (bf16[512,768]{1,0:T(8,128)(2,1)S(1)}, bf16[512,768]{1,0:T(8,128)(2,1)S(1)}, u32[]{:S(2)}, u32[]{:S(2)}) collective-permute-start(bf16[512,768]{1,0:T(8,128)(2,1)S(1)} %stacked.12.refs_0_), channel_id=1, source_target_pairs={{0,4},{12,8},{1,5},{13,9},{2,6},{14,10},{3,7},{15,11},{16,20},{28,... | collective-permute-start | bytes 2359304 | tf_op jit(solution)/shard_map/ppermute | solution.py:335
  179.8 11.0 %collective-permute-start.17 = (bf16[256,768]{1,0:T(8,128)(2,1)S(1)}, bf16[256,768]{1,0:T(8,128)(2,1)S(1)}, u32[]{:S(2)}, u32[]{:S(2)}) collective-permute-start(bf16[256,768]{1,0:T(8,128)(2,1)S(1)} %copy-done.9), channel_id=1, source_target_pairs={{0,16},{16,0},{1,17},{17,1},{2,18},{18,2},{3,19},{19,3},{4,20},{20... | collective-permute-start | bytes 1179656 | tf_op jit(solution)/shard_map/ppermute | solution.py:273
  182.4 36.2 %collective-permute-start.21 = (bf16[512,768]{1,0:T(8,128)(2,1)S(1)}, bf16[512,768]{1,0:T(8,128)(2,1)S(1)}, u32[]{:S(2)}, u32[]{:S(2)}) collective-permute-start(bf16[512,768]{1,0:T(8,128)(2,1)S(1)} %added.11.refs_1_), channel_id=1, source_target_pairs={{4,8},{8,4},{5,9},{9,5},{6,10},{10,6},{7,11},{11,7},{20,24},{24,20... | collective-permute-start | bytes 2359304 | tf_op jit(solution)/shard_map/ppermute | solution.py:340
  183.1 17.9 %collective-permute-start.19 = (bf16[256,768]{1,0:T(8,128)(2,1)S(1)}, bf16[256,768]{1,0:T(8,128)(2,1)S(1)}, u32[]{:S(2)}, u32[]{:S(2)}) collective-permute-start(bf16[256,768]{1,0:T(8,128)(2,1)S(1)} %get-tuple-element.208), channel_id=1, source_target_pairs={{0,16},{16,0},{1,17},{17,1},{2,18},{18,2},{3,19},{19,3},{4,20},{20... | collective-permute-start | bytes 1179656 | tf_op jit(solution)/shard_map/ppermute | solution.py:273
  190.7 15.0 %collective-permute-start.18 = (bf16[256,768]{1,0:T(8,128)(2,1)S(1)}, bf16[256,768]{1,0:T(8,128)(2,1)S(1)}, u32[]{:S(2)}, u32[]{:S(2)}) collective-permute-start(bf16[256,768]{1,0:T(8,128)(2,1)S(1)} %get-tuple-element.207), channel_id=1, source_target_pairs={{0,16},{16,0},{1,17},{17,1},{2,18},{18,2},{3,19},{19,3},{4,20},{20... | collective-permute-start | bytes 1179656 | tf_op jit(solution)/shard_map/ppermute | solution.py:273
  190.8 30.2 %collective-permute-start.22 = (bf16[512,768]{1,0:T(8,128)(2,1)S(1)}, bf16[512,768]{1,0:T(8,128)(2,1)S(1)}, u32[]{:S(2)}, u32[]{:S(2)}) collective-permute-start(bf16[512,768]{1,0:T(8,128)(2,1)S(1)} %activated.10.refs_1_), channel_id=1, source_target_pairs={{4,0},{8,12},{5,1},{9,13},{6,2},{10,14},{7,3},{11,15},{20,16},{24,... | collective-permute-start | bytes 2359304 | tf_op jit(solution)/shard_map/ppermute | solution.py:346
  201.0 36.1 %collective-permute-start.24 = (bf16[512,768]{1,0:T(8,128)(2,1)S(1)}, bf16[512,768]{1,0:T(8,128)(2,1)S(1)}, u32[]{:S(2)}, u32[]{:S(2)}) collective-permute-start(bf16[512,768]{1,0:T(8,128)(2,1)S(1)} %stacked.13.refs_0_), channel_id=1, source_target_pairs={{0,4},{12,8},{1,5},{13,9},{2,6},{14,10},{3,7},{15,11},{16,20},{28,... | collective-permute-start | bytes 2359304 | tf_op jit(solution)/shard_map/ppermute | solution.py:335
  217.7 5.2 %copy-start = (bf16[512,3072]{0,1:T(8,128)(2,1)S(1)}, bf16[512,3072]{0,1:T(8,128)(2,1)}, u32[]{:S(2)}) copy-start(bf16[512,3072]{0,1:T(8,128)(2,1)} %copy.14) | copy-start | bytes 9437188
  217.8 20.5 %collective-permute-start.25 = (bf16[512,768]{1,0:T(8,128)(2,1)S(1)}, bf16[512,768]{1,0:T(8,128)(2,1)S(1)}, u32[]{:S(2)}, u32[]{:S(2)}) collective-permute-start(bf16[512,768]{1,0:T(8,128)(2,1)S(1)} %added.12.refs_1_), channel_id=1, source_target_pairs={{4,8},{8,4},{5,9},{9,5},{6,10},{10,6},{7,11},{11,7},{20,24},{24,20... | collective-permute-start | bytes 2359304 | tf_op jit(solution)/shard_map/ppermute | solution.py:340
  219.6 21.3 %collective-permute-start.26 = (bf16[512,768]{1,0:T(8,128)(2,1)S(1)}, bf16[512,768]{1,0:T(8,128)(2,1)S(1)}, u32[]{:S(2)}, u32[]{:S(2)}) collective-permute-start(bf16[512,768]{1,0:T(8,128)(2,1)S(1)} %activated.11.refs_1_), channel_id=1, source_target_pairs={{4,0},{8,12},{5,1},{9,13},{6,2},{10,14},{7,3},{11,15},{20,16},{24,... | collective-permute-start | bytes 2359304 | tf_op jit(solution)/shard_map/ppermute | solution.py:346
  220.9 1.8 collective-permute-start.23
  221.0 20.3 %collective-permute-start.27 = (bf16[256,768]{1,0:T(8,128)(2,1)}, bf16[256,768]{1,0:T(8,128)(2,1)S(1)}, u32[]{:S(2)}, u32[]{:S(2)}) collective-permute-start(bf16[256,768]{1,0:T(8,128)(2,1)} %get-tuple-element.232), channel_id=1, source_target_pairs={{0,16},{16,0},{1,17},{17,1},{2,18},{18,2},{3,19},{19,3},{4,20},{20... | collective-permute-start | bytes 1179656 | tf_op jit(solution)/shard_map/ppermute | solution.py:273
  232.5 26.8 %collective-permute-start.30 = (bf16[512,768]{1,0:T(8,128)(2,1)S(1)}, bf16[512,768]{1,0:T(8,128)(2,1)S(1)}, u32[]{:S(2)}, u32[]{:S(2)}) collective-permute-start(bf16[512,768]{1,0:T(8,128)(2,1)S(1)} %stacked.14.refs_0_), channel_id=1, source_target_pairs={{0,4},{12,8},{1,5},{13,9},{2,6},{14,10},{3,7},{15,11},{16,20},{28,... | collective-permute-start | bytes 2359304 | tf_op jit(solution)/shard_map/ppermute | solution.py:335
  237.5 22.9 %collective-permute-start.31 = (bf16[512,768]{1,0:T(8,128)(2,1)S(1)}, bf16[512,768]{1,0:T(8,128)(2,1)S(1)}, u32[]{:S(2)}, u32[]{:S(2)}) collective-permute-start(bf16[512,768]{1,0:T(8,128)(2,1)S(1)} %added.13.refs_1_), channel_id=1, source_target_pairs={{4,8},{8,4},{5,9},{9,5},{6,10},{10,6},{7,11},{11,7},{20,24},{24,20... | collective-permute-start | bytes 2359304 | tf_op jit(solution)/shard_map/ppermute | solution.py:340
  238.3 4.6 %collective-permute-start.29 = (bf16[256,768]{1,0:T(8,128)(2,1)S(1)}, bf16[256,768]{1,0:T(8,128)(2,1)S(1)}, u32[]{:S(2)}, u32[]{:S(2)}) collective-permute-start(bf16[256,768]{1,0:T(8,128)(2,1)S(1)} %get-tuple-element.236), channel_id=1, source_target_pairs={{0,16},{16,0},{1,17},{17,1},{2,18},{18,2},{3,19},{19,3},{4,20},{20... | collective-permute-start | bytes 1179656 | tf_op jit(solution)/shard_map/ppermute | solution.py:273
  241.2 6.3 %collective-permute-start.28 = (bf16[256,768]{1,0:T(8,128)(2,1)S(1)}, bf16[256,768]{1,0:T(8,128)(2,1)S(1)}, u32[]{:S(2)}, u32[]{:S(2)}) collective-permute-start(bf16[256,768]{1,0:T(8,128)(2,1)S(1)} %get-tuple-element.235), channel_id=1, source_target_pairs={{0,16},{16,0},{1,17},{17,1},{2,18},{18,2},{3,19},{19,3},{4,20},{20... | collective-permute-start | bytes 1179656 | tf_op jit(solution)/shard_map/ppermute | solution.py:273
  241.3 21.8 %collective-permute-start.32 = (bf16[512,768]{1,0:T(8,128)(2,1)S(1)}, bf16[512,768]{1,0:T(8,128)(2,1)S(1)}, u32[]{:S(2)}, u32[]{:S(2)}) collective-permute-start(bf16[512,768]{1,0:T(8,128)(2,1)S(1)} %activated.12.refs_1_), channel_id=1, source_target_pairs={{4,0},{8,12},{5,1},{9,13},{6,2},{10,14},{7,3},{11,15},{20,16},{24,... | collective-permute-start | bytes 2359304 | tf_op jit(solution)/shard_map/ppermute | solution.py:346
  242.9 30.1 %collective-permute-start.33 = (bf16[512,768]{1,0:T(8,128)(2,1)S(1)}, bf16[512,768]{1,0:T(8,128)(2,1)S(1)}, u32[]{:S(2)}, u32[]{:S(2)}) collective-permute-start(bf16[512,768]{1,0:T(8,128)(2,1)S(1)} %stacked.15.refs_0_), channel_id=1, source_target_pairs={{0,4},{12,8},{1,5},{13,9},{2,6},{14,10},{3,7},{15,11},{16,20},{28,... | collective-permute-start | bytes 2359304 | tf_op jit(solution)/shard_map/ppermute | solution.py:335
  259.7 14.4 %collective-permute-start.34 = (bf16[512,768]{1,0:T(8,128)(2,1)S(1)}, bf16[512,768]{1,0:T(8,128)(2,1)S(1)}, u32[]{:S(2)}, u32[]{:S(2)}) collective-permute-start(bf16[512,768]{1,0:T(8,128)(2,1)S(1)} %added.14.refs_1_), channel_id=1, source_target_pairs={{4,8},{8,4},{5,9},{9,5},{6,10},{10,6},{7,11},{11,7},{20,24},{24,20... | collective-permute-start | bytes 2359304 | tf_op jit(solution)/shard_map/ppermute | solution.py:340
  261.5 21.3 %collective-permute-start.35 = (bf16[512,768]{1,0:T(8,128)(2,1)S(1)}, bf16[512,768]{1,0:T(8,128)(2,1)S(1)}, u32[]{:S(2)}, u32[]{:S(2)}) collective-permute-start(bf16[512,768]{1,0:T(8,128)(2,1)S(1)} %activated.13.refs_1_), channel_id=1, source_target_pairs={{4,0},{8,12},{5,1},{9,13},{6,2},{10,14},{7,3},{11,15},{20,16},{24,... | collective-permute-start | bytes 2359304 | tf_op jit(solution)/shard_map/ppermute | solution.py:346
  273.4 23.2 %collective-permute-start.38 = (bf16[512,768]{1,0:T(8,128)(2,1)S(1)}, bf16[512,768]{1,0:T(8,128)(2,1)S(1)}, u32[]{:S(2)}, u32[]{:S(2)}) collective-permute-start(bf16[512,768]{1,0:T(8,128)(2,1)S(1)} %added.15.refs_1_), channel_id=1, source_target_pairs={{4,8},{8,4},{5,9},{9,5},{6,10},{10,6},{7,11},{11,7},{20,24},{24,20... | collective-permute-start | bytes 2359304 | tf_op jit(solution)/shard_map/ppermute | solution.py:340
  274.1 9.1 %collective-permute-start.37 = (bf16[256,768]{1,0:T(8,128)(2,1)S(1)}, bf16[256,768]{1,0:T(8,128)(2,1)S(1)}, u32[]{:S(2)}, u32[]{:S(2)}) collective-permute-start(bf16[256,768]{1,0:T(8,128)(2,1)S(1)} %get-tuple-element.258), channel_id=1, source_target_pairs={{0,16},{16,0},{1,17},{17,1},{2,18},{18,2},{3,19},{19,3},{4,20},{20... | collective-permute-start | bytes 1179656 | tf_op jit(solution)/shard_map/ppermute | solution.py:273
  275.2 24.8 %collective-permute-start.39 = (bf16[512,768]{1,0:T(8,128)(2,1)S(1)}, bf16[512,768]{1,0:T(8,128)(2,1)S(1)}, u32[]{:S(2)}, u32[]{:S(2)}) collective-permute-start(bf16[512,768]{1,0:T(8,128)(2,1)S(1)} %activated.14.refs_1_), channel_id=1, source_target_pairs={{4,0},{8,12},{5,1},{9,13},{6,2},{10,14},{7,3},{11,15},{20,16},{24,... | collective-permute-start | bytes 2359304 | tf_op jit(solution)/shard_map/ppermute | solution.py:346
  283.1 1.8 collective-permute-start.36
  297.7 22.4 %collective-permute-start.41 = (bf16[512,768]{1,0:T(8,128)(2,1)S(1)}, bf16[512,768]{1,0:T(8,128)(2,1)S(1)}, u32[]{:S(2)}, u32[]{:S(2)}) collective-permute-start(bf16[512,768]{1,0:T(8,128)(2,1)S(1)} %activated.15.refs_1_), channel_id=1, source_target_pairs={{4,0},{8,12},{5,1},{9,13},{6,2},{10,14},{7,3},{11,15},{20,16},{24,... | collective-permute-start | bytes 2359304 | tf_op jit(solution)/shard_map/ppermute | solution.py:346
  300.3 9.6 %collective-permute-start.40 = (bf16[256,768]{1,0:T(8,128)(2,1)S(1)}, bf16[256,768]{1,0:T(8,128)(2,1)S(1)}, u32[]{:S(2)}, u32[]{:S(2)}) collective-permute-start(bf16[256,768]{1,0:T(8,128)(2,1)S(1)} %get-tuple-element.269), channel_id=1, source_target_pairs={{0,16},{16,0},{1,17},{17,1},{2,18},{18,2},{3,19},{19,3},{4,20},{20... | collective-permute-start | bytes 1179656 | tf_op jit(solution)/shard_map/ppermute | solution.py:273
  320.4 1.9 collective-permute-start.42
  320.9 23.2 %collective-permute-start.45 = (bf16[128,3072]{1,0:T(8,128)(2,1)S(1)}, bf16[128,3072]{1,0:T(8,128)(2,1)S(1)}, u32[]{:S(2)}, u32[]{:S(2)}) collective-permute-start(bf16[128,3072]{1,0:T(8,128)(2,1)S(1)} %get-tuple-element.282), channel_id=1, source_target_pairs={{0,3},{1,2},{2,1},{3,0},{4,7},{5,6},{6,5},{7,4},{8,11},{9,10},{10,... | collective-permute-start | bytes 2359304 | tf_op jit(solution)/shard_map/ppermute | solution.py:269
  320.9 36.5 %collective-permute-start.44 = (bf16[128,3072]{1,0:T(8,128)(2,1)S(1)}, bf16[128,3072]{1,0:T(8,128)(2,1)S(1)}, u32[]{:S(2)}, u32[]{:S(2)}) collective-permute-start(bf16[128,3072]{1,0:T(8,128)(2,1)S(1)} %get-tuple-element.281), channel_id=1, source_target_pairs={{0,2},{1,3},{2,0},{3,1},{4,6},{5,7},{6,4},{7,5},{8,10},{9,11},{10,... | collective-permute-start | bytes 2359304 | tf_op jit(solution)/shard_map/ppermute | solution.py:269
  332.4 24.9 %collective-permute-start.43 = (bf16[128,3072]{1,0:T(8,128)(2,1)S(1)}, bf16[128,3072]{1,0:T(8,128)(2,1)S(1)}, u32[]{:S(2)}, u32[]{:S(2)}) collective-permute-start(bf16[128,3072]{1,0:T(8,128)(2,1)S(1)} %get-tuple-element.280), channel_id=1, source_target_pairs={{0,1},{1,0},{2,3},{3,2},{4,5},{5,4},{6,7},{7,6},{8,9},{9,8},{10,11... | collective-permute-start | bytes 2359304 | tf_op jit(solution)/shard_map/ppermute | solution.py:269

commit v3 on v2

--- a/solution.py
+++ b/solution.py
@@ -6,7 +6,8 @@
 from jax.sharding import PartitionSpec as P
 
 D = 12288
-VMEM = 40 * 1024 * 1024
+MATMUL_VMEM = 28 * 1024 * 1024
+SMALL_VMEM = 8 * 1024 * 1024
 FAR, NEAR = 0, 1
 
 
@@ -23,7 +24,7 @@
     return max(t for t in range(128, limit + 1, 128) if extent % t == 0)
 
 
-def call(kernel, name, grid, scalars, operands, in_specs, out_specs, out_shape, scratch=(), aliases={}):
+def call(kernel, name, grid, scalars, operands, in_specs, out_specs, out_shape, scratch=(), aliases={}, vmem=MATMUL_VMEM):
     return pl.pallas_call(
         kernel,
         grid_spec=pltpu.PrefetchScalarGridSpec(
@@ -35,24 +36,24 @@
         ),
         out_shape=out_shape,
         input_output_aliases=aliases,
-        compiler_params=pltpu.CompilerParams(vmem_limit_bytes=VMEM),
+        compiler_params=pltpu.CompilerParams(vmem_limit_bytes=vmem),
         name=name,
     )(*scalars, *operands)
 
 
-def normalize(first, blocks, scale, gain, group, into):
+def normalize(first, blocks, scales, gain, group, into):
     rows, width = blocks[0].shape
     count = rows * len(blocks)
     tile = tile_of(width, 768)
 
-    def kernel(first_ref, scale_ref, gain_ref, *refs):
+    def kernel(first_ref, gain_ref, *refs):
         out = refs[-1]
-        for i, ref in enumerate(refs[: len(blocks)]):
-            own = pl.ds(i * rows, rows)
+        for i in range(len(blocks)):
+            ref, scale_ref = refs[i], refs[len(blocks) + i]
             value = ref[...].astype(jnp.float32)
-            centred = (value - scale_ref[own, 0:1]) * scale_ref[own, 1:2]
+            centred = (value - scale_ref[:, 0:1]) * scale_ref[:, 1:2]
             normed = (centred * gain_ref[...]).astype(jnp.bfloat16)
-            out[own, :] = jnp.where(first_ref[0] == 1, normed, ref[...])
+            out[i * rows : (i + 1) * rows, :] = jnp.where(first_ref[0] == 1, normed, ref[...])
 
     column = lambda i, _: (0, i)
     extra = [] if into is None else [into]
@@ -61,13 +62,15 @@
         "normalize",
         (width // tile,),
         [first],
-        [scale, gain.reshape(1, width), *blocks, *extra],
-        [pl.BlockSpec((count, 2), lambda i, _: (0, 0)), pl.BlockSpec((1, tile), column)]
+        [gain.reshape(1, width), *blocks, *scales, *extra],
+        [pl.BlockSpec((1, tile), column)]
         + [pl.BlockSpec((rows, tile), column)] * len(blocks)
+        + [pl.BlockSpec((rows, 2), lambda i, _: (0, 0))] * len(blocks)
         + [pl.BlockSpec(memory_space=pl.ANY)] * len(extra),
         pl.BlockSpec((count, tile), lambda i, _: (group, i)),
         jax.ShapeDtypeStruct((2 * count, width), jnp.bfloat16),
-        aliases={3 + len(blocks): 0} if extra else {},
+        aliases={2 + 2 * len(blocks): 0} if extra else {},
+        vmem=SMALL_VMEM,
     )
 
 
@@ -126,6 +129,7 @@
         [pl.BlockSpec((o.shape[0], tile), column) for o in operands],
         [pl.BlockSpec((r, tile), column) for r in out_rows],
         [jax.ShapeDtypeStruct((r, columns), jnp.bfloat16) for r in out_rows],
+        vmem=SMALL_VMEM,
     )
 
 
@@ -175,12 +179,11 @@
     return elementwise(body, "chosen", [receives], [value, arrived], out_rows)
 
 
-def down_product(section, kept, came, weight, part, parts, before, before_row, kinds):
+def down_product(section, kept, came, weight, part, parts, before, group, kinds):
     counts = [k.shape[0] for k in kept]
     count, half = sum(counts), kept[0].shape[1]
     width = weight.shape[0]
-    tile = tile_of(width, 256)
-    piece = count // len(kinds)
+    tile = tile_of(width, 512)
     n = len(kept)
 
     def kernel(section_ref, *refs):
@@ -192,19 +195,30 @@
         def _():
             at = 0
             for i, rows in enumerate(counts):
-                held_mine[at : at + rows, :] = refs[i][...]
-                held_theirs[at : at + rows, :] = refs[n + i][...]
+                held_mine[:, at : at + rows] = refs[i][...].T
+                held_theirs[:, at : at + rows] = refs[n + i][...].T
                 at += rows
 
-        product = dot_f32(held_mine[...], weight_mine[...], (1, 1))
-        product = product + dot_f32(held_theirs[...], weight_theirs[...], (1, 1))
+        product = dot_f32(weight_mine[...], held_mine[...], (1, 0))
+        product = product + dot_f32(weight_theirs[...], held_theirs[...], (1, 0))
         if before is not None:
             product = product + refs[2 * n + 2][...]
-        for i, result in enumerate(results):
-            result[...] = product[i * piece : (i + 1) * piece].astype(result.dtype)
+        if kinds:
+            product = product.T
+            piece = count // len(kinds)
+            for i, result in enumerate(results):
+                result[...] = product[i * piece : (i + 1) * piece].astype(result.dtype)
+        else:
+            results[0][...] = product
 
     whole = [pl.BlockSpec((rows, half), lambda i, s: (0, 0)) for rows in counts]
     extra = [] if before is None else [before]
+    if kinds:
+        out_specs = [pl.BlockSpec((count // len(kinds), tile), lambda i, s: (0, i))] * len(kinds)
+        out_shape = [jax.ShapeDtypeStruct((count // len(kinds), width), kind) for kind in kinds]
+    else:
+        out_specs = [pl.BlockSpec((tile, count), lambda i, s: (i, 0))]
+        out_shape = [jax.ShapeDtypeStruct((width, count), jnp.float32)]
     return call(
         kernel,
         "down_product",
@@ -217,10 +231,10 @@
             pl.BlockSpec((tile, half), lambda i, s: (i, 2 * part + s[0])),
             pl.BlockSpec((tile, half), lambda i, s: (i, 2 * part + 1 - s[0])),
         ]
-        + [pl.BlockSpec((count, tile), lambda i, s: (before_row, i))] * len(extra),
-        [pl.BlockSpec((piece, tile), lambda i, s: (0, i))] * len(kinds),
-        [jax.ShapeDtypeStruct((piece, width), kind) for kind in kinds],
-        [pltpu.VMEM((count, half), jnp.bfloat16)] * 2,
+        + [pl.BlockSpec((tile, count), lambda i, s: (i, group))] * len(extra),
+        out_specs,
+        out_shape,
+        [pltpu.VMEM((half, count), jnp.bfloat16)] * 2,
     )
 
 
@@ -228,7 +242,7 @@
     width, count = turned.shape
     counts = [k.shape[0] for k in kept]
     half = kept[0].shape[1]
-    tile = tile_of(width, 512)
+    tile = tile_of(width, 1024)
     n = len(kept)
 
     def kernel(section_ref, turned_ref, *refs):
@@ -300,22 +314,19 @@
     gathered[0] = raw
 
     values = tokens.astype(jnp.float32)
-    sums = jnp.stack([jnp.sum(values, 1), jnp.sum(values * values, 1)], 1)
-    mine = jnp.arange(peers)[:, None, None] == lax.axis_index("mp")
-    sums = lax.psum(jnp.where(mine, sums[None], 0.0), ("dp", "mp"))
-    average = sums[:, :, 0] / D
-    inverse_std = lax.rsqrt(sums[:, :, 1] / D - average * average + epsilon)
-    scale = jnp.stack([average, inverse_std], 2)
+    row_total, row_squares = lax.psum((jnp.sum(values, 1), jnp.sum(values * values, 1)), "dp")
+    average = row_total / D
+    inverse_std = lax.rsqrt(row_squares / D - average * average + epsilon)
+    own_scale = jnp.stack([average, inverse_std], 1)
+    scale = {by: from_peer(own_scale, by) for by in range(1, peers)}
+    scale[0] = own_scale
 
     far = list(range(2 * each, 4 * each))
     near = list(range(each, 2 * each)) + list(range(each))
 
     def prepare(members, group, into):
-        mp = lax.axis_index("mp")
-        scales = jnp.concatenate([lax.dynamic_index_in_dim(scale, mp ^ by, 0, False) for by in members], 0)
-        return run(
-            lambda s: normalize(first, [gathered[by] for by in members], s, gain, group, into), scales
-        )["value"]
+        blocks, scales = [gathered[by] for by in members], [scale[by] for by in members]
+        return run(lambda g: normalize(first, blocks, scales, g, group, into), gain)["value"]
 
     chunks = {}
 
@@ -358,10 +369,16 @@
         return kept, [chunks[part, g]["came"] for g in groups]
 
     both = (FAR, NEAR)
-    order = [(part, g) for part in range(parts - 1) for g in (NEAR, FAR)]
-    order += [(parts - 1, g) for g in (FAR, NEAR)]
+    order = [(part, g) for part in range(parts - 2) for g in (NEAR, FAR)]
+    order += [(part, g) for g in (FAR, NEAR) for part in (parts - 2, parts - 1)]
     count = len(order)
+    multiplied = {0}
     held = {"partial": None, "gradient": None}
+
+    def need(c):
+        if c < count and order[c][0] not in multiplied:
+            multiplied.add(order[c][0])
+            multiply(x_all, order[c][0], both)
 
     def tick(t):
         if 0 <= t - 1 < count:
@@ -371,11 +388,11 @@
         if 2 <= t + 2 < count:
             stack(chunks[order[t + 2]])
 
-    def go_down(part):
-        kept, came = hidden(part, both)
-        before = None if held["partial"] is None else held["partial"]["value"][0]
-        held["partial"] = run(
-            lambda k: down_product(section, [k] + kept[1:], came, weight, part, parts, before, 0, [jnp.float32]),
+    def go_down(part, groups, before, column, kinds=()):
+        kept, came = hidden(part, groups)
+        before = None if before is None else before["value"][0]
+        return run(
+            lambda k: down_product(section, [k] + kept[1:], came, weight, part, parts, before, column, kinds),
             kept[0],
         )
 
@@ -384,13 +401,6 @@
         into = None if held["gradient"] is None else held["gradient"]["value"]
         held["gradient"] = run(
             lambda k: weight_gradient(section, turned, [k] + kept[1:], came, part, parts, into), kept[0]
-        )
-
-    def go_last(group, kinds):
-        kept, came = hidden(parts - 1, [group])
-        before = held["partial"]["value"][0]
-        return run(
-            lambda k: down_product(section, [k], came, weight, parts - 1, parts, before, group, kinds), kept[0]
         )
 
     x_near = prepare(near, NEAR, None)
@@ -403,22 +413,23 @@
         if 0 <= t < count:
             inward(chunks[order[t]])
         if t == 0:
-            multiply(x_all, 1, both)
+            need(2)
         tick(t)
         if t == 0:
             turned = run(lambda a: a.T, x_all)["value"]
-        part, odd = t // 2 + 2, t % 2 == 1
-        if odd and part < parts:
-            multiply(x_all, part, both)
-        done, late = (t - 3) // 2, t % 2 == 1
-        if t >= 3 and done < parts - 1:
-            if late:
-                go_down(done)
+        need(t + 3)
+        if t >= 3 and (t - 3) // 2 < parts - 2:
+            if t % 2 == 1:
+                held["partial"] = go_down((t - 3) // 2, both, held["partial"], 0)
             else:
-                go_gradient(done)
+                go_gradient((t - 3) // 2)
+        if t == count - 1:
+            far_sum = go_down(parts - 2, [FAR], held["partial"], FAR)
         if t == count:
-            sent_far = go_last(FAR, [jnp.bfloat16] * 2)
-    sent_near = go_last(NEAR, [jnp.bfloat16, jnp.float32])
+            sent_far = go_down(parts - 1, [FAR], far_sum, 0, [jnp.bfloat16] * 2)
+            go_gradient(parts - 2)
+            near_sum = go_down(parts - 2, [NEAR], held["partial"], NEAR)
+    sent_near = go_down(parts - 1, [NEAR], near_sum, 0, [jnp.bfloat16, jnp.float32])
     go_gradient(parts - 1)
 
     own = sent_near["value"][1]

time: 361 us -> 324 us (0.90)
  blocking collectives: 65.5 us -> 12.4 us
  waiting for transfers between devices: 35.5 us -> 69 us
  Pallas kernels: 172 us -> 155 us
    psum x1, blocking collectives: 65.5 us -> 12.4 us  [local(): lax.psum((jnp.sum(values, 1), jnp.sum(values * values, 1)), 'dp')]
    ppermute x6 -> x9, waiting for transfers between devices: 13.3 us -> 41.5 us  [from_peer(): return lax.ppermute(value, 'mp', [(i, i ^ by) for i in range(peers)])]
    pallas_call x48 -> x49, Pallas kernels: 172 us -> 155 us  [call(): pl.pallas_call(kernel, grid_spec=pltpu.PrefetchScalarGridSpec(num_scalar_...]
    ppermute x8, waiting for transfers between devices: 11.3 us -> 23.9 us  [outward(): lax.ppermute(value, 'dp', [(hop + 1, hop), (line - 2 - hop, line - 1 - ho...]
    ppermute x6 -> x9, starting transfers between devices: 6.68 us -> 12.6 us  [from_peer(): return lax.ppermute(value, 'mp', [(i, i ^ by) for i in range(peers)])]
    ppermute x16, waiting for transfers between devices: 7.42 us -> 3.46 us  [across_sections(): return lax.ppermute(value, 'section', [(0, 1), (1, 0)])]
    ppermute x8, starting transfers between devices: 43.5 us -> 39.7 us  [inward(): lax.ppermute(value, 'dp', [(hop, hop + 1), (line - 1 - hop, line - 2 - ho...]
  transfers between devices with their start and end apart: 46 -> 49, of which waited for: 13 -> 14; matrix products, arithmetic and copies ran while one was open for 1% -> 1% of each run, Pallas kernels for 48% -> 48%
where the time goes in v3:
time: 324 us; the launch traced here: 322 us
  Pallas kernels  155 us (48%)
  starting transfers between devices  73.2 us (23%)
  waiting for transfers between devices  69 us (21%)
  blocking collectives  12.4 us (4%)
  local copies, waits for them, and re-layouts  5.92 us (2%)
  other arithmetic  4.88 us (2%)
    pallas_call x49, Pallas kernels, call(): pl.pallas_call(kernel, grid_spec=pltpu.PrefetchScalarGridSpec(num_scalar_...  155 us
    ppermute x9, waiting for transfers between devices, from_peer(): return lax.ppermute(value, 'mp', [(i, i ^ by) for i in range(peers)])  41.5 us
    ppermute x8, starting transfers between devices, inward(): lax.ppermute(value, 'dp', [(hop, hop + 1), (line - 1 - hop, line - 2 - ho...  39.7 us
    ppermute x8, waiting for transfers between devices, outward(): lax.ppermute(value, 'dp', [(hop + 1, hop), (line - 2 - hop, line - 1 - ho...  23.9 us
    ppermute x9, starting transfers between devices, from_peer(): return lax.ppermute(value, 'mp', [(i, i ^ by) for i in range(peers)])  12.6 us
    psum x1, blocking collectives, local(): lax.psum((jnp.sum(values, 1), jnp.sum(values * values, 1)), 'dp')  12.4 us
    ppermute x8, starting transfers between devices, outward(): lax.ppermute(value, 'dp', [(hop + 1, hop), (line - 2 - hop, line - 1 - ho...  10.7 us
    ppermute x8, starting transfers between devices, middle(): arrived = lax.ppermute(value, 'dp', [(half - 1, half), (half, half - 1)])  7.47 us
  transfers between devices with their start and end apart: 49, of which 14 were waited for; matrix products, arithmetic and copies ran while one was open for 1% of the time, Pallas kernels for 48%

profile of v3, /device:TPU:0, one launch (start us, length us, event | category | flops | bytes accessed | tf_op | source)
XLA Modules:
  0.0 322.0 jit_solution(10993620554222711107)
XLA Ops:
  0.6 2.1 broadcast_select_fusion.refs_1_
  2.8 2.9 collective-permute-start
  5.7 1.5 collective-permute-start.3
  7.2 1.4 convert_reduce_fusion
  8.6 12.4 %all-reduce = (f32[128]{0:T(128)S(1)}, f32[128]{0:T(128)S(1)}) all-reduce(f32[128]{0:T(128)S(1)} %get-tuple-element.293, f32[128]{0:T(128)S(1)} %get-tuple-element.292), channel_id=1, replica_groups=mesh['section'=2,'dp'=4,'mp'=4] {'dp'}, use_global_device_ids=true, to_apply=%region_3.4 | all-reduce | flops 256 | bytes 2048 | tf_op jit(solution)/shard_map/psum | solution.py:317
  21.2 1.6 collective-permute-start.1
  22.8 19.0 %collective-permute-done.1.refs_2_ = f32[128,2]{1,0:T(8,128)S(1)} collective-permute-done((f32[128,2]{1,0:T(8,128)S(1)}, f32[128,2]{1,0:T(8,128)S(1)}, u32[]{:S(2)}, u32[]{:S(2)}) %collective-permute-start.1) | collective-permute-done | bytes 1056 | tf_op jit(solution)/shard_map/ppermute | solution.py:283
  43.8 2.7 normalize.2.rows_ref.refs_4_
  46.5 5.3 %up_product.5 = (bf16[256,768]{1,0:T(8,128)(2,1)S(1)}, bf16[256,768]{1,0:T(8,128)(2,1)S(1)}) custom-call(s32[1]{0:T(128)} %bitcast.section_ref, bf16[512,3072]{1,0:T(8,128)(2,1)S(1)} %normalize.2.rows_ref.refs_4_, bf16[3072,6144]{1,0:T(8,128)(2,1)} %bitcast.20), custom_call_target="tpu_custom_call" | custom-call | tf_op jit(solution)/shard_map/up_product/pallas_call | solution.py:28
  51.8 1.7 collective-permute-done.2.refs_1_
  53.8 3.8 %collective-permute-start.8 = (bf16[512,768]{1,0:T(8,128)(2,1)S(1)}, bf16[512,768]{1,0:T(8,128)(2,1)S(1)}, u32[]{:S(2)}, u32[]{:S(2)}) collective-permute-start(bf16[512,768]{1,0:T(8,128)(2,1)S(1)} %stacked.8.refs_0_), channel_id=1, source_target_pairs={{0,4},{12,8},{1,5},{13,9},{2,6},{14,10},{3,7},{15,11},{16,20},{28,... | collective-permute-start | bytes 2359304 | tf_op jit(solution)/shard_map/ppermute | solution.py:346
  57.6 1.6 collective-permute-start.5
  59.2 1.4 collective-permute-start.6
  61.9 2.4 collective-permute-done.6.refs_3_
  64.3 2.9 normalize.3.rows_ref
  67.3 5.3 %up_product.6 = (bf16[256,768]{1,0:T(8,128)(2,1)S(1)}, bf16[256,768]{1,0:T(8,128)(2,1)S(1)}) custom-call(s32[1]{0:T(128)} %bitcast.section_ref, bf16[512,3072]{1,0:T(8,128)(2,1)S(1)} %normalize.3.rows_ref, bf16[3072,6144]{1,0:T(8,128)(2,1)} %bitcast.21), custom_call_target="tpu_custom_call" | custom-call | tf_op jit(solution)/shard_map/up_product/pallas_call | solution.py:28
  72.6 1.7 collective-permute-done.7.refs_1_
  74.3 1.5 stacked.9.refs_0_
  75.8 2.2 collective-permute-start.10
  78.0 1.7 added.8.refs_1_
  79.6 7.7 %up_product.7 = (bf16[256,768]{1,0:T(8,128)(2,1)S(1)}, bf16[256,768]{1,0:T(8,128)(2,1)S(1)}, bf16[256,768]{1,0:T(8,128)(2,1)S(1)}, bf16[256,768]{1,0:T(8,128)(2,1)S(1)}) custom-call(s32[1]{0:T(128)} %bitcast.section_ref, bf16[512,3072]{1,0:T(8,128)(2,1)S(1)} %normalize.3.rows_ref, bf16[3072,6144]{1,0:T(8,128)(2,1)} %bitcast.22), custom_call_target="tpu_custom_call" | custom-call | tf_op jit(solution)/shard_map/up_product/pallas_call | solution.py:28
  87.6 1.5 collective-permute-start.11
  89.2 1.5 stacked.10.refs_0_
  90.7 3.7 %collective-permute-start.13 = (bf16[512,768]{1,0:T(8,128)(2,1)}, bf16[512,768]{1,0:T(8,128)(2,1)}, u32[]{:S(2)}, u32[]{:S(2)}) collective-permute-start(bf16[512,768]{1,0:T(8,128)(2,1)} %stacked.10.refs_0_), channel_id=1, source_target_pairs={{0,4},{12,8},{1,5},{13,9},{2,6},{14,10},{3,7},{15,11},{16,20},{28,... | collective-permute-start | bytes 2359304 | tf_op jit(solution)/shard_map/ppermute | solution.py:346
  94.5 2.8 copy.17
  97.2 2.3 added.9.refs_1_
  100.3 3.4 %activated.8.refs_1_ = bf16[512,768]{1,0:T(8,128)(2,1)} custom-call(s32[1]{0:T(128)S(6)} %sub.6.first_ref.refs_0_, bf16[512,768]{1,0:T(8,128)(2,1)} %added.8.refs_1_, bf16[512,768]{1,0:T(8,128)(2,1)} %collective-permute-done.11.refs_2_), custom_call_target="tpu_custom_call" | custom-call | tf_op jit(solution)/shard_map/activated/pallas_call | solution.py:28
  105.0 1.5 stacked.11.refs_0_
  106.5 12.5 %collective-permute-start.17 = (bf16[512,768]{1,0:T(8,128)(2,1)}, bf16[512,768]{1,0:T(8,128)(2,1)}, u32[]{:S(2)}, u32[]{:S(2)}) collective-permute-start(bf16[512,768]{1,0:T(8,128)(2,1)} %stacked.11.refs_0_), channel_id=1, source_target_pairs={{0,4},{12,8},{1,5},{13,9},{2,6},{14,10},{3,7},{15,11},{16,20},{28,... | collective-permute-start | bytes 2359304 | tf_op jit(solution)/shard_map/ppermute | solution.py:346
  119.0 8.5 %up_product.8 = (bf16[256,768]{1,0:T(8,128)(2,1)S(1)}, bf16[256,768]{1,0:T(8,128)(2,1)S(1)}, bf16[256,768]{1,0:T(8,128)(2,1)}, bf16[256,768]{1,0:T(8,128)(2,1)S(1)}) custom-call(s32[1]{0:T(128)} %bitcast.section_ref, bf16[512,3072]{1,0:T(8,128)(2,1)S(1)} %normalize.3.rows_ref, bf16[3072,6144]{1,0:T(8,128)(2,1)} %bitcast.23), custom_call_target="tpu_custom_call" | custom-call | tf_op jit(solution)/shard_map/up_product/pallas_call | solution.py:28
  127.5 3.4 %added.10.refs_1_ = bf16[512,768]{1,0:T(8,128)(2,1)} custom-call(bf16[512,768]{1,0:T(8,128)(2,1)} %stacked.10.refs_0_, bf16[512,768]{1,0:T(8,128)(2,1)} %collective-permute-done.13.refs_1_), custom_call_target="tpu_custom_call" | custom-call | tf_op jit(solution)/shard_map/added/pallas_call | solution.py:28
  131.0 1.5 collective-permute-start.18
  132.5 2.1 activated.9.refs_1_
  134.6 1.5 collective-permute-start.19
  136.2 2.2 chosen.8
  139.4 1.9 stacked.12.refs_0_
  141.3 7.7 %up_product.9 = (bf16[256,768]{1,0:T(8,128)(2,1)S(1)}, bf16[256,768]{1,0:T(8,128)(2,1)S(1)}, bf16[256,768]{1,0:T(8,128)(2,1)S(1)}, bf16[256,768]{1,0:T(8,128)(2,1)S(1)}) custom-call(s32[1]{0:T(128)} %bitcast.section_ref, bf16[512,3072]{1,0:T(8,128)(2,1)S(1)} %normalize.3.rows_ref, bf16[3072,6144]{1,0:T(8,128)(2,1)} %bitcast.24), custom_call_target="tpu_custom_call" | custom-call | tf_op jit(solution)/shard_map/up_product/pallas_call | solution.py:28
  149.1 5.2 %collective-permute-start.23 = (bf16[512,768]{1,0:T(8,128)(2,1)S(1)}, bf16[512,768]{1,0:T(8,128)(2,1)S(1)}, u32[]{:S(2)}, u32[]{:S(2)}) collective-permute-start(bf16[512,768]{1,0:T(8,128)(2,1)S(1)} %stacked.12.refs_0_), channel_id=1, source_target_pairs={{0,4},{12,8},{1,5},{13,9},{2,6},{14,10},{3,7},{15,11},{16,20},{28,... | collective-permute-start | bytes 2359304 | tf_op jit(solution)/shard_map/ppermute | solution.py:346
  154.3 2.3 added.11.refs_1_
  157.9 2.7 activated.10.refs_1_
  160.6 2.2 chosen.9
  164.6 4.6 %collective-permute-start.27 = (bf16[512,768]{1,0:T(8,128)(2,1)S(1)}, bf16[512,768]{1,0:T(8,128)(2,1)S(1)}, u32[]{:S(2)}, u32[]{:S(2)}) collective-permute-start(bf16[512,768]{1,0:T(8,128)(2,1)S(1)} %stacked.13.refs_0_), channel_id=1, source_target_pairs={{0,4},{12,8},{1,5},{13,9},{2,6},{14,10},{3,7},{15,11},{16,20},{28,... | collective-permute-start | bytes 2359304 | tf_op jit(solution)/shard_map/ppermute | solution.py:346
  169.3 8.7 %down_product.6.refs_6_ = f32[3072,512]{1,0:T(8,128)S(1)} custom-call(s32[1]{0:T(128)} %bitcast.section_ref, bf16[256,768]{1,0:T(8,128)(2,1)S(1)} %get-tuple-element.224.refs_0_, bf16[256,768]{1,0:T(8,128)(2,1)S(1)} %get-tuple-element.210.refs_1_, bf16[256,768]{1,0:T(8,128)(2,1)S(1)} %collective-permute-done.21.refs_2_, ...), custom_call_target="tpu_custom_call" | custom-call | tf_op jit(solution)/shard_map/down_product/pallas_call | solution.py:28
  181.8 3.0 collective-permute-done.25.refs_2_
  185.3 3.0 collective-permute-start.33
  189.0 7.5 %weight_gradient.4.refs_4_ = bf16[3072,6144]{1,0:T(8,128)(2,1)} custom-call(s32[1]{0:T(128)} %bitcast.section_ref, bf16[3072,512]{1,0:T(8,128)(2,1)S(1)} %bitcast.14, bf16[256,768]{1,0:T(8,128)(2,1)S(1)} %get-tuple-element.224.refs_0_, bf16[256,768]{1,0:T(8,128)(2,1)S(1)} %get-tuple-element.210.refs_1_, ...), custom_call_target="tpu_custom_call" | custom-call | tf_op jit(solution)/shard_map/weight_gradient/pallas_call | solution.py:28
  197.9 3.7 %collective-permute-done.29.refs_2_ = bf16[512,768]{1,0:T(8,128)(2,1)S(1)} collective-permute-done((bf16[512,768]{1,0:T(8,128)(2,1)S(1)}, bf16[512,768]{1,0:T(8,128)(2,1)S(1)}, u32[]{:S(2)}, u32[]{:S(2)}) %collective-permute-start.29) | collective-permute-done | bytes 786464 | tf_op jit(solution)/shard_map/ppermute | solution.py:357
  204.3 4.6 %collective-permute-start.36 = (bf16[512,768]{1,0:T(8,128)(2,1)S(1)}, bf16[512,768]{1,0:T(8,128)(2,1)S(1)}, u32[]{:S(2)}, u32[]{:S(2)}) collective-permute-start(bf16[512,768]{1,0:T(8,128)(2,1)S(1)} %stacked.15.refs_0_), channel_id=1, source_target_pairs={{0,4},{12,8},{1,5},{13,9},{2,6},{14,10},{3,7},{15,11},{16,20},{28,... | collective-permute-start | bytes 2359304 | tf_op jit(solution)/shard_map/ppermute | solution.py:346
  208.9 8.8 %down_product.7.refs_4_ = f32[3072,512]{1,0:T(8,128)S(1)} custom-call(s32[1]{0:T(128)} %bitcast.section_ref, bf16[256,768]{1,0:T(8,128)(2,1)S(1)} %get-tuple-element.250.refs_0_, bf16[256,768]{1,0:T(8,128)(2,1)S(1)} %get-tuple-element.237.refs_1_, bf16[256,768]{1,0:T(8,128)(2,1)S(1)} %collective-permute-done.31.refs_2_, ...), custom_call_target="tpu_custom_call" | custom-call | tf_op jit(solution)/shard_map/down_product/pallas_call | solution.py:28
  221.2 3.3 %collective-permute-done.35.refs_2_ = bf16[512,768]{1,0:T(8,128)(2,1)S(1)} collective-permute-done((bf16[512,768]{1,0:T(8,128)(2,1)S(1)}, bf16[512,768]{1,0:T(8,128)(2,1)S(1)}, u32[]{:S(2)}, u32[]{:S(2)}) %collective-permute-start.35) | collective-permute-done | bytes 786464 | tf_op jit(solution)/shard_map/ppermute | solution.py:357
  224.9 7.5 %weight_gradient.5.refs_4_ = bf16[3072,6144]{1,0:T(8,128)(2,1)} custom-call(s32[1]{0:T(128)} %bitcast.section_ref, bf16[3072,512]{1,0:T(8,128)(2,1)S(1)} %bitcast.15, bf16[256,768]{1,0:T(8,128)(2,1)S(1)} %get-tuple-element.250.refs_0_, bf16[256,768]{1,0:T(8,128)(2,1)S(1)} %get-tuple-element.237.refs_1_, ...), custom_call_target="tpu_custom_call", output_to_operand_aliasing={{}: (6, {})} | custom-call | tf_op jit(solution)/shard_map/weight_gradient/pallas_call | solution.py:28
  234.6 1.5 collective-permute-start.41
  236.2 6.9 %collective-permute-done.38.refs_2_ = bf16[512,768]{1,0:T(8,128)(2,1)S(1)} collective-permute-done((bf16[512,768]{1,0:T(8,128)(2,1)S(1)}, bf16[512,768]{1,0:T(8,128)(2,1)S(1)}, u32[]{:S(2)}, u32[]{:S(2)}) %collective-permute-start.38) | collective-permute-done | bytes 786464 | tf_op jit(solution)/shard_map/ppermute | solution.py:357
  243.4 7.1 %down_product.8.refs_4_ = f32[3072,256]{1,0:T(8,128)S(1)} custom-call(s32[1]{0:T(128)} %bitcast.section_ref, bf16[256,768]{1,0:T(8,128)(2,1)S(1)} %get-tuple-element.274.refs_0_, bf16[256,768]{1,0:T(8,128)(2,1)S(1)} %collective-permute-done.39.refs_1_.refs_2_, bf16[3072,6144]{1,0:T(8,128)(2,1)} %bitcast.29, bf16[3072,6144]{1,0:T(8,128)(2,1)} %bitcast.30, ...), custom_call_target="tpu_custom_call" | custom-call | tf_op jit(solution)/shard_map/down_product/pallas_call | solution.py:28
  252.9 7.0 %collective-permute-done.41.refs_2_ = bf16[512,768]{1,0:T(8,128)(2,1)S(1)} collective-permute-done((bf16[512,768]{1,0:T(8,128)(2,1)S(1)}, bf16[512,768]{1,0:T(8,128)(2,1)S(1)}, u32[]{:S(2)}, u32[]{:S(2)}) %collective-permute-start.41) | collective-permute-done | bytes 786464 | tf_op jit(solution)/shard_map/ppermute | solution.py:357
  260.3 7.4 %down_product.9 = (bf16[128,3072]{1,0:T(8,128)(2,1)S(1)}, bf16[128,3072]{1,0:T(8,128)(2,1)S(1)}) custom-call(s32[1]{0:T(128)} %bitcast.section_ref, bf16[256,768]{1,0:T(8,128)(2,1)S(1)} %get-tuple-element.289.refs_0_, bf16[256,768]{1,0:T(8,128)(2,1)S(1)} %collective-permute-done.42.refs_1_.refs_2_, bf16[3072,6144]{1,0:T(8,128)(2,1)} %bitcast.31, ...), custom_call_target="tpu_custom_call" | custom-call | tf_op jit(solution)/shard_map/down_product/pallas_call | solution.py:28
  267.8 7.5 %weight_gradient.6.refs_4_ = bf16[3072,6144]{1,0:T(8,128)(2,1)} custom-call(s32[1]{0:T(128)} %bitcast.section_ref, bf16[3072,512]{1,0:T(8,128)(2,1)S(1)} %bitcast.16, bf16[256,768]{1,0:T(8,128)(2,1)S(1)} %get-tuple-element.274.refs_0_, bf16[256,768]{1,0:T(8,128)(2,1)S(1)} %get-tuple-element.277.refs_1_.refs_0_, ...), custom_call_target="tpu_custom_call", output_to_operand_aliasing={{}: (6, {})} | custom-call | tf_op jit(solution)/shard_map/weight_gradient/pallas_call | solution.py:28
  275.3 7.1 %down_product.10.refs_4_ = f32[3072,256]{1,0:T(8,128)S(1)} custom-call(s32[1]{0:T(128)} %bitcast.section_ref, bf16[256,768]{1,0:T(8,128)(2,1)S(1)} %get-tuple-element.277.refs_1_.refs_0_, bf16[256,768]{1,0:T(8,128)(2,1)S(1)} %collective-permute-done.43.refs_3_.refs_1_, bf16[3072,6144]{1,0:T(8,128)(2,1)} %bitcast.33, bf16[3072,6144]{1,0:T(8,128)(2,1)} %bitcast.34, ...), custom_call_target="tpu_custom_call" | custom-call | tf_op jit(solution)/shard_map/down_product/pallas_call | solution.py:28
  283.3 2.4 collective-permute-start.48
  286.2 7.5 %down_product.11 = (bf16[128,3072]{1,0:T(8,128)(2,1)S(1)}, f32[128,3072]{1,0:T(8,128)S(1)}) custom-call(s32[1]{0:T(128)} %bitcast.section_ref, bf16[256,768]{1,0:T(8,128)(2,1)S(1)} %get-tuple-element.290.refs_0_.refs_1_, bf16[256,768]{1,0:T(8,128)(2,1)S(1)} %collective-permute-done.45.refs_1_.refs_3_, bf16[3072,6144]{1,0:T(8,128)(2,1)} %bitcast.35, ...), custom_call_target="tpu_custom_call" | custom-call | tf_op jit(solution)/shard_map/down_product/pallas_call | solution.py:28
  294.4 7.5 %weight_gradient.7 = bf16[3072,6144]{1,0:T(8,128)(2,1)} custom-call(s32[1]{0:T(128)} %bitcast.section_ref, bf16[3072,512]{1,0:T(8,128)(2,1)S(1)} %bitcast.17, bf16[256,768]{1,0:T(8,128)(2,1)S(1)} %get-tuple-element.289.refs_0_, bf16[256,768]{1,0:T(8,128)(2,1)S(1)} %get-tuple-element.290.refs_0_.refs_1_, ...), custom_call_target="tpu_custom_call", output_to_operand_aliasing={{}: (6, {})} | custom-call | tf_op jit(solution)/shard_map/weight_gradient/pallas_call | solution.py:28
  301.9 2.7 collective-permute-done.48
  304.6 15.9 %collective-permute-done.47 = bf16[128,3072]{1,0:T(8,128)(2,1)S(1)} collective-permute-done((bf16[128,3072]{1,0:T(8,128)(2,1)S(1)}, bf16[128,3072]{1,0:T(8,128)(2,1)S(1)}, u32[]{:S(2)}, u32[]{:S(2)}) %collective-permute-start.47) | collective-permute-done | bytes 786464 | tf_op jit(solution)/shard_map/ppermute | solution.py:283
  320.6 1.3 fusion.1
  (109 shorter events, 30.5 us)
Async XLA Ops:
  0.6 42.0 %copy-start.5 = (f32[3072]{0:T(1024)S(1)}, f32[3072]{0:T(1024)}, u32[]{:S(2)}) copy-start(f32[3072]{0:T(1024)} %param.6) | copy-start | bytes 36868
  2.8 39.0 %collective-permute-start = (bf16[128,3072]{1,0:T(8,128)(2,1)}, bf16[128,3072]{1,0:T(8,128)(2,1)S(1)}, u32[]{:S(2)}, u32[]{:S(2)}) collective-permute-start(bf16[128,3072]{1,0:T(8,128)(2,1)} %broadcast_select_fusion.refs_1_), channel_id=1, source_target_pairs={{0,1},{1,0},{2,3},{3,2},{4,5},{5,4},{6,7},{7,6},{8,9},{9,8},{10,11... | collective-permute-start | bytes 2359304 | tf_op jit(solution)/shard_map/ppermute | solution.py:283
  5.7 58.7 %collective-permute-start.3 = (bf16[128,3072]{1,0:T(8,128)(2,1)}, bf16[128,3072]{1,0:T(8,128)(2,1)}, u32[]{:S(2)}, u32[]{:S(2)}) collective-permute-start(bf16[128,3072]{1,0:T(8,128)(2,1)} %broadcast_select_fusion.refs_1_), channel_id=1, source_target_pairs={{0,2},{1,3},{2,0},{3,1},{4,6},{5,7},{6,4},{7,5},{8,10},{9,11},{10,... | collective-permute-start | bytes 2359304 | tf_op jit(solution)/shard_map/ppermute | solution.py:283
  7.2 57.1 %collective-permute-start.4 = (bf16[128,3072]{1,0:T(8,128)(2,1)}, bf16[128,3072]{1,0:T(8,128)(2,1)}, u32[]{:S(2)}, u32[]{:S(2)}) collective-permute-start(bf16[128,3072]{1,0:T(8,128)(2,1)} %broadcast_select_fusion.refs_1_), channel_id=1, source_target_pairs={{0,3},{1,2},{2,1},{3,0},{4,7},{5,6},{6,5},{7,4},{8,11},{9,10},{10,... | collective-permute-start | bytes 2359304 | tf_op jit(solution)/shard_map/ppermute | solution.py:283
  21.2 20.5 %collective-permute-start.1 = (f32[128,2]{1,0:T(8,128)S(1)}, f32[128,2]{1,0:T(8,128)S(1)}, u32[]{:S(2)}, u32[]{:S(2)}) collective-permute-start(f32[128,2]{1,0:T(8,128)S(1)} %copy.13.refs_3_), channel_id=1, source_target_pairs={{0,1},{1,0},{2,3},{3,2},{4,5},{5,4},{6,7},{7,6},{8,9},{9,8},{10,11... | collective-permute-start | bytes 3080 | tf_op jit(solution)/shard_map/ppermute | solution.py:283
  41.7 0.9 copy-start.1
  42.6 1.1 copy-start.2
  51.8 1.8 collective-permute-start.2
  53.8 24.2 %collective-permute-start.8 = (bf16[512,768]{1,0:T(8,128)(2,1)S(1)}, bf16[512,768]{1,0:T(8,128)(2,1)S(1)}, u32[]{:S(2)}, u32[]{:S(2)}) collective-permute-start(bf16[512,768]{1,0:T(8,128)(2,1)S(1)} %stacked.8.refs_0_), channel_id=1, source_target_pairs={{0,4},{12,8},{1,5},{13,9},{2,6},{14,10},{3,7},{15,11},{16,20},{28,... | collective-permute-start | bytes 2359304 | tf_op jit(solution)/shard_map/ppermute | solution.py:346
  57.6 4.3 %collective-permute-start.5 = (f32[128,2]{1,0:T(8,128)S(1)}, f32[128,2]{1,0:T(8,128)S(1)}, u32[]{:S(2)}, u32[]{:S(2)}) collective-permute-start(f32[128,2]{1,0:T(8,128)S(1)} %copy.13.refs_3_), channel_id=1, source_target_pairs={{0,2},{1,3},{2,0},{3,1},{4,6},{5,7},{6,4},{7,5},{8,10},{9,11},{10,... | collective-permute-start | bytes 3080 | tf_op jit(solution)/shard_map/ppermute | solution.py:283
  59.2 5.2 %collective-permute-start.6 = (f32[128,2]{1,0:T(8,128)S(1)}, f32[128,2]{1,0:T(8,128)S(1)}, u32[]{:S(2)}, u32[]{:S(2)}) collective-permute-start(f32[128,2]{1,0:T(8,128)S(1)} %copy.13.refs_3_), channel_id=1, source_target_pairs={{0,3},{1,2},{2,1},{3,0},{4,7},{5,6},{6,5},{7,4},{8,11},{9,10},{10,... | collective-permute-start | bytes 3080 | tf_op jit(solution)/shard_map/ppermute | solution.py:283
  72.5 1.8 collective-permute-start.7
  75.8 21.4 %collective-permute-start.10 = (bf16[512,768]{1,0:T(8,128)(2,1)}, bf16[512,768]{1,0:T(8,128)(2,1)}, u32[]{:S(2)}, u32[]{:S(2)}) collective-permute-start(bf16[512,768]{1,0:T(8,128)(2,1)} %stacked.9.refs_0_), channel_id=1, source_target_pairs={{0,4},{12,8},{1,5},{13,9},{2,6},{14,10},{3,7},{15,11},{16,20},{28,... | collective-permute-start | bytes 2359304 | tf_op jit(solution)/shard_map/ppermute | solution.py:346
  87.4 3.3 %copy-start.8 = (bf16[256,768]{1,0:T(8,128)(2,1)}, bf16[256,768]{1,0:T(8,128)(2,1)S(1)}, u32[]{:S(2)}) copy-start(bf16[256,768]{1,0:T(8,128)(2,1)S(1)} %get-tuple-element.171) | copy-start | bytes 1179652
  87.4 1.8 collective-permute-start.9
  87.6 12.7 %collective-permute-start.11 = (bf16[512,768]{1,0:T(8,128)(2,1)}, bf16[512,768]{1,0:T(8,128)(2,1)}, u32[]{:S(2)}, u32[]{:S(2)}) collective-permute-start(bf16[512,768]{1,0:T(8,128)(2,1)} %added.8.refs_1_), channel_id=1, source_target_pairs={{4,8},{8,4},{5,9},{9,5},{6,10},{10,6},{7,11},{11,7},{20,24},{24,20... | collective-permute-start | bytes 2359304 | tf_op jit(solution)/shard_map/ppermute | solution.py:351
  90.7 36.8 %collective-permute-start.13 = (bf16[512,768]{1,0:T(8,128)(2,1)}, bf16[512,768]{1,0:T(8,128)(2,1)}, u32[]{:S(2)}, u32[]{:S(2)}) collective-permute-start(bf16[512,768]{1,0:T(8,128)(2,1)} %stacked.10.refs_0_), channel_id=1, source_target_pairs={{0,4},{12,8},{1,5},{13,9},{2,6},{14,10},{3,7},{15,11},{16,20},{28,... | collective-permute-start | bytes 2359304 | tf_op jit(solution)/shard_map/ppermute | solution.py:346
  99.5 33.0 %collective-permute-start.14 = (bf16[512,768]{1,0:T(8,128)(2,1)S(1)}, bf16[512,768]{1,0:T(8,128)(2,1)S(1)}, u32[]{:S(2)}, u32[]{:S(2)}) collective-permute-start(bf16[512,768]{1,0:T(8,128)(2,1)S(1)} %added.9.refs_1_), channel_id=1, source_target_pairs={{4,8},{8,4},{5,9},{9,5},{6,10},{10,6},{7,11},{11,7},{20,24},{24,20... | collective-permute-start | bytes 2359304 | tf_op jit(solution)/shard_map/ppermute | solution.py:351
  100.2 4.8 %collective-permute-start.12 = (bf16[256,768]{1,0:T(8,128)(2,1)}, bf16[256,768]{1,0:T(8,128)(2,1)S(1)}, u32[]{:S(2)}, u32[]{:S(2)}) collective-permute-start(bf16[256,768]{1,0:T(8,128)(2,1)} %copy-done.8), channel_id=1, source_target_pairs={{0,16},{16,0},{1,17},{17,1},{2,18},{18,2},{3,19},{19,3},{4,20},{20... | collective-permute-start | bytes 1179656 | tf_op jit(solution)/shard_map/ppermute | solution.py:287
  103.7 32.4 %collective-permute-start.15 = (bf16[512,768]{1,0:T(8,128)(2,1)}, bf16[512,768]{1,0:T(8,128)(2,1)}, u32[]{:S(2)}, u32[]{:S(2)}) collective-permute-start(bf16[512,768]{1,0:T(8,128)(2,1)} %activated.8.refs_1_), channel_id=1, source_target_pairs={{4,0},{8,12},{5,1},{9,13},{6,2},{10,14},{7,3},{11,15},{20,16},{24,... | collective-permute-start | bytes 2359304 | tf_op jit(solution)/shard_map/ppermute | solution.py:357
  106.5 47.8 %collective-permute-start.17 = (bf16[512,768]{1,0:T(8,128)(2,1)}, bf16[512,768]{1,0:T(8,128)(2,1)}, u32[]{:S(2)}, u32[]{:S(2)}) collective-permute-start(bf16[512,768]{1,0:T(8,128)(2,1)} %stacked.11.refs_0_), channel_id=1, source_target_pairs={{0,4},{12,8},{1,5},{13,9},{2,6},{14,10},{3,7},{15,11},{16,20},{28,... | collective-permute-start | bytes 2359304 | tf_op jit(solution)/shard_map/ppermute | solution.py:346
  127.5 7.1 %copy-start.3 = (bf16[256,768]{1,0:T(8,128)(2,1)}, bf16[256,768]{1,0:T(8,128)(2,1)S(1)}, u32[]{:S(2)}) copy-start(bf16[256,768]{1,0:T(8,128)(2,1)S(1)} %get-tuple-element.187.refs_0_) | copy-start | bytes 1179652
  127.5 8.5 %copy-start.6 = (bf16[256,768]{1,0:T(8,128)(2,1)}, bf16[256,768]{1,0:T(8,128)(2,1)S(1)}, u32[]{:S(2)}) copy-start(bf16[256,768]{1,0:T(8,128)(2,1)S(1)} %get-tuple-element.223) | copy-start | bytes 1179652
  131.0 26.6 %collective-permute-start.18 = (bf16[512,768]{1,0:T(8,128)(2,1)}, bf16[512,768]{1,0:T(8,128)(2,1)}, u32[]{:S(2)}, u32[]{:S(2)}) collective-permute-start(bf16[512,768]{1,0:T(8,128)(2,1)} %added.10.refs_1_), channel_id=1, source_target_pairs={{4,8},{8,4},{5,9},{9,5},{6,10},{10,6},{7,11},{11,7},{20,24},{24,20... | collective-permute-start | bytes 2359304 | tf_op jit(solution)/shard_map/ppermute | solution.py:351
  134.6 26.0 %collective-permute-start.19 = (bf16[512,768]{1,0:T(8,128)(2,1)}, bf16[512,768]{1,0:T(8,128)(2,1)}, u32[]{:S(2)}, u32[]{:S(2)}) collective-permute-start(bf16[512,768]{1,0:T(8,128)(2,1)} %activated.9.refs_1_), channel_id=1, source_target_pairs={{4,0},{8,12},{5,1},{9,13},{6,2},{10,14},{7,3},{11,15},{20,16},{24,... | collective-permute-start | bytes 2359304 | tf_op jit(solution)/shard_map/ppermute | solution.py:357
  136.1 2.3 collective-permute-start.16
  138.4 1.0 copy-start.4
  149.1 29.0 %collective-permute-start.23 = (bf16[512,768]{1,0:T(8,128)(2,1)S(1)}, bf16[512,768]{1,0:T(8,128)(2,1)S(1)}, u32[]{:S(2)}, u32[]{:S(2)}) collective-permute-start(bf16[512,768]{1,0:T(8,128)(2,1)S(1)} %stacked.12.refs_0_), channel_id=1, source_target_pairs={{0,4},{12,8},{1,5},{13,9},{2,6},{14,10},{3,7},{15,11},{16,20},{28,... | collective-permute-start | bytes 2359304 | tf_op jit(solution)/shard_map/ppermute | solution.py:346
  156.6 22.7 %collective-permute-start.24 = (bf16[512,768]{1,0:T(8,128)(2,1)S(1)}, bf16[512,768]{1,0:T(8,128)(2,1)S(1)}, u32[]{:S(2)}, u32[]{:S(2)}) collective-permute-start(bf16[512,768]{1,0:T(8,128)(2,1)S(1)} %added.11.refs_1_), channel_id=1, source_target_pairs={{4,8},{8,4},{5,9},{9,5},{6,10},{10,6},{7,11},{11,7},{20,24},{24,20... | collective-permute-start | bytes 2359304 | tf_op jit(solution)/shard_map/ppermute | solution.py:351
  157.3 5.8 %collective-permute-start.20 = (bf16[256,768]{1,0:T(8,128)(2,1)S(1)}, bf16[256,768]{1,0:T(8,128)(2,1)S(1)}, u32[]{:S(2)}, u32[]{:S(2)}) collective-permute-start(bf16[256,768]{1,0:T(8,128)(2,1)S(1)} %get-tuple-element.208), channel_id=1, source_target_pairs={{0,16},{16,0},{1,17},{17,1},{2,18},{18,2},{3,19},{19,3},{4,20},{20... | collective-permute-start | bytes 1179656 | tf_op jit(solution)/shard_map/ppermute | solution.py:287
  157.6 7.0 %collective-permute-start.22 = (bf16[256,768]{1,0:T(8,128)(2,1)S(1)}, bf16[256,768]{1,0:T(8,128)(2,1)S(1)}, u32[]{:S(2)}, u32[]{:S(2)}) collective-permute-start(bf16[256,768]{1,0:T(8,128)(2,1)S(1)} %get-tuple-element.212), channel_id=1, source_target_pairs={{0,16},{16,0},{1,17},{17,1},{2,18},{18,2},{3,19},{19,3},{4,20},{20... | collective-permute-start | bytes 1179656 | tf_op jit(solution)/shard_map/ppermute | solution.py:287
  162.8 6.5 %collective-permute-start.21 = (bf16[256,768]{1,0:T(8,128)(2,1)S(1)}, bf16[256,768]{1,0:T(8,128)(2,1)S(1)}, u32[]{:S(2)}, u32[]{:S(2)}) collective-permute-start(bf16[256,768]{1,0:T(8,128)(2,1)S(1)} %get-tuple-element.211), channel_id=1, source_target_pairs={{0,16},{16,0},{1,17},{17,1},{2,18},{18,2},{3,19},{19,3},{4,20},{20... | collective-permute-start | bytes 1179656 | tf_op jit(solution)/shard_map/ppermute | solution.py:287
  163.1 21.7 %collective-permute-start.25 = (bf16[512,768]{1,0:T(8,128)(2,1)S(1)}, bf16[512,768]{1,0:T(8,128)(2,1)S(1)}, u32[]{:S(2)}, u32[]{:S(2)}) collective-permute-start(bf16[512,768]{1,0:T(8,128)(2,1)S(1)} %activated.10.refs_1_), channel_id=1, source_target_pairs={{4,0},{8,12},{5,1},{9,13},{6,2},{10,14},{7,3},{11,15},{20,16},{24,... | collective-permute-start | bytes 2359304 | tf_op jit(solution)/shard_map/ppermute | solution.py:357
  164.6 23.9 %collective-permute-start.27 = (bf16[512,768]{1,0:T(8,128)(2,1)S(1)}, bf16[512,768]{1,0:T(8,128)(2,1)S(1)}, u32[]{:S(2)}, u32[]{:S(2)}) collective-permute-start(bf16[512,768]{1,0:T(8,128)(2,1)S(1)} %stacked.13.refs_0_), channel_id=1, source_target_pairs={{0,4},{12,8},{1,5},{13,9},{2,6},{14,10},{3,7},{15,11},{16,20},{28,... | collective-permute-start | bytes 2359304 | tf_op jit(solution)/shard_map/ppermute | solution.py:346
  178.0 3.6 %copy-start.7 = (bf16[256,768]{1,0:T(8,128)(2,1)S(1)}, bf16[256,768]{1,0:T(8,128)(2,1)}, u32[]{:S(2)}) copy-start(bf16[256,768]{1,0:T(8,128)(2,1)} %copy-done.6) | copy-start | bytes 1179652
  178.5 10.5 %copy-start = (bf16[512,3072]{0,1:T(8,128)(2,1)S(1)}, bf16[512,3072]{0,1:T(8,128)(2,1)}, u32[]{:S(2)}) copy-start(bf16[512,3072]{0,1:T(8,128)(2,1)} %copy.17) | copy-start | bytes 9437188
  178.5 18.4 %collective-permute-start.28 = (bf16[512,768]{1,0:T(8,128)(2,1)S(1)}, bf16[512,768]{1,0:T(8,128)(2,1)S(1)}, u32[]{:S(2)}, u32[]{:S(2)}) collective-permute-start(bf16[512,768]{1,0:T(8,128)(2,1)S(1)} %added.12.refs_1_), channel_id=1, source_target_pairs={{4,8},{8,4},{5,9},{9,5},{6,10},{10,6},{7,11},{11,7},{20,24},{24,20... | collective-permute-start | bytes 2359304 | tf_op jit(solution)/shard_map/ppermute | solution.py:351
  180.4 21.2 %collective-permute-start.29 = (bf16[512,768]{1,0:T(8,128)(2,1)S(1)}, bf16[512,768]{1,0:T(8,128)(2,1)S(1)}, u32[]{:S(2)}, u32[]{:S(2)}) collective-permute-start(bf16[512,768]{1,0:T(8,128)(2,1)S(1)} %activated.11.refs_1_), channel_id=1, source_target_pairs={{4,0},{8,12},{5,1},{9,13},{6,2},{10,14},{7,3},{11,15},{20,16},{24,... | collective-permute-start | bytes 2359304 | tf_op jit(solution)/shard_map/ppermute | solution.py:357
  181.7 3.4 %collective-permute-start.26 = (bf16[256,768]{1,0:T(8,128)(2,1)S(1)}, bf16[256,768]{1,0:T(8,128)(2,1)S(1)}, u32[]{:S(2)}, u32[]{:S(2)}) collective-permute-start(bf16[256,768]{1,0:T(8,128)(2,1)S(1)} %copy-done.7), channel_id=1, source_target_pairs={{0,16},{16,0},{1,17},{17,1},{2,18},{18,2},{3,19},{19,3},{4,20},{20... | collective-permute-start | bytes 1179656 | tf_op jit(solution)/shard_map/ppermute | solution.py:287
  185.3 32.3 %collective-permute-start.33 = (bf16[512,768]{1,0:T(8,128)(2,1)S(1)}, bf16[512,768]{1,0:T(8,128)(2,1)S(1)}, u32[]{:S(2)}, u32[]{:S(2)}) collective-permute-start(bf16[512,768]{1,0:T(8,128)(2,1)S(1)} %stacked.14.refs_0_), channel_id=1, source_target_pairs={{0,4},{12,8},{1,5},{13,9},{2,6},{14,10},{3,7},{15,11},{16,20},{28,... | collective-permute-start | bytes 2359304 | tf_op jit(solution)/shard_map/ppermute | solution.py:346
  188.4 14.3 %collective-permute-start.30 = (bf16[256,768]{1,0:T(8,128)(2,1)S(1)}, bf16[256,768]{1,0:T(8,128)(2,1)S(1)}, u32[]{:S(2)}, u32[]{:S(2)}) collective-permute-start(bf16[256,768]{1,0:T(8,128)(2,1)S(1)} %get-tuple-element.235), channel_id=1, source_target_pairs={{0,16},{16,0},{1,17},{17,1},{2,18},{18,2},{3,19},{19,3},{4,20},{20... | collective-permute-start | bytes 1179656 | tf_op jit(solution)/shard_map/ppermute | solution.py:287
  188.6 15.7 %collective-permute-start.32 = (bf16[256,768]{1,0:T(8,128)(2,1)S(1)}, bf16[256,768]{1,0:T(8,128)(2,1)S(1)}, u32[]{:S(2)}, u32[]{:S(2)}) collective-permute-start(bf16[256,768]{1,0:T(8,128)(2,1)S(1)} %get-tuple-element.239), channel_id=1, source_target_pairs={{0,16},{16,0},{1,17},{17,1},{2,18},{18,2},{3,19},{19,3},{4,20},{20... | collective-permute-start | bytes 1179656 | tf_op jit(solution)/shard_map/ppermute | solution.py:287
  201.9 7.0 %collective-permute-start.31 = (bf16[256,768]{1,0:T(8,128)(2,1)S(1)}, bf16[256,768]{1,0:T(8,128)(2,1)S(1)}, u32[]{:S(2)}, u32[]{:S(2)}) collective-permute-start(bf16[256,768]{1,0:T(8,128)(2,1)S(1)} %get-tuple-element.238), channel_id=1, source_target_pairs={{0,16},{16,0},{1,17},{17,1},{2,18},{18,2},{3,19},{19,3},{4,20},{20... | collective-permute-start | bytes 1179656 | tf_op jit(solution)/shard_map/ppermute | solution.py:287
  202.0 16.9 %collective-permute-start.34 = (bf16[512,768]{1,0:T(8,128)(2,1)S(1)}, bf16[512,768]{1,0:T(8,128)(2,1)S(1)}, u32[]{:S(2)}, u32[]{:S(2)}) collective-permute-start(bf16[512,768]{1,0:T(8,128)(2,1)S(1)} %added.13.refs_1_), channel_id=1, source_target_pairs={{4,8},{8,4},{5,9},{9,5},{6,10},{10,6},{7,11},{11,7},{20,24},{24,20... | collective-permute-start | bytes 2359304 | tf_op jit(solution)/shard_map/ppermute | solution.py:351
  202.7 21.8 %collective-permute-start.35 = (bf16[512,768]{1,0:T(8,128)(2,1)S(1)}, bf16[512,768]{1,0:T(8,128)(2,1)S(1)}, u32[]{:S(2)}, u32[]{:S(2)}) collective-permute-start(bf16[512,768]{1,0:T(8,128)(2,1)S(1)} %activated.12.refs_1_), channel_id=1, source_target_pairs={{4,0},{8,12},{5,1},{9,13},{6,2},{10,14},{7,3},{11,15},{20,16},{24,... | collective-permute-start | bytes 2359304 | tf_op jit(solution)/shard_map/ppermute | solution.py:357
  204.3 28.1 %collective-permute-start.36 = (bf16[512,768]{1,0:T(8,128)(2,1)S(1)}, bf16[512,768]{1,0:T(8,128)(2,1)S(1)}, u32[]{:S(2)}, u32[]{:S(2)}) collective-permute-start(bf16[512,768]{1,0:T(8,128)(2,1)S(1)} %stacked.15.refs_0_), channel_id=1, source_target_pairs={{0,4},{12,8},{1,5},{13,9},{2,6},{14,10},{3,7},{15,11},{16,20},{28,... | collective-permute-start | bytes 2359304 | tf_op jit(solution)/shard_map/ppermute | solution.py:346
  218.1 15.4 %collective-permute-start.37 = (bf16[512,768]{1,0:T(8,128)(2,1)S(1)}, bf16[512,768]{1,0:T(8,128)(2,1)S(1)}, u32[]{:S(2)}, u32[]{:S(2)}) collective-permute-start(bf16[512,768]{1,0:T(8,128)(2,1)S(1)} %added.14.refs_1_), channel_id=1, source_target_pairs={{4,8},{8,4},{5,9},{9,5},{6,10},{10,6},{7,11},{11,7},{20,24},{24,20... | collective-permute-start | bytes 2359304 | tf_op jit(solution)/shard_map/ppermute | solution.py:351
  219.9 23.2 %collective-permute-start.38 = (bf16[512,768]{1,0:T(8,128)(2,1)S(1)}, bf16[512,768]{1,0:T(8,128)(2,1)S(1)}, u32[]{:S(2)}, u32[]{:S(2)}) collective-permute-start(bf16[512,768]{1,0:T(8,128)(2,1)S(1)} %activated.13.refs_1_), channel_id=1, source_target_pairs={{4,0},{8,12},{5,1},{9,13},{6,2},{10,14},{7,3},{11,15},{20,16},{24,... | collective-permute-start | bytes 2359304 | tf_op jit(solution)/shard_map/ppermute | solution.py:357
  232.8 17.7 %collective-permute-start.40 = (bf16[512,768]{1,0:T(8,128)(2,1)S(1)}, bf16[512,768]{1,0:T(8,128)(2,1)S(1)}, u32[]{:S(2)}, u32[]{:S(2)}) collective-permute-start(bf16[512,768]{1,0:T(8,128)(2,1)S(1)} %added.15.refs_1_), channel_id=1, source_target_pairs={{4,8},{8,4},{5,9},{9,5},{6,10},{10,6},{7,11},{11,7},{20,24},{24,20... | collective-permute-start | bytes 2359304 | tf_op jit(solution)/shard_map/ppermute | solution.py:351
  234.6 25.3 %collective-permute-start.41 = (bf16[512,768]{1,0:T(8,128)(2,1)S(1)}, bf16[512,768]{1,0:T(8,128)(2,1)S(1)}, u32[]{:S(2)}, u32[]{:S(2)}) collective-permute-start(bf16[512,768]{1,0:T(8,128)(2,1)S(1)} %activated.14.refs_1_), channel_id=1, source_target_pairs={{4,0},{8,12},{5,1},{9,13},{6,2},{10,14},{7,3},{11,15},{20,16},{24,... | collective-permute-start | bytes 2359304 | tf_op jit(solution)/shard_map/ppermute | solution.py:357
  236.1 7.3 %collective-permute-start.39 = (bf16[256,768]{1,0:T(8,128)(2,1)S(1)}, bf16[256,768]{1,0:T(8,128)(2,1)S(1)}, u32[]{:S(2)}, u32[]{:S(2)}) collective-permute-start(bf16[256,768]{1,0:T(8,128)(2,1)S(1)} %get-tuple-element.261), channel_id=1, source_target_pairs={{0,16},{16,0},{1,17},{17,1},{2,18},{18,2},{3,19},{19,3},{4,20},{20... | collective-permute-start | bytes 1179656 | tf_op jit(solution)/shard_map/ppermute | solution.py:287
  251.5 30.9 %collective-permute-start.44 = (bf16[512,768]{1,0:T(8,128)(2,1)S(1)}, bf16[512,768]{1,0:T(8,128)(2,1)S(1)}, u32[]{:S(2)}, u32[]{:S(2)}) collective-permute-start(bf16[512,768]{1,0:T(8,128)(2,1)S(1)} %activated.15.refs_1_), channel_id=1, source_target_pairs={{4,0},{8,12},{5,1},{9,13},{6,2},{10,14},{7,3},{11,15},{20,16},{24,... | collective-permute-start | bytes 2359304 | tf_op jit(solution)/shard_map/ppermute | solution.py:357
  252.8 7.5 %collective-permute-start.42 = (bf16[256,768]{1,0:T(8,128)(2,1)S(1)}, bf16[256,768]{1,0:T(8,128)(2,1)S(1)}, u32[]{:S(2)}, u32[]{:S(2)}) collective-permute-start(bf16[256,768]{1,0:T(8,128)(2,1)S(1)} %get-tuple-element.270), channel_id=1, source_target_pairs={{0,16},{16,0},{1,17},{17,1},{2,18},{18,2},{3,19},{19,3},{4,20},{20... | collective-permute-start | bytes 1179656 | tf_op jit(solution)/shard_map/ppermute | solution.py:287
  260.2 7.5 %collective-permute-start.43 = (bf16[256,768]{1,0:T(8,128)(2,1)S(1)}, bf16[256,768]{1,0:T(8,128)(2,1)S(1)}, u32[]{:S(2)}, u32[]{:S(2)}) collective-permute-start(bf16[256,768]{1,0:T(8,128)(2,1)S(1)} %get-tuple-element.275), channel_id=1, source_target_pairs={{0,16},{16,0},{1,17},{17,1},{2,18},{18,2},{3,19},{19,3},{4,20},{20... | collective-permute-start | bytes 1179656 | tf_op jit(solution)/shard_map/ppermute | solution.py:287
  282.7 3.5 %collective-permute-start.45 = (bf16[256,768]{1,0:T(8,128)(2,1)S(1)}, bf16[256,768]{1,0:T(8,128)(2,1)S(1)}, u32[]{:S(2)}, u32[]{:S(2)}) collective-permute-start(bf16[256,768]{1,0:T(8,128)(2,1)S(1)} %get-tuple-element.280), channel_id=1, source_target_pairs={{0,16},{16,0},{1,17},{17,1},{2,18},{18,2},{3,19},{19,3},{4,20},{20... | collective-permute-start | bytes 1179656 | tf_op jit(solution)/shard_map/ppermute | solution.py:287
  283.3 21.3 %collective-permute-start.48 = (bf16[128,3072]{1,0:T(8,128)(2,1)S(1)}, bf16[128,3072]{1,0:T(8,128)(2,1)S(1)}, u32[]{:S(2)}, u32[]{:S(2)}) collective-permute-start(bf16[128,3072]{1,0:T(8,128)(2,1)S(1)} %get-tuple-element.288), channel_id=1, source_target_pairs={{0,3},{1,2},{2,1},{3,0},{4,7},{5,6},{6,5},{7,4},{8,11},{9,10},{10,... | collective-permute-start | bytes 2359304 | tf_op jit(solution)/shard_map/ppermute | solution.py:283
  285.7 34.9 %collective-permute-start.47 = (bf16[128,3072]{1,0:T(8,128)(2,1)S(1)}, bf16[128,3072]{1,0:T(8,128)(2,1)S(1)}, u32[]{:S(2)}, u32[]{:S(2)}) collective-permute-start(bf16[128,3072]{1,0:T(8,128)(2,1)S(1)} %get-tuple-element.287), channel_id=1, source_target_pairs={{0,2},{1,3},{2,0},{3,1},{4,6},{5,7},{6,4},{7,5},{8,10},{9,11},{10,... | collective-permute-start | bytes 2359304 | tf_op jit(solution)/shard_map/ppermute | solution.py:283
  293.8 26.9 %collective-permute-start.46 = (bf16[128,3072]{1,0:T(8,128)(2,1)S(1)}, bf16[128,3072]{1,0:T(8,128)(2,1)S(1)}, u32[]{:S(2)}, u32[]{:S(2)}) collective-permute-start(bf16[128,3072]{1,0:T(8,128)(2,1)S(1)} %get-tuple-element.286), channel_id=1, source_target_pairs={{0,1},{1,0},{2,3},{3,2},{4,5},{5,4},{6,7},{7,6},{8,9},{9,8},{10,11... | collective-permute-start | bytes 2359304 | tf_op jit(solution)/shard_map/ppermute | solution.py:283

commit v4 on v3

--- a/solution.py
+++ b/solution.py
@@ -6,7 +6,7 @@
 from jax.sharding import PartitionSpec as P
 
 D = 12288
-MATMUL_VMEM = 28 * 1024 * 1024
+MATMUL_VMEM = 18 * 1024 * 1024
 SMALL_VMEM = 8 * 1024 * 1024
 FAR, NEAR = 0, 1
 
@@ -22,6 +22,10 @@
 
 def tile_of(extent, limit):
     return max(t for t in range(128, limit + 1, 128) if extent % t == 0)
+
+
+def fixed(shape, index):
+    return pl.BlockSpec(shape, lambda *_: index, pipeline_mode=pl.Buffered(1))
 
 
 def call(kernel, name, grid, scalars, operands, in_specs, out_specs, out_shape, scratch=(), aliases={}, vmem=MATMUL_VMEM):
@@ -41,19 +45,19 @@
     )(*scalars, *operands)
 
 
-def normalize(first, blocks, scales, gain, group, into):
+def normalize(first, blocks, scale, gain, group, into):
     rows, width = blocks[0].shape
     count = rows * len(blocks)
     tile = tile_of(width, 768)
 
-    def kernel(first_ref, gain_ref, *refs):
+    def kernel(first_ref, gain_ref, scale_ref, *refs):
         out = refs[-1]
         for i in range(len(blocks)):
-            ref, scale_ref = refs[i], refs[len(blocks) + i]
-            value = ref[...].astype(jnp.float32)
-            centred = (value - scale_ref[:, 0:1]) * scale_ref[:, 1:2]
+            own = slice(i * rows, (i + 1) * rows)
+            value = refs[i][...].astype(jnp.float32)
+            centred = (value - scale_ref[own, 0:1]) * scale_ref[own, 1:2]
             normed = (centred * gain_ref[...]).astype(jnp.bfloat16)
-            out[i * rows : (i + 1) * rows, :] = jnp.where(first_ref[0] == 1, normed, ref[...])
+            out[own, :] = jnp.where(first_ref[0] == 1, normed, refs[i][...])
 
     column = lambda i, _: (0, i)
     extra = [] if into is None else [into]
@@ -62,14 +66,13 @@
         "normalize",
         (width // tile,),
         [first],
-        [gain.reshape(1, width), *blocks, *scales, *extra],
-        [pl.BlockSpec((1, tile), column)]
+        [gain.reshape(1, width), scale, *blocks, *extra],
+        [pl.BlockSpec((1, tile), column), fixed((count, 2), (0, 0))]
         + [pl.BlockSpec((rows, tile), column)] * len(blocks)
-        + [pl.BlockSpec((rows, 2), lambda i, _: (0, 0))] * len(blocks)
         + [pl.BlockSpec(memory_space=pl.ANY)] * len(extra),
         pl.BlockSpec((count, tile), lambda i, _: (group, i)),
         jax.ShapeDtypeStruct((2 * count, width), jnp.bfloat16),
-        aliases={2 + 2 * len(blocks): 0} if extra else {},
+        aliases={3 + len(blocks): 0} if extra else {},
         vmem=SMALL_VMEM,
     )
 
@@ -79,13 +82,15 @@
     count, width = rows.shape[0] // 2 * pieces, rows.shape[1]
     at = groups[0]
     columns = weight.shape[1] // parts
-    tile = tile_of(columns // 2, 768)
+    tile = tile_of(columns // 2, 384)
     steps = columns // tile
     mine = steps // 2
     piece = count // pieces
 
-    def kernel(section_ref, rows_ref, weight_ref, *results):
-        product = dot_f32(rows_ref[...], weight_ref[...], (1, 0)).astype(jnp.bfloat16)
+    def kernel(section_ref, rows_ref, upper_ref, lower_ref, *results):
+        product = dot_f32(rows_ref[:, : width // 2], upper_ref[...], (1, 0))
+        product = product + dot_f32(rows_ref[:, width // 2 :], lower_ref[...], (1, 0))
+        product = product.astype(jnp.bfloat16)
 
         def store(refs):
             for i, result in enumerate(refs):
@@ -94,14 +99,20 @@
         pl.when(pl.program_id(0) < mine)(lambda: store(results[:pieces]))
         pl.when(pl.program_id(0) >= mine)(lambda: store(results[pieces:]))
 
-    column = lambda i, s: (0, part * steps + lax.rem(i + s[0] * mine, steps))
+    def column(k):
+        return lambda i, s: (k, part * steps + lax.rem(i + s[0] * mine, steps))
+
     return call(
         kernel,
         "up_product",
         (steps,),
         [section],
-        [rows, weight],
-        [pl.BlockSpec((count, width), lambda i, s: (at, 0)), pl.BlockSpec((width, tile), column)],
+        [rows, weight, weight],
+        [
+            fixed((count, width), (at, 0)),
+            pl.BlockSpec((width // 2, tile), column(0)),
+            pl.BlockSpec((width // 2, tile), column(1)),
+        ],
         [pl.BlockSpec((piece, tile), lambda i, s: (0, jnp.minimum(i, mine - 1)))] * pieces
         + [pl.BlockSpec((piece, tile), lambda i, s: (0, jnp.maximum(i - mine, 0)))] * pieces,
         [jax.ShapeDtypeStruct((piece, columns // 2), jnp.bfloat16)] * (2 * pieces),
@@ -179,42 +190,51 @@
     return elementwise(body, "chosen", [receives], [value, arrived], out_rows)
 
 
-def down_product(section, kept, came, weight, part, parts, before, group, kinds):
+def down_product(section, kept, came, weight, part, parts, before, group, arrived, kinds):
     counts = [k.shape[0] for k in kept]
     count, half = sum(counts), kept[0].shape[1]
     width = weight.shape[0]
-    tile = tile_of(width, 512)
+    tile = 2 * tile_of(width // 2, 256)
     n = len(kept)
+    extra = [] if before is None else [before]
 
     def kernel(section_ref, *refs):
-        weight_mine, weight_theirs = refs[2 * n : 2 * n + 2]
-        results = refs[2 * n + 2 + (before is not None) : -2]
-        held_mine, held_theirs = refs[-2:]
+        upper_ref, lower_ref = refs[2 * n : 2 * n + 2]
+        added = refs[2 * n + 2 : 2 * n + 2 + len(extra)]
+        others = refs[2 * n + 2 + len(extra) : 2 * n + 2 + len(extra) + len(arrived)]
+        results = refs[2 * n + 2 + len(extra) + len(arrived) : -1]
+        held = refs[-1]
 
         @pl.when(pl.program_id(0) == 0)
         def _():
+            mine = pl.ds(pl.multiple_of(section_ref[0] * half, half), half)
+            theirs = pl.ds(pl.multiple_of((1 - section_ref[0]) * half, half), half)
             at = 0
             for i, rows in enumerate(counts):
-                held_mine[:, at : at + rows] = refs[i][...].T
-                held_theirs[:, at : at + rows] = refs[n + i][...].T
+                held[mine, at : at + rows] = refs[i][...].T
+                held[theirs, at : at + rows] = refs[n + i][...].T
                 at += rows
 
-        product = dot_f32(weight_mine[...], held_mine[...], (1, 0))
-        product = product + dot_f32(weight_theirs[...], held_theirs[...], (1, 0))
-        if before is not None:
-            product = product + refs[2 * n + 2][...]
-        if kinds:
-            product = product.T
-            piece = count // len(kinds)
-            for i, result in enumerate(results):
-                result[...] = product[i * piece : (i + 1) * piece].astype(result.dtype)
-        else:
-            results[0][...] = product
-
-    whole = [pl.BlockSpec((rows, half), lambda i, s: (0, 0)) for rows in counts]
-    extra = [] if before is None else [before]
+        for k, weight_ref in enumerate((upper_ref, lower_ref)):
+            own = slice(k * tile // 2, (k + 1) * tile // 2)
+            product = dot_f32(weight_ref[...], held[...], (1, 0))
+            for ref in added:
+                product = product + ref[own, :]
+            if kinds:
+                product = product.T
+                piece = count // len(kinds)
+                for i, result in enumerate(results):
+                    value = product[i * piece : (i + 1) * piece]
+                    if arrived:
+                        value = value + others[i][:, own].astype(jnp.float32)
+                    result[:, own] = value.astype(result.dtype)
+            else:
+                results[0][own, :] = product
+
+    whole = [fixed((rows, half), (0, 0)) for rows in counts]
     if kinds:
-        out_specs = [pl.BlockSpec((count // len(kinds), tile), lambda i, s: (0, i))] * len(kinds)
+        piece_spec = pl.BlockSpec((count // len(kinds), tile), lambda i, s: (0, i))
+        out_specs = [piece_spec] * len(kinds)
         out_shape = [jax.ShapeDtypeStruct((count // len(kinds), width), kind) for kind in kinds]
     else:
         out_specs = [pl.BlockSpec((tile, count), lambda i, s: (i, 0))]
@@ -224,17 +244,18 @@
         "down_product",
         (width // tile,),
         [section],
-        [*kept, *came, weight, weight, *extra],
+        [*kept, *came, weight, weight, *extra, *arrived],
         whole
         + whole
         + [
-            pl.BlockSpec((tile, half), lambda i, s: (i, 2 * part + s[0])),
-            pl.BlockSpec((tile, half), lambda i, s: (i, 2 * part + 1 - s[0])),
+            pl.BlockSpec((tile // 2, 2 * half), lambda i, s: (2 * i, part)),
+            pl.BlockSpec((tile // 2, 2 * half), lambda i, s: (2 * i + 1, part)),
         ]
-        + [pl.BlockSpec((tile, count), lambda i, s: (i, group))] * len(extra),
+        + [pl.BlockSpec((tile, count), lambda i, s: (i, group))] * len(extra)
+        + [pl.BlockSpec((count // max(len(kinds), 1), tile), lambda i, s: (0, i))] * len(arrived),
         out_specs,
         out_shape,
-        [pltpu.VMEM((half, count), jnp.bfloat16)] * 2,
+        [pltpu.VMEM((2 * half, count), jnp.bfloat16)],
     )
 
 
@@ -242,38 +263,39 @@
     width, count = turned.shape
     counts = [k.shape[0] for k in kept]
     half = kept[0].shape[1]
-    tile = tile_of(width, 1024)
+    tile = tile_of(width, 512)
     n = len(kept)
 
     def kernel(section_ref, turned_ref, *refs):
         out, held = refs[-2:]
 
-        def hold(blocks):
+        @pl.when(pl.program_id(0) == 0)
+        def _():
+            mine = pl.ds(pl.multiple_of(section_ref[0] * half, half), half)
+            theirs = pl.ds(pl.multiple_of((1 - section_ref[0]) * half, half), half)
             at = 0
-            for rows, block in zip(counts, blocks):
-                held[at : at + rows, :] = block[...]
+            for i, rows in enumerate(counts):
+                held[at : at + rows, mine] = refs[i][...]
+                held[at : at + rows, theirs] = refs[n + i][...]
                 at += rows
 
-        start = pl.program_id(1) == 0
-        pl.when(jnp.logical_and(start, pl.program_id(0) == 0))(lambda: hold(refs[:n]))
-        pl.when(jnp.logical_and(start, pl.program_id(0) == 1))(lambda: hold(refs[n : 2 * n]))
         out[...] = dot_f32(turned_ref[...], held[...], (1, 0)).astype(jnp.bfloat16)
 
-    whole = [pl.BlockSpec((rows, half), lambda j, i, s: (0, 0)) for rows in counts]
+    whole = [fixed((rows, half), (0, 0)) for rows in counts]
     extra = [] if into is None else [into]
     return call(
         kernel,
         "weight_gradient",
-        (2, width // tile),
+        (width // tile,),
         [section],
         [turned, *kept, *came, *extra],
-        [pl.BlockSpec((tile, count), lambda j, i, s: (i, 0))]
+        [pl.BlockSpec((tile, count), lambda i, s: (i, 0))]
         + whole
         + whole
         + [pl.BlockSpec(memory_space=pl.ANY)] * len(extra),
-        pl.BlockSpec((tile, half), lambda j, i, s: (i, 2 * part + lax.rem(j + s[0], 2))),
+        pl.BlockSpec((tile, 2 * half), lambda i, s: (i, part)),
         jax.ShapeDtypeStruct((width, 2 * half * parts), jnp.bfloat16),
-        [pltpu.VMEM((count, half), jnp.bfloat16)],
+        [pltpu.VMEM((count, 2 * half), jnp.bfloat16)],
         {2 + 2 * n: 0} if extra else {},
     )
 
@@ -310,23 +332,23 @@
         return held
 
     raw = run(lambda a, b: jnp.where(first[0] == 1, a, b), tokens, cotangent)["value"]
-    gathered = {by: from_peer(raw, by) for by in range(1, peers)}
-    gathered[0] = raw
+    across = peers // 2
+    near = list(range(each, 2 * each)) + list(range(each))
+    far = [by ^ across for by in near]
+    gathered = {by: from_peer(raw, by) if by else raw for by in near}
+    gathered.update({by: from_peer(gathered[by ^ across], across) for by in far})
 
     values = tokens.astype(jnp.float32)
     row_total, row_squares = lax.psum((jnp.sum(values, 1), jnp.sum(values * values, 1)), "dp")
     average = row_total / D
     inverse_std = lax.rsqrt(row_squares / D - average * average + epsilon)
     own_scale = jnp.stack([average, inverse_std], 1)
-    scale = {by: from_peer(own_scale, by) for by in range(1, peers)}
-    scale[0] = own_scale
-
-    far = list(range(2 * each, 4 * each))
-    near = list(range(each, 2 * each)) + list(range(each))
-
-    def prepare(members, group, into):
-        blocks, scales = [gathered[by] for by in members], [scale[by] for by in members]
-        return run(lambda g: normalize(first, blocks, scales, g, group, into), gain)["value"]
+    near_scale = jnp.concatenate([from_peer(own_scale, by) if by else own_scale for by in near], 0)
+    far_scale = from_peer(near_scale, across)
+
+    def prepare(members, scale, group, into):
+        blocks = [gathered[by] for by in members]
+        return run(lambda g: normalize(first, blocks, scale, g, group, into), gain)["value"]
 
     chunks = {}
 
@@ -388,11 +410,11 @@
         if 2 <= t + 2 < count:
             stack(chunks[order[t + 2]])
 
-    def go_down(part, groups, before, column, kinds=()):
+    def go_down(part, groups, before, column, kinds=(), arrived=()):
         kept, came = hidden(part, groups)
         before = None if before is None else before["value"][0]
         return run(
-            lambda k: down_product(section, [k] + kept[1:], came, weight, part, parts, before, column, kinds),
+            lambda k: down_product(section, [k] + kept[1:], came, weight, part, parts, before, column, arrived, kinds),
             kept[0],
         )
 
@@ -403,10 +425,10 @@
             lambda k: weight_gradient(section, turned, [k] + kept[1:], came, part, parts, into), kept[0]
         )
 
-    x_near = prepare(near, NEAR, None)
+    x_near = prepare(near, near_scale, NEAR, None)
     multiply(x_near, 0, [NEAR])
     stack(chunks[order[0]])
-    x_all = prepare(far, FAR, x_near)
+    x_all = prepare(far, far_scale, FAR, x_near)
     multiply(x_all, 0, [FAR])
     stack(chunks[order[1]])
     for t in range(count + 2):
@@ -425,18 +447,19 @@
                 go_gradient((t - 3) // 2)
         if t == count - 1:
             far_sum = go_down(parts - 2, [FAR], held["partial"], FAR)
+            sent_far = go_down(parts - 1, [FAR], far_sum, 0, [jnp.bfloat16] * 2)
         if t == count:
-            sent_far = go_down(parts - 1, [FAR], far_sum, 0, [jnp.bfloat16] * 2)
             go_gradient(parts - 2)
             near_sum = go_down(parts - 2, [NEAR], held["partial"], NEAR)
-    sent_near = go_down(parts - 1, [NEAR], near_sum, 0, [jnp.bfloat16, jnp.float32])
+            arrived = [from_peer(value, across) for value in sent_far["value"]]
+            near_sum["value"], arrived[0] = lax.optimization_barrier((near_sum["value"], arrived[0]))
+    sent_near = go_down(parts - 1, [NEAR], near_sum, 0, [jnp.bfloat16, jnp.float32], arrived)
     go_gradient(parts - 1)
 
     own = sent_near["value"][1]
     blocks = {0: own.astype(jnp.bfloat16), 1: sent_near["value"][0]}
-    blocks[2], blocks[3] = sent_far["value"]
     result = own[:rows]
-    for by in range(1, peers):
+    for by in range(1, across):
         at = (by % each) * rows
         result = result + from_peer(blocks[by // each][at : at + rows], by).astype(jnp.float32)
     return (result.astype(jnp.bfloat16)[None], held["gradient"]["value"][None])

time: 324 us -> 313 us (0.966)
  waiting for transfers between devices: 69 us -> 50.6 us
  Pallas kernels: 155 us -> 160 us
  starting transfers between devices: 73.2 us -> 76.9 us
    ppermute x9 -> x8, waiting for transfers between devices: 41.5 us -> 30.1 us  [from_peer(): return lax.ppermute(value, 'mp', [(i, i ^ by) for i in range(peers)])]
    ppermute x8, waiting for transfers between devices: 23.9 us -> 17.1 us  [outward(): lax.ppermute(value, 'dp', [(hop + 1, hop), (line - 2 - hop, line - 1 - ho...]
    ppermute x8, starting transfers between devices: 39.7 us -> 44.8 us  [inward(): lax.ppermute(value, 'dp', [(hop, hop + 1), (line - 1 - hop, line - 2 - ho...]
    pallas_call x49, Pallas kernels: 155 us -> 160 us  [call(): pl.pallas_call(kernel, grid_spec=pltpu.PrefetchScalarGridSpec(num_scalar_...]
    ppermute x9 -> x8, starting transfers between devices: 12.6 us -> 11.8 us  [from_peer(): return lax.ppermute(value, 'mp', [(i, i ^ by) for i in range(peers)])]
  transfers between devices with their start and end apart: 49 -> 48, of which waited for: 14 -> 14; matrix products, arithmetic and copies ran while one was open for 1% -> 1% of each run, Pallas kernels for 48% -> 49%
where the time goes in v4:
time: 313 us; the launch traced here: 311 us
  Pallas kernels  160 us (51%)
  starting transfers between devices  76.9 us (25%)
  waiting for transfers between devices  50.6 us (16%)
  blocking collectives  12 us (4%)
  local copies, waits for them, and re-layouts  5.54 us (2%)
  other arithmetic  4.62 us (1%)
    pallas_call x49, Pallas kernels, call(): pl.pallas_call(kernel, grid_spec=pltpu.PrefetchScalarGridSpec(num_scalar_...  160 us
    ppermute x8, starting transfers between devices, inward(): lax.ppermute(value, 'dp', [(hop, hop + 1), (line - 1 - hop, line - 2 - ho...  44.8 us
    ppermute x8, waiting for transfers between devices, from_peer(): return lax.ppermute(value, 'mp', [(i, i ^ by) for i in range(peers)])  30.1 us
    ppermute x8, waiting for transfers between devices, outward(): lax.ppermute(value, 'dp', [(hop + 1, hop), (line - 2 - hop, line - 1 - ho...  17.1 us
    psum x1, blocking collectives, local(): lax.psum((jnp.sum(values, 1), jnp.sum(values * values, 1)), 'dp')  12 us
    ppermute x8, starting transfers between devices, from_peer(): return lax.ppermute(value, 'mp', [(i, i ^ by) for i in range(peers)])  11.8 us
    ppermute x8, starting transfers between devices, outward(): lax.ppermute(value, 'dp', [(hop + 1, hop), (line - 2 - hop, line - 1 - ho...  10.5 us
    ppermute x8, starting transfers between devices, middle(): arrived = lax.ppermute(value, 'dp', [(half - 1, half), (half, half - 1)])  7.48 us
  transfers between devices with their start and end apart: 48, of which 14 were waited for; matrix products, arithmetic and copies ran while one was open for 1% of the time, Pallas kernels for 49%

profile of v4, /device:TPU:0, one launch (start us, length us, event | category | flops | bytes accessed | tf_op | source)
XLA Modules:
  0.0 311.2 jit_solution(6982401824140006405)
XLA Ops:
  0.6 2.1 broadcast_select_fusion.refs_1_
  2.8 2.9 collective-permute-start.1
  5.7 1.5 collective-permute-start.5
  7.2 1.4 convert_reduce_fusion
  8.6 12.0 %all-reduce = (f32[128]{0:T(128)S(1)}, f32[128]{0:T(128)S(1)}) all-reduce(f32[128]{0:T(128)S(1)} %get-tuple-element.293, f32[128]{0:T(128)S(1)} %get-tuple-element.292), channel_id=1, replica_groups=mesh['section'=2,'dp'=4,'mp'=4] {'dp'}, use_global_device_ids=true, to_apply=%region_3.4 | all-reduce | flops 256 | bytes 2048 | tf_op jit(solution)/shard_map/psum | solution.py:342
  20.6 3.0 collective-permute-done.1.refs_0_
  23.5 1.8 collective-permute-start.4
  25.3 1.6 collective-permute-start
  26.9 2.1 collective-permute-done
  29.1 2.9 normalize.2.rows_ref.refs_2_
  32.1 6.7 %up_product.5 = (bf16[256,768]{1,0:T(8,128)(2,1)S(1)}, bf16[256,768]{1,0:T(8,128)(2,1)S(1)}) custom-call(s32[1]{0:T(128)} %bitcast.section_ref, bf16[512,3072]{1,0:T(8,128)(2,1)S(1)} %normalize.2.rows_ref.refs_2_, bf16[3072,6144]{1,0:T(8,128)(2,1)} %bitcast.20, bf16[3072,6144]{1,0:T(8,128)(2,1)} %bitcast.21), custom_call_target="tpu_custom_call" | custom-call | tf_op jit(solution)/shard_map/up_product/pallas_call | solution.py:32
  39.1 1.4 collective-permute-done.2.refs_1_
  40.8 3.5 %collective-permute-start.7 = (bf16[512,768]{1,0:T(8,128)(2,1)S(1)}, bf16[512,768]{1,0:T(8,128)(2,1)S(1)}, u32[]{:S(2)}, u32[]{:S(2)}) collective-permute-start(bf16[512,768]{1,0:T(8,128)(2,1)S(1)} %stacked.8.refs_0_), channel_id=1, source_target_pairs={{0,4},{12,8},{1,5},{13,9},{2,6},{14,10},{3,7},{15,11},{16,20},{28,... | collective-permute-start | bytes 2359304 | tf_op jit(solution)/shard_map/ppermute | solution.py:368
  45.3 2.9 normalize.3.rows_ref
  48.2 6.7 %up_product.6 = (bf16[256,768]{1,0:T(8,128)(2,1)S(1)}, bf16[256,768]{1,0:T(8,128)(2,1)S(1)}) custom-call(s32[1]{0:T(128)} %bitcast.section_ref, bf16[512,3072]{1,0:T(8,128)(2,1)S(1)} %normalize.3.rows_ref, bf16[3072,6144]{1,0:T(8,128)(2,1)} %bitcast.22, bf16[3072,6144]{1,0:T(8,128)(2,1)} %bitcast.23), custom_call_target="tpu_custom_call" | custom-call | tf_op jit(solution)/shard_map/up_product/pallas_call | solution.py:32
  55.0 1.7 collective-permute-done.6.refs_1_
  56.7 1.5 stacked.9.refs_0_
  58.2 4.3 %collective-permute-start.9 = (bf16[512,768]{1,0:T(8,128)(2,1)}, bf16[512,768]{1,0:T(8,128)(2,1)}, u32[]{:S(2)}, u32[]{:S(2)}) collective-permute-start(bf16[512,768]{1,0:T(8,128)(2,1)} %stacked.9.refs_0_), channel_id=1, source_target_pairs={{0,4},{12,8},{1,5},{13,9},{2,6},{14,10},{3,7},{15,11},{16,20},{28,... | collective-permute-start | bytes 2359304 | tf_op jit(solution)/shard_map/ppermute | solution.py:368
  62.5 1.7 added.8.refs_1_
  64.2 9.3 %up_product.7 = (bf16[256,768]{1,0:T(8,128)(2,1)S(1)}, bf16[256,768]{1,0:T(8,128)(2,1)S(1)}, bf16[256,768]{1,0:T(8,128)(2,1)S(1)}, bf16[256,768]{1,0:T(8,128)(2,1)S(1)}) custom-call(s32[1]{0:T(128)} %bitcast.section_ref, bf16[512,3072]{1,0:T(8,128)(2,1)S(1)} %normalize.3.rows_ref, bf16[3072,6144]{1,0:T(8,128)(2,1)} %bitcast.24, bf16[3072,6144]{1,0:T(8,128)(2,1)} %bitcast.25), custom_call_target="tpu_custom_call" | custom-call | tf_op jit(solution)/shard_map/up_product/pallas_call | solution.py:32
  74.3 1.5 collective-permute-start.10
  77.1 2.8 copy.15
  79.9 5.1 %collective-permute-start.12 = (bf16[512,768]{1,0:T(8,128)(2,1)}, bf16[512,768]{1,0:T(8,128)(2,1)S(1)}, u32[]{:S(2)}, u32[]{:S(2)}) collective-permute-start(bf16[512,768]{1,0:T(8,128)(2,1)} %copy-done.1), channel_id=1, source_target_pairs={{0,4},{12,8},{1,5},{13,9},{2,6},{14,10},{3,7},{15,11},{16,20},{28,... | collective-permute-start | bytes 2359304 | tf_op jit(solution)/shard_map/ppermute | solution.py:368
  85.0 2.3 added.9.refs_1_
  88.0 3.4 %activated.8.refs_1_ = bf16[512,768]{1,0:T(8,128)(2,1)} custom-call(s32[1]{0:T(128)S(6)} %sub.6.first_ref.refs_0_, bf16[512,768]{1,0:T(8,128)(2,1)} %added.8.refs_1_, bf16[512,768]{1,0:T(8,128)(2,1)} %collective-permute-done.10.refs_2_), custom_call_target="tpu_custom_call" | custom-call | tf_op jit(solution)/shard_map/activated/pallas_call | solution.py:32
  92.8 1.5 stacked.11.refs_0_
  94.3 13.9 %collective-permute-start.16 = (bf16[512,768]{1,0:T(8,128)(2,1)}, bf16[512,768]{1,0:T(8,128)(2,1)}, u32[]{:S(2)}, u32[]{:S(2)}) collective-permute-start(bf16[512,768]{1,0:T(8,128)(2,1)} %stacked.11.refs_0_), channel_id=1, source_target_pairs={{0,4},{12,8},{1,5},{13,9},{2,6},{14,10},{3,7},{15,11},{16,20},{28,... | collective-permute-start | bytes 2359304 | tf_op jit(solution)/shard_map/ppermute | solution.py:368
  108.2 9.9 %up_product.8 = (bf16[256,768]{1,0:T(8,128)(2,1)S(1)}, bf16[256,768]{1,0:T(8,128)(2,1)S(1)}, bf16[256,768]{1,0:T(8,128)(2,1)}, bf16[256,768]{1,0:T(8,128)(2,1)S(1)}) custom-call(s32[1]{0:T(128)} %bitcast.section_ref, bf16[512,3072]{1,0:T(8,128)(2,1)S(1)} %normalize.3.rows_ref, bf16[3072,6144]{1,0:T(8,128)(2,1)} %bitcast.26, bf16[3072,6144]{1,0:T(8,128)(2,1)} %bitcast.27), custom_call_target="tpu_custom_call" | custom-call | tf_op jit(solution)/shard_map/up_product/pallas_call | solution.py:32
  118.1 1.7 added.10.refs_1_
  119.9 1.5 collective-permute-start.17
  121.4 2.1 activated.9.refs_1_
  124.9 2.2 chosen.8
  128.1 1.9 stacked.12.refs_0_
  130.1 5.4 %collective-permute-start.22 = (bf16[512,768]{1,0:T(8,128)(2,1)S(1)}, bf16[512,768]{1,0:T(8,128)(2,1)S(1)}, u32[]{:S(2)}, u32[]{:S(2)}) collective-permute-start(bf16[512,768]{1,0:T(8,128)(2,1)S(1)} %stacked.12.refs_0_), channel_id=1, source_target_pairs={{0,4},{12,8},{1,5},{13,9},{2,6},{14,10},{3,7},{15,11},{16,20},{28,... | collective-permute-start | bytes 2359304 | tf_op jit(solution)/shard_map/ppermute | solution.py:368
  135.5 9.4 %up_product.9 = (bf16[256,768]{1,0:T(8,128)(2,1)S(1)}, bf16[256,768]{1,0:T(8,128)(2,1)S(1)}, bf16[256,768]{1,0:T(8,128)(2,1)S(1)}, bf16[256,768]{1,0:T(8,128)(2,1)S(1)}) custom-call(s32[1]{0:T(128)} %bitcast.section_ref, bf16[512,3072]{1,0:T(8,128)(2,1)S(1)} %normalize.3.rows_ref, bf16[3072,6144]{1,0:T(8,128)(2,1)} %bitcast.28, bf16[3072,6144]{1,0:T(8,128)(2,1)} %bitcast.29), custom_call_target="tpu_custom_call" | custom-call | tf_op jit(solution)/shard_map/up_product/pallas_call | solution.py:32
  144.9 2.3 added.11.refs_1_
  148.5 2.7 activated.10.refs_1_
  151.1 2.2 chosen.9
  155.2 4.8 %collective-permute-start.26 = (bf16[512,768]{1,0:T(8,128)(2,1)S(1)}, bf16[512,768]{1,0:T(8,128)(2,1)S(1)}, u32[]{:S(2)}, u32[]{:S(2)}) collective-permute-start(bf16[512,768]{1,0:T(8,128)(2,1)S(1)} %stacked.13.refs_0_), channel_id=1, source_target_pairs={{0,4},{12,8},{1,5},{13,9},{2,6},{14,10},{3,7},{15,11},{16,20},{28,... | collective-permute-start | bytes 2359304 | tf_op jit(solution)/shard_map/ppermute | solution.py:368
  160.0 8.7 %down_product.6.refs_6_ = f32[3072,512]{1,0:T(8,128)S(1)} custom-call(s32[1]{0:T(128)} %bitcast.section_ref, bf16[256,768]{1,0:T(8,128)(2,1)S(1)} %get-tuple-element.224.refs_0_, bf16[256,768]{1,0:T(8,128)(2,1)S(1)} %get-tuple-element.210.refs_1_, bf16[256,768]{1,0:T(8,128)(2,1)S(1)} %collective-permute-done.20.refs_2_, ...), custom_call_target="tpu_custom_call" | custom-call | tf_op jit(solution)/shard_map/down_product/pallas_call | solution.py:32
  171.1 1.3 collective-permute-start.28
  172.5 2.8 collective-permute-done.24.refs_2_
  175.9 7.5 %weight_gradient.4.refs_4_ = bf16[3072,6144]{1,0:T(8,128)(2,1)} custom-call(s32[1]{0:T(128)} %bitcast.section_ref, bf16[3072,512]{1,0:T(8,128)(2,1)S(1)} %bitcast.14, bf16[256,768]{1,0:T(8,128)(2,1)S(1)} %get-tuple-element.224.refs_0_, bf16[256,768]{1,0:T(8,128)(2,1)S(1)} %get-tuple-element.210.refs_1_, ...), custom_call_target="tpu_custom_call" | custom-call | tf_op jit(solution)/shard_map/weight_gradient/pallas_call | solution.py:32
  183.4 3.2 %collective-permute-start.32 = (bf16[512,768]{1,0:T(8,128)(2,1)S(1)}, bf16[512,768]{1,0:T(8,128)(2,1)S(1)}, u32[]{:S(2)}, u32[]{:S(2)}) collective-permute-start(bf16[512,768]{1,0:T(8,128)(2,1)S(1)} %stacked.14.refs_0_), channel_id=1, source_target_pairs={{0,4},{12,8},{1,5},{13,9},{2,6},{14,10},{3,7},{15,11},{16,20},{28,... | collective-permute-start | bytes 2359304 | tf_op jit(solution)/shard_map/ppermute | solution.py:368
  189.4 2.8 collective-permute-done.28.refs_2_
  192.6 1.3 collective-permute-start.34
  194.2 4.6 %collective-permute-start.35 = (bf16[512,768]{1,0:T(8,128)(2,1)S(1)}, bf16[512,768]{1,0:T(8,128)(2,1)S(1)}, u32[]{:S(2)}, u32[]{:S(2)}) collective-permute-start(bf16[512,768]{1,0:T(8,128)(2,1)S(1)} %stacked.15.refs_0_), channel_id=1, source_target_pairs={{0,4},{12,8},{1,5},{13,9},{2,6},{14,10},{3,7},{15,11},{16,20},{28,... | collective-permute-start | bytes 2359304 | tf_op jit(solution)/shard_map/ppermute | solution.py:368
  198.8 8.7 %down_product.7.refs_4_ = f32[3072,512]{1,0:T(8,128)S(1)} custom-call(s32[1]{0:T(128)} %bitcast.section_ref, bf16[256,768]{1,0:T(8,128)(2,1)S(1)} %get-tuple-element.250.refs_0_, bf16[256,768]{1,0:T(8,128)(2,1)S(1)} %get-tuple-element.237.refs_1_, bf16[256,768]{1,0:T(8,128)(2,1)S(1)} %collective-permute-done.30.refs_2_, ...), custom_call_target="tpu_custom_call" | custom-call | tf_op jit(solution)/shard_map/down_product/pallas_call | solution.py:32
  211.1 3.5 %collective-permute-done.34.refs_2_ = bf16[512,768]{1,0:T(8,128)(2,1)S(1)} collective-permute-done((bf16[512,768]{1,0:T(8,128)(2,1)S(1)}, bf16[512,768]{1,0:T(8,128)(2,1)S(1)}, u32[]{:S(2)}, u32[]{:S(2)}) %collective-permute-start.34) | collective-permute-done | bytes 786464 | tf_op jit(solution)/shard_map/ppermute | solution.py:379
  214.9 7.5 %weight_gradient.5.refs_4_ = bf16[3072,6144]{1,0:T(8,128)(2,1)} custom-call(s32[1]{0:T(128)} %bitcast.section_ref, bf16[3072,512]{1,0:T(8,128)(2,1)S(1)} %bitcast.15, bf16[256,768]{1,0:T(8,128)(2,1)S(1)} %get-tuple-element.250.refs_0_, bf16[256,768]{1,0:T(8,128)(2,1)S(1)} %get-tuple-element.237.refs_1_, ...), custom_call_target="tpu_custom_call", output_to_operand_aliasing={{}: (6, {})} | custom-call | tf_op jit(solution)/shard_map/weight_gradient/pallas_call | solution.py:32
  224.7 1.3 collective-permute-start.41
  226.0 5.3 %collective-permute-done.37.refs_2_ = bf16[512,768]{1,0:T(8,128)(2,1)S(1)} collective-permute-done((bf16[512,768]{1,0:T(8,128)(2,1)S(1)}, bf16[512,768]{1,0:T(8,128)(2,1)S(1)}, u32[]{:S(2)}, u32[]{:S(2)}) %collective-permute-start.37) | collective-permute-done | bytes 786464 | tf_op jit(solution)/shard_map/ppermute | solution.py:379
  231.7 7.1 %down_product.8.refs_4_ = f32[3072,256]{1,0:T(8,128)S(1)} custom-call(s32[1]{0:T(128)} %bitcast.section_ref, bf16[256,768]{1,0:T(8,128)(2,1)S(1)} %get-tuple-element.273.refs_0_, bf16[256,768]{1,0:T(8,128)(2,1)S(1)} %collective-permute-done.38.refs_1_.refs_2_, bf16[3072,6144]{1,0:T(8,128)(2,1)} %bitcast.34, bf16[3072,6144]{1,0:T(8,128)(2,1)} %bitcast.35, ...), custom_call_target="tpu_custom_call" | custom-call | tf_op jit(solution)/shard_map/down_product/pallas_call | solution.py:32
  238.8 7.6 %down_product.9 = (bf16[128,3072]{1,0:T(8,128)(2,1)S(1)}, bf16[128,3072]{1,0:T(8,128)(2,1)S(1)}) custom-call(s32[1]{0:T(128)} %bitcast.section_ref, bf16[256,768]{1,0:T(8,128)(2,1)S(1)} %get-tuple-element.289.refs_0_, bf16[256,768]{1,0:T(8,128)(2,1)S(1)} %collective-permute-done.39.refs_1_.refs_2_, bf16[3072,6144]{1,0:T(8,128)(2,1)} %bitcast.36, ...), custom_call_target="tpu_custom_call" | custom-call | tf_op jit(solution)/shard_map/down_product/pallas_call | solution.py:32
  248.0 1.5 collective-permute-start.44
  250.1 1.5 collective-permute-start.46
  251.6 7.5 %weight_gradient.6.refs_4_ = bf16[3072,6144]{1,0:T(8,128)(2,1)} custom-call(s32[1]{0:T(128)} %bitcast.section_ref, bf16[3072,512]{1,0:T(8,128)(2,1)S(1)} %bitcast.16, bf16[256,768]{1,0:T(8,128)(2,1)S(1)} %get-tuple-element.273.refs_0_, bf16[256,768]{1,0:T(8,128)(2,1)S(1)} %get-tuple-element.275.refs_1_.refs_0_, ...), custom_call_target="tpu_custom_call", output_to_operand_aliasing={{}: (6, {})} | custom-call | tf_op jit(solution)/shard_map/weight_gradient/pallas_call | solution.py:32
  259.1 7.0 %down_product.10.refs_4_ = f32[3072,256]{1,0:T(8,128)S(1)} custom-call(s32[1]{0:T(128)} %bitcast.section_ref, bf16[256,768]{1,0:T(8,128)(2,1)S(1)} %get-tuple-element.275.refs_1_.refs_0_, bf16[256,768]{1,0:T(8,128)(2,1)S(1)} %collective-permute-done.42.refs_3_.refs_1_, bf16[3072,6144]{1,0:T(8,128)(2,1)} %bitcast.38, bf16[3072,6144]{1,0:T(8,128)(2,1)} %bitcast.39, ...), custom_call_target="tpu_custom_call" | custom-call | tf_op jit(solution)/shard_map/down_product/pallas_call | solution.py:32
  266.8 2.7 collective-permute-done.44.refs_2_
  269.9 13.3 %collective-permute-done.46.refs_6_ = bf16[128,3072]{1,0:T(8,128)(2,1)S(1)} collective-permute-done((bf16[128,3072]{1,0:T(8,128)(2,1)S(1)}, bf16[128,3072]{1,0:T(8,128)(2,1)S(1)}, u32[]{:S(2)}, u32[]{:S(2)}) %collective-permute-start.46) | collective-permute-done | bytes 786464 | tf_op jit(solution)/shard_map/ppermute | solution.py:305
  283.2 7.7 %down_product.11 = (bf16[128,3072]{1,0:T(8,128)(2,1)S(1)}, f32[128,3072]{1,0:T(8,128)S(1)}) custom-call(s32[1]{0:T(128)} %bitcast.section_ref, bf16[256,768]{1,0:T(8,128)(2,1)S(1)} %get-tuple-element.290.refs_0_.refs_1_, bf16[256,768]{1,0:T(8,128)(2,1)S(1)} %collective-permute-done.45.refs_1_.refs_3_, bf16[3072,6144]{1,0:T(8,128)(2,1)} %bitcast.40, ...), custom_call_target="tpu_custom_call" | custom-call | tf_op jit(solution)/shard_map/down_product/pallas_call | solution.py:32
  290.9 1.6 collective-permute-start.47
  292.5 7.5 %weight_gradient.7 = bf16[3072,6144]{1,0:T(8,128)(2,1)} custom-call(s32[1]{0:T(128)} %bitcast.section_ref, bf16[3072,512]{1,0:T(8,128)(2,1)S(1)} %bitcast.17, bf16[256,768]{1,0:T(8,128)(2,1)S(1)} %get-tuple-element.289.refs_0_, bf16[256,768]{1,0:T(8,128)(2,1)S(1)} %get-tuple-element.290.refs_0_.refs_1_, ...), custom_call_target="tpu_custom_call", output_to_operand_aliasing={{}: (6, {})} | custom-call | tf_op jit(solution)/shard_map/weight_gradient/pallas_call | solution.py:32
  300.0 10.1 %collective-permute-done.47 = bf16[128,3072]{1,0:T(8,128)(2,1)S(1)} collective-permute-done((bf16[128,3072]{1,0:T(8,128)(2,1)S(1)}, bf16[128,3072]{1,0:T(8,128)(2,1)S(1)}, u32[]{:S(2)}, u32[]{:S(2)}) %collective-permute-start.47) | collective-permute-done | bytes 786464 | tf_op jit(solution)/shard_map/ppermute | solution.py:305
  (108 shorter events, 28.4 us)
Async XLA Ops:
  0.6 28.5 %copy-start.5 = (f32[3072]{0:T(1024)S(1)}, f32[3072]{0:T(1024)}, u32[]{:S(2)}) copy-start(f32[3072]{0:T(1024)} %param.6) | copy-start | bytes 36868
  2.8 20.8 %collective-permute-start.1 = (bf16[128,3072]{1,0:T(8,128)(2,1)}, bf16[128,3072]{1,0:T(8,128)(2,1)}, u32[]{:S(2)}, u32[]{:S(2)}) collective-permute-start(bf16[128,3072]{1,0:T(8,128)(2,1)} %broadcast_select_fusion.refs_1_), channel_id=1, source_target_pairs={{0,1},{1,0},{2,3},{3,2},{4,5},{5,4},{6,7},{7,6},{8,9},{9,8},{10,11... | collective-permute-start | bytes 2359304 | tf_op jit(solution)/shard_map/ppermute | solution.py:305
  5.7 39.6 %collective-permute-start.5 = (bf16[128,3072]{1,0:T(8,128)(2,1)}, bf16[128,3072]{1,0:T(8,128)(2,1)}, u32[]{:S(2)}, u32[]{:S(2)}) collective-permute-start(bf16[128,3072]{1,0:T(8,128)(2,1)} %broadcast_select_fusion.refs_1_), channel_id=1, source_target_pairs={{0,2},{1,3},{2,0},{3,1},{4,6},{5,7},{6,4},{7,5},{8,10},{9,11},{10,... | collective-permute-start | bytes 2359304 | tf_op jit(solution)/shard_map/ppermute | solution.py:305
  23.5 21.8 %collective-permute-start.4 = (bf16[128,3072]{1,0:T(8,128)(2,1)}, bf16[128,3072]{1,0:T(8,128)(2,1)}, u32[]{:S(2)}, u32[]{:S(2)}) collective-permute-start(bf16[128,3072]{1,0:T(8,128)(2,1)} %collective-permute-done.1.refs_0_), channel_id=1, source_target_pairs={{0,2},{1,3},{2,0},{3,1},{4,6},{5,7},{6,4},{7,5},{8,10},{9,11},{10,... | collective-permute-start | bytes 2359304 | tf_op jit(solution)/shard_map/ppermute | solution.py:305
  25.3 3.6 %collective-permute-start = (f32[128,2]{0,1:T(2,128)S(1)}, f32[128,2]{0,1:T(2,128)S(1)}, u32[]{:S(2)}, u32[]{:S(2)}) collective-permute-start(f32[128,2]{0,1:T(2,128)S(1)} %pad_maximum_fusion), channel_id=1, source_target_pairs={{0,1},{1,0},{2,3},{3,2},{4,5},{5,4},{6,7},{7,6},{8,9},{9,8},{10,11... | collective-permute-start | bytes 3080 | tf_op jit(solution)/shard_map/ppermute | solution.py:305
  38.7 1.8 collective-permute-start.2
  38.8 6.5 %collective-permute-start.3 = (f32[256,2]{1,0:T(8,128)S(1)}, f32[256,2]{1,0:T(8,128)S(1)}, u32[]{:S(2)}, u32[]{:S(2)}) collective-permute-start(f32[256,2]{1,0:T(8,128)S(1)} %copy.13.scale_ref), channel_id=1, source_target_pairs={{0,2},{1,3},{2,0},{3,1},{4,6},{5,7},{6,4},{7,5},{8,10},{9,11},{10,... | collective-permute-start | bytes 6152 | tf_op jit(solution)/shard_map/ppermute | solution.py:305
  40.8 21.7 %collective-permute-start.7 = (bf16[512,768]{1,0:T(8,128)(2,1)S(1)}, bf16[512,768]{1,0:T(8,128)(2,1)S(1)}, u32[]{:S(2)}, u32[]{:S(2)}) collective-permute-start(bf16[512,768]{1,0:T(8,128)(2,1)S(1)} %stacked.8.refs_0_), channel_id=1, source_target_pairs={{0,4},{12,8},{1,5},{13,9},{2,6},{14,10},{3,7},{15,11},{16,20},{28,... | collective-permute-start | bytes 2359304 | tf_op jit(solution)/shard_map/ppermute | solution.py:368
  54.9 1.8 collective-permute-start.6
  58.2 26.8 %collective-permute-start.9 = (bf16[512,768]{1,0:T(8,128)(2,1)}, bf16[512,768]{1,0:T(8,128)(2,1)}, u32[]{:S(2)}, u32[]{:S(2)}) collective-permute-start(bf16[512,768]{1,0:T(8,128)(2,1)} %stacked.9.refs_0_), channel_id=1, source_target_pairs={{0,4},{12,8},{1,5},{13,9},{2,6},{14,10},{3,7},{15,11},{16,20},{28,... | collective-permute-start | bytes 2359304 | tf_op jit(solution)/shard_map/ppermute | solution.py:368
  73.5 0.7 copy-start.8
  74.2 1.7 collective-permute-start.8
  74.3 13.8 %collective-permute-start.10 = (bf16[512,768]{1,0:T(8,128)(2,1)}, bf16[512,768]{1,0:T(8,128)(2,1)}, u32[]{:S(2)}, u32[]{:S(2)}) collective-permute-start(bf16[512,768]{1,0:T(8,128)(2,1)} %added.8.refs_1_), channel_id=1, source_target_pairs={{4,8},{8,4},{5,9},{9,5},{6,10},{10,6},{7,11},{11,7},{20,24},{24,20... | collective-permute-start | bytes 2359304 | tf_op jit(solution)/shard_map/ppermute | solution.py:373
  76.2 0.9 copy-start.1
  79.9 38.2 %collective-permute-start.12 = (bf16[512,768]{1,0:T(8,128)(2,1)}, bf16[512,768]{1,0:T(8,128)(2,1)S(1)}, u32[]{:S(2)}, u32[]{:S(2)}) collective-permute-start(bf16[512,768]{1,0:T(8,128)(2,1)} %copy-done.1), channel_id=1, source_target_pairs={{0,4},{12,8},{1,5},{13,9},{2,6},{14,10},{3,7},{15,11},{16,20},{28,... | collective-permute-start | bytes 2359304 | tf_op jit(solution)/shard_map/ppermute | solution.py:368
  87.2 34.2 %collective-permute-start.13 = (bf16[512,768]{1,0:T(8,128)(2,1)S(1)}, bf16[512,768]{1,0:T(8,128)(2,1)S(1)}, u32[]{:S(2)}, u32[]{:S(2)}) collective-permute-start(bf16[512,768]{1,0:T(8,128)(2,1)S(1)} %added.9.refs_1_), channel_id=1, source_target_pairs={{4,8},{8,4},{5,9},{9,5},{6,10},{10,6},{7,11},{11,7},{20,24},{24,20... | collective-permute-start | bytes 2359304 | tf_op jit(solution)/shard_map/ppermute | solution.py:373
  88.0 4.8 %collective-permute-start.11 = (bf16[256,768]{1,0:T(8,128)(2,1)}, bf16[256,768]{1,0:T(8,128)(2,1)S(1)}, u32[]{:S(2)}, u32[]{:S(2)}) collective-permute-start(bf16[256,768]{1,0:T(8,128)(2,1)} %copy-done.8), channel_id=1, source_target_pairs={{0,16},{16,0},{1,17},{17,1},{2,18},{18,2},{3,19},{19,3},{4,20},{20... | collective-permute-start | bytes 1179656 | tf_op jit(solution)/shard_map/ppermute | solution.py:309
  91.5 33.4 %collective-permute-start.14 = (bf16[512,768]{1,0:T(8,128)(2,1)}, bf16[512,768]{1,0:T(8,128)(2,1)}, u32[]{:S(2)}, u32[]{:S(2)}) collective-permute-start(bf16[512,768]{1,0:T(8,128)(2,1)} %activated.8.refs_1_), channel_id=1, source_target_pairs={{4,0},{8,12},{5,1},{9,13},{6,2},{10,14},{7,3},{11,15},{20,16},{24,... | collective-permute-start | bytes 2359304 | tf_op jit(solution)/shard_map/ppermute | solution.py:379
  94.3 23.8 %copy-start.2 = (bf16[512,768]{1,0:T(8,128)(2,1)S(1)}, bf16[512,768]{1,0:T(8,128)(2,1)}, u32[]{:S(2)}) copy-start(bf16[512,768]{1,0:T(8,128)(2,1)} %copy-done.1) | copy-start | bytes 2359300
  94.3 50.6 %collective-permute-start.16 = (bf16[512,768]{1,0:T(8,128)(2,1)}, bf16[512,768]{1,0:T(8,128)(2,1)}, u32[]{:S(2)}, u32[]{:S(2)}) collective-permute-start(bf16[512,768]{1,0:T(8,128)(2,1)} %stacked.11.refs_0_), channel_id=1, source_target_pairs={{0,4},{12,8},{1,5},{13,9},{2,6},{14,10},{3,7},{15,11},{16,20},{28,... | collective-permute-start | bytes 2359304 | tf_op jit(solution)/shard_map/ppermute | solution.py:368
  118.1 5.4 %copy-start.3 = (bf16[256,768]{1,0:T(8,128)(2,1)}, bf16[256,768]{1,0:T(8,128)(2,1)S(1)}, u32[]{:S(2)}) copy-start(bf16[256,768]{1,0:T(8,128)(2,1)S(1)} %get-tuple-element.187.refs_0_) | copy-start | bytes 1179652
  118.1 6.7 %copy-start.6 = (bf16[256,768]{1,0:T(8,128)(2,1)}, bf16[256,768]{1,0:T(8,128)(2,1)S(1)}, u32[]{:S(2)}) copy-start(bf16[256,768]{1,0:T(8,128)(2,1)S(1)} %get-tuple-element.223) | copy-start | bytes 1179652
  119.9 28.3 %collective-permute-start.17 = (bf16[512,768]{1,0:T(8,128)(2,1)}, bf16[512,768]{1,0:T(8,128)(2,1)}, u32[]{:S(2)}, u32[]{:S(2)}) collective-permute-start(bf16[512,768]{1,0:T(8,128)(2,1)} %added.10.refs_1_), channel_id=1, source_target_pairs={{4,8},{8,4},{5,9},{9,5},{6,10},{10,6},{7,11},{11,7},{20,24},{24,20... | collective-permute-start | bytes 2359304 | tf_op jit(solution)/shard_map/ppermute | solution.py:373
  123.5 27.6 %collective-permute-start.18 = (bf16[512,768]{1,0:T(8,128)(2,1)}, bf16[512,768]{1,0:T(8,128)(2,1)}, u32[]{:S(2)}, u32[]{:S(2)}) collective-permute-start(bf16[512,768]{1,0:T(8,128)(2,1)} %activated.9.refs_1_), channel_id=1, source_target_pairs={{4,0},{8,12},{5,1},{9,13},{6,2},{10,14},{7,3},{11,15},{20,16},{24,... | collective-permute-start | bytes 2359304 | tf_op jit(solution)/shard_map/ppermute | solution.py:379
  124.8 2.3 collective-permute-start.15
  127.1 1.0 copy-start.4
  130.1 38.7 %collective-permute-start.22 = (bf16[512,768]{1,0:T(8,128)(2,1)S(1)}, bf16[512,768]{1,0:T(8,128)(2,1)S(1)}, u32[]{:S(2)}, u32[]{:S(2)}) collective-permute-start(bf16[512,768]{1,0:T(8,128)(2,1)S(1)} %stacked.12.refs_0_), channel_id=1, source_target_pairs={{0,4},{12,8},{1,5},{13,9},{2,6},{14,10},{3,7},{15,11},{16,20},{28,... | collective-permute-start | bytes 2359304 | tf_op jit(solution)/shard_map/ppermute | solution.py:368
  147.2 22.9 %collective-permute-start.23 = (bf16[512,768]{1,0:T(8,128)(2,1)S(1)}, bf16[512,768]{1,0:T(8,128)(2,1)S(1)}, u32[]{:S(2)}, u32[]{:S(2)}) collective-permute-start(bf16[512,768]{1,0:T(8,128)(2,1)S(1)} %added.11.refs_1_), channel_id=1, source_target_pairs={{4,8},{8,4},{5,9},{9,5},{6,10},{10,6},{7,11},{11,7},{20,24},{24,20... | collective-permute-start | bytes 2359304 | tf_op jit(solution)/shard_map/ppermute | solution.py:373
  147.9 5.8 %collective-permute-start.19 = (bf16[256,768]{1,0:T(8,128)(2,1)S(1)}, bf16[256,768]{1,0:T(8,128)(2,1)S(1)}, u32[]{:S(2)}, u32[]{:S(2)}) collective-permute-start(bf16[256,768]{1,0:T(8,128)(2,1)S(1)} %get-tuple-element.208), channel_id=1, source_target_pairs={{0,16},{16,0},{1,17},{17,1},{2,18},{18,2},{3,19},{19,3},{4,20},{20... | collective-permute-start | bytes 1179656 | tf_op jit(solution)/shard_map/ppermute | solution.py:309
  148.2 7.0 %collective-permute-start.21 = (bf16[256,768]{1,0:T(8,128)(2,1)S(1)}, bf16[256,768]{1,0:T(8,128)(2,1)S(1)}, u32[]{:S(2)}, u32[]{:S(2)}) collective-permute-start(bf16[256,768]{1,0:T(8,128)(2,1)S(1)} %get-tuple-element.212), channel_id=1, source_target_pairs={{0,16},{16,0},{1,17},{17,1},{2,18},{18,2},{3,19},{19,3},{4,20},{20... | collective-permute-start | bytes 1179656 | tf_op jit(solution)/shard_map/ppermute | solution.py:309
  153.4 6.7 %collective-permute-start.20 = (bf16[256,768]{1,0:T(8,128)(2,1)S(1)}, bf16[256,768]{1,0:T(8,128)(2,1)S(1)}, u32[]{:S(2)}, u32[]{:S(2)}) collective-permute-start(bf16[256,768]{1,0:T(8,128)(2,1)S(1)} %get-tuple-element.211), channel_id=1, source_target_pairs={{0,16},{16,0},{1,17},{17,1},{2,18},{18,2},{3,19},{19,3},{4,20},{20... | collective-permute-start | bytes 1179656 | tf_op jit(solution)/shard_map/ppermute | solution.py:309
  153.7 21.6 %collective-permute-start.24 = (bf16[512,768]{1,0:T(8,128)(2,1)S(1)}, bf16[512,768]{1,0:T(8,128)(2,1)S(1)}, u32[]{:S(2)}, u32[]{:S(2)}) collective-permute-start(bf16[512,768]{1,0:T(8,128)(2,1)S(1)} %activated.10.refs_1_), channel_id=1, source_target_pairs={{4,0},{8,12},{5,1},{9,13},{6,2},{10,14},{7,3},{11,15},{20,16},{24,... | collective-permute-start | bytes 2359304 | tf_op jit(solution)/shard_map/ppermute | solution.py:379
  155.2 31.4 %collective-permute-start.26 = (bf16[512,768]{1,0:T(8,128)(2,1)S(1)}, bf16[512,768]{1,0:T(8,128)(2,1)S(1)}, u32[]{:S(2)}, u32[]{:S(2)}) collective-permute-start(bf16[512,768]{1,0:T(8,128)(2,1)S(1)} %stacked.13.refs_0_), channel_id=1, source_target_pairs={{0,4},{12,8},{1,5},{13,9},{2,6},{14,10},{3,7},{15,11},{16,20},{28,... | collective-permute-start | bytes 2359304 | tf_op jit(solution)/shard_map/ppermute | solution.py:368
  168.8 3.6 %copy-start.7 = (bf16[256,768]{1,0:T(8,128)(2,1)S(1)}, bf16[256,768]{1,0:T(8,128)(2,1)}, u32[]{:S(2)}) copy-start(bf16[256,768]{1,0:T(8,128)(2,1)} %copy-done.6) | copy-start | bytes 1179652
  169.2 6.7 %copy-start = (bf16[512,3072]{0,1:T(8,128)(2,1)S(1)}, bf16[512,3072]{0,1:T(8,128)(2,1)}, u32[]{:S(2)}) copy-start(bf16[512,3072]{0,1:T(8,128)(2,1)} %copy.15) | copy-start | bytes 9437188
  169.2 18.6 %collective-permute-start.27 = (bf16[512,768]{1,0:T(8,128)(2,1)S(1)}, bf16[512,768]{1,0:T(8,128)(2,1)S(1)}, u32[]{:S(2)}, u32[]{:S(2)}) collective-permute-start(bf16[512,768]{1,0:T(8,128)(2,1)S(1)} %added.12.refs_1_), channel_id=1, source_target_pairs={{4,8},{8,4},{5,9},{9,5},{6,10},{10,6},{7,11},{11,7},{20,24},{24,20... | collective-permute-start | bytes 2359304 | tf_op jit(solution)/shard_map/ppermute | solution.py:373
  171.1 21.1 %collective-permute-start.28 = (bf16[512,768]{1,0:T(8,128)(2,1)S(1)}, bf16[512,768]{1,0:T(8,128)(2,1)S(1)}, u32[]{:S(2)}, u32[]{:S(2)}) collective-permute-start(bf16[512,768]{1,0:T(8,128)(2,1)S(1)} %activated.11.refs_1_), channel_id=1, source_target_pairs={{4,0},{8,12},{5,1},{9,13},{6,2},{10,14},{7,3},{11,15},{20,16},{24,... | collective-permute-start | bytes 2359304 | tf_op jit(solution)/shard_map/ppermute | solution.py:379
  172.4 3.2 %collective-permute-start.25 = (bf16[256,768]{1,0:T(8,128)(2,1)S(1)}, bf16[256,768]{1,0:T(8,128)(2,1)S(1)}, u32[]{:S(2)}, u32[]{:S(2)}) collective-permute-start(bf16[256,768]{1,0:T(8,128)(2,1)S(1)} %copy-done.7), channel_id=1, source_target_pairs={{0,16},{16,0},{1,17},{17,1},{2,18},{18,2},{3,19},{19,3},{4,20},{20... | collective-permute-start | bytes 1179656 | tf_op jit(solution)/shard_map/ppermute | solution.py:309
  183.4 24.2 %collective-permute-start.32 = (bf16[512,768]{1,0:T(8,128)(2,1)S(1)}, bf16[512,768]{1,0:T(8,128)(2,1)S(1)}, u32[]{:S(2)}, u32[]{:S(2)}) collective-permute-start(bf16[512,768]{1,0:T(8,128)(2,1)S(1)} %stacked.14.refs_0_), channel_id=1, source_target_pairs={{0,4},{12,8},{1,5},{13,9},{2,6},{14,10},{3,7},{15,11},{16,20},{28,... | collective-permute-start | bytes 2359304 | tf_op jit(solution)/shard_map/ppermute | solution.py:368
  187.1 21.7 %collective-permute-start.33 = (bf16[512,768]{1,0:T(8,128)(2,1)S(1)}, bf16[512,768]{1,0:T(8,128)(2,1)S(1)}, u32[]{:S(2)}, u32[]{:S(2)}) collective-permute-start(bf16[512,768]{1,0:T(8,128)(2,1)S(1)} %added.13.refs_1_), channel_id=1, source_target_pairs={{4,8},{8,4},{5,9},{9,5},{6,10},{10,6},{7,11},{11,7},{20,24},{24,20... | collective-permute-start | bytes 2359304 | tf_op jit(solution)/shard_map/ppermute | solution.py:373
  187.8 4.8 %collective-permute-start.29 = (bf16[256,768]{1,0:T(8,128)(2,1)S(1)}, bf16[256,768]{1,0:T(8,128)(2,1)S(1)}, u32[]{:S(2)}, u32[]{:S(2)}) collective-permute-start(bf16[256,768]{1,0:T(8,128)(2,1)S(1)} %get-tuple-element.235), channel_id=1, source_target_pairs={{0,16},{16,0},{1,17},{17,1},{2,18},{18,2},{3,19},{19,3},{4,20},{20... | collective-permute-start | bytes 1179656 | tf_op jit(solution)/shard_map/ppermute | solution.py:309
  187.9 6.3 %collective-permute-start.31 = (bf16[256,768]{1,0:T(8,128)(2,1)S(1)}, bf16[256,768]{1,0:T(8,128)(2,1)S(1)}, u32[]{:S(2)}, u32[]{:S(2)}) collective-permute-start(bf16[256,768]{1,0:T(8,128)(2,1)S(1)} %get-tuple-element.239), channel_id=1, source_target_pairs={{0,16},{16,0},{1,17},{17,1},{2,18},{18,2},{3,19},{19,3},{4,20},{20... | collective-permute-start | bytes 1179656 | tf_op jit(solution)/shard_map/ppermute | solution.py:309
  192.5 6.3 %collective-permute-start.30 = (bf16[256,768]{1,0:T(8,128)(2,1)S(1)}, bf16[256,768]{1,0:T(8,128)(2,1)S(1)}, u32[]{:S(2)}, u32[]{:S(2)}) collective-permute-start(bf16[256,768]{1,0:T(8,128)(2,1)S(1)} %get-tuple-element.238), channel_id=1, source_target_pairs={{0,16},{16,0},{1,17},{17,1},{2,18},{18,2},{3,19},{19,3},{4,20},{20... | collective-permute-start | bytes 1179656 | tf_op jit(solution)/shard_map/ppermute | solution.py:309
  192.6 22.0 %collective-permute-start.34 = (bf16[512,768]{1,0:T(8,128)(2,1)S(1)}, bf16[512,768]{1,0:T(8,128)(2,1)S(1)}, u32[]{:S(2)}, u32[]{:S(2)}) collective-permute-start(bf16[512,768]{1,0:T(8,128)(2,1)S(1)} %activated.12.refs_1_), channel_id=1, source_target_pairs={{4,0},{8,12},{5,1},{9,13},{6,2},{10,14},{7,3},{11,15},{20,16},{24,... | collective-permute-start | bytes 2359304 | tf_op jit(solution)/shard_map/ppermute | solution.py:379
  194.2 28.3 %collective-permute-start.35 = (bf16[512,768]{1,0:T(8,128)(2,1)S(1)}, bf16[512,768]{1,0:T(8,128)(2,1)S(1)}, u32[]{:S(2)}, u32[]{:S(2)}) collective-permute-start(bf16[512,768]{1,0:T(8,128)(2,1)S(1)} %stacked.15.refs_0_), channel_id=1, source_target_pairs={{0,4},{12,8},{1,5},{13,9},{2,6},{14,10},{3,7},{15,11},{16,20},{28,... | collective-permute-start | bytes 2359304 | tf_op jit(solution)/shard_map/ppermute | solution.py:368
  208.0 15.6 %collective-permute-start.36 = (bf16[512,768]{1,0:T(8,128)(2,1)S(1)}, bf16[512,768]{1,0:T(8,128)(2,1)S(1)}, u32[]{:S(2)}, u32[]{:S(2)}) collective-permute-start(bf16[512,768]{1,0:T(8,128)(2,1)S(1)} %added.14.refs_1_), channel_id=1, source_target_pairs={{4,8},{8,4},{5,9},{9,5},{6,10},{10,6},{7,11},{11,7},{20,24},{24,20... | collective-permute-start | bytes 2359304 | tf_op jit(solution)/shard_map/ppermute | solution.py:373
  209.8 21.5 %collective-permute-start.37 = (bf16[512,768]{1,0:T(8,128)(2,1)S(1)}, bf16[512,768]{1,0:T(8,128)(2,1)S(1)}, u32[]{:S(2)}, u32[]{:S(2)}) collective-permute-start(bf16[512,768]{1,0:T(8,128)(2,1)S(1)} %activated.13.refs_1_), channel_id=1, source_target_pairs={{4,0},{8,12},{5,1},{9,13},{6,2},{10,14},{7,3},{11,15},{20,16},{24,... | collective-permute-start | bytes 2359304 | tf_op jit(solution)/shard_map/ppermute | solution.py:379
  222.9 24.1 %collective-permute-start.40 = (bf16[512,768]{1,0:T(8,128)(2,1)S(1)}, bf16[512,768]{1,0:T(8,128)(2,1)S(1)}, u32[]{:S(2)}, u32[]{:S(2)}) collective-permute-start(bf16[512,768]{1,0:T(8,128)(2,1)S(1)} %added.15.refs_1_), channel_id=1, source_target_pairs={{4,8},{8,4},{5,9},{9,5},{6,10},{10,6},{7,11},{11,7},{20,24},{24,20... | collective-permute-start | bytes 2359304 | tf_op jit(solution)/shard_map/ppermute | solution.py:373
  223.6 8.1 %collective-permute-start.38 = (bf16[256,768]{1,0:T(8,128)(2,1)S(1)}, bf16[256,768]{1,0:T(8,128)(2,1)S(1)}, u32[]{:S(2)}, u32[]{:S(2)}) collective-permute-start(bf16[256,768]{1,0:T(8,128)(2,1)S(1)} %get-tuple-element.261), channel_id=1, source_target_pairs={{0,16},{16,0},{1,17},{17,1},{2,18},{18,2},{3,19},{19,3},{4,20},{20... | collective-permute-start | bytes 1179656 | tf_op jit(solution)/shard_map/ppermute | solution.py:309
  224.7 24.8 %collective-permute-start.41 = (bf16[512,768]{1,0:T(8,128)(2,1)S(1)}, bf16[512,768]{1,0:T(8,128)(2,1)S(1)}, u32[]{:S(2)}, u32[]{:S(2)}) collective-permute-start(bf16[512,768]{1,0:T(8,128)(2,1)S(1)} %activated.14.refs_1_), channel_id=1, source_target_pairs={{4,0},{8,12},{5,1},{9,13},{6,2},{10,14},{7,3},{11,15},{20,16},{24,... | collective-permute-start | bytes 2359304 | tf_op jit(solution)/shard_map/ppermute | solution.py:379
  231.6 7.2 %collective-permute-start.39 = (bf16[256,768]{1,0:T(8,128)(2,1)S(1)}, bf16[256,768]{1,0:T(8,128)(2,1)S(1)}, u32[]{:S(2)}, u32[]{:S(2)}) collective-permute-start(bf16[256,768]{1,0:T(8,128)(2,1)S(1)} %get-tuple-element.264), channel_id=1, source_target_pairs={{0,16},{16,0},{1,17},{17,1},{2,18},{18,2},{3,19},{19,3},{4,20},{20... | collective-permute-start | bytes 1179656 | tf_op jit(solution)/shard_map/ppermute | solution.py:309
  246.4 20.4 %collective-permute-start.43 = (bf16[128,3072]{1,0:T(8,128)(2,1)S(1)}, bf16[128,3072]{1,0:T(8,128)(2,1)S(1)}, u32[]{:S(2)}, u32[]{:S(2)}) collective-permute-start(bf16[128,3072]{1,0:T(8,128)(2,1)S(1)} %get-tuple-element.276), channel_id=1, source_target_pairs={{0,2},{1,3},{2,0},{3,1},{4,6},{5,7},{6,4},{7,5},{8,10},{9,11},{10,... | collective-permute-start | bytes 2359304 | tf_op jit(solution)/shard_map/ppermute | solution.py:305
  248.0 21.5 %collective-permute-start.44 = (bf16[512,768]{1,0:T(8,128)(2,1)S(1)}, bf16[512,768]{1,0:T(8,128)(2,1)S(1)}, u32[]{:S(2)}, u32[]{:S(2)}) collective-permute-start(bf16[512,768]{1,0:T(8,128)(2,1)S(1)} %activated.15.refs_1_), channel_id=1, source_target_pairs={{4,0},{8,12},{5,1},{9,13},{6,2},{10,14},{7,3},{11,15},{20,16},{24,... | collective-permute-start | bytes 2359304 | tf_op jit(solution)/shard_map/ppermute | solution.py:379
  249.8 1.8 collective-permute-start.42
  250.1 33.1 %collective-permute-start.46 = (bf16[128,3072]{1,0:T(8,128)(2,1)S(1)}, bf16[128,3072]{1,0:T(8,128)(2,1)S(1)}, u32[]{:S(2)}, u32[]{:S(2)}) collective-permute-start(bf16[128,3072]{1,0:T(8,128)(2,1)S(1)} %get-tuple-element.284), channel_id=1, source_target_pairs={{0,2},{1,3},{2,0},{3,1},{4,6},{5,7},{6,4},{7,5},{8,10},{9,11},{10,... | collective-permute-start | bytes 2359304 | tf_op jit(solution)/shard_map/ppermute | solution.py:305
  269.8 13.4 %collective-permute-start.45 = (bf16[256,768]{1,0:T(8,128)(2,1)S(1)}, bf16[256,768]{1,0:T(8,128)(2,1)S(1)}, u32[]{:S(2)}, u32[]{:S(2)}) collective-permute-start(bf16[256,768]{1,0:T(8,128)(2,1)S(1)} %get-tuple-element.280), channel_id=1, source_target_pairs={{0,16},{16,0},{1,17},{17,1},{2,18},{18,2},{3,19},{19,3},{4,20},{20... | collective-permute-start | bytes 1179656 | tf_op jit(solution)/shard_map/ppermute | solution.py:309
  290.9 19.2 %collective-permute-start.47 = (bf16[128,3072]{1,0:T(8,128)(2,1)S(1)}, bf16[128,3072]{1,0:T(8,128)(2,1)S(1)}, u32[]{:S(2)}, u32[]{:S(2)}) collective-permute-start(bf16[128,3072]{1,0:T(8,128)(2,1)S(1)} %get-tuple-element.288), channel_id=1, source_target_pairs={{0,1},{1,0},{2,3},{3,2},{4,5},{5,4},{6,7},{7,6},{8,9},{9,8},{10,11... | collective-permute-start | bytes 2359304 | tf_op jit(solution)/shard_map/ppermute | solution.py:305

commit v5 on v4

--- a/solution.py
+++ b/solution.py
@@ -6,7 +6,7 @@
 from jax.sharding import PartitionSpec as P
 
 D = 12288
-MATMUL_VMEM = 18 * 1024 * 1024
+MATMUL_VMEM = 22 * 1024 * 1024
 SMALL_VMEM = 8 * 1024 * 1024
 FAR, NEAR = 0, 1
 
@@ -87,10 +87,8 @@
     mine = steps // 2
     piece = count // pieces
 
-    def kernel(section_ref, rows_ref, upper_ref, lower_ref, *results):
-        product = dot_f32(rows_ref[:, : width // 2], upper_ref[...], (1, 0))
-        product = product + dot_f32(rows_ref[:, width // 2 :], lower_ref[...], (1, 0))
-        product = product.astype(jnp.bfloat16)
+    def kernel(section_ref, rows_ref, weight_ref, *results):
+        product = dot_f32(rows_ref[...], weight_ref[...], (1, 0)).astype(jnp.bfloat16)
 
         def store(refs):
             for i, result in enumerate(refs):
@@ -99,19 +97,16 @@
         pl.when(pl.program_id(0) < mine)(lambda: store(results[:pieces]))
         pl.when(pl.program_id(0) >= mine)(lambda: store(results[pieces:]))
 
-    def column(k):
-        return lambda i, s: (k, part * steps + lax.rem(i + s[0] * mine, steps))
-
+    column = lambda i, s: (0, part * steps + lax.rem(i + s[0] * mine, steps))
     return call(
         kernel,
         "up_product",
         (steps,),
         [section],
-        [rows, weight, weight],
+        [rows, weight],
         [
             fixed((count, width), (at, 0)),
-            pl.BlockSpec((width // 2, tile), column(0)),
-            pl.BlockSpec((width // 2, tile), column(1)),
+            pl.BlockSpec((width, tile), column),
         ],
         [pl.BlockSpec((piece, tile), lambda i, s: (0, jnp.minimum(i, mine - 1)))] * pieces
         + [pl.BlockSpec((piece, tile), lambda i, s: (0, jnp.maximum(i - mine, 0)))] * pieces,
@@ -194,15 +189,15 @@
     counts = [k.shape[0] for k in kept]
     count, half = sum(counts), kept[0].shape[1]
     width = weight.shape[0]
-    tile = 2 * tile_of(width // 2, 256)
+    tile = tile_of(width, 1024)
     n = len(kept)
     extra = [] if before is None else [before]
 
     def kernel(section_ref, *refs):
-        upper_ref, lower_ref = refs[2 * n : 2 * n + 2]
-        added = refs[2 * n + 2 : 2 * n + 2 + len(extra)]
-        others = refs[2 * n + 2 + len(extra) : 2 * n + 2 + len(extra) + len(arrived)]
-        results = refs[2 * n + 2 + len(extra) + len(arrived) : -1]
+        weight_ref = refs[2 * n]
+        added = refs[2 * n + 1 : 2 * n + 1 + len(extra)]
+        others = refs[2 * n + 1 + len(extra) : 2 * n + 1 + len(extra) + len(arrived)]
+        results = refs[2 * n + 1 + len(extra) + len(arrived) : -1]
         held = refs[-1]
 
         @pl.when(pl.program_id(0) == 0)
@@ -215,21 +210,21 @@
                 held[theirs, at : at + rows] = refs[n + i][...].T
                 at += rows
 
-        for k, weight_ref in enumerate((upper_ref, lower_ref)):
-            own = slice(k * tile // 2, (k + 1) * tile // 2)
-            product = dot_f32(weight_ref[...], held[...], (1, 0))
+        for at in range(0, count, 256):
+            own = slice(at, at + 256)
+            product = dot_f32(weight_ref[...], held[:, own], (1, 0))
             for ref in added:
-                product = product + ref[own, :]
+                product = product + ref[:, own]
             if kinds:
                 product = product.T
                 piece = count // len(kinds)
                 for i, result in enumerate(results):
                     value = product[i * piece : (i + 1) * piece]
                     if arrived:
-                        value = value + others[i][:, own].astype(jnp.float32)
-                    result[:, own] = value.astype(result.dtype)
+                        value = value + others[i][...].astype(jnp.float32)
+                    result[...] = value.astype(result.dtype)
             else:
-                results[0][own, :] = product
+                results[0][:, own] = product
 
     whole = [fixed((rows, half), (0, 0)) for rows in counts]
     if kinds:
@@ -244,13 +239,10 @@
         "down_product",
         (width // tile,),
         [section],
-        [*kept, *came, weight, weight, *extra, *arrived],
+        [*kept, *came, weight, *extra, *arrived],
         whole
         + whole
-        + [
-            pl.BlockSpec((tile // 2, 2 * half), lambda i, s: (2 * i, part)),
-            pl.BlockSpec((tile // 2, 2 * half), lambda i, s: (2 * i + 1, part)),
-        ]
+        + [pl.BlockSpec((tile, 2 * half), lambda i, s: (i, part))]
         + [pl.BlockSpec((tile, count), lambda i, s: (i, group))] * len(extra)
         + [pl.BlockSpec((count // max(len(kinds), 1), tile), lambda i, s: (0, i))] * len(arrived),
         out_specs,
@@ -263,7 +255,8 @@
     width, count = turned.shape
     counts = [k.shape[0] for k in kept]
     half = kept[0].shape[1]
-    tile = tile_of(width, 512)
+    tile = tile_of(width, 1024)
+    step = tile_of(2 * half, 256)
     n = len(kept)
 
     def kernel(section_ref, turned_ref, *refs):
@@ -279,7 +272,9 @@
                 held[at : at + rows, theirs] = refs[n + i][...]
                 at += rows
 
-        out[...] = dot_f32(turned_ref[...], held[...], (1, 0)).astype(jnp.bfloat16)
+        for at in range(0, 2 * half, step):
+            own = slice(at, at + step)
+            out[:, own] = dot_f32(turned_ref[...], held[:, own], (1, 0)).astype(jnp.bfloat16)
 
     whole = [fixed((rows, half), (0, 0)) for rows in counts]
     extra = [] if into is None else [into]
@@ -300,6 +295,26 @@
     )
 
 
+def transposed(value):
+    count, width = value.shape
+    tile = tile_of(width, 512)
+
+    def kernel(value_ref, out):
+        out[...] = value_ref[...].T
+
+    return call(
+        kernel,
+        "transposed",
+        (width // tile,),
+        [],
+        [value],
+        [pl.BlockSpec((count, tile), lambda i: (0, i))],
+        pl.BlockSpec((tile, count), lambda i: (i, 0)),
+        jax.ShapeDtypeStruct((width, count), value.dtype),
+        vmem=SMALL_VMEM,
+    )
+
+
 def from_peer(value, by):
     peers = lax.axis_size("mp")
     return lax.ppermute(value, "mp", [(i, i ^ by) for i in range(peers)])
@@ -331,12 +346,17 @@
         last.append(held)
         return held
 
+    receives = {
+        hop: jnp.logical_or(place == hop, place == line - 1 - hop).astype(jnp.int32).reshape(1)
+        for hop in range(half - 1)
+    }
+    tokens, section, first, receives = lax.optimization_barrier((tokens, section, first, receives))
+
     raw = run(lambda a, b: jnp.where(first[0] == 1, a, b), tokens, cotangent)["value"]
     across = peers // 2
     near = list(range(each, 2 * each)) + list(range(each))
     far = [by ^ across for by in near]
     gathered = {by: from_peer(raw, by) if by else raw for by in near}
-    gathered.update({by: from_peer(gathered[by ^ across], across) for by in far})
 
     values = tokens.astype(jnp.float32)
     row_total, row_squares = lax.psum((jnp.sum(values, 1), jnp.sum(values * values, 1)), "dp")
@@ -344,6 +364,9 @@
     inverse_std = lax.rsqrt(row_squares / D - average * average + epsilon)
     own_scale = jnp.stack([average, inverse_std], 1)
     near_scale = jnp.concatenate([from_peer(own_scale, by) if by else own_scale for by in near], 0)
+    gathered[across] = from_peer(raw, across)
+    gathered, near_scale = lax.optimization_barrier((gathered, near_scale))
+    gathered.update({by: from_peer(gathered[by ^ across], across) for by in far if by != across})
     far_scale = from_peer(near_scale, across)
 
     def prepare(members, scale, group, into):
@@ -377,11 +400,10 @@
         for hop in reversed(range(half - 1)):
             value = chunk["result"]["value"]
             arrived = lax.ppermute(value, "dp", [(hop + 1, hop), (line - 2 - hop, line - 1 - hop)])
-            receives = jnp.logical_or(place == hop, place == line - 1 - hop).astype(jnp.int32).reshape(1)
             if hop:
-                chunk["result"] = run(lambda a, b: chosen(receives, a, b, False)[0], value, arrived)
+                chunk["result"] = run(lambda a, b: chosen(receives[hop], a, b, False)[0], value, arrived)
             else:
-                chunk["halves"] = run(lambda a, b: chosen(receives, a, b, True), value, arrived)
+                chunk["halves"] = run(lambda a, b: chosen(receives[hop], a, b, True), value, arrived)
 
     def hidden(part, groups):
         kept = [chunks[part, g]["halves"]["value"][0] for g in groups]
@@ -391,11 +413,10 @@
         return kept, [chunks[part, g]["came"] for g in groups]
 
     both = (FAR, NEAR)
-    order = [(part, g) for part in range(parts - 2) for g in (NEAR, FAR)]
-    order += [(part, g) for g in (FAR, NEAR) for part in (parts - 2, parts - 1)]
+    order = [(0, NEAR)] + [(part, FAR) for part in range(parts)] + [(part, NEAR) for part in range(1, parts)]
     count = len(order)
     multiplied = {0}
-    held = {"partial": None, "gradient": None}
+    held = {"gradient": None}
 
     def need(c):
         if c < count and order[c][0] not in multiplied:
@@ -438,22 +459,25 @@
             need(2)
         tick(t)
         if t == 0:
-            turned = run(lambda a: a.T, x_all)["value"]
+            turned = run(transposed, x_all)["value"]
         need(t + 3)
-        if t >= 3 and (t - 3) // 2 < parts - 2:
-            if t % 2 == 1:
-                held["partial"] = go_down((t - 3) // 2, both, held["partial"], 0)
-            else:
-                go_gradient((t - 3) // 2)
-        if t == count - 1:
-            far_sum = go_down(parts - 2, [FAR], held["partial"], FAR)
-            sent_far = go_down(parts - 1, [FAR], far_sum, 0, [jnp.bfloat16] * 2)
-        if t == count:
-            go_gradient(parts - 2)
-            near_sum = go_down(parts - 2, [NEAR], held["partial"], NEAR)
+        far_part, near_part = t - 3, t - 2 - parts
+        if far_part == 0:
+            near_sum = far_sum = go_down(0, both, None, 0)
+        elif 0 < far_part < parts - 1:
+            far_sum = go_down(far_part, [FAR], far_sum, FAR if far_part == 1 else 0)
+            if far_part == 1:
+                go_gradient(0)
+        elif far_part == parts - 1:
+            sent_far = go_down(far_part, [FAR], far_sum, FAR if far_part == 1 else 0, [jnp.bfloat16] * 2)
             arrived = [from_peer(value, across) for value in sent_far["value"]]
-            near_sum["value"], arrived[0] = lax.optimization_barrier((near_sum["value"], arrived[0]))
-    sent_near = go_down(parts - 1, [NEAR], near_sum, 0, [jnp.bfloat16, jnp.float32], arrived)
+        elif 0 < near_part < parts - 1:
+            go_gradient(near_part)
+            near_sum = go_down(near_part, [NEAR], near_sum, NEAR if near_part == 1 else 0)
+            if near_part == 1:
+                near_sum["value"], arrived[0] = lax.optimization_barrier((near_sum["value"], arrived[0]))
+    column = NEAR if parts == 2 else 0
+    sent_near = go_down(parts - 1, [NEAR], near_sum, column, [jnp.bfloat16, jnp.float32], arrived)
     go_gradient(parts - 1)
 
     own = sent_near["value"][1]

time: 313 us -> 277 us (0.88)
  Pallas kernels: 160 us -> 135 us
  starting transfers between devices: 76.9 us -> 65.4 us
  waiting for transfers between devices: 50.6 us -> 58.6 us
  local copies, waits for them, and re-layouts: 5.54 us -> 0.14 us
    pallas_call x49 -> x51, Pallas kernels: 160 us -> 135 us  [call(): pl.pallas_call(kernel, grid_spec=pltpu.PrefetchScalarGridSpec(num_scalar_...]
    ppermute x8, waiting for transfers between devices: 0.02 us -> 7.77 us  [inward(): lax.ppermute(value, 'dp', [(hop, hop + 1), (line - 1 - hop, line - 2 - ho...]
    ppermute x8, starting transfers between devices: 44.8 us -> 37.1 us  [inward(): lax.ppermute(value, 'dp', [(hop, hop + 1), (line - 1 - hop, line - 2 - ho...]
    ppermute x8, waiting for transfers between devices: 30.1 us -> 24.1 us  [from_peer(): return lax.ppermute(value, 'mp', [(i, i ^ by) for i in range(peers)])]
    ppermute x16, waiting for transfers between devices: 3.33 us -> 8.05 us  [across_sections(): return lax.ppermute(value, 'section', [(0, 1), (1, 0)])]
  transfers between devices with their start and end apart: 48 -> 48, of which waited for: 14 -> 20; matrix products, arithmetic and copies ran while one was open for 1% -> 1% of each run, Pallas kernels for 49% -> 47%
where the time goes in v5:
time: 277 us; the launch traced here: 276 us
  Pallas kernels  135 us (49%)
  starting transfers between devices  65.4 us (24%)
  waiting for transfers between devices  58.6 us (21%)
  blocking collectives  12 us (4%)
  other arithmetic  3.71 us (1%)
    pallas_call x51, Pallas kernels, call(): pl.pallas_call(kernel, grid_spec=pltpu.PrefetchScalarGridSpec(num_scalar_...  135 us
    ppermute x8, starting transfers between devices, inward(): lax.ppermute(value, 'dp', [(hop, hop + 1), (line - 1 - hop, line - 2 - ho...  37.1 us
    ppermute x8, waiting for transfers between devices, from_peer(): return lax.ppermute(value, 'mp', [(i, i ^ by) for i in range(peers)])  24.1 us
    ppermute x8, waiting for transfers between devices, outward(): lax.ppermute(value, 'dp', [(hop + 1, hop), (line - 2 - hop, line - 1 - ho...  18.7 us
    psum x1, blocking collectives, local(): lax.psum((jnp.sum(values, 1), jnp.sum(values * values, 1)), 'dp')  12 us
    ppermute x8, starting transfers between devices, outward(): lax.ppermute(value, 'dp', [(hop + 1, hop), (line - 2 - hop, line - 1 - ho...  10.7 us
    ppermute x8, starting transfers between devices, from_peer(): return lax.ppermute(value, 'mp', [(i, i ^ by) for i in range(peers)])  9.42 us
    ppermute x16, waiting for transfers between devices, across_sections(): return lax.ppermute(value, 'section', [(0, 1), (1, 0)])  8.05 us
  transfers between devices with their start and end apart: 48, of which 20 were waited for; matrix products, arithmetic and copies ran while one was open for 1% of the time, Pallas kernels for 47%

profile of v5, /device:TPU:0, one launch (start us, length us, event | category | flops | bytes accessed | tf_op | source)
XLA Modules:
  0.0 275.9 jit_solution(16140919648361548500)
XLA Ops:
  0.7 1.2 broadcast_select_fusion.refs_1_
  1.9 3.0 %collective-permute-start = (bf16[128,3072]{1,0:T(8,128)(2,1)S(1)}, bf16[128,3072]{1,0:T(8,128)(2,1)S(1)}, u32[]{:S(2)}, u32[]{:S(2)}) collective-permute-start(bf16[128,3072]{1,0:T(8,128)(2,1)S(1)} %broadcast_select_fusion.refs_1_), channel_id=1, source_target_pairs={{0,1},{1,0},{2,3},{3,2},{4,5},{5,4},{6,7},{7,6},{8,9},{9,8},{10,11... | collective-permute-start | bytes 2359304 | tf_op jit(solution)/shard_map/ppermute | solution.py:320
  4.9 1.5 collective-permute-start.1
  6.4 1.4 convert_reduce_fusion
  7.8 12.0 %all-reduce = (f32[128]{0:T(128)S(1)}, f32[128]{0:T(128)S(1)}) all-reduce(f32[128]{0:T(128)S(1)} %get-tuple-element.310, f32[128]{0:T(128)S(1)} %get-tuple-element.309), channel_id=1, replica_groups=mesh['section'=2,'dp'=4,'mp'=4] {'dp'}, use_global_device_ids=true, to_apply=%region_3.4 | all-reduce | flops 256 | bytes 2048 | tf_op jit(solution)/shard_map/psum | solution.py:362
  20.4 3.0 %collective-permute-done.2 = f32[128,2]{0,1:T(2,128)S(1)} collective-permute-done((f32[128,2]{0,1:T(2,128)S(1)}, f32[128,2]{0,1:T(2,128)S(1)}, u32[]{:S(2)}, u32[]{:S(2)}) %collective-permute-start.2) | collective-permute-done | bytes 1056 | tf_op jit(solution)/shard_map/ppermute | solution.py:320
  23.9 1.5 collective-permute-start.5
  25.6 1.2 normalize.2.rows_ref.refs_2_
  26.8 6.7 %up_product.5 = (bf16[256,768]{1,0:T(8,128)(2,1)S(1)}, bf16[256,768]{1,0:T(8,128)(2,1)S(1)}) custom-call(s32[1]{0:T(128)} %bitcast.section_ref, bf16[512,3072]{1,0:T(8,128)(2,1)S(1)} %normalize.2.rows_ref.refs_2_, bf16[3072,6144]{1,0:T(8,128)(2,1)} %bitcast.15), custom_call_target="tpu_custom_call" | custom-call | tf_op jit(solution)/shard_map/up_product/pallas_call | solution.py:32
  34.2 1.1 collective-permute-done.3.refs_1_
  35.6 3.5 %collective-permute-start.7 = (bf16[512,768]{1,0:T(8,128)(2,1)S(1)}, bf16[512,768]{1,0:T(8,128)(2,1)S(1)}, u32[]{:S(2)}, u32[]{:S(2)}) collective-permute-start(bf16[512,768]{1,0:T(8,128)(2,1)S(1)} %stacked.8.refs_0_), channel_id=1, source_target_pairs={{0,4},{12,8},{1,5},{13,9},{2,6},{14,10},{3,7},{15,11},{16,20},{28,... | collective-permute-start | bytes 2359304 | tf_op jit(solution)/shard_map/ppermute | solution.py:391
  39.1 5.7 %collective-permute-done.4.scale_ref = f32[256,2]{1,0:T(8,128)S(1)} collective-permute-done((f32[256,2]{1,0:T(8,128)S(1)}, f32[256,2]{1,0:T(8,128)S(1)}, u32[]{:S(2)}, u32[]{:S(2)}) %collective-permute-start.4) | collective-permute-done | bytes 2080 | tf_op jit(solution)/shard_map/ppermute | solution.py:320
  44.8 1.2 normalize.3.rows_ref.value_ref
  46.0 6.7 %up_product.6 = (bf16[256,768]{1,0:T(8,128)(2,1)S(1)}, bf16[256,768]{1,0:T(8,128)(2,1)S(1)}) custom-call(s32[1]{0:T(128)} %bitcast.section_ref, bf16[512,3072]{1,0:T(8,128)(2,1)S(1)} %normalize.3.rows_ref.value_ref, bf16[3072,6144]{1,0:T(8,128)(2,1)} %bitcast.16), custom_call_target="tpu_custom_call" | custom-call | tf_op jit(solution)/shard_map/up_product/pallas_call | solution.py:32
  52.8 1.7 collective-permute-done.6.refs_1_
  54.8 3.5 %collective-permute-start.9 = (bf16[512,768]{1,0:T(8,128)(2,1)S(1)}, bf16[512,768]{1,0:T(8,128)(2,1)S(1)}, u32[]{:S(2)}, u32[]{:S(2)}) collective-permute-start(bf16[512,768]{1,0:T(8,128)(2,1)S(1)} %stacked.9.refs_0_), channel_id=1, source_target_pairs={{0,4},{12,8},{1,5},{13,9},{2,6},{14,10},{3,7},{15,11},{16,20},{28,... | collective-permute-start | bytes 2359304 | tf_op jit(solution)/shard_map/ppermute | solution.py:391
  58.7 9.4 %up_product.7 = (bf16[256,768]{1,0:T(8,128)(2,1)S(1)}, bf16[256,768]{1,0:T(8,128)(2,1)S(1)}, bf16[256,768]{1,0:T(8,128)(2,1)S(1)}, bf16[256,768]{1,0:T(8,128)(2,1)S(1)}) custom-call(s32[1]{0:T(128)} %bitcast.section_ref, bf16[512,3072]{1,0:T(8,128)(2,1)S(1)} %normalize.3.rows_ref.value_ref, bf16[3072,6144]{1,0:T(8,128)(2,1)} %bitcast.17), custom_call_target="tpu_custom_call" | custom-call | tf_op jit(solution)/shard_map/up_product/pallas_call | solution.py:32
  68.9 1.0 collective-permute-done.8.refs_1_
  70.2 1.4 transposed.1.turned_ref
  71.6 9.4 %up_product.8 = (bf16[256,768]{1,0:T(8,128)(2,1)S(1)}, bf16[256,768]{1,0:T(8,128)(2,1)S(1)}, bf16[256,768]{1,0:T(8,128)(2,1)S(1)}, bf16[256,768]{1,0:T(8,128)(2,1)S(1)}) custom-call(s32[1]{0:T(128)} %bitcast.section_ref, bf16[512,3072]{1,0:T(8,128)(2,1)S(1)} %normalize.3.rows_ref.value_ref, bf16[3072,6144]{1,0:T(8,128)(2,1)} %bitcast.18), custom_call_target="tpu_custom_call" | custom-call | tf_op jit(solution)/shard_map/up_product/pallas_call | solution.py:32
  81.0 4.0 %collective-permute-start.12 = (bf16[512,768]{1,0:T(8,128)(2,1)S(1)}, bf16[512,768]{1,0:T(8,128)(2,1)S(1)}, u32[]{:S(2)}, u32[]{:S(2)}) collective-permute-start(bf16[512,768]{1,0:T(8,128)(2,1)S(1)} %stacked.10.refs_0_), channel_id=1, source_target_pairs={{0,4},{12,8},{1,5},{13,9},{2,6},{14,10},{3,7},{15,11},{16,20},{28,... | collective-permute-start | bytes 2359304 | tf_op jit(solution)/shard_map/ppermute | solution.py:391
  86.2 1.0 activated.8.refs_1_
  87.3 1.3 collective-permute-start.14
  88.8 9.4 %up_product.9 = (bf16[256,768]{1,0:T(8,128)(2,1)S(1)}, bf16[256,768]{1,0:T(8,128)(2,1)S(1)}, bf16[256,768]{1,0:T(8,128)(2,1)S(1)}, bf16[256,768]{1,0:T(8,128)(2,1)S(1)}) custom-call(s32[1]{0:T(128)} %bitcast.section_ref, bf16[512,3072]{1,0:T(8,128)(2,1)S(1)} %normalize.3.rows_ref.value_ref, bf16[3072,6144]{1,0:T(8,128)(2,1)} %bitcast.19), custom_call_target="tpu_custom_call" | custom-call | tf_op jit(solution)/shard_map/up_product/pallas_call | solution.py:32
  98.2 6.4 %collective-permute-start.16 = (bf16[512,768]{1,0:T(8,128)(2,1)S(1)}, bf16[512,768]{1,0:T(8,128)(2,1)S(1)}, u32[]{:S(2)}, u32[]{:S(2)}) collective-permute-start(bf16[512,768]{1,0:T(8,128)(2,1)S(1)} %stacked.11.refs_0_), channel_id=1, source_target_pairs={{0,4},{12,8},{1,5},{13,9},{2,6},{14,10},{3,7},{15,11},{16,20},{28,... | collective-permute-start | bytes 2359304 | tf_op jit(solution)/shard_map/ppermute | solution.py:391
  105.8 1.0 activated.9.refs_1_
  106.9 1.3 collective-permute-start.18
  108.2 1.8 collective-permute-done.14.refs_2_
  110.6 4.2 %collective-permute-start.22 = (bf16[512,768]{1,0:T(8,128)(2,1)S(1)}, bf16[512,768]{1,0:T(8,128)(2,1)S(1)}, u32[]{:S(2)}, u32[]{:S(2)}) collective-permute-start(bf16[512,768]{1,0:T(8,128)(2,1)S(1)} %stacked.12.refs_0_), channel_id=1, source_target_pairs={{0,4},{12,8},{1,5},{13,9},{2,6},{14,10},{3,7},{15,11},{16,20},{28,... | collective-permute-start | bytes 2359304 | tf_op jit(solution)/shard_map/ppermute | solution.py:391
  114.8 7.8 %collective-permute-done.16.refs_1_ = bf16[512,768]{1,0:T(8,128)(2,1)S(1)} collective-permute-done((bf16[512,768]{1,0:T(8,128)(2,1)S(1)}, bf16[512,768]{1,0:T(8,128)(2,1)S(1)}, u32[]{:S(2)}, u32[]{:S(2)}) %collective-permute-start.16) | collective-permute-done | bytes 786464 | tf_op jit(solution)/shard_map/ppermute | solution.py:391
  123.7 1.0 activated.10.refs_1_
  124.8 1.5 collective-permute-start.24
  128.9 6.3 %collective-permute-start.27 = (bf16[512,768]{1,0:T(8,128)(2,1)S(1)}, bf16[512,768]{1,0:T(8,128)(2,1)S(1)}, u32[]{:S(2)}, u32[]{:S(2)}) collective-permute-start(bf16[512,768]{1,0:T(8,128)(2,1)S(1)} %stacked.13.refs_0_), channel_id=1, source_target_pairs={{0,4},{12,8},{1,5},{13,9},{2,6},{14,10},{3,7},{15,11},{16,20},{28,... | collective-permute-start | bytes 2359304 | tf_op jit(solution)/shard_map/ppermute | solution.py:391
  135.3 7.8 %down_product.7.refs_3_ = f32[3072,512]{1,0:T(8,128)S(1)} custom-call(s32[1]{0:T(128)} %bitcast.section_ref, bf16[256,768]{1,0:T(8,128)(2,1)S(1)} %get-tuple-element.245.refs_0_, bf16[256,768]{1,0:T(8,128)(2,1)S(1)} %get-tuple-element.227.refs_1_, bf16[256,768]{1,0:T(8,128)(2,1)S(1)} %collective-permute-done.20.refs_2_, ...), custom_call_target="tpu_custom_call" | custom-call | tf_op jit(solution)/shard_map/down_product/pallas_call | solution.py:32
  144.4 1.0 activated.11.refs_1_
  145.4 1.3 collective-permute-start.29
  147.9 4.4 %collective-permute-start.32 = (bf16[512,768]{1,0:T(8,128)(2,1)S(1)}, bf16[512,768]{1,0:T(8,128)(2,1)S(1)}, u32[]{:S(2)}, u32[]{:S(2)}) collective-permute-start(bf16[512,768]{1,0:T(8,128)(2,1)S(1)} %stacked.14.refs_0_), channel_id=1, source_target_pairs={{0,4},{12,8},{1,5},{13,9},{2,6},{14,10},{3,7},{15,11},{16,20},{28,... | collective-permute-start | bytes 2359304 | tf_op jit(solution)/shard_map/ppermute | solution.py:391
  152.2 6.0 %down_product.8.refs_3_ = f32[3072,256]{1,0:T(8,128)S(1)} custom-call(s32[1]{0:T(128)} %bitcast.section_ref, bf16[256,768]{1,0:T(8,128)(2,1)S(1)} %get-tuple-element.282.refs_0_, bf16[256,768]{1,0:T(8,128)(2,1)S(1)} %collective-permute-done.26.refs_1_.refs_2_, bf16[3072,6144]{1,0:T(8,128)(2,1)} %bitcast.21, f32[3072,512]{1,0:T(8,128)S(1)} %down_product.7.refs_3_), custom_call_target="tpu_custom_call" | custom-call | tf_op jit(solution)/shard_map/down_product/pallas_call | solution.py:32
  158.3 7.2 %weight_gradient.4.refs_4_ = bf16[3072,6144]{1,0:T(8,128)(2,1)} custom-call(s32[1]{0:T(128)} %bitcast.section_ref, bf16[3072,512]{1,0:T(8,128)(2,1)S(1)} %transposed.1.turned_ref, bf16[256,768]{1,0:T(8,128)(2,1)S(1)} %get-tuple-element.245.refs_0_, bf16[256,768]{1,0:T(8,128)(2,1)S(1)} %get-tuple-element.227.refs_1_, ...), custom_call_target="tpu_custom_call" | custom-call | tf_op jit(solution)/shard_map/weight_gradient/pallas_call | solution.py:32
  166.7 1.0 activated.12.refs_1_
  167.7 1.3 collective-permute-start.34
  171.0 4.6 %collective-permute-start.36 = (bf16[512,768]{1,0:T(8,128)(2,1)S(1)}, bf16[512,768]{1,0:T(8,128)(2,1)S(1)}, u32[]{:S(2)}, u32[]{:S(2)}) collective-permute-start(bf16[512,768]{1,0:T(8,128)(2,1)S(1)} %stacked.15.refs_0_), channel_id=1, source_target_pairs={{0,4},{12,8},{1,5},{13,9},{2,6},{14,10},{3,7},{15,11},{16,20},{28,... | collective-permute-start | bytes 2359304 | tf_op jit(solution)/shard_map/ppermute | solution.py:391
  175.7 6.0 %down_product.9.refs_3_ = f32[3072,256]{1,0:T(8,128)S(1)} custom-call(s32[1]{0:T(128)} %bitcast.section_ref, bf16[256,768]{1,0:T(8,128)(2,1)S(1)} %get-tuple-element.292.refs_0_, bf16[256,768]{1,0:T(8,128)(2,1)S(1)} %collective-permute-done.31.refs_1_.refs_2_, bf16[3072,6144]{1,0:T(8,128)(2,1)} %bitcast.22, f32[3072,256]{1,0:T(8,128)S(1)} %down_product.8.refs_3_), custom_call_target="tpu_custom_call" | custom-call | tf_op jit(solution)/shard_map/down_product/pallas_call | solution.py:32
  182.9 1.0 activated.13.refs_1_
  183.9 1.3 collective-permute-start.38
  185.2 3.8 %collective-permute-done.34.refs_2_ = bf16[512,768]{1,0:T(8,128)(2,1)S(1)} collective-permute-done((bf16[512,768]{1,0:T(8,128)(2,1)S(1)}, bf16[512,768]{1,0:T(8,128)(2,1)S(1)}, u32[]{:S(2)}, u32[]{:S(2)}) %collective-permute-start.34) | collective-permute-done | bytes 786464 | tf_op jit(solution)/shard_map/ppermute | solution.py:402
  189.5 1.7 collective-permute-done.35.refs_1_.refs_2_
  191.2 6.2 %down_product.10 = (bf16[128,3072]{1,0:T(8,128)(2,1)S(1)}, bf16[128,3072]{1,0:T(8,128)(2,1)S(1)}) custom-call(s32[1]{0:T(128)} %bitcast.section_ref, bf16[256,768]{1,0:T(8,128)(2,1)S(1)} %get-tuple-element.306.refs_0_, bf16[256,768]{1,0:T(8,128)(2,1)S(1)} %collective-permute-done.35.refs_1_.refs_2_, bf16[3072,6144]{1,0:T(8,128)(2,1)} %bitcast.23, ...), custom_call_target="tpu_custom_call" | custom-call | tf_op jit(solution)/shard_map/down_product/pallas_call | solution.py:32
  199.4 1.0 activated.14.refs_1_
  200.4 6.0 %collective-permute-done.38.refs_2_ = bf16[512,768]{1,0:T(8,128)(2,1)S(1)} collective-permute-done((bf16[512,768]{1,0:T(8,128)(2,1)S(1)}, bf16[512,768]{1,0:T(8,128)(2,1)S(1)}, u32[]{:S(2)}, u32[]{:S(2)}) %collective-permute-start.38) | collective-permute-done | bytes 786464 | tf_op jit(solution)/shard_map/ppermute | solution.py:402
  206.8 1.5 collective-permute-start.42
  208.5 7.2 %weight_gradient.5.refs_4_ = bf16[3072,6144]{1,0:T(8,128)(2,1)} custom-call(s32[1]{0:T(128)} %bitcast.section_ref, bf16[3072,512]{1,0:T(8,128)(2,1)S(1)} %transposed.1.turned_ref, bf16[256,768]{1,0:T(8,128)(2,1)S(1)} %get-tuple-element.282.refs_0_, bf16[256,768]{1,0:T(8,128)(2,1)S(1)} %get-tuple-element.284.refs_1_.refs_0_, ...), custom_call_target="tpu_custom_call", output_to_operand_aliasing={{}: (6, {})} | custom-call | tf_op jit(solution)/shard_map/weight_gradient/pallas_call | solution.py:32
  215.7 6.0 %down_product.11.refs_3_ = f32[3072,256]{1,0:T(8,128)S(1)} custom-call(s32[1]{0:T(128)} %bitcast.section_ref, bf16[256,768]{1,0:T(8,128)(2,1)S(1)} %get-tuple-element.284.refs_1_.refs_0_, bf16[256,768]{1,0:T(8,128)(2,1)S(1)} %collective-permute-done.39.refs_3_.refs_1_, bf16[3072,6144]{1,0:T(8,128)(2,1)} %bitcast.24, f32[3072,512]{1,0:T(8,128)S(1)} %down_product.7.refs_3_), custom_call_target="tpu_custom_call" | custom-call | tf_op jit(solution)/shard_map/down_product/pallas_call | solution.py:32
  221.8 1.0 activated.15.refs_1_
  222.8 1.3 collective-permute-start.44
  224.1 4.9 %collective-permute-done.42.refs_2_ = bf16[512,768]{1,0:T(8,128)(2,1)S(1)} collective-permute-done((bf16[512,768]{1,0:T(8,128)(2,1)S(1)}, bf16[512,768]{1,0:T(8,128)(2,1)S(1)}, u32[]{:S(2)}, u32[]{:S(2)}) %collective-permute-start.42) | collective-permute-done | bytes 786464 | tf_op jit(solution)/shard_map/ppermute | solution.py:402
  231.2 7.2 %weight_gradient.6.refs_4_ = bf16[3072,6144]{1,0:T(8,128)(2,1)} custom-call(s32[1]{0:T(128)} %bitcast.section_ref, bf16[3072,512]{1,0:T(8,128)(2,1)S(1)} %transposed.1.turned_ref, bf16[256,768]{1,0:T(8,128)(2,1)S(1)} %get-tuple-element.292.refs_0_, bf16[256,768]{1,0:T(8,128)(2,1)S(1)} %get-tuple-element.294.refs_1_.refs_0_, ...), custom_call_target="tpu_custom_call", output_to_operand_aliasing={{}: (6, {})} | custom-call | tf_op jit(solution)/shard_map/weight_gradient/pallas_call | solution.py:32
  238.4 6.0 %down_product.12.refs_3_ = f32[3072,256]{1,0:T(8,128)S(1)} custom-call(s32[1]{0:T(128)} %bitcast.section_ref, bf16[256,768]{1,0:T(8,128)(2,1)S(1)} %get-tuple-element.294.refs_1_.refs_0_, bf16[256,768]{1,0:T(8,128)(2,1)S(1)} %collective-permute-done.43.refs_3_.refs_1_, bf16[3072,6144]{1,0:T(8,128)(2,1)} %bitcast.25, f32[3072,256]{1,0:T(8,128)S(1)} %down_product.11.refs_3_), custom_call_target="tpu_custom_call" | custom-call | tf_op jit(solution)/shard_map/down_product/pallas_call | solution.py:32
  244.4 1.1 collective-permute-done.44.refs_2_
  245.9 3.5 %collective-permute-done.46.refs_5_ = bf16[128,3072]{1,0:T(8,128)(2,1)S(1)} collective-permute-done((bf16[128,3072]{1,0:T(8,128)(2,1)S(1)}, bf16[128,3072]{1,0:T(8,128)(2,1)S(1)}, u32[]{:S(2)}, u32[]{:S(2)}) %collective-permute-start.46) | collective-permute-done | bytes 786464 | tf_op jit(solution)/shard_map/ppermute | solution.py:320
  249.4 6.3 %down_product.13 = (bf16[128,3072]{1,0:T(8,128)(2,1)S(1)}, f32[128,3072]{1,0:T(8,128)S(1)}) custom-call(s32[1]{0:T(128)} %bitcast.section_ref, bf16[256,768]{1,0:T(8,128)(2,1)S(1)} %get-tuple-element.307.refs_0_.refs_1_, bf16[256,768]{1,0:T(8,128)(2,1)S(1)} %collective-permute-done.45.refs_1_.refs_3_, bf16[3072,6144]{1,0:T(8,128)(2,1)} %bitcast.26, ...), custom_call_target="tpu_custom_call" | custom-call | tf_op jit(solution)/shard_map/down_product/pallas_call | solution.py:32
  256.3 7.2 %weight_gradient.7 = bf16[3072,6144]{1,0:T(8,128)(2,1)} custom-call(s32[1]{0:T(128)} %bitcast.section_ref, bf16[3072,512]{1,0:T(8,128)(2,1)S(1)} %transposed.1.turned_ref, bf16[256,768]{1,0:T(8,128)(2,1)S(1)} %get-tuple-element.306.refs_0_, bf16[256,768]{1,0:T(8,128)(2,1)S(1)} %get-tuple-element.307.refs_0_.refs_1_, ...), custom_call_target="tpu_custom_call", output_to_operand_aliasing={{}: (6, {})} | custom-call | tf_op jit(solution)/shard_map/weight_gradient/pallas_call | solution.py:32
  263.5 11.4 %collective-permute-done.47 = bf16[128,3072]{1,0:T(8,128)(2,1)S(1)} collective-permute-done((bf16[128,3072]{1,0:T(8,128)(2,1)S(1)}, bf16[128,3072]{1,0:T(8,128)(2,1)S(1)}, u32[]{:S(2)}, u32[]{:S(2)}) %collective-permute-start.47) | collective-permute-done | bytes 786464 | tf_op jit(solution)/shard_map/ppermute | solution.py:320
  274.9 1.0 fusion.1
  (93 shorter events, 23.4 us)
Async XLA Ops:
  0.6 24.9 %copy-start = (f32[3072]{0:T(1024)S(1)}, f32[3072]{0:T(1024)}, u32[]{:S(2)}) copy-start(f32[3072]{0:T(1024)} %param.6) | copy-start | bytes 36868
  1.9 21.6 %collective-permute-start = (bf16[128,3072]{1,0:T(8,128)(2,1)S(1)}, bf16[128,3072]{1,0:T(8,128)(2,1)S(1)}, u32[]{:S(2)}, u32[]{:S(2)}) collective-permute-start(bf16[128,3072]{1,0:T(8,128)(2,1)S(1)} %broadcast_select_fusion.refs_1_), channel_id=1, source_target_pairs={{0,1},{1,0},{2,3},{3,2},{4,5},{5,4},{6,7},{7,6},{8,9},{9,8},{10,11... | collective-permute-start | bytes 2359304 | tf_op jit(solution)/shard_map/ppermute | solution.py:320
  4.9 19.0 %collective-permute-start.1 = (bf16[128,3072]{1,0:T(8,128)(2,1)S(1)}, bf16[128,3072]{1,0:T(8,128)(2,1)S(1)}, u32[]{:S(2)}, u32[]{:S(2)}) collective-permute-start(bf16[128,3072]{1,0:T(8,128)(2,1)S(1)} %broadcast_select_fusion.refs_1_), channel_id=1, source_target_pairs={{0,2},{1,3},{2,0},{3,1},{4,6},{5,7},{6,4},{7,5},{8,10},{9,11},{10,... | collective-permute-start | bytes 2359304 | tf_op jit(solution)/shard_map/ppermute | solution.py:320
  19.8 3.6 %collective-permute-start.2 = (f32[128,2]{0,1:T(2,128)S(1)}, f32[128,2]{0,1:T(2,128)S(1)}, u32[]{:S(2)}, u32[]{:S(2)}) collective-permute-start(f32[128,2]{0,1:T(2,128)S(1)} %pad_maximum_fusion), channel_id=1, source_target_pairs={{0,1},{1,0},{2,3},{3,2},{4,5},{5,4},{6,7},{7,6},{8,9},{9,8},{10,11... | collective-permute-start | bytes 3080 | tf_op jit(solution)/shard_map/ppermute | solution.py:320
  23.9 20.9 %collective-permute-start.5 = (bf16[128,3072]{1,0:T(8,128)(2,1)S(1)}, bf16[128,3072]{1,0:T(8,128)(2,1)S(1)}, u32[]{:S(2)}, u32[]{:S(2)}) collective-permute-start(bf16[128,3072]{1,0:T(8,128)(2,1)S(1)} %collective-permute-done.refs_0_), channel_id=1, source_target_pairs={{0,2},{1,3},{2,0},{3,1},{4,6},{5,7},{6,4},{7,5},{8,10},{9,11},{10,... | collective-permute-start | bytes 2359304 | tf_op jit(solution)/shard_map/ppermute | solution.py:320
  33.5 1.8 collective-permute-start.3
  33.6 11.2 %collective-permute-start.4 = (f32[256,2]{1,0:T(8,128)S(1)}, f32[256,2]{1,0:T(8,128)S(1)}, u32[]{:S(2)}, u32[]{:S(2)}) collective-permute-start(f32[256,2]{1,0:T(8,128)S(1)} %copy.12.scale_ref), channel_id=1, source_target_pairs={{0,2},{1,3},{2,0},{3,1},{4,6},{5,7},{6,4},{7,5},{8,10},{9,11},{10,... | collective-permute-start | bytes 6152 | tf_op jit(solution)/shard_map/ppermute | solution.py:320
  35.6 22.8 %collective-permute-start.7 = (bf16[512,768]{1,0:T(8,128)(2,1)S(1)}, bf16[512,768]{1,0:T(8,128)(2,1)S(1)}, u32[]{:S(2)}, u32[]{:S(2)}) collective-permute-start(bf16[512,768]{1,0:T(8,128)(2,1)S(1)} %stacked.8.refs_0_), channel_id=1, source_target_pairs={{0,4},{12,8},{1,5},{13,9},{2,6},{14,10},{3,7},{15,11},{16,20},{28,... | collective-permute-start | bytes 2359304 | tf_op jit(solution)/shard_map/ppermute | solution.py:391
  52.7 1.8 collective-permute-start.6
  54.8 30.2 %collective-permute-start.9 = (bf16[512,768]{1,0:T(8,128)(2,1)S(1)}, bf16[512,768]{1,0:T(8,128)(2,1)S(1)}, u32[]{:S(2)}, u32[]{:S(2)}) collective-permute-start(bf16[512,768]{1,0:T(8,128)(2,1)S(1)} %stacked.9.refs_0_), channel_id=1, source_target_pairs={{0,4},{12,8},{1,5},{13,9},{2,6},{14,10},{3,7},{15,11},{16,20},{28,... | collective-permute-start | bytes 2359304 | tf_op jit(solution)/shard_map/ppermute | solution.py:391
  68.1 1.8 collective-permute-start.8
  68.2 18.0 %collective-permute-start.10 = (bf16[512,768]{1,0:T(8,128)(2,1)S(1)}, bf16[512,768]{1,0:T(8,128)(2,1)S(1)}, u32[]{:S(2)}, u32[]{:S(2)}) collective-permute-start(bf16[512,768]{1,0:T(8,128)(2,1)S(1)} %added.8.refs_1_), channel_id=1, source_target_pairs={{4,8},{8,4},{5,9},{9,5},{6,10},{10,6},{7,11},{11,7},{20,24},{24,20... | collective-permute-start | bytes 2359304 | tf_op jit(solution)/shard_map/ppermute | solution.py:396
  81.0 23.7 %collective-permute-start.12 = (bf16[512,768]{1,0:T(8,128)(2,1)S(1)}, bf16[512,768]{1,0:T(8,128)(2,1)S(1)}, u32[]{:S(2)}, u32[]{:S(2)}) collective-permute-start(bf16[512,768]{1,0:T(8,128)(2,1)S(1)} %stacked.10.refs_0_), channel_id=1, source_target_pairs={{0,4},{12,8},{1,5},{13,9},{2,6},{14,10},{3,7},{15,11},{16,20},{28,... | collective-permute-start | bytes 2359304 | tf_op jit(solution)/shard_map/ppermute | solution.py:391
  85.4 20.4 %collective-permute-start.13 = (bf16[512,768]{1,0:T(8,128)(2,1)S(1)}, bf16[512,768]{1,0:T(8,128)(2,1)S(1)}, u32[]{:S(2)}, u32[]{:S(2)}) collective-permute-start(bf16[512,768]{1,0:T(8,128)(2,1)S(1)} %added.9.refs_1_), channel_id=1, source_target_pairs={{4,8},{8,4},{5,9},{9,5},{6,10},{10,6},{7,11},{11,7},{20,24},{24,20... | collective-permute-start | bytes 2359304 | tf_op jit(solution)/shard_map/ppermute | solution.py:396
  86.1 2.4 collective-permute-start.11
  87.3 22.7 %collective-permute-start.14 = (bf16[512,768]{1,0:T(8,128)(2,1)S(1)}, bf16[512,768]{1,0:T(8,128)(2,1)S(1)}, u32[]{:S(2)}, u32[]{:S(2)}) collective-permute-start(bf16[512,768]{1,0:T(8,128)(2,1)S(1)} %activated.8.refs_1_), channel_id=1, source_target_pairs={{4,0},{8,12},{5,1},{9,13},{6,2},{10,14},{7,3},{11,15},{20,16},{24,... | collective-permute-start | bytes 2359304 | tf_op jit(solution)/shard_map/ppermute | solution.py:402
  98.2 24.4 %collective-permute-start.16 = (bf16[512,768]{1,0:T(8,128)(2,1)S(1)}, bf16[512,768]{1,0:T(8,128)(2,1)S(1)}, u32[]{:S(2)}, u32[]{:S(2)}) collective-permute-start(bf16[512,768]{1,0:T(8,128)(2,1)S(1)} %stacked.11.refs_0_), channel_id=1, source_target_pairs={{0,4},{12,8},{1,5},{13,9},{2,6},{14,10},{3,7},{15,11},{16,20},{28,... | collective-permute-start | bytes 2359304 | tf_op jit(solution)/shard_map/ppermute | solution.py:391
  105.1 18.6 %collective-permute-start.17 = (bf16[512,768]{1,0:T(8,128)(2,1)S(1)}, bf16[512,768]{1,0:T(8,128)(2,1)S(1)}, u32[]{:S(2)}, u32[]{:S(2)}) collective-permute-start(bf16[512,768]{1,0:T(8,128)(2,1)S(1)} %added.10.refs_1_), channel_id=1, source_target_pairs={{4,8},{8,4},{5,9},{9,5},{6,10},{10,6},{7,11},{11,7},{20,24},{24,20... | collective-permute-start | bytes 2359304 | tf_op jit(solution)/shard_map/ppermute | solution.py:396
  106.9 20.4 %collective-permute-start.18 = (bf16[512,768]{1,0:T(8,128)(2,1)S(1)}, bf16[512,768]{1,0:T(8,128)(2,1)S(1)}, u32[]{:S(2)}, u32[]{:S(2)}) collective-permute-start(bf16[512,768]{1,0:T(8,128)(2,1)S(1)} %activated.9.refs_1_), channel_id=1, source_target_pairs={{4,0},{8,12},{5,1},{9,13},{6,2},{10,14},{7,3},{11,15},{20,16},{24,... | collective-permute-start | bytes 2359304 | tf_op jit(solution)/shard_map/ppermute | solution.py:402
  108.2 2.2 collective-permute-start.15
  110.0 17.6 %collective-permute-start.19 = (bf16[256,768]{1,0:T(8,128)(2,1)S(1)}, bf16[256,768]{1,0:T(8,128)(2,1)S(1)}, u32[]{:S(2)}, u32[]{:S(2)}) collective-permute-start(bf16[256,768]{1,0:T(8,128)(2,1)S(1)} %get-tuple-element.225), channel_id=1, source_target_pairs={{0,16},{16,0},{1,17},{17,1},{2,18},{18,2},{3,19},{19,3},{4,20},{20... | collective-permute-start | bytes 1179656 | tf_op jit(solution)/shard_map/ppermute | solution.py:324
  110.6 32.6 %collective-permute-start.22 = (bf16[512,768]{1,0:T(8,128)(2,1)S(1)}, bf16[512,768]{1,0:T(8,128)(2,1)S(1)}, u32[]{:S(2)}, u32[]{:S(2)}) collective-permute-start(bf16[512,768]{1,0:T(8,128)(2,1)S(1)} %stacked.12.refs_0_), channel_id=1, source_target_pairs={{0,4},{12,8},{1,5},{13,9},{2,6},{14,10},{3,7},{15,11},{16,20},{28,... | collective-permute-start | bytes 2359304 | tf_op jit(solution)/shard_map/ppermute | solution.py:391
  123.0 21.4 %collective-permute-start.23 = (bf16[512,768]{1,0:T(8,128)(2,1)S(1)}, bf16[512,768]{1,0:T(8,128)(2,1)S(1)}, u32[]{:S(2)}, u32[]{:S(2)}) collective-permute-start(bf16[512,768]{1,0:T(8,128)(2,1)S(1)} %added.11.refs_1_), channel_id=1, source_target_pairs={{4,8},{8,4},{5,9},{9,5},{6,10},{10,6},{7,11},{11,7},{20,24},{24,20... | collective-permute-start | bytes 2359304 | tf_op jit(solution)/shard_map/ppermute | solution.py:396
  124.8 22.0 %collective-permute-start.24 = (bf16[512,768]{1,0:T(8,128)(2,1)S(1)}, bf16[512,768]{1,0:T(8,128)(2,1)S(1)}, u32[]{:S(2)}, u32[]{:S(2)}) collective-permute-start(bf16[512,768]{1,0:T(8,128)(2,1)S(1)} %activated.10.refs_1_), channel_id=1, source_target_pairs={{4,0},{8,12},{5,1},{9,13},{6,2},{10,14},{7,3},{11,15},{20,16},{24,... | collective-permute-start | bytes 2359304 | tf_op jit(solution)/shard_map/ppermute | solution.py:402
  127.2 1.7 collective-permute-start.21
  127.6 7.7 %collective-permute-start.20 = (bf16[256,768]{1,0:T(8,128)(2,1)S(1)}, bf16[256,768]{1,0:T(8,128)(2,1)S(1)}, u32[]{:S(2)}, u32[]{:S(2)}) collective-permute-start(bf16[256,768]{1,0:T(8,128)(2,1)S(1)} %get-tuple-element.228), channel_id=1, source_target_pairs={{0,16},{16,0},{1,17},{17,1},{2,18},{18,2},{3,19},{19,3},{4,20},{20... | collective-permute-start | bytes 1179656 | tf_op jit(solution)/shard_map/ppermute | solution.py:324
  128.9 36.6 %collective-permute-start.27 = (bf16[512,768]{1,0:T(8,128)(2,1)S(1)}, bf16[512,768]{1,0:T(8,128)(2,1)S(1)}, u32[]{:S(2)}, u32[]{:S(2)}) collective-permute-start(bf16[512,768]{1,0:T(8,128)(2,1)S(1)} %stacked.13.refs_0_), channel_id=1, source_target_pairs={{0,4},{12,8},{1,5},{13,9},{2,6},{14,10},{3,7},{15,11},{16,20},{28,... | collective-permute-start | bytes 2359304 | tf_op jit(solution)/shard_map/ppermute | solution.py:391
  143.6 23.1 %collective-permute-start.28 = (bf16[512,768]{1,0:T(8,128)(2,1)S(1)}, bf16[512,768]{1,0:T(8,128)(2,1)S(1)}, u32[]{:S(2)}, u32[]{:S(2)}) collective-permute-start(bf16[512,768]{1,0:T(8,128)(2,1)S(1)} %added.12.refs_1_), channel_id=1, source_target_pairs={{4,8},{8,4},{5,9},{9,5},{6,10},{10,6},{7,11},{11,7},{20,24},{24,20... | collective-permute-start | bytes 2359304 | tf_op jit(solution)/shard_map/ppermute | solution.py:396
  144.3 3.3 %collective-permute-start.25 = (bf16[256,768]{1,0:T(8,128)(2,1)S(1)}, bf16[256,768]{1,0:T(8,128)(2,1)S(1)}, u32[]{:S(2)}, u32[]{:S(2)}) collective-permute-start(bf16[256,768]{1,0:T(8,128)(2,1)S(1)} %get-tuple-element.241), channel_id=1, source_target_pairs={{0,16},{16,0},{1,17},{17,1},{2,18},{18,2},{3,19},{19,3},{4,20},{20... | collective-permute-start | bytes 1179656 | tf_op jit(solution)/shard_map/ppermute | solution.py:324
  145.4 23.7 %collective-permute-start.29 = (bf16[512,768]{1,0:T(8,128)(2,1)S(1)}, bf16[512,768]{1,0:T(8,128)(2,1)S(1)}, u32[]{:S(2)}, u32[]{:S(2)}) collective-permute-start(bf16[512,768]{1,0:T(8,128)(2,1)S(1)} %activated.11.refs_1_), channel_id=1, source_target_pairs={{4,0},{8,12},{5,1},{9,13},{6,2},{10,14},{7,3},{11,15},{20,16},{24,... | collective-permute-start | bytes 2359304 | tf_op jit(solution)/shard_map/ppermute | solution.py:402
  147.1 5.2 %collective-permute-start.26 = (bf16[256,768]{1,0:T(8,128)(2,1)S(1)}, bf16[256,768]{1,0:T(8,128)(2,1)S(1)}, u32[]{:S(2)}, u32[]{:S(2)}) collective-permute-start(bf16[256,768]{1,0:T(8,128)(2,1)S(1)} %get-tuple-element.243), channel_id=1, source_target_pairs={{0,16},{16,0},{1,17},{17,1},{2,18},{18,2},{3,19},{19,3},{4,20},{20... | collective-permute-start | bytes 1179656 | tf_op jit(solution)/shard_map/ppermute | solution.py:324
  147.9 33.9 %collective-permute-start.32 = (bf16[512,768]{1,0:T(8,128)(2,1)S(1)}, bf16[512,768]{1,0:T(8,128)(2,1)S(1)}, u32[]{:S(2)}, u32[]{:S(2)}) collective-permute-start(bf16[512,768]{1,0:T(8,128)(2,1)S(1)} %stacked.14.refs_0_), channel_id=1, source_target_pairs={{0,4},{12,8},{1,5},{13,9},{2,6},{14,10},{3,7},{15,11},{16,20},{28,... | collective-permute-start | bytes 2359304 | tf_op jit(solution)/shard_map/ppermute | solution.py:391
  165.9 16.9 %collective-permute-start.33 = (bf16[512,768]{1,0:T(8,128)(2,1)S(1)}, bf16[512,768]{1,0:T(8,128)(2,1)S(1)}, u32[]{:S(2)}, u32[]{:S(2)}) collective-permute-start(bf16[512,768]{1,0:T(8,128)(2,1)S(1)} %added.13.refs_1_), channel_id=1, source_target_pairs={{4,8},{8,4},{5,9},{9,5},{6,10},{10,6},{7,11},{11,7},{20,24},{24,20... | collective-permute-start | bytes 2359304 | tf_op jit(solution)/shard_map/ppermute | solution.py:396
  167.7 21.4 %collective-permute-start.34 = (bf16[512,768]{1,0:T(8,128)(2,1)S(1)}, bf16[512,768]{1,0:T(8,128)(2,1)S(1)}, u32[]{:S(2)}, u32[]{:S(2)}) collective-permute-start(bf16[512,768]{1,0:T(8,128)(2,1)S(1)} %activated.12.refs_1_), channel_id=1, source_target_pairs={{4,0},{8,12},{5,1},{9,13},{6,2},{10,14},{7,3},{11,15},{20,16},{24,... | collective-permute-start | bytes 2359304 | tf_op jit(solution)/shard_map/ppermute | solution.py:402
  169.0 1.8 collective-permute-start.30
  169.4 6.2 %collective-permute-start.31 = (bf16[256,768]{1,0:T(8,128)(2,1)S(1)}, bf16[256,768]{1,0:T(8,128)(2,1)S(1)}, u32[]{:S(2)}, u32[]{:S(2)}) collective-permute-start(bf16[256,768]{1,0:T(8,128)(2,1)S(1)} %get-tuple-element.259), channel_id=1, source_target_pairs={{0,16},{16,0},{1,17},{17,1},{2,18},{18,2},{3,19},{19,3},{4,20},{20... | collective-permute-start | bytes 1179656 | tf_op jit(solution)/shard_map/ppermute | solution.py:324
  171.0 27.2 %collective-permute-start.36 = (bf16[512,768]{1,0:T(8,128)(2,1)S(1)}, bf16[512,768]{1,0:T(8,128)(2,1)S(1)}, u32[]{:S(2)}, u32[]{:S(2)}) collective-permute-start(bf16[512,768]{1,0:T(8,128)(2,1)S(1)} %stacked.15.refs_0_), channel_id=1, source_target_pairs={{0,4},{12,8},{1,5},{13,9},{2,6},{14,10},{3,7},{15,11},{16,20},{28,... | collective-permute-start | bytes 2359304 | tf_op jit(solution)/shard_map/ppermute | solution.py:391
  182.2 17.2 %collective-permute-start.37 = (bf16[512,768]{1,0:T(8,128)(2,1)S(1)}, bf16[512,768]{1,0:T(8,128)(2,1)S(1)}, u32[]{:S(2)}, u32[]{:S(2)}) collective-permute-start(bf16[512,768]{1,0:T(8,128)(2,1)S(1)} %added.14.refs_1_), channel_id=1, source_target_pairs={{4,8},{8,4},{5,9},{9,5},{6,10},{10,6},{7,11},{11,7},{20,24},{24,20... | collective-permute-start | bytes 2359304 | tf_op jit(solution)/shard_map/ppermute | solution.py:396
  183.9 22.5 %collective-permute-start.38 = (bf16[512,768]{1,0:T(8,128)(2,1)S(1)}, bf16[512,768]{1,0:T(8,128)(2,1)S(1)}, u32[]{:S(2)}, u32[]{:S(2)}) collective-permute-start(bf16[512,768]{1,0:T(8,128)(2,1)S(1)} %activated.13.refs_1_), channel_id=1, source_target_pairs={{4,0},{8,12},{5,1},{9,13},{6,2},{10,14},{7,3},{11,15},{20,16},{24,... | collective-permute-start | bytes 2359304 | tf_op jit(solution)/shard_map/ppermute | solution.py:402
  189.4 1.8 collective-permute-start.35
  197.4 24.4 %collective-permute-start.40 = (bf16[128,3072]{1,0:T(8,128)(2,1)S(1)}, bf16[128,3072]{1,0:T(8,128)(2,1)S(1)}, u32[]{:S(2)}, u32[]{:S(2)}) collective-permute-start(bf16[128,3072]{1,0:T(8,128)(2,1)S(1)} %get-tuple-element.272), channel_id=1, source_target_pairs={{0,2},{1,3},{2,0},{3,1},{4,6},{5,7},{6,4},{7,5},{8,10},{9,11},{10,... | collective-permute-start | bytes 2359304 | tf_op jit(solution)/shard_map/ppermute | solution.py:320
  198.6 23.1 %collective-permute-start.41 = (bf16[512,768]{1,0:T(8,128)(2,1)S(1)}, bf16[512,768]{1,0:T(8,128)(2,1)S(1)}, u32[]{:S(2)}, u32[]{:S(2)}) collective-permute-start(bf16[512,768]{1,0:T(8,128)(2,1)S(1)} %added.15.refs_1_), channel_id=1, source_target_pairs={{4,8},{8,4},{5,9},{9,5},{6,10},{10,6},{7,11},{11,7},{20,24},{24,20... | collective-permute-start | bytes 2359304 | tf_op jit(solution)/shard_map/ppermute | solution.py:396
  206.8 1.8 collective-permute-start.39
  206.8 22.2 %collective-permute-start.42 = (bf16[512,768]{1,0:T(8,128)(2,1)S(1)}, bf16[512,768]{1,0:T(8,128)(2,1)S(1)}, u32[]{:S(2)}, u32[]{:S(2)}) collective-permute-start(bf16[512,768]{1,0:T(8,128)(2,1)S(1)} %activated.14.refs_1_), channel_id=1, source_target_pairs={{4,0},{8,12},{5,1},{9,13},{6,2},{10,14},{7,3},{11,15},{20,16},{24,... | collective-permute-start | bytes 2359304 | tf_op jit(solution)/shard_map/ppermute | solution.py:402
  222.8 22.7 %collective-permute-start.44 = (bf16[512,768]{1,0:T(8,128)(2,1)S(1)}, bf16[512,768]{1,0:T(8,128)(2,1)S(1)}, u32[]{:S(2)}, u32[]{:S(2)}) collective-permute-start(bf16[512,768]{1,0:T(8,128)(2,1)S(1)} %activated.15.refs_1_), channel_id=1, source_target_pairs={{4,0},{8,12},{5,1},{9,13},{6,2},{10,14},{7,3},{11,15},{20,16},{24,... | collective-permute-start | bytes 2359304 | tf_op jit(solution)/shard_map/ppermute | solution.py:402
  229.4 1.8 collective-permute-start.43
  229.5 20.0 %collective-permute-start.46 = (bf16[128,3072]{1,0:T(8,128)(2,1)S(1)}, bf16[128,3072]{1,0:T(8,128)(2,1)S(1)}, u32[]{:S(2)}, u32[]{:S(2)}) collective-permute-start(bf16[128,3072]{1,0:T(8,128)(2,1)S(1)} %get-tuple-element.273), channel_id=1, source_target_pairs={{0,2},{1,3},{2,0},{3,1},{4,6},{5,7},{6,4},{7,5},{8,10},{9,11},{10,... | collective-permute-start | bytes 2359304 | tf_op jit(solution)/shard_map/ppermute | solution.py:320
  245.8 3.6 %collective-permute-start.45 = (bf16[256,768]{1,0:T(8,128)(2,1)S(1)}, bf16[256,768]{1,0:T(8,128)(2,1)S(1)}, u32[]{:S(2)}, u32[]{:S(2)}) collective-permute-start(bf16[256,768]{1,0:T(8,128)(2,1)S(1)} %get-tuple-element.298), channel_id=1, source_target_pairs={{0,16},{16,0},{1,17},{17,1},{2,18},{18,2},{3,19},{19,3},{4,20},{20... | collective-permute-start | bytes 1179656 | tf_op jit(solution)/shard_map/ppermute | solution.py:324
  255.7 19.2 %collective-permute-start.47 = (bf16[128,3072]{1,0:T(8,128)(2,1)S(1)}, bf16[128,3072]{1,0:T(8,128)(2,1)S(1)}, u32[]{:S(2)}, u32[]{:S(2)}) collective-permute-start(bf16[128,3072]{1,0:T(8,128)(2,1)S(1)} %get-tuple-element.305), channel_id=1, source_target_pairs={{0,1},{1,0},{2,3},{3,2},{4,5},{5,4},{6,7},{7,6},{8,9},{9,8},{10,11... | collective-permute-start | bytes 2359304 | tf_op jit(solution)/shard_map/ppermute | solution.py:320

commit v6 on v5

--- a/solution.py
+++ b/solution.py
@@ -82,34 +82,38 @@
     count, width = rows.shape[0] // 2 * pieces, rows.shape[1]
     at = groups[0]
     columns = weight.shape[1] // parts
-    tile = tile_of(columns // 2, 384)
-    steps = columns // tile
-    mine = steps // 2
+    tile = columns // 2
+    narrow = tile_of(tile, 256)
+    copies = tile // narrow
     piece = count // pieces
 
-    def kernel(section_ref, rows_ref, weight_ref, *results):
-        product = dot_f32(rows_ref[...], weight_ref[...], (1, 0)).astype(jnp.bfloat16)
-
-        def store(refs):
-            for i, result in enumerate(refs):
-                result[...] = product[i * piece : (i + 1) * piece]
-
-        pl.when(pl.program_id(0) < mine)(lambda: store(results[:pieces]))
-        pl.when(pl.program_id(0) >= mine)(lambda: store(results[pieces:]))
-
-    column = lambda i, s: (0, part * steps + lax.rem(i + s[0] * mine, steps))
+    def kernel(section_ref, rows_ref, *refs):
+        results = refs[copies:]
+        for k in range(copies):
+            own = slice(k * narrow, (k + 1) * narrow)
+            product = dot_f32(rows_ref[...], refs[k][...], (1, 0)).astype(jnp.bfloat16)
+
+            def store(refs):
+                for i, result in enumerate(refs):
+                    result[:, own] = product[i * piece : (i + 1) * piece]
+
+            pl.when(pl.program_id(0) == 0)(lambda: store(results[:pieces]))
+            pl.when(pl.program_id(0) == 1)(lambda: store(results[pieces:]))
+
+    def column(k):
+        return lambda i, s: (0, (2 * part + lax.rem(i + s[0], 2)) * copies + k)
+
     return call(
         kernel,
         "up_product",
-        (steps,),
+        (2,),
         [section],
-        [rows, weight],
+        [rows] + [weight] * copies,
         [
             fixed((count, width), (at, 0)),
-            pl.BlockSpec((width, tile), column),
+            *[pl.BlockSpec((width, narrow), column(k)) for k in range(copies)],
         ],
-        [pl.BlockSpec((piece, tile), lambda i, s: (0, jnp.minimum(i, mine - 1)))] * pieces
-        + [pl.BlockSpec((piece, tile), lambda i, s: (0, jnp.maximum(i - mine, 0)))] * pieces,
+        [fixed((piece, tile), (0, 0))] * (2 * pieces),
         [jax.ShapeDtypeStruct((piece, columns // 2), jnp.bfloat16)] * (2 * pieces),
     )
 
@@ -190,14 +194,16 @@
     count, half = sum(counts), kept[0].shape[1]
     width = weight.shape[0]
     tile = tile_of(width, 1024)
+    copies = 2 if tile % 256 == 0 else 1
+    short = tile // copies
     n = len(kept)
     extra = [] if before is None else [before]
 
     def kernel(section_ref, *refs):
-        weight_ref = refs[2 * n]
-        added = refs[2 * n + 1 : 2 * n + 1 + len(extra)]
-        others = refs[2 * n + 1 + len(extra) : 2 * n + 1 + len(extra) + len(arrived)]
-        results = refs[2 * n + 1 + len(extra) + len(arrived) : -1]
+        weight_refs = refs[2 * n : 2 * n + copies]
+        added = refs[2 * n + copies : 2 * n + copies + len(extra)]
+        others = refs[2 * n + copies + len(extra) : 2 * n + copies + len(extra) + len(arrived)]
+        results = refs[2 * n + copies + len(extra) + len(arrived) : -1]
         held = refs[-1]
 
         @pl.when(pl.program_id(0) == 0)
@@ -210,21 +216,21 @@
                 held[theirs, at : at + rows] = refs[n + i][...].T
                 at += rows
 
-        for at in range(0, count, 256):
-            own = slice(at, at + 256)
-            product = dot_f32(weight_ref[...], held[:, own], (1, 0))
+        for k, at in [(k, at) for k in range(copies) for at in range(0, count, 256)]:
+            there, own = slice(k * short, (k + 1) * short), slice(at, at + 256)
+            product = dot_f32(weight_refs[k][...], held[:, own], (1, 0))
             for ref in added:
-                product = product + ref[:, own]
+                product = product + ref[there, own]
             if kinds:
                 product = product.T
                 piece = count // len(kinds)
                 for i, result in enumerate(results):
                     value = product[i * piece : (i + 1) * piece]
                     if arrived:
-                        value = value + others[i][...].astype(jnp.float32)
-                    result[...] = value.astype(result.dtype)
+                        value = value + others[i][:, there].astype(jnp.float32)
+                    result[:, there] = value.astype(result.dtype)
             else:
-                results[0][:, own] = product
+                results[0][there, own] = product
 
     whole = [fixed((rows, half), (0, 0)) for rows in counts]
     if kinds:
@@ -239,10 +245,10 @@
         "down_product",
         (width // tile,),
         [section],
-        [*kept, *came, weight, *extra, *arrived],
+        [*kept, *came, *[weight] * copies, *extra, *arrived],
         whole
         + whole
-        + [pl.BlockSpec((tile, 2 * half), lambda i, s: (i, part))]
+        + [pl.BlockSpec((short, 2 * half), lambda i, s, k=k: (copies * i + k, part)) for k in range(copies)]
         + [pl.BlockSpec((tile, count), lambda i, s: (i, group))] * len(extra)
         + [pl.BlockSpec((count // max(len(kinds), 1), tile), lambda i, s: (0, i))] * len(arrived),
         out_specs,
@@ -413,15 +419,15 @@
         return kept, [chunks[part, g]["came"] for g in groups]
 
     both = (FAR, NEAR)
-    order = [(0, NEAR)] + [(part, FAR) for part in range(parts)] + [(part, NEAR) for part in range(1, parts)]
+    order = [(part, g) for part in (0, 1) for g in (NEAR, FAR)]
+    order += [(part, g) for g in (FAR, NEAR) for part in range(2, parts)]
     count = len(order)
-    multiplied = {0}
     held = {"gradient": None}
 
     def need(c):
-        if c < count and order[c][0] not in multiplied:
-            multiplied.add(order[c][0])
-            multiply(x_all, order[c][0], both)
+        if c < count and order[c] not in chunks:
+            part, group = order[c]
+            multiply(x_all, part, [group] if part < 2 else both)
 
     def tick(t):
         if 0 <= t - 1 < count:
@@ -449,34 +455,36 @@
     x_near = prepare(near, near_scale, NEAR, None)
     multiply(x_near, 0, [NEAR])
     stack(chunks[order[0]])
+    multiply(x_near, 1, [NEAR])
     x_all = prepare(far, far_scale, FAR, x_near)
     multiply(x_all, 0, [FAR])
+    inward(chunks[order[0]])
     stack(chunks[order[1]])
     for t in range(count + 2):
-        if 0 <= t < count:
+        if 0 < t < count:
             inward(chunks[order[t]])
-        if t == 0:
-            need(2)
         tick(t)
-        if t == 0:
+        need(t + 3)
+        far_part, near_part = t - 4, t - 2 - parts
+        if t == 3:
             turned = run(transposed, x_all)["value"]
-        need(t + 3)
-        far_part, near_part = t - 3, t - 2 - parts
-        if far_part == 0:
-            near_sum = far_sum = go_down(0, both, None, 0)
-        elif 0 < far_part < parts - 1:
-            far_sum = go_down(far_part, [FAR], far_sum, FAR if far_part == 1 else 0)
-            if far_part == 1:
-                go_gradient(0)
+            near_sum = go_down(0, both, None, 0)
+        elif t == 4:
+            go_gradient(0)
+        elif t == 5:
+            near_sum = far_sum = go_down(1, both, near_sum, 0)
+        if 2 <= far_part < parts - 1:
+            far_sum = go_down(far_part, [FAR], far_sum, FAR if far_part == 2 else 0)
         elif far_part == parts - 1:
-            sent_far = go_down(far_part, [FAR], far_sum, FAR if far_part == 1 else 0, [jnp.bfloat16] * 2)
+            sent_far = go_down(far_part, [FAR], far_sum, FAR if far_part == 2 else 0, [jnp.bfloat16] * 2)
             arrived = [from_peer(value, across) for value in sent_far["value"]]
-        elif 0 < near_part < parts - 1:
+        if t == 6:
+            go_gradient(1)
+        if 2 <= near_part < parts - 1:
             go_gradient(near_part)
-            near_sum = go_down(near_part, [NEAR], near_sum, NEAR if near_part == 1 else 0)
-            if near_part == 1:
-                near_sum["value"], arrived[0] = lax.optimization_barrier((near_sum["value"], arrived[0]))
-    column = NEAR if parts == 2 else 0
+            near_sum = go_down(near_part, [NEAR], near_sum, NEAR if near_part == 2 else 0)
+            near_sum["value"], arrived[0] = lax.optimization_barrier((near_sum["value"], arrived[0]))
+    column = NEAR if parts == 3 else 0
     sent_near = go_down(parts - 1, [NEAR], near_sum, column, [jnp.bfloat16, jnp.float32], arrived)
     go_gradient(parts - 1)
 

time: 277 us -> 279 us (level)
  Pallas kernels: 135 us -> 143 us
  starting transfers between devices: 65.4 us -> 59.9 us
    pallas_call x51, Pallas kernels: 135 us -> 143 us  [call(): pl.pallas_call(kernel, grid_spec=pltpu.PrefetchScalarGridSpec(num_scalar_...]
    ppermute x8, starting transfers between devices: 37.1 us -> 32.2 us  [inward(): lax.ppermute(value, 'dp', [(hop, hop + 1), (line - 1 - hop, line - 2 - ho...]
    ppermute x8, waiting for transfers between devices: 18.7 us -> 21.7 us  [outward(): lax.ppermute(value, 'dp', [(hop + 1, hop), (line - 2 - hop, line - 1 - ho...]
  transfers between devices with their start and end apart: 48 -> 48, of which waited for: 20 -> 20; matrix products, arithmetic and copies ran while one was open for 1% -> 1% of each run, Pallas kernels for 47% -> 49%
where the time goes in v6:
time: 279 us; the launch traced here: 278 us
  Pallas kernels  143 us (51%)
  starting transfers between devices  59.9 us (21%)
  waiting for transfers between devices  58 us (21%)
  blocking collectives  12 us (4%)
  other arithmetic  3.71 us (1%)
    pallas_call x51, Pallas kernels, call(): pl.pallas_call(kernel, grid_spec=pltpu.PrefetchScalarGridSpec(num_scalar_...  143 us
    ppermute x8, starting transfers between devices, inward(): lax.ppermute(value, 'dp', [(hop, hop + 1), (line - 1 - hop, line - 2 - ho...  32.2 us
    ppermute x8, waiting for transfers between devices, from_peer(): return lax.ppermute(value, 'mp', [(i, i ^ by) for i in range(peers)])  22.2 us
    ppermute x8, waiting for transfers between devices, outward(): lax.ppermute(value, 'dp', [(hop + 1, hop), (line - 2 - hop, line - 1 - ho...  21.7 us
    psum x1, blocking collectives, local(): lax.psum((jnp.sum(values, 1), jnp.sum(values * values, 1)), 'dp')  12 us
    ppermute x8, starting transfers between devices, outward(): lax.ppermute(value, 'dp', [(hop + 1, hop), (line - 2 - hop, line - 1 - ho...  10.8 us
    ppermute x8, starting transfers between devices, from_peer(): return lax.ppermute(value, 'mp', [(i, i ^ by) for i in range(peers)])  8.98 us
    ppermute x16, waiting for transfers between devices, across_sections(): return lax.ppermute(value, 'section', [(0, 1), (1, 0)])  8.76 us
  transfers between devices with their start and end apart: 48, of which 20 were waited for; matrix products, arithmetic and copies ran while one was open for 1% of the time, Pallas kernels for 49%

profile of v6, /device:TPU:0, one launch (start us, length us, event | category | flops | bytes accessed | tf_op | source)
XLA Modules:
  0.0 278.1 jit_solution(15837902080703901411)
XLA Ops:
  0.7 1.2 broadcast_select_fusion.refs_1_
  1.9 3.0 %collective-permute-start = (bf16[128,3072]{1,0:T(8,128)(2,1)S(1)}, bf16[128,3072]{1,0:T(8,128)(2,1)S(1)}, u32[]{:S(2)}, u32[]{:S(2)}) collective-permute-start(bf16[128,3072]{1,0:T(8,128)(2,1)S(1)} %broadcast_select_fusion.refs_1_), channel_id=1, source_target_pairs={{0,1},{1,0},{2,3},{3,2},{4,5},{5,4},{6,7},{7,6},{8,9},{9,8},{10,11... | collective-permute-start | bytes 2359304 | tf_op jit(solution)/shard_map/ppermute | solution.py:326
  4.9 1.5 collective-permute-start.1
  6.4 1.4 convert_reduce_fusion
  7.8 12.0 %all-reduce = (f32[128]{0:T(128)S(1)}, f32[128]{0:T(128)S(1)}) all-reduce(f32[128]{0:T(128)S(1)} %get-tuple-element.314, f32[128]{0:T(128)S(1)} %get-tuple-element.313), channel_id=1, replica_groups=mesh['section'=2,'dp'=4,'mp'=4] {'dp'}, use_global_device_ids=true, to_apply=%region_3.4 | all-reduce | flops 256 | bytes 2048 | tf_op jit(solution)/shard_map/psum | solution.py:368
  20.4 3.0 %collective-permute-done.2 = f32[128,2]{0,1:T(2,128)S(1)} collective-permute-done((f32[128,2]{0,1:T(2,128)S(1)}, f32[128,2]{0,1:T(2,128)S(1)}, u32[]{:S(2)}, u32[]{:S(2)}) %collective-permute-start.2) | collective-permute-done | bytes 1056 | tf_op jit(solution)/shard_map/ppermute | solution.py:326
  24.0 1.6 collective-permute-start.5
  25.6 1.2 normalize.2.rows_ref.refs_2_
  26.8 7.6 %up_product.6 = (bf16[256,768]{1,0:T(8,128)(2,1)S(1)}, bf16[256,768]{1,0:T(8,128)(2,1)S(1)}) custom-call(s32[1]{0:T(128)} %bitcast.section_ref, bf16[512,3072]{1,0:T(8,128)(2,1)S(1)} %normalize.2.rows_ref.refs_2_, bf16[3072,6144]{1,0:T(8,128)(2,1)} %bitcast.15, bf16[3072,6144]{1,0:T(8,128)(2,1)} %bitcast.16, bf16[3072,6144]{1,0:T(8,128)(2,1)} %bitcast.17), custom_call_target="tpu_custom_call" | custom-call | tf_op jit(solution)/shard_map/up_product/pallas_call | solution.py:32
  34.5 1.7 collective-permute-done.3.refs_1_
  36.4 3.5 %collective-permute-start.6 = (bf16[512,768]{1,0:T(8,128)(2,1)S(1)}, bf16[512,768]{1,0:T(8,128)(2,1)S(1)}, u32[]{:S(2)}, u32[]{:S(2)}) collective-permute-start(bf16[512,768]{1,0:T(8,128)(2,1)S(1)} %stacked.8.refs_0_), channel_id=1, source_target_pairs={{0,4},{12,8},{1,5},{13,9},{2,6},{14,10},{3,7},{15,11},{16,20},{28,... | collective-permute-start | bytes 2359304 | tf_op jit(solution)/shard_map/ppermute | solution.py:397
  40.5 7.5 %up_product.7 = (bf16[256,768]{1,0:T(8,128)(2,1)S(1)}, bf16[256,768]{1,0:T(8,128)(2,1)S(1)}) custom-call(s32[1]{0:T(128)} %bitcast.section_ref, bf16[512,3072]{1,0:T(8,128)(2,1)S(1)} %normalize.2.rows_ref.refs_2_, bf16[3072,6144]{1,0:T(8,128)(2,1)} %bitcast.18, bf16[3072,6144]{1,0:T(8,128)(2,1)} %bitcast.19, bf16[3072,6144]{1,0:T(8,128)(2,1)} %bitcast.20), custom_call_target="tpu_custom_call" | custom-call | tf_op jit(solution)/shard_map/up_product/pallas_call | solution.py:32
  48.1 1.2 normalize.3.rows_ref.value_ref
  49.3 7.6 %up_product.8 = (bf16[256,768]{1,0:T(8,128)(2,1)S(1)}, bf16[256,768]{1,0:T(8,128)(2,1)S(1)}) custom-call(s32[1]{0:T(128)} %bitcast.section_ref, bf16[512,3072]{1,0:T(8,128)(2,1)S(1)} %normalize.3.rows_ref.value_ref, bf16[3072,6144]{1,0:T(8,128)(2,1)} %bitcast.21, bf16[3072,6144]{1,0:T(8,128)(2,1)} %bitcast.22, bf16[3072,6144]{1,0:T(8,128)(2,1)} %bitcast.23), custom_call_target="tpu_custom_call" | custom-call | tf_op jit(solution)/shard_map/up_product/pallas_call | solution.py:32
  57.4 1.3 collective-permute-done.7.refs_1_
  58.9 3.2 %collective-permute-start.9 = (bf16[512,768]{1,0:T(8,128)(2,1)S(1)}, bf16[512,768]{1,0:T(8,128)(2,1)S(1)}, u32[]{:S(2)}, u32[]{:S(2)}) collective-permute-start(bf16[512,768]{1,0:T(8,128)(2,1)S(1)} %stacked.9.refs_0_), channel_id=1, source_target_pairs={{0,4},{12,8},{1,5},{13,9},{2,6},{14,10},{3,7},{15,11},{16,20},{28,... | collective-permute-start | bytes 2359304 | tf_op jit(solution)/shard_map/ppermute | solution.py:397
  64.1 7.6 %up_product.9 = (bf16[256,768]{1,0:T(8,128)(2,1)S(1)}, bf16[256,768]{1,0:T(8,128)(2,1)S(1)}) custom-call(s32[1]{0:T(128)} %bitcast.section_ref, bf16[512,3072]{1,0:T(8,128)(2,1)S(1)} %normalize.3.rows_ref.value_ref, bf16[3072,6144]{1,0:T(8,128)(2,1)} %bitcast.24, bf16[3072,6144]{1,0:T(8,128)(2,1)} %bitcast.25, bf16[3072,6144]{1,0:T(8,128)(2,1)} %bitcast.26), custom_call_target="tpu_custom_call" | custom-call | tf_op jit(solution)/shard_map/up_product/pallas_call | solution.py:32
  71.7 3.1 %collective-permute-start.12 = (bf16[512,768]{1,0:T(8,128)(2,1)S(1)}, bf16[512,768]{1,0:T(8,128)(2,1)S(1)}, u32[]{:S(2)}, u32[]{:S(2)}) collective-permute-start(bf16[512,768]{1,0:T(8,128)(2,1)S(1)} %stacked.10.refs_0_), channel_id=1, source_target_pairs={{0,4},{12,8},{1,5},{13,9},{2,6},{14,10},{3,7},{15,11},{16,20},{28,... | collective-permute-start | bytes 2359304 | tf_op jit(solution)/shard_map/ppermute | solution.py:397
  74.8 5.2 %collective-permute-done.9.refs_1_ = bf16[512,768]{1,0:T(8,128)(2,1)S(1)} collective-permute-done((bf16[512,768]{1,0:T(8,128)(2,1)S(1)}, bf16[512,768]{1,0:T(8,128)(2,1)S(1)}, u32[]{:S(2)}, u32[]{:S(2)}) %collective-permute-start.9) | collective-permute-done | bytes 786464 | tf_op jit(solution)/shard_map/ppermute | solution.py:397
  81.3 1.0 activated.8.refs_1_
  82.3 1.3 collective-permute-start.14
  83.9 7.4 %collective-permute-start.16 = (bf16[512,768]{1,0:T(8,128)(2,1)S(1)}, bf16[512,768]{1,0:T(8,128)(2,1)S(1)}, u32[]{:S(2)}, u32[]{:S(2)}) collective-permute-start(bf16[512,768]{1,0:T(8,128)(2,1)S(1)} %stacked.11.refs_0_), channel_id=1, source_target_pairs={{0,4},{12,8},{1,5},{13,9},{2,6},{14,10},{3,7},{15,11},{16,20},{28,... | collective-permute-start | bytes 2359304 | tf_op jit(solution)/shard_map/ppermute | solution.py:397
  91.3 11.6 %up_product.10 = (bf16[256,768]{1,0:T(8,128)(2,1)S(1)}, bf16[256,768]{1,0:T(8,128)(2,1)S(1)}, bf16[256,768]{1,0:T(8,128)(2,1)S(1)}, bf16[256,768]{1,0:T(8,128)(2,1)S(1)}) custom-call(s32[1]{0:T(128)} %bitcast.section_ref, bf16[512,3072]{1,0:T(8,128)(2,1)S(1)} %normalize.3.rows_ref.value_ref, bf16[3072,6144]{1,0:T(8,128)(2,1)} %bitcast.29, ...), custom_call_target="tpu_custom_call" | custom-call | tf_op jit(solution)/shard_map/up_product/pallas_call | solution.py:32
  104.1 1.0 activated.9.refs_1_
  105.2 1.3 collective-permute-start.18
  108.5 4.6 %collective-permute-start.22 = (bf16[512,768]{1,0:T(8,128)(2,1)S(1)}, bf16[512,768]{1,0:T(8,128)(2,1)S(1)}, u32[]{:S(2)}, u32[]{:S(2)}) collective-permute-start(bf16[512,768]{1,0:T(8,128)(2,1)S(1)} %stacked.12.refs_0_), channel_id=1, source_target_pairs={{0,4},{12,8},{1,5},{13,9},{2,6},{14,10},{3,7},{15,11},{16,20},{28,... | collective-permute-start | bytes 2359304 | tf_op jit(solution)/shard_map/ppermute | solution.py:397
  113.1 11.6 %up_product.11 = (bf16[256,768]{1,0:T(8,128)(2,1)S(1)}, bf16[256,768]{1,0:T(8,128)(2,1)S(1)}, bf16[256,768]{1,0:T(8,128)(2,1)S(1)}, bf16[256,768]{1,0:T(8,128)(2,1)S(1)}) custom-call(s32[1]{0:T(128)} %bitcast.section_ref, bf16[512,3072]{1,0:T(8,128)(2,1)S(1)} %normalize.3.rows_ref.value_ref, bf16[3072,6144]{1,0:T(8,128)(2,1)} %bitcast.30, ...), custom_call_target="tpu_custom_call" | custom-call | tf_op jit(solution)/shard_map/up_product/pallas_call | solution.py:32
  126.0 1.0 activated.10.refs_1_
  128.0 1.3 collective-permute-start.24
  129.6 1.4 transposed.1.turned_ref
  131.0 4.6 %collective-permute-start.26 = (bf16[512,768]{1,0:T(8,128)(2,1)S(1)}, bf16[512,768]{1,0:T(8,128)(2,1)S(1)}, u32[]{:S(2)}, u32[]{:S(2)}) collective-permute-start(bf16[512,768]{1,0:T(8,128)(2,1)S(1)} %stacked.13.refs_0_), channel_id=1, source_target_pairs={{0,4},{12,8},{1,5},{13,9},{2,6},{14,10},{3,7},{15,11},{16,20},{28,... | collective-permute-start | bytes 2359304 | tf_op jit(solution)/shard_map/ppermute | solution.py:397
  135.7 7.9 %down_product.6.refs_6_ = f32[3072,512]{1,0:T(8,128)S(1)} custom-call(s32[1]{0:T(128)} %bitcast.section_ref, bf16[256,768]{1,0:T(8,128)(2,1)S(1)} %get-tuple-element.247.refs_0_, bf16[256,768]{1,0:T(8,128)(2,1)S(1)} %get-tuple-element.233.refs_1_, bf16[256,768]{1,0:T(8,128)(2,1)S(1)} %collective-permute-done.20.refs_2_, ...), custom_call_target="tpu_custom_call" | custom-call | tf_op jit(solution)/shard_map/down_product/pallas_call | solution.py:32
  144.7 1.0 activated.11.refs_1_
  145.7 1.3 collective-permute-start.28
  147.1 2.7 collective-permute-done.24.refs_2_
  150.4 7.2 %weight_gradient.4.refs_4_ = bf16[3072,6144]{1,0:T(8,128)(2,1)} custom-call(s32[1]{0:T(128)} %bitcast.section_ref, bf16[3072,512]{1,0:T(8,128)(2,1)S(1)} %transposed.1.turned_ref, bf16[256,768]{1,0:T(8,128)(2,1)S(1)} %get-tuple-element.247.refs_0_, bf16[256,768]{1,0:T(8,128)(2,1)S(1)} %get-tuple-element.233.refs_1_, ...), custom_call_target="tpu_custom_call" | custom-call | tf_op jit(solution)/shard_map/weight_gradient/pallas_call | solution.py:32
  157.7 3.3 %collective-permute-start.32 = (bf16[512,768]{1,0:T(8,128)(2,1)S(1)}, bf16[512,768]{1,0:T(8,128)(2,1)S(1)}, u32[]{:S(2)}, u32[]{:S(2)}) collective-permute-start(bf16[512,768]{1,0:T(8,128)(2,1)S(1)} %stacked.14.refs_0_), channel_id=1, source_target_pairs={{0,4},{12,8},{1,5},{13,9},{2,6},{14,10},{3,7},{15,11},{16,20},{28,... | collective-permute-start | bytes 2359304 | tf_op jit(solution)/shard_map/ppermute | solution.py:397
  162.1 1.0 activated.12.refs_1_
  163.1 1.5 collective-permute-start.34
  164.6 2.3 collective-permute-done.28.refs_2_
  168.7 2.5 collective-permute-start.36
  171.2 7.9 %down_product.7.refs_4_ = f32[3072,512]{1,0:T(8,128)S(1)} custom-call(s32[1]{0:T(128)} %bitcast.section_ref, bf16[256,768]{1,0:T(8,128)(2,1)S(1)} %get-tuple-element.275.refs_0_, bf16[256,768]{1,0:T(8,128)(2,1)S(1)} %get-tuple-element.261.refs_1_, bf16[256,768]{1,0:T(8,128)(2,1)S(1)} %collective-permute-done.30.refs_2_, ...), custom_call_target="tpu_custom_call" | custom-call | tf_op jit(solution)/shard_map/down_product/pallas_call | solution.py:32
  179.5 1.0 activated.13.refs_1_
  181.3 3.1 %collective-permute-done.34.refs_2_ = bf16[512,768]{1,0:T(8,128)(2,1)S(1)} collective-permute-done((bf16[512,768]{1,0:T(8,128)(2,1)S(1)}, bf16[512,768]{1,0:T(8,128)(2,1)S(1)}, u32[]{:S(2)}, u32[]{:S(2)}) %collective-permute-start.34) | collective-permute-done | bytes 786464 | tf_op jit(solution)/shard_map/ppermute | solution.py:408
  184.8 1.3 collective-permute-start.38
  186.5 6.0 %down_product.8.refs_4_ = f32[3072,256]{1,0:T(8,128)S(1)} custom-call(s32[1]{0:T(128)} %bitcast.section_ref, bf16[256,768]{1,0:T(8,128)(2,1)S(1)} %get-tuple-element.296.refs_0_, bf16[256,768]{1,0:T(8,128)(2,1)S(1)} %collective-permute-done.35.refs_1_.refs_2_, bf16[3072,6144]{1,0:T(8,128)(2,1)} %bitcast.37, bf16[3072,6144]{1,0:T(8,128)(2,1)} %bitcast.38, ...), custom_call_target="tpu_custom_call" | custom-call | tf_op jit(solution)/shard_map/down_product/pallas_call | solution.py:32
  192.6 7.2 %weight_gradient.5.refs_4_ = bf16[3072,6144]{1,0:T(8,128)(2,1)} custom-call(s32[1]{0:T(128)} %bitcast.section_ref, bf16[3072,512]{1,0:T(8,128)(2,1)S(1)} %transposed.1.turned_ref, bf16[256,768]{1,0:T(8,128)(2,1)S(1)} %get-tuple-element.275.refs_0_, bf16[256,768]{1,0:T(8,128)(2,1)S(1)} %get-tuple-element.261.refs_1_, ...), custom_call_target="tpu_custom_call", output_to_operand_aliasing={{}: (6, {})} | custom-call | tf_op jit(solution)/shard_map/weight_gradient/pallas_call | solution.py:32
  201.0 1.0 activated.14.refs_1_
  202.0 1.3 collective-permute-start.41
  203.3 3.4 %collective-permute-done.38.refs_2_ = bf16[512,768]{1,0:T(8,128)(2,1)S(1)} collective-permute-done((bf16[512,768]{1,0:T(8,128)(2,1)S(1)}, bf16[512,768]{1,0:T(8,128)(2,1)S(1)}, u32[]{:S(2)}, u32[]{:S(2)}) %collective-permute-start.38) | collective-permute-done | bytes 786464 | tf_op jit(solution)/shard_map/ppermute | solution.py:408
  207.1 1.7 collective-permute-done.39.refs_1_.refs_2_
  208.8 6.3 %down_product.9 = (bf16[128,3072]{1,0:T(8,128)(2,1)S(1)}, bf16[128,3072]{1,0:T(8,128)(2,1)S(1)}) custom-call(s32[1]{0:T(128)} %bitcast.section_ref, bf16[256,768]{1,0:T(8,128)(2,1)S(1)} %get-tuple-element.310.refs_0_, bf16[256,768]{1,0:T(8,128)(2,1)S(1)} %collective-permute-done.39.refs_1_.refs_2_, bf16[3072,6144]{1,0:T(8,128)(2,1)} %bitcast.39, ...), custom_call_target="tpu_custom_call" | custom-call | tf_op jit(solution)/shard_map/down_product/pallas_call | solution.py:32
  215.7 1.0 activated.15.refs_1_
  216.7 1.6 collective-permute-start.44
  218.2 6.6 %collective-permute-done.41.refs_2_ = bf16[512,768]{1,0:T(8,128)(2,1)S(1)} collective-permute-done((bf16[512,768]{1,0:T(8,128)(2,1)S(1)}, bf16[512,768]{1,0:T(8,128)(2,1)S(1)}, u32[]{:S(2)}, u32[]{:S(2)}) %collective-permute-start.41) | collective-permute-done | bytes 786464 | tf_op jit(solution)/shard_map/ppermute | solution.py:408
  225.8 1.2 collective-permute-done.42.refs_3_.refs_1_
  227.0 7.2 %weight_gradient.6.refs_4_ = bf16[3072,6144]{1,0:T(8,128)(2,1)} custom-call(s32[1]{0:T(128)} %bitcast.section_ref, bf16[3072,512]{1,0:T(8,128)(2,1)S(1)} %transposed.1.turned_ref, bf16[256,768]{1,0:T(8,128)(2,1)S(1)} %get-tuple-element.296.refs_0_, bf16[256,768]{1,0:T(8,128)(2,1)S(1)} %get-tuple-element.298.refs_1_.refs_0_, ...), custom_call_target="tpu_custom_call", output_to_operand_aliasing={{}: (6, {})} | custom-call | tf_op jit(solution)/shard_map/weight_gradient/pallas_call | solution.py:32
  234.2 6.0 %down_product.10.refs_4_ = f32[3072,256]{1,0:T(8,128)S(1)} custom-call(s32[1]{0:T(128)} %bitcast.section_ref, bf16[256,768]{1,0:T(8,128)(2,1)S(1)} %get-tuple-element.298.refs_1_.refs_0_, bf16[256,768]{1,0:T(8,128)(2,1)S(1)} %collective-permute-done.42.refs_3_.refs_1_, bf16[3072,6144]{1,0:T(8,128)(2,1)} %bitcast.41, bf16[3072,6144]{1,0:T(8,128)(2,1)} %bitcast.42, ...), custom_call_target="tpu_custom_call" | custom-call | tf_op jit(solution)/shard_map/down_product/pallas_call | solution.py:32
  240.2 3.2 %collective-permute-done.44.refs_2_ = bf16[512,768]{1,0:T(8,128)(2,1)S(1)} collective-permute-done((bf16[512,768]{1,0:T(8,128)(2,1)S(1)}, bf16[512,768]{1,0:T(8,128)(2,1)S(1)}, u32[]{:S(2)}, u32[]{:S(2)}) %collective-permute-start.44) | collective-permute-done | bytes 786464 | tf_op jit(solution)/shard_map/ppermute | solution.py:408
  243.9 7.7 %collective-permute-done.46.refs_6_ = bf16[128,3072]{1,0:T(8,128)(2,1)S(1)} collective-permute-done((bf16[128,3072]{1,0:T(8,128)(2,1)S(1)}, bf16[128,3072]{1,0:T(8,128)(2,1)S(1)}, u32[]{:S(2)}, u32[]{:S(2)}) %collective-permute-start.46) | collective-permute-done | bytes 786464 | tf_op jit(solution)/shard_map/ppermute | solution.py:326
  251.6 6.6 %down_product.11 = (bf16[128,3072]{1,0:T(8,128)(2,1)S(1)}, f32[128,3072]{1,0:T(8,128)S(1)}) custom-call(s32[1]{0:T(128)} %bitcast.section_ref, bf16[256,768]{1,0:T(8,128)(2,1)S(1)} %get-tuple-element.311.refs_0_.refs_1_, bf16[256,768]{1,0:T(8,128)(2,1)S(1)} %collective-permute-done.45.refs_1_.refs_3_, bf16[3072,6144]{1,0:T(8,128)(2,1)} %bitcast.43, ...), custom_call_target="tpu_custom_call" | custom-call | tf_op jit(solution)/shard_map/down_product/pallas_call | solution.py:32
  258.8 7.2 %weight_gradient.7 = bf16[3072,6144]{1,0:T(8,128)(2,1)} custom-call(s32[1]{0:T(128)} %bitcast.section_ref, bf16[3072,512]{1,0:T(8,128)(2,1)S(1)} %transposed.1.turned_ref, bf16[256,768]{1,0:T(8,128)(2,1)S(1)} %get-tuple-element.310.refs_0_, bf16[256,768]{1,0:T(8,128)(2,1)S(1)} %get-tuple-element.311.refs_0_.refs_1_, ...), custom_call_target="tpu_custom_call", output_to_operand_aliasing={{}: (6, {})} | custom-call | tf_op jit(solution)/shard_map/weight_gradient/pallas_call | solution.py:32
  266.0 11.0 %collective-permute-done.47 = bf16[128,3072]{1,0:T(8,128)(2,1)S(1)} collective-permute-done((bf16[128,3072]{1,0:T(8,128)(2,1)S(1)}, bf16[128,3072]{1,0:T(8,128)(2,1)S(1)}, u32[]{:S(2)}, u32[]{:S(2)}) %collective-permute-start.47) | collective-permute-done | bytes 786464 | tf_op jit(solution)/shard_map/ppermute | solution.py:326
  277.0 1.0 fusion.1
  (93 shorter events, 22.3 us)
Async XLA Ops:
  0.6 25.0 %copy-start = (f32[3072]{0:T(1024)S(1)}, f32[3072]{0:T(1024)}, u32[]{:S(2)}) copy-start(f32[3072]{0:T(1024)} %param.6) | copy-start | bytes 36868
  1.9 21.6 %collective-permute-start = (bf16[128,3072]{1,0:T(8,128)(2,1)S(1)}, bf16[128,3072]{1,0:T(8,128)(2,1)S(1)}, u32[]{:S(2)}, u32[]{:S(2)}) collective-permute-start(bf16[128,3072]{1,0:T(8,128)(2,1)S(1)} %broadcast_select_fusion.refs_1_), channel_id=1, source_target_pairs={{0,1},{1,0},{2,3},{3,2},{4,5},{5,4},{6,7},{7,6},{8,9},{9,8},{10,11... | collective-permute-start | bytes 2359304 | tf_op jit(solution)/shard_map/ppermute | solution.py:326
  4.9 19.0 %collective-permute-start.1 = (bf16[128,3072]{1,0:T(8,128)(2,1)S(1)}, bf16[128,3072]{1,0:T(8,128)(2,1)S(1)}, u32[]{:S(2)}, u32[]{:S(2)}) collective-permute-start(bf16[128,3072]{1,0:T(8,128)(2,1)S(1)} %broadcast_select_fusion.refs_1_), channel_id=1, source_target_pairs={{0,2},{1,3},{2,0},{3,1},{4,6},{5,7},{6,4},{7,5},{8,10},{9,11},{10,... | collective-permute-start | bytes 2359304 | tf_op jit(solution)/shard_map/ppermute | solution.py:326
  19.8 3.6 %collective-permute-start.2 = (f32[128,2]{0,1:T(2,128)S(1)}, f32[128,2]{0,1:T(2,128)S(1)}, u32[]{:S(2)}, u32[]{:S(2)}) collective-permute-start(f32[128,2]{0,1:T(2,128)S(1)} %pad_maximum_fusion), channel_id=1, source_target_pairs={{0,1},{1,0},{2,3},{3,2},{4,5},{5,4},{6,7},{7,6},{8,9},{9,8},{10,11... | collective-permute-start | bytes 3080 | tf_op jit(solution)/shard_map/ppermute | solution.py:326
  24.0 24.1 %collective-permute-start.5 = (bf16[128,3072]{1,0:T(8,128)(2,1)S(1)}, bf16[128,3072]{1,0:T(8,128)(2,1)S(1)}, u32[]{:S(2)}, u32[]{:S(2)}) collective-permute-start(bf16[128,3072]{1,0:T(8,128)(2,1)S(1)} %collective-permute-done.refs_0_), channel_id=1, source_target_pairs={{0,2},{1,3},{2,0},{3,1},{4,6},{5,7},{6,4},{7,5},{8,10},{9,11},{10,... | collective-permute-start | bytes 2359304 | tf_op jit(solution)/shard_map/ppermute | solution.py:326
  34.4 1.8 collective-permute-start.3
  36.4 20.6 %collective-permute-start.6 = (bf16[512,768]{1,0:T(8,128)(2,1)S(1)}, bf16[512,768]{1,0:T(8,128)(2,1)S(1)}, u32[]{:S(2)}, u32[]{:S(2)}) collective-permute-start(bf16[512,768]{1,0:T(8,128)(2,1)S(1)} %stacked.8.refs_0_), channel_id=1, source_target_pairs={{0,4},{12,8},{1,5},{13,9},{2,6},{14,10},{3,7},{15,11},{16,20},{28,... | collective-permute-start | bytes 2359304 | tf_op jit(solution)/shard_map/ppermute | solution.py:397
  40.0 8.1 %collective-permute-start.4 = (f32[256,2]{1,0:T(8,128)S(1)}, f32[256,2]{1,0:T(8,128)S(1)}, u32[]{:S(2)}, u32[]{:S(2)}) collective-permute-start(f32[256,2]{1,0:T(8,128)S(1)} %copy.12.scale_ref), channel_id=1, source_target_pairs={{0,2},{1,3},{2,0},{3,1},{4,6},{5,7},{6,4},{7,5},{8,10},{9,11},{10,... | collective-permute-start | bytes 6152 | tf_op jit(solution)/shard_map/ppermute | solution.py:326
  56.9 1.8 collective-permute-start.7
  58.9 21.1 %collective-permute-start.9 = (bf16[512,768]{1,0:T(8,128)(2,1)S(1)}, bf16[512,768]{1,0:T(8,128)(2,1)S(1)}, u32[]{:S(2)}, u32[]{:S(2)}) collective-permute-start(bf16[512,768]{1,0:T(8,128)(2,1)S(1)} %stacked.9.refs_0_), channel_id=1, source_target_pairs={{0,4},{12,8},{1,5},{13,9},{2,6},{14,10},{3,7},{15,11},{16,20},{28,... | collective-permute-start | bytes 2359304 | tf_op jit(solution)/shard_map/ppermute | solution.py:397
  62.1 1.8 collective-permute-start.8
  62.2 19.1 %collective-permute-start.10 = (bf16[512,768]{1,0:T(8,128)(2,1)S(1)}, bf16[512,768]{1,0:T(8,128)(2,1)S(1)}, u32[]{:S(2)}, u32[]{:S(2)}) collective-permute-start(bf16[512,768]{1,0:T(8,128)(2,1)S(1)} %added.8.refs_1_), channel_id=1, source_target_pairs={{4,8},{8,4},{5,9},{9,5},{6,10},{10,6},{7,11},{11,7},{20,24},{24,20... | collective-permute-start | bytes 2359304 | tf_op jit(solution)/shard_map/ppermute | solution.py:402
  71.7 31.2 %collective-permute-start.12 = (bf16[512,768]{1,0:T(8,128)(2,1)S(1)}, bf16[512,768]{1,0:T(8,128)(2,1)S(1)}, u32[]{:S(2)}, u32[]{:S(2)}) collective-permute-start(bf16[512,768]{1,0:T(8,128)(2,1)S(1)} %stacked.10.refs_0_), channel_id=1, source_target_pairs={{0,4},{12,8},{1,5},{13,9},{2,6},{14,10},{3,7},{15,11},{16,20},{28,... | collective-permute-start | bytes 2359304 | tf_op jit(solution)/shard_map/ppermute | solution.py:397
  80.5 23.7 %collective-permute-start.13 = (bf16[512,768]{1,0:T(8,128)(2,1)S(1)}, bf16[512,768]{1,0:T(8,128)(2,1)S(1)}, u32[]{:S(2)}, u32[]{:S(2)}) collective-permute-start(bf16[512,768]{1,0:T(8,128)(2,1)S(1)} %added.9.refs_1_), channel_id=1, source_target_pairs={{4,8},{8,4},{5,9},{9,5},{6,10},{10,6},{7,11},{11,7},{20,24},{24,20... | collective-permute-start | bytes 2359304 | tf_op jit(solution)/shard_map/ppermute | solution.py:402
  81.2 2.4 collective-permute-start.11
  82.3 24.7 %collective-permute-start.14 = (bf16[512,768]{1,0:T(8,128)(2,1)S(1)}, bf16[512,768]{1,0:T(8,128)(2,1)S(1)}, u32[]{:S(2)}, u32[]{:S(2)}) collective-permute-start(bf16[512,768]{1,0:T(8,128)(2,1)S(1)} %activated.8.refs_1_), channel_id=1, source_target_pairs={{4,0},{8,12},{5,1},{9,13},{6,2},{10,14},{7,3},{11,15},{20,16},{24,... | collective-permute-start | bytes 2359304 | tf_op jit(solution)/shard_map/ppermute | solution.py:408
  83.9 40.9 %collective-permute-start.16 = (bf16[512,768]{1,0:T(8,128)(2,1)S(1)}, bf16[512,768]{1,0:T(8,128)(2,1)S(1)}, u32[]{:S(2)}, u32[]{:S(2)}) collective-permute-start(bf16[512,768]{1,0:T(8,128)(2,1)S(1)} %stacked.11.refs_0_), channel_id=1, source_target_pairs={{0,4},{12,8},{1,5},{13,9},{2,6},{14,10},{3,7},{15,11},{16,20},{28,... | collective-permute-start | bytes 2359304 | tf_op jit(solution)/shard_map/ppermute | solution.py:397
  103.4 22.6 %collective-permute-start.17 = (bf16[512,768]{1,0:T(8,128)(2,1)S(1)}, bf16[512,768]{1,0:T(8,128)(2,1)S(1)}, u32[]{:S(2)}, u32[]{:S(2)}) collective-permute-start(bf16[512,768]{1,0:T(8,128)(2,1)S(1)} %added.10.refs_1_), channel_id=1, source_target_pairs={{4,8},{8,4},{5,9},{9,5},{6,10},{10,6},{7,11},{11,7},{20,24},{24,20... | collective-permute-start | bytes 2359304 | tf_op jit(solution)/shard_map/ppermute | solution.py:402
  105.2 22.4 %collective-permute-start.18 = (bf16[512,768]{1,0:T(8,128)(2,1)S(1)}, bf16[512,768]{1,0:T(8,128)(2,1)S(1)}, u32[]{:S(2)}, u32[]{:S(2)}) collective-permute-start(bf16[512,768]{1,0:T(8,128)(2,1)S(1)} %activated.9.refs_1_), channel_id=1, source_target_pairs={{4,0},{8,12},{5,1},{9,13},{6,2},{10,14},{7,3},{11,15},{20,16},{24,... | collective-permute-start | bytes 2359304 | tf_op jit(solution)/shard_map/ppermute | solution.py:408
  106.5 1.8 collective-permute-start.15
  108.5 35.1 %collective-permute-start.22 = (bf16[512,768]{1,0:T(8,128)(2,1)S(1)}, bf16[512,768]{1,0:T(8,128)(2,1)S(1)}, u32[]{:S(2)}, u32[]{:S(2)}) collective-permute-start(bf16[512,768]{1,0:T(8,128)(2,1)S(1)} %stacked.12.refs_0_), channel_id=1, source_target_pairs={{0,4},{12,8},{1,5},{13,9},{2,6},{14,10},{3,7},{15,11},{16,20},{28,... | collective-permute-start | bytes 2359304 | tf_op jit(solution)/shard_map/ppermute | solution.py:397
  125.2 19.5 %collective-permute-start.23 = (bf16[512,768]{1,0:T(8,128)(2,1)S(1)}, bf16[512,768]{1,0:T(8,128)(2,1)S(1)}, u32[]{:S(2)}, u32[]{:S(2)}) collective-permute-start(bf16[512,768]{1,0:T(8,128)(2,1)S(1)} %added.11.refs_1_), channel_id=1, source_target_pairs={{4,8},{8,4},{5,9},{9,5},{6,10},{10,6},{7,11},{11,7},{20,24},{24,20... | collective-permute-start | bytes 2359304 | tf_op jit(solution)/shard_map/ppermute | solution.py:402
  125.9 2.1 collective-permute-start.19
  127.1 3.9 %collective-permute-start.21 = (bf16[256,768]{1,0:T(8,128)(2,1)S(1)}, bf16[256,768]{1,0:T(8,128)(2,1)S(1)}, u32[]{:S(2)}, u32[]{:S(2)}) collective-permute-start(bf16[256,768]{1,0:T(8,128)(2,1)S(1)} %get-tuple-element.235), channel_id=1, source_target_pairs={{0,16},{16,0},{1,17},{17,1},{2,18},{18,2},{3,19},{19,3},{4,20},{20... | collective-permute-start | bytes 1179656 | tf_op jit(solution)/shard_map/ppermute | solution.py:330
  127.9 7.7 %collective-permute-start.20 = (bf16[256,768]{1,0:T(8,128)(2,1)S(1)}, bf16[256,768]{1,0:T(8,128)(2,1)S(1)}, u32[]{:S(2)}, u32[]{:S(2)}) collective-permute-start(bf16[256,768]{1,0:T(8,128)(2,1)S(1)} %get-tuple-element.234), channel_id=1, source_target_pairs={{0,16},{16,0},{1,17},{17,1},{2,18},{18,2},{3,19},{19,3},{4,20},{20... | collective-permute-start | bytes 1179656 | tf_op jit(solution)/shard_map/ppermute | solution.py:330
  128.0 21.8 %collective-permute-start.24 = (bf16[512,768]{1,0:T(8,128)(2,1)S(1)}, bf16[512,768]{1,0:T(8,128)(2,1)S(1)}, u32[]{:S(2)}, u32[]{:S(2)}) collective-permute-start(bf16[512,768]{1,0:T(8,128)(2,1)S(1)} %activated.10.refs_1_), channel_id=1, source_target_pairs={{4,0},{8,12},{5,1},{9,13},{6,2},{10,14},{7,3},{11,15},{20,16},{24,... | collective-permute-start | bytes 2359304 | tf_op jit(solution)/shard_map/ppermute | solution.py:408
  131.0 29.9 %collective-permute-start.26 = (bf16[512,768]{1,0:T(8,128)(2,1)S(1)}, bf16[512,768]{1,0:T(8,128)(2,1)S(1)}, u32[]{:S(2)}, u32[]{:S(2)}) collective-permute-start(bf16[512,768]{1,0:T(8,128)(2,1)S(1)} %stacked.13.refs_0_), channel_id=1, source_target_pairs={{0,4},{12,8},{1,5},{13,9},{2,6},{14,10},{3,7},{15,11},{16,20},{28,... | collective-permute-start | bytes 2359304 | tf_op jit(solution)/shard_map/ppermute | solution.py:397
  144.0 18.1 %collective-permute-start.27 = (bf16[512,768]{1,0:T(8,128)(2,1)S(1)}, bf16[512,768]{1,0:T(8,128)(2,1)S(1)}, u32[]{:S(2)}, u32[]{:S(2)}) collective-permute-start(bf16[512,768]{1,0:T(8,128)(2,1)S(1)} %added.12.refs_1_), channel_id=1, source_target_pairs={{4,8},{8,4},{5,9},{9,5},{6,10},{10,6},{7,11},{11,7},{20,24},{24,20... | collective-permute-start | bytes 2359304 | tf_op jit(solution)/shard_map/ppermute | solution.py:402
  145.7 21.3 %collective-permute-start.28 = (bf16[512,768]{1,0:T(8,128)(2,1)S(1)}, bf16[512,768]{1,0:T(8,128)(2,1)S(1)}, u32[]{:S(2)}, u32[]{:S(2)}) collective-permute-start(bf16[512,768]{1,0:T(8,128)(2,1)S(1)} %activated.11.refs_1_), channel_id=1, source_target_pairs={{4,0},{8,12},{5,1},{9,13},{6,2},{10,14},{7,3},{11,15},{20,16},{24,... | collective-permute-start | bytes 2359304 | tf_op jit(solution)/shard_map/ppermute | solution.py:408
  147.0 3.1 %collective-permute-start.25 = (bf16[256,768]{1,0:T(8,128)(2,1)S(1)}, bf16[256,768]{1,0:T(8,128)(2,1)S(1)}, u32[]{:S(2)}, u32[]{:S(2)}) collective-permute-start(bf16[256,768]{1,0:T(8,128)(2,1)S(1)} %get-tuple-element.246), channel_id=1, source_target_pairs={{0,16},{16,0},{1,17},{17,1},{2,18},{18,2},{3,19},{19,3},{4,20},{20... | collective-permute-start | bytes 1179656 | tf_op jit(solution)/shard_map/ppermute | solution.py:330
  149.8 17.5 %collective-permute-start.29 = (bf16[256,768]{1,0:T(8,128)(2,1)S(1)}, bf16[256,768]{1,0:T(8,128)(2,1)S(1)}, u32[]{:S(2)}, u32[]{:S(2)}) collective-permute-start(bf16[256,768]{1,0:T(8,128)(2,1)S(1)} %get-tuple-element.259), channel_id=1, source_target_pairs={{0,16},{16,0},{1,17},{17,1},{2,18},{18,2},{3,19},{19,3},{4,20},{20... | collective-permute-start | bytes 1179656 | tf_op jit(solution)/shard_map/ppermute | solution.py:330
  157.7 21.4 %collective-permute-start.32 = (bf16[512,768]{1,0:T(8,128)(2,1)S(1)}, bf16[512,768]{1,0:T(8,128)(2,1)S(1)}, u32[]{:S(2)}, u32[]{:S(2)}) collective-permute-start(bf16[512,768]{1,0:T(8,128)(2,1)S(1)} %stacked.14.refs_0_), channel_id=1, source_target_pairs={{0,4},{12,8},{1,5},{13,9},{2,6},{14,10},{3,7},{15,11},{16,20},{28,... | collective-permute-start | bytes 2359304 | tf_op jit(solution)/shard_map/ppermute | solution.py:397
  161.4 18.2 %collective-permute-start.33 = (bf16[512,768]{1,0:T(8,128)(2,1)S(1)}, bf16[512,768]{1,0:T(8,128)(2,1)S(1)}, u32[]{:S(2)}, u32[]{:S(2)}) collective-permute-start(bf16[512,768]{1,0:T(8,128)(2,1)S(1)} %added.13.refs_1_), channel_id=1, source_target_pairs={{4,8},{8,4},{5,9},{9,5},{6,10},{10,6},{7,11},{11,7},{20,24},{24,20... | collective-permute-start | bytes 2359304 | tf_op jit(solution)/shard_map/ppermute | solution.py:402
  163.1 21.3 %collective-permute-start.34 = (bf16[512,768]{1,0:T(8,128)(2,1)S(1)}, bf16[512,768]{1,0:T(8,128)(2,1)S(1)}, u32[]{:S(2)}, u32[]{:S(2)}) collective-permute-start(bf16[512,768]{1,0:T(8,128)(2,1)S(1)} %activated.12.refs_1_), channel_id=1, source_target_pairs={{4,0},{8,12},{5,1},{9,13},{6,2},{10,14},{7,3},{11,15},{20,16},{24,... | collective-permute-start | bytes 2359304 | tf_op jit(solution)/shard_map/ppermute | solution.py:408
  167.0 1.7 collective-permute-start.31
  167.3 3.9 %collective-permute-start.30 = (bf16[256,768]{1,0:T(8,128)(2,1)S(1)}, bf16[256,768]{1,0:T(8,128)(2,1)S(1)}, u32[]{:S(2)}, u32[]{:S(2)}) collective-permute-start(bf16[256,768]{1,0:T(8,128)(2,1)S(1)} %get-tuple-element.262), channel_id=1, source_target_pairs={{0,16},{16,0},{1,17},{17,1},{2,18},{18,2},{3,19},{19,3},{4,20},{20... | collective-permute-start | bytes 1179656 | tf_op jit(solution)/shard_map/ppermute | solution.py:330
  168.7 31.1 %collective-permute-start.36 = (bf16[512,768]{1,0:T(8,128)(2,1)S(1)}, bf16[512,768]{1,0:T(8,128)(2,1)S(1)}, u32[]{:S(2)}, u32[]{:S(2)}) collective-permute-start(bf16[512,768]{1,0:T(8,128)(2,1)S(1)} %stacked.15.refs_0_), channel_id=1, source_target_pairs={{0,4},{12,8},{1,5},{13,9},{2,6},{14,10},{3,7},{15,11},{16,20},{28,... | collective-permute-start | bytes 2359304 | tf_op jit(solution)/shard_map/ppermute | solution.py:397
  180.6 20.4 %collective-permute-start.37 = (bf16[512,768]{1,0:T(8,128)(2,1)S(1)}, bf16[512,768]{1,0:T(8,128)(2,1)S(1)}, u32[]{:S(2)}, u32[]{:S(2)}) collective-permute-start(bf16[512,768]{1,0:T(8,128)(2,1)S(1)} %added.14.refs_1_), channel_id=1, source_target_pairs={{4,8},{8,4},{5,9},{9,5},{6,10},{10,6},{7,11},{11,7},{20,24},{24,20... | collective-permute-start | bytes 2359304 | tf_op jit(solution)/shard_map/ppermute | solution.py:402
  184.8 1.8 collective-permute-start.35
  184.8 21.8 %collective-permute-start.38 = (bf16[512,768]{1,0:T(8,128)(2,1)S(1)}, bf16[512,768]{1,0:T(8,128)(2,1)S(1)}, u32[]{:S(2)}, u32[]{:S(2)}) collective-permute-start(bf16[512,768]{1,0:T(8,128)(2,1)S(1)} %activated.13.refs_1_), channel_id=1, source_target_pairs={{4,0},{8,12},{5,1},{9,13},{6,2},{10,14},{7,3},{11,15},{20,16},{24,... | collective-permute-start | bytes 2359304 | tf_op jit(solution)/shard_map/ppermute | solution.py:408
  200.2 15.4 %collective-permute-start.40 = (bf16[512,768]{1,0:T(8,128)(2,1)S(1)}, bf16[512,768]{1,0:T(8,128)(2,1)S(1)}, u32[]{:S(2)}, u32[]{:S(2)}) collective-permute-start(bf16[512,768]{1,0:T(8,128)(2,1)S(1)} %added.15.refs_1_), channel_id=1, source_target_pairs={{4,8},{8,4},{5,9},{9,5},{6,10},{10,6},{7,11},{11,7},{20,24},{24,20... | collective-permute-start | bytes 2359304 | tf_op jit(solution)/shard_map/ppermute | solution.py:402
  202.0 22.9 %collective-permute-start.41 = (bf16[512,768]{1,0:T(8,128)(2,1)S(1)}, bf16[512,768]{1,0:T(8,128)(2,1)S(1)}, u32[]{:S(2)}, u32[]{:S(2)}) collective-permute-start(bf16[512,768]{1,0:T(8,128)(2,1)S(1)} %activated.14.refs_1_), channel_id=1, source_target_pairs={{4,0},{8,12},{5,1},{9,13},{6,2},{10,14},{7,3},{11,15},{20,16},{24,... | collective-permute-start | bytes 2359304 | tf_op jit(solution)/shard_map/ppermute | solution.py:408
  207.0 1.8 collective-permute-start.39
  215.1 25.1 %collective-permute-start.43 = (bf16[128,3072]{1,0:T(8,128)(2,1)S(1)}, bf16[128,3072]{1,0:T(8,128)(2,1)S(1)}, u32[]{:S(2)}, u32[]{:S(2)}) collective-permute-start(bf16[128,3072]{1,0:T(8,128)(2,1)S(1)} %get-tuple-element.287), channel_id=1, source_target_pairs={{0,2},{1,3},{2,0},{3,1},{4,6},{5,7},{6,4},{7,5},{8,10},{9,11},{10,... | collective-permute-start | bytes 2359304 | tf_op jit(solution)/shard_map/ppermute | solution.py:326
  216.7 26.8 %collective-permute-start.44 = (bf16[512,768]{1,0:T(8,128)(2,1)S(1)}, bf16[512,768]{1,0:T(8,128)(2,1)S(1)}, u32[]{:S(2)}, u32[]{:S(2)}) collective-permute-start(bf16[512,768]{1,0:T(8,128)(2,1)S(1)} %activated.15.refs_1_), channel_id=1, source_target_pairs={{4,0},{8,12},{5,1},{9,13},{6,2},{10,14},{7,3},{11,15},{20,16},{24,... | collective-permute-start | bytes 2359304 | tf_op jit(solution)/shard_map/ppermute | solution.py:408
  225.2 1.8 collective-permute-start.42
  225.3 26.3 %collective-permute-start.46 = (bf16[128,3072]{1,0:T(8,128)(2,1)S(1)}, bf16[128,3072]{1,0:T(8,128)(2,1)S(1)}, u32[]{:S(2)}, u32[]{:S(2)}) collective-permute-start(bf16[128,3072]{1,0:T(8,128)(2,1)S(1)} %get-tuple-element.288), channel_id=1, source_target_pairs={{0,2},{1,3},{2,0},{3,1},{4,6},{5,7},{6,4},{7,5},{8,10},{9,11},{10,... | collective-permute-start | bytes 2359304 | tf_op jit(solution)/shard_map/ppermute | solution.py:326
  243.8 7.8 %collective-permute-start.45 = (bf16[256,768]{1,0:T(8,128)(2,1)S(1)}, bf16[256,768]{1,0:T(8,128)(2,1)S(1)}, u32[]{:S(2)}, u32[]{:S(2)}) collective-permute-start(bf16[256,768]{1,0:T(8,128)(2,1)S(1)} %get-tuple-element.302), channel_id=1, source_target_pairs={{0,16},{16,0},{1,17},{17,1},{2,18},{18,2},{3,19},{19,3},{4,20},{20... | collective-permute-start | bytes 1179656 | tf_op jit(solution)/shard_map/ppermute | solution.py:330
  258.2 18.8 %collective-permute-start.47 = (bf16[128,3072]{1,0:T(8,128)(2,1)S(1)}, bf16[128,3072]{1,0:T(8,128)(2,1)S(1)}, u32[]{:S(2)}, u32[]{:S(2)}) collective-permute-start(bf16[128,3072]{1,0:T(8,128)(2,1)S(1)} %get-tuple-element.309), channel_id=1, source_target_pairs={{0,1},{1,0},{2,3},{3,2},{4,5},{5,4},{6,7},{7,6},{8,9},{9,8},{10,11... | collective-permute-start | bytes 2359304 | tf_op jit(solution)/shard_map/ppermute | solution.py:326

commit v7 on v6

--- a/solution.py
+++ b/solution.py
@@ -82,38 +82,33 @@
     count, width = rows.shape[0] // 2 * pieces, rows.shape[1]
     at = groups[0]
     columns = weight.shape[1] // parts
-    tile = columns // 2
-    narrow = tile_of(tile, 256)
-    copies = tile // narrow
+    tile = tile_of(columns // 2, 768)
+    steps = columns // tile
+    mine = steps // 2
     piece = count // pieces
 
-    def kernel(section_ref, rows_ref, *refs):
-        results = refs[copies:]
-        for k in range(copies):
-            own = slice(k * narrow, (k + 1) * narrow)
-            product = dot_f32(rows_ref[...], refs[k][...], (1, 0)).astype(jnp.bfloat16)
-
-            def store(refs):
-                for i, result in enumerate(refs):
-                    result[:, own] = product[i * piece : (i + 1) * piece]
-
-            pl.when(pl.program_id(0) == 0)(lambda: store(results[:pieces]))
-            pl.when(pl.program_id(0) == 1)(lambda: store(results[pieces:]))
-
-    def column(k):
-        return lambda i, s: (0, (2 * part + lax.rem(i + s[0], 2)) * copies + k)
+    def kernel(section_ref, rows_ref, weight_ref, *results):
+        product = dot_f32(rows_ref[...], weight_ref[...], (1, 0)).astype(jnp.bfloat16)
+
+        def store(refs):
+            for i, result in enumerate(refs):
+                result[...] = product[i * piece : (i + 1) * piece]
+
+        pl.when(pl.program_id(0) < mine)(lambda: store(results[:pieces]))
+        pl.when(pl.program_id(0) >= mine)(lambda: store(results[pieces:]))
 
     return call(
         kernel,
         "up_product",
-        (2,),
+        (steps,),
         [section],
-        [rows] + [weight] * copies,
+        [rows, weight],
         [
             fixed((count, width), (at, 0)),
-            *[pl.BlockSpec((width, narrow), column(k)) for k in range(copies)],
+            pl.BlockSpec((width, tile), lambda i, s: (0, part * steps + lax.rem(i + s[0] * mine, steps))),
         ],
-        [fixed((piece, tile), (0, 0))] * (2 * pieces),
+        [pl.BlockSpec((piece, tile), lambda i, s: (0, jnp.minimum(i, mine - 1)))] * pieces
+        + [pl.BlockSpec((piece, tile), lambda i, s: (0, jnp.maximum(i - mine, 0)))] * pieces,
         [jax.ShapeDtypeStruct((piece, columns // 2), jnp.bfloat16)] * (2 * pieces),
     )
 
@@ -194,16 +189,15 @@
     count, half = sum(counts), kept[0].shape[1]
     width = weight.shape[0]
     tile = tile_of(width, 1024)
-    copies = 2 if tile % 256 == 0 else 1
-    short = tile // copies
     n = len(kept)
     extra = [] if before is None else [before]
+    others = list(arrived)
 
     def kernel(section_ref, *refs):
-        weight_refs = refs[2 * n : 2 * n + copies]
-        added = refs[2 * n + copies : 2 * n + copies + len(extra)]
-        others = refs[2 * n + copies + len(extra) : 2 * n + copies + len(extra) + len(arrived)]
-        results = refs[2 * n + copies + len(extra) + len(arrived) : -1]
+        weight_ref = refs[2 * n]
+        added = refs[2 * n + 1 : 2 * n + 1 + len(extra)]
+        arrived_refs = refs[2 * n + 1 + len(extra) : 2 * n + 1 + len(extra) + len(others)]
+        results = refs[2 * n + 1 + len(extra) + len(others) : -1]
         held = refs[-1]
 
         @pl.when(pl.program_id(0) == 0)
@@ -216,26 +210,23 @@
                 held[theirs, at : at + rows] = refs[n + i][...].T
                 at += rows
 
-        for k, at in [(k, at) for k in range(copies) for at in range(0, count, 256)]:
-            there, own = slice(k * short, (k + 1) * short), slice(at, at + 256)
-            product = dot_f32(weight_refs[k][...], held[:, own], (1, 0))
-            for ref in added:
-                product = product + ref[there, own]
-            if kinds:
-                product = product.T
-                piece = count // len(kinds)
-                for i, result in enumerate(results):
-                    value = product[i * piece : (i + 1) * piece]
-                    if arrived:
-                        value = value + others[i][:, there].astype(jnp.float32)
-                    result[:, there] = value.astype(result.dtype)
-            else:
-                results[0][there, own] = product
+        product = dot_f32(weight_ref[...], held[...], (1, 0))
+        for ref in added:
+            product = product + ref[...]
+        if kinds:
+            product = product.T
+            piece = count // len(kinds)
+            for i, result in enumerate(results):
+                value = product[i * piece : (i + 1) * piece]
+                if others:
+                    value = value + arrived_refs[i][...].astype(jnp.float32)
+                result[...] = value.astype(result.dtype)
+        else:
+            results[0][...] = product
 
     whole = [fixed((rows, half), (0, 0)) for rows in counts]
     if kinds:
-        piece_spec = pl.BlockSpec((count // len(kinds), tile), lambda i, s: (0, i))
-        out_specs = [piece_spec] * len(kinds)
+        out_specs = [pl.BlockSpec((count // len(kinds), tile), lambda i, s: (0, i))] * len(kinds)
         out_shape = [jax.ShapeDtypeStruct((count // len(kinds), width), kind) for kind in kinds]
     else:
         out_specs = [pl.BlockSpec((tile, count), lambda i, s: (i, 0))]
@@ -245,12 +236,12 @@
         "down_product",
         (width // tile,),
         [section],
-        [*kept, *came, *[weight] * copies, *extra, *arrived],
+        [*kept, *came, weight, *extra, *others],
         whole
         + whole
-        + [pl.BlockSpec((short, 2 * half), lambda i, s, k=k: (copies * i + k, part)) for k in range(copies)]
+        + [pl.BlockSpec((tile, 2 * half), lambda i, s: (i, part))]
         + [pl.BlockSpec((tile, count), lambda i, s: (i, group))] * len(extra)
-        + [pl.BlockSpec((count // max(len(kinds), 1), tile), lambda i, s: (0, i))] * len(arrived),
+        + [pl.BlockSpec((count // max(len(kinds), 1), tile), lambda i, s: (0, i))] * len(others),
         out_specs,
         out_shape,
         [pltpu.VMEM((2 * half, count), jnp.bfloat16)],
@@ -262,7 +253,7 @@
     counts = [k.shape[0] for k in kept]
     half = kept[0].shape[1]
     tile = tile_of(width, 1024)
-    step = tile_of(2 * half, 256)
+    step = half
     n = len(kept)
 
     def kernel(section_ref, turned_ref, *refs):
@@ -470,6 +461,10 @@
             turned = run(transposed, x_all)["value"]
             near_sum = go_down(0, both, None, 0)
         elif t == 4:
+            hidden(1, [NEAR])
+            kept = chunks[0, NEAR]["halves"]
+            waited = chunks[1, NEAR]
+            kept["value"], waited["came"] = lax.optimization_barrier((kept["value"], waited["came"]))
             go_gradient(0)
         elif t == 5:
             near_sum = far_sum = go_down(1, both, near_sum, 0)
@@ -483,7 +478,7 @@
         if 2 <= near_part < parts - 1:
             go_gradient(near_part)
             near_sum = go_down(near_part, [NEAR], near_sum, NEAR if near_part == 2 else 0)
-            near_sum["value"], arrived[0] = lax.optimization_barrier((near_sum["value"], arrived[0]))
+            near_sum["value"], arrived = lax.optimization_barrier((near_sum["value"], arrived))
     column = NEAR if parts == 3 else 0
     sent_near = go_down(parts - 1, [NEAR], near_sum, column, [jnp.bfloat16, jnp.float32], arrived)
     go_gradient(parts - 1)

time: 279 us -> 272 us (0.975)
  Pallas kernels: 143 us -> 125 us
  waiting for transfers between devices: 58 us -> 71.1 us
    pallas_call x51, Pallas kernels: 143 us -> 125 us  [call(): pl.pallas_call(kernel, grid_spec=pltpu.PrefetchScalarGridSpec(num_scalar_...]
    ppermute x8, waiting for transfers between devices: 5.26 us -> 10.7 us  [inward(): lax.ppermute(value, 'dp', [(hop, hop + 1), (line - 1 - hop, line - 2 - ho...]
    ppermute x8, waiting for transfers between devices: 22.2 us -> 26.8 us  [from_peer(): return lax.ppermute(value, 'mp', [(i, i ^ by) for i in range(peers)])]
    ppermute x8, waiting for transfers between devices: 21.7 us -> 25.6 us  [outward(): lax.ppermute(value, 'dp', [(hop + 1, hop), (line - 2 - hop, line - 1 - ho...]
  transfers between devices with their start and end apart: 48 -> 48, of which waited for: 20 -> 20; matrix products, arithmetic and copies ran while one was open for 1% -> 1% of each run, Pallas kernels for 49% -> 44%
where the time goes in v7:
time: 272 us
  Pallas kernels  125 us (46%)
  waiting for transfers between devices  71.1 us (26%)
  starting transfers between devices  57.7 us (21%)
  blocking collectives  12 us (4%)
  other arithmetic  3.71 us (1%)
    pallas_call x51, Pallas kernels, call(): pl.pallas_call(kernel, grid_spec=pltpu.PrefetchScalarGridSpec(num_scalar_...  125 us
    ppermute x8, starting transfers between devices, inward(): lax.ppermute(value, 'dp', [(hop, hop + 1), (line - 1 - hop, line - 2 - ho...  29.5 us
    ppermute x8, waiting for transfers between devices, from_peer(): return lax.ppermute(value, 'mp', [(i, i ^ by) for i in range(peers)])  26.8 us
    ppermute x8, waiting for transfers between devices, outward(): lax.ppermute(value, 'dp', [(hop + 1, hop), (line - 2 - hop, line - 1 - ho...  25.6 us
    psum x1, blocking collectives, local(): lax.psum((jnp.sum(values, 1), jnp.sum(values * values, 1)), 'dp')  12 us
    ppermute x8, starting transfers between devices, outward(): lax.ppermute(value, 'dp', [(hop + 1, hop), (line - 2 - hop, line - 1 - ho...  10.7 us
    ppermute x8, waiting for transfers between devices, inward(): lax.ppermute(value, 'dp', [(hop, hop + 1), (line - 1 - hop, line - 2 - ho...  10.7 us
    ppermute x8, starting transfers between devices, from_peer(): return lax.ppermute(value, 'mp', [(i, i ^ by) for i in range(peers)])  9.98 us
  transfers between devices with their start and end apart: 48, of which 20 were waited for; matrix products, arithmetic and copies ran while one was open for 1% of the time, Pallas kernels for 44%

profile of v7, /device:TPU:0, one launch (start us, length us, event | category | flops | bytes accessed | tf_op | source)
XLA Modules:
  0.0 271.5 jit_solution(2606479182616209665)
XLA Ops:
  0.7 1.2 broadcast_select_fusion.refs_1_
  1.9 3.0 %collective-permute-start = (bf16[128,3072]{1,0:T(8,128)(2,1)S(1)}, bf16[128,3072]{1,0:T(8,128)(2,1)S(1)}, u32[]{:S(2)}, u32[]{:S(2)}) collective-permute-start(bf16[128,3072]{1,0:T(8,128)(2,1)S(1)} %broadcast_select_fusion.refs_1_), channel_id=1, source_target_pairs={{0,1},{1,0},{2,3},{3,2},{4,5},{5,4},{6,7},{7,6},{8,9},{9,8},{10,11... | collective-permute-start | bytes 2359304 | tf_op jit(solution)/shard_map/ppermute | solution.py:317
  4.9 1.5 collective-permute-start.1
  6.4 1.4 convert_reduce_fusion
  7.8 12.0 %all-reduce = (f32[128]{0:T(128)S(1)}, f32[128]{0:T(128)S(1)}) all-reduce(f32[128]{0:T(128)S(1)} %get-tuple-element.320, f32[128]{0:T(128)S(1)} %get-tuple-element.319), channel_id=1, replica_groups=mesh['section'=2,'dp'=4,'mp'=4] {'dp'}, use_global_device_ids=true, to_apply=%region_3.4 | all-reduce | flops 256 | bytes 2048 | tf_op jit(solution)/shard_map/psum | solution.py:359
  20.4 3.0 %collective-permute-done.2 = f32[128,2]{0,1:T(2,128)S(1)} collective-permute-done((f32[128,2]{0,1:T(2,128)S(1)}, f32[128,2]{0,1:T(2,128)S(1)}, u32[]{:S(2)}, u32[]{:S(2)}) %collective-permute-start.2) | collective-permute-done | bytes 1056 | tf_op jit(solution)/shard_map/ppermute | solution.py:317
  24.0 1.6 collective-permute-start.5
  25.6 1.2 normalize.2.rows_ref.refs_2_
  26.8 5.3 %up_product.6 = (bf16[256,768]{1,0:T(8,128)(2,1)S(1)}, bf16[256,768]{1,0:T(8,128)(2,1)S(1)}) custom-call(s32[1]{0:T(128)} %bitcast.section_ref, bf16[512,3072]{1,0:T(8,128)(2,1)S(1)} %normalize.2.rows_ref.refs_2_, bf16[3072,6144]{1,0:T(8,128)(2,1)} %bitcast.15), custom_call_target="tpu_custom_call" | custom-call | tf_op jit(solution)/shard_map/up_product/pallas_call | solution.py:32
  32.2 1.7 collective-permute-done.3.refs_1_
  34.1 3.5 %collective-permute-start.6 = (bf16[512,768]{1,0:T(8,128)(2,1)S(1)}, bf16[512,768]{1,0:T(8,128)(2,1)S(1)}, u32[]{:S(2)}, u32[]{:S(2)}) collective-permute-start(bf16[512,768]{1,0:T(8,128)(2,1)S(1)} %stacked.8.refs_0_), channel_id=1, source_target_pairs={{0,4},{12,8},{1,5},{13,9},{2,6},{14,10},{3,7},{15,11},{16,20},{28,... | collective-permute-start | bytes 2359304 | tf_op jit(solution)/shard_map/ppermute | solution.py:388
  38.2 5.2 %up_product.7 = (bf16[256,768]{1,0:T(8,128)(2,1)S(1)}, bf16[256,768]{1,0:T(8,128)(2,1)S(1)}) custom-call(s32[1]{0:T(128)} %bitcast.section_ref, bf16[512,3072]{1,0:T(8,128)(2,1)S(1)} %normalize.2.rows_ref.refs_2_, bf16[3072,6144]{1,0:T(8,128)(2,1)} %bitcast.16), custom_call_target="tpu_custom_call" | custom-call | tf_op jit(solution)/shard_map/up_product/pallas_call | solution.py:32
  43.5 1.5 collective-permute-done.4.scale_ref
  45.0 1.2 normalize.3.rows_ref.value_ref
  46.2 5.3 %up_product.8 = (bf16[256,768]{1,0:T(8,128)(2,1)S(1)}, bf16[256,768]{1,0:T(8,128)(2,1)S(1)}) custom-call(s32[1]{0:T(128)} %bitcast.section_ref, bf16[512,3072]{1,0:T(8,128)(2,1)S(1)} %normalize.3.rows_ref.value_ref, bf16[3072,6144]{1,0:T(8,128)(2,1)} %bitcast.17), custom_call_target="tpu_custom_call" | custom-call | tf_op jit(solution)/shard_map/up_product/pallas_call | solution.py:32
  51.6 3.1 %collective-permute-done.6.refs_1_ = bf16[512,768]{1,0:T(8,128)(2,1)S(1)} collective-permute-done((bf16[512,768]{1,0:T(8,128)(2,1)S(1)}, bf16[512,768]{1,0:T(8,128)(2,1)S(1)}, u32[]{:S(2)}, u32[]{:S(2)}) %collective-permute-start.6) | collective-permute-done | bytes 786464 | tf_op jit(solution)/shard_map/ppermute | solution.py:388
  55.4 4.4 %collective-permute-start.9 = (bf16[512,768]{1,0:T(8,128)(2,1)S(1)}, bf16[512,768]{1,0:T(8,128)(2,1)S(1)}, u32[]{:S(2)}, u32[]{:S(2)}) collective-permute-start(bf16[512,768]{1,0:T(8,128)(2,1)S(1)} %stacked.9.refs_0_), channel_id=1, source_target_pairs={{0,4},{12,8},{1,5},{13,9},{2,6},{14,10},{3,7},{15,11},{16,20},{28,... | collective-permute-start | bytes 2359304 | tf_op jit(solution)/shard_map/ppermute | solution.py:388
  61.9 5.3 %up_product.9 = (bf16[256,768]{1,0:T(8,128)(2,1)S(1)}, bf16[256,768]{1,0:T(8,128)(2,1)S(1)}) custom-call(s32[1]{0:T(128)} %bitcast.section_ref, bf16[512,3072]{1,0:T(8,128)(2,1)S(1)} %normalize.3.rows_ref.value_ref, bf16[3072,6144]{1,0:T(8,128)(2,1)} %bitcast.18), custom_call_target="tpu_custom_call" | custom-call | tf_op jit(solution)/shard_map/up_product/pallas_call | solution.py:32
  67.1 3.1 %collective-permute-start.12 = (bf16[512,768]{1,0:T(8,128)(2,1)S(1)}, bf16[512,768]{1,0:T(8,128)(2,1)S(1)}, u32[]{:S(2)}, u32[]{:S(2)}) collective-permute-start(bf16[512,768]{1,0:T(8,128)(2,1)S(1)} %stacked.10.refs_0_), channel_id=1, source_target_pairs={{0,4},{12,8},{1,5},{13,9},{2,6},{14,10},{3,7},{15,11},{16,20},{28,... | collective-permute-start | bytes 2359304 | tf_op jit(solution)/shard_map/ppermute | solution.py:388
  70.2 7.5 %collective-permute-done.9.refs_1_ = bf16[512,768]{1,0:T(8,128)(2,1)S(1)} collective-permute-done((bf16[512,768]{1,0:T(8,128)(2,1)S(1)}, bf16[512,768]{1,0:T(8,128)(2,1)S(1)}, u32[]{:S(2)}, u32[]{:S(2)}) %collective-permute-start.9) | collective-permute-done | bytes 786464 | tf_op jit(solution)/shard_map/ppermute | solution.py:388
  80.0 1.3 collective-permute-start.14
  81.6 7.8 %up_product.10 = (bf16[256,768]{1,0:T(8,128)(2,1)S(1)}, bf16[256,768]{1,0:T(8,128)(2,1)S(1)}, bf16[256,768]{1,0:T(8,128)(2,1)S(1)}, bf16[256,768]{1,0:T(8,128)(2,1)S(1)}) custom-call(s32[1]{0:T(128)} %bitcast.section_ref, bf16[512,3072]{1,0:T(8,128)(2,1)S(1)} %normalize.3.rows_ref.value_ref, bf16[3072,6144]{1,0:T(8,128)(2,1)} %bitcast.19), custom_call_target="tpu_custom_call" | custom-call | tf_op jit(solution)/shard_map/up_product/pallas_call | solution.py:32
  89.4 7.3 %collective-permute-start.16 = (bf16[512,768]{1,0:T(8,128)(2,1)S(1)}, bf16[512,768]{1,0:T(8,128)(2,1)S(1)}, u32[]{:S(2)}, u32[]{:S(2)}) collective-permute-start(bf16[512,768]{1,0:T(8,128)(2,1)S(1)} %stacked.11.refs_0_), channel_id=1, source_target_pairs={{0,4},{12,8},{1,5},{13,9},{2,6},{14,10},{3,7},{15,11},{16,20},{28,... | collective-permute-start | bytes 2359304 | tf_op jit(solution)/shard_map/ppermute | solution.py:388
  98.0 1.0 activated.9.refs_1_
  99.1 1.5 collective-permute-start.18
  100.5 4.4 %collective-permute-done.14.refs_2_ = bf16[512,768]{1,0:T(8,128)(2,1)S(1)} collective-permute-done((bf16[512,768]{1,0:T(8,128)(2,1)S(1)}, bf16[512,768]{1,0:T(8,128)(2,1)S(1)}, u32[]{:S(2)}, u32[]{:S(2)}) %collective-permute-start.14) | collective-permute-done | bytes 786464 | tf_op jit(solution)/shard_map/ppermute | solution.py:399
  105.5 7.8 %up_product.11 = (bf16[256,768]{1,0:T(8,128)(2,1)S(1)}, bf16[256,768]{1,0:T(8,128)(2,1)S(1)}, bf16[256,768]{1,0:T(8,128)(2,1)S(1)}, bf16[256,768]{1,0:T(8,128)(2,1)S(1)}) custom-call(s32[1]{0:T(128)} %bitcast.section_ref, bf16[512,3072]{1,0:T(8,128)(2,1)S(1)} %normalize.3.rows_ref.value_ref, bf16[3072,6144]{1,0:T(8,128)(2,1)} %bitcast.20), custom_call_target="tpu_custom_call" | custom-call | tf_op jit(solution)/shard_map/up_product/pallas_call | solution.py:32
  113.4 1.5 collective-permute-start.22
  116.1 1.0 activated.10.refs_1_
  117.1 1.3 collective-permute-start.24
  118.4 3.2 %collective-permute-done.18.refs_2_ = bf16[512,768]{1,0:T(8,128)(2,1)S(1)} collective-permute-done((bf16[512,768]{1,0:T(8,128)(2,1)S(1)}, bf16[512,768]{1,0:T(8,128)(2,1)S(1)}, u32[]{:S(2)}, u32[]{:S(2)}) %collective-permute-start.18) | collective-permute-done | bytes 786464 | tf_op jit(solution)/shard_map/ppermute | solution.py:399
  122.7 1.4 transposed.1.turned_ref
  124.2 2.1 collective-permute-start.27
  126.3 7.8 %down_product.6.refs_5_ = f32[3072,512]{1,0:T(8,128)S(1)} custom-call(s32[1]{0:T(128)} %bitcast.section_ref, bf16[256,768]{1,0:T(8,128)(2,1)S(1)} %get-tuple-element.250.refs_0_, bf16[256,768]{1,0:T(8,128)(2,1)S(1)} %get-tuple-element.252.refs_1_, bf16[256,768]{1,0:T(8,128)(2,1)S(1)} %collective-permute-done.20.refs_2_, ...), custom_call_target="tpu_custom_call" | custom-call | tf_op jit(solution)/shard_map/down_product/pallas_call | solution.py:32
  136.4 1.3 collective-permute-start.29
  137.7 1.1 collective-permute-done.24.refs_2_
  139.4 4.1 %collective-permute-start.32 = (bf16[512,768]{1,0:T(8,128)(2,1)S(1)}, bf16[512,768]{1,0:T(8,128)(2,1)S(1)}, u32[]{:S(2)}, u32[]{:S(2)}) collective-permute-start(bf16[512,768]{1,0:T(8,128)(2,1)S(1)} %stacked.14.refs_0_), channel_id=1, source_target_pairs={{0,4},{12,8},{1,5},{13,9},{2,6},{14,10},{3,7},{15,11},{16,20},{28,... | collective-permute-start | bytes 2359304 | tf_op jit(solution)/shard_map/ppermute | solution.py:388
  143.5 7.2 %weight_gradient.4.refs_4_ = bf16[3072,6144]{1,0:T(8,128)(2,1)} custom-call(s32[1]{0:T(128)} %bitcast.section_ref, bf16[3072,512]{1,0:T(8,128)(2,1)S(1)} %transposed.1.turned_ref, bf16[256,768]{1,0:T(8,128)(2,1)S(1)} %get-tuple-element.250.refs_0_, bf16[256,768]{1,0:T(8,128)(2,1)S(1)} %get-tuple-element.252.refs_1_, ...), custom_call_target="tpu_custom_call" | custom-call | tf_op jit(solution)/shard_map/weight_gradient/pallas_call | solution.py:32
  151.9 1.0 activated.12.refs_1_
  152.9 1.3 collective-permute-start.34
  154.3 4.3 %collective-permute-done.29.refs_2_ = bf16[512,768]{1,0:T(8,128)(2,1)S(1)} collective-permute-done((bf16[512,768]{1,0:T(8,128)(2,1)S(1)}, bf16[512,768]{1,0:T(8,128)(2,1)S(1)}, u32[]{:S(2)}, u32[]{:S(2)}) %collective-permute-start.29) | collective-permute-done | bytes 786464 | tf_op jit(solution)/shard_map/ppermute | solution.py:399
  159.3 3.5 %collective-permute-start.36 = (bf16[512,768]{1,0:T(8,128)(2,1)S(1)}, bf16[512,768]{1,0:T(8,128)(2,1)S(1)}, u32[]{:S(2)}, u32[]{:S(2)}) collective-permute-start(bf16[512,768]{1,0:T(8,128)(2,1)S(1)} %stacked.15.refs_0_), channel_id=1, source_target_pairs={{0,4},{12,8},{1,5},{13,9},{2,6},{14,10},{3,7},{15,11},{16,20},{28,... | collective-permute-start | bytes 2359304 | tf_op jit(solution)/shard_map/ppermute | solution.py:388
  162.8 7.8 %down_product.7.refs_3_ = f32[3072,512]{1,0:T(8,128)S(1)} custom-call(s32[1]{0:T(128)} %bitcast.section_ref, bf16[256,768]{1,0:T(8,128)(2,1)S(1)} %get-tuple-element.280.refs_0_, bf16[256,768]{1,0:T(8,128)(2,1)S(1)} %get-tuple-element.266.refs_1_, bf16[256,768]{1,0:T(8,128)(2,1)S(1)} %collective-permute-done.31.refs_2_, ...), custom_call_target="tpu_custom_call" | custom-call | tf_op jit(solution)/shard_map/down_product/pallas_call | solution.py:32
  171.1 1.0 activated.13.refs_1_
  172.9 2.5 collective-permute-done.34.refs_2_
  175.8 1.5 collective-permute-start.38
  177.5 6.0 %down_product.8.refs_3_ = f32[3072,256]{1,0:T(8,128)S(1)} custom-call(s32[1]{0:T(128)} %bitcast.section_ref, bf16[256,768]{1,0:T(8,128)(2,1)S(1)} %get-tuple-element.301.refs_0_, bf16[256,768]{1,0:T(8,128)(2,1)S(1)} %collective-permute-done.35.refs_1_.refs_2_, bf16[3072,6144]{1,0:T(8,128)(2,1)} %bitcast.23, f32[3072,512]{1,0:T(8,128)S(1)} %down_product.7.refs_3_), custom_call_target="tpu_custom_call" | custom-call | tf_op jit(solution)/shard_map/down_product/pallas_call | solution.py:32
  183.5 7.2 %weight_gradient.5.refs_4_ = bf16[3072,6144]{1,0:T(8,128)(2,1)} custom-call(s32[1]{0:T(128)} %bitcast.section_ref, bf16[3072,512]{1,0:T(8,128)(2,1)S(1)} %transposed.1.turned_ref, bf16[256,768]{1,0:T(8,128)(2,1)S(1)} %get-tuple-element.280.refs_0_, bf16[256,768]{1,0:T(8,128)(2,1)S(1)} %get-tuple-element.266.refs_1_, ...), custom_call_target="tpu_custom_call", output_to_operand_aliasing={{}: (6, {})} | custom-call | tf_op jit(solution)/shard_map/weight_gradient/pallas_call | solution.py:32
  192.9 1.3 collective-permute-start.41
  194.2 3.4 %collective-permute-done.38.refs_2_ = bf16[512,768]{1,0:T(8,128)(2,1)S(1)} collective-permute-done((bf16[512,768]{1,0:T(8,128)(2,1)S(1)}, bf16[512,768]{1,0:T(8,128)(2,1)S(1)}, u32[]{:S(2)}, u32[]{:S(2)}) %collective-permute-start.38) | collective-permute-done | bytes 786464 | tf_op jit(solution)/shard_map/ppermute | solution.py:399
  198.0 1.7 collective-permute-done.39.refs_1_.refs_2_
  199.7 6.2 %down_product.9 = (bf16[128,3072]{1,0:T(8,128)(2,1)S(1)}, bf16[128,3072]{1,0:T(8,128)(2,1)S(1)}) custom-call(s32[1]{0:T(128)} %bitcast.section_ref, bf16[256,768]{1,0:T(8,128)(2,1)S(1)} %get-tuple-element.316.refs_0_, bf16[256,768]{1,0:T(8,128)(2,1)S(1)} %collective-permute-done.39.refs_1_.refs_2_, bf16[3072,6144]{1,0:T(8,128)(2,1)} %bitcast.24, ...), custom_call_target="tpu_custom_call" | custom-call | tf_op jit(solution)/shard_map/down_product/pallas_call | solution.py:32
  206.5 1.5 collective-permute-start.44
  209.1 1.3 collective-permute-start.45
  210.4 6.7 %collective-permute-done.41.refs_2_ = bf16[512,768]{1,0:T(8,128)(2,1)S(1)} collective-permute-done((bf16[512,768]{1,0:T(8,128)(2,1)S(1)}, bf16[512,768]{1,0:T(8,128)(2,1)S(1)}, u32[]{:S(2)}, u32[]{:S(2)}) %collective-permute-start.41) | collective-permute-done | bytes 786464 | tf_op jit(solution)/shard_map/ppermute | solution.py:399
  217.5 1.7 collective-permute-done.42.refs_3_.refs_1_
  219.2 7.2 %weight_gradient.6.refs_4_ = bf16[3072,6144]{1,0:T(8,128)(2,1)} custom-call(s32[1]{0:T(128)} %bitcast.section_ref, bf16[3072,512]{1,0:T(8,128)(2,1)S(1)} %transposed.1.turned_ref, bf16[256,768]{1,0:T(8,128)(2,1)S(1)} %get-tuple-element.301.refs_0_, bf16[256,768]{1,0:T(8,128)(2,1)S(1)} %get-tuple-element.303.refs_1_.refs_0_, ...), custom_call_target="tpu_custom_call", output_to_operand_aliasing={{}: (6, {})} | custom-call | tf_op jit(solution)/shard_map/weight_gradient/pallas_call | solution.py:32
  226.4 6.0 %down_product.10.refs_3_ = f32[3072,256]{1,0:T(8,128)S(1)} custom-call(s32[1]{0:T(128)} %bitcast.section_ref, bf16[256,768]{1,0:T(8,128)(2,1)S(1)} %get-tuple-element.303.refs_1_.refs_0_, bf16[256,768]{1,0:T(8,128)(2,1)S(1)} %collective-permute-done.42.refs_3_.refs_1_, bf16[3072,6144]{1,0:T(8,128)(2,1)} %bitcast.25, f32[3072,512]{1,0:T(8,128)S(1)} %down_product.7.refs_3_), custom_call_target="tpu_custom_call" | custom-call | tf_op jit(solution)/shard_map/down_product/pallas_call | solution.py:32
  232.5 10.0 %collective-permute-done.44.refs_5_ = bf16[128,3072]{1,0:T(8,128)(2,1)S(1)} collective-permute-done((bf16[128,3072]{1,0:T(8,128)(2,1)S(1)}, bf16[128,3072]{1,0:T(8,128)(2,1)S(1)}, u32[]{:S(2)}, u32[]{:S(2)}) %collective-permute-start.44) | collective-permute-done | bytes 786464 | tf_op jit(solution)/shard_map/ppermute | solution.py:317
  242.8 1.7 collective-permute-done.46.refs_1_.refs_3_
  244.6 6.3 %down_product.11 = (bf16[128,3072]{1,0:T(8,128)(2,1)S(1)}, f32[128,3072]{1,0:T(8,128)S(1)}) custom-call(s32[1]{0:T(128)} %bitcast.section_ref, bf16[256,768]{1,0:T(8,128)(2,1)S(1)} %get-tuple-element.317.refs_0_.refs_1_, bf16[256,768]{1,0:T(8,128)(2,1)S(1)} %collective-permute-done.46.refs_1_.refs_3_, bf16[3072,6144]{1,0:T(8,128)(2,1)} %bitcast.26, ...), custom_call_target="tpu_custom_call" | custom-call | tf_op jit(solution)/shard_map/down_product/pallas_call | solution.py:32
  251.4 7.2 %weight_gradient.7 = bf16[3072,6144]{1,0:T(8,128)(2,1)} custom-call(s32[1]{0:T(128)} %bitcast.section_ref, bf16[3072,512]{1,0:T(8,128)(2,1)S(1)} %transposed.1.turned_ref, bf16[256,768]{1,0:T(8,128)(2,1)S(1)} %get-tuple-element.316.refs_0_, bf16[256,768]{1,0:T(8,128)(2,1)S(1)} %get-tuple-element.317.refs_0_.refs_1_, ...), custom_call_target="tpu_custom_call", output_to_operand_aliasing={{}: (6, {})} | custom-call | tf_op jit(solution)/shard_map/weight_gradient/pallas_call | solution.py:32
  258.6 11.9 %collective-permute-done.47 = bf16[128,3072]{1,0:T(8,128)(2,1)S(1)} collective-permute-done((bf16[128,3072]{1,0:T(8,128)(2,1)S(1)}, bf16[128,3072]{1,0:T(8,128)(2,1)S(1)}, u32[]{:S(2)}, u32[]{:S(2)}) %collective-permute-start.47) | collective-permute-done | bytes 786464 | tf_op jit(solution)/shard_map/ppermute | solution.py:317
  270.5 1.0 fusion.1
  (93 shorter events, 23.5 us)
Async XLA Ops:
  0.6 25.0 %copy-start = (f32[3072]{0:T(1024)S(1)}, f32[3072]{0:T(1024)}, u32[]{:S(2)}) copy-start(f32[3072]{0:T(1024)} %param.6) | copy-start | bytes 36868
  1.9 21.6 %collective-permute-start = (bf16[128,3072]{1,0:T(8,128)(2,1)S(1)}, bf16[128,3072]{1,0:T(8,128)(2,1)S(1)}, u32[]{:S(2)}, u32[]{:S(2)}) collective-permute-start(bf16[128,3072]{1,0:T(8,128)(2,1)S(1)} %broadcast_select_fusion.refs_1_), channel_id=1, source_target_pairs={{0,1},{1,0},{2,3},{3,2},{4,5},{5,4},{6,7},{7,6},{8,9},{9,8},{10,11... | collective-permute-start | bytes 2359304 | tf_op jit(solution)/shard_map/ppermute | solution.py:317
  4.9 19.0 %collective-permute-start.1 = (bf16[128,3072]{1,0:T(8,128)(2,1)S(1)}, bf16[128,3072]{1,0:T(8,128)(2,1)S(1)}, u32[]{:S(2)}, u32[]{:S(2)}) collective-permute-start(bf16[128,3072]{1,0:T(8,128)(2,1)S(1)} %broadcast_select_fusion.refs_1_), channel_id=1, source_target_pairs={{0,2},{1,3},{2,0},{3,1},{4,6},{5,7},{6,4},{7,5},{8,10},{9,11},{10,... | collective-permute-start | bytes 2359304 | tf_op jit(solution)/shard_map/ppermute | solution.py:317
  19.8 3.6 %collective-permute-start.2 = (f32[128,2]{0,1:T(2,128)S(1)}, f32[128,2]{0,1:T(2,128)S(1)}, u32[]{:S(2)}, u32[]{:S(2)}) collective-permute-start(f32[128,2]{0,1:T(2,128)S(1)} %pad_maximum_fusion), channel_id=1, source_target_pairs={{0,1},{1,0},{2,3},{3,2},{4,5},{5,4},{6,7},{7,6},{8,9},{9,8},{10,11... | collective-permute-start | bytes 3080 | tf_op jit(solution)/shard_map/ppermute | solution.py:317
  24.0 21.0 %collective-permute-start.5 = (bf16[128,3072]{1,0:T(8,128)(2,1)S(1)}, bf16[128,3072]{1,0:T(8,128)(2,1)S(1)}, u32[]{:S(2)}, u32[]{:S(2)}) collective-permute-start(bf16[128,3072]{1,0:T(8,128)(2,1)S(1)} %collective-permute-done.refs_0_), channel_id=1, source_target_pairs={{0,2},{1,3},{2,0},{3,1},{4,6},{5,7},{6,4},{7,5},{8,10},{9,11},{10,... | collective-permute-start | bytes 2359304 | tf_op jit(solution)/shard_map/ppermute | solution.py:317
  32.1 1.8 collective-permute-start.3
  34.1 20.6 %collective-permute-start.6 = (bf16[512,768]{1,0:T(8,128)(2,1)S(1)}, bf16[512,768]{1,0:T(8,128)(2,1)S(1)}, u32[]{:S(2)}, u32[]{:S(2)}) collective-permute-start(bf16[512,768]{1,0:T(8,128)(2,1)S(1)} %stacked.8.refs_0_), channel_id=1, source_target_pairs={{0,4},{12,8},{1,5},{13,9},{2,6},{14,10},{3,7},{15,11},{16,20},{28,... | collective-permute-start | bytes 2359304 | tf_op jit(solution)/shard_map/ppermute | solution.py:388
  37.7 7.3 %collective-permute-start.4 = (f32[256,2]{1,0:T(8,128)S(1)}, f32[256,2]{1,0:T(8,128)S(1)}, u32[]{:S(2)}, u32[]{:S(2)}) collective-permute-start(f32[256,2]{1,0:T(8,128)S(1)} %copy.12.scale_ref), channel_id=1, source_target_pairs={{0,2},{1,3},{2,0},{3,1},{4,6},{5,7},{6,4},{7,5},{8,10},{9,11},{10,... | collective-permute-start | bytes 6152 | tf_op jit(solution)/shard_map/ppermute | solution.py:317
  51.5 3.6 %collective-permute-start.7 = (bf16[256,768]{1,0:T(8,128)(2,1)S(1)}, bf16[256,768]{1,0:T(8,128)(2,1)S(1)}, u32[]{:S(2)}, u32[]{:S(2)}) collective-permute-start(bf16[256,768]{1,0:T(8,128)(2,1)S(1)} %get-tuple-element.185), channel_id=1, source_target_pairs={{0,16},{16,0},{1,17},{17,1},{2,18},{18,2},{3,19},{19,3},{4,20},{20... | collective-permute-start | bytes 1179656 | tf_op jit(solution)/shard_map/ppermute | solution.py:321
  55.4 22.4 %collective-permute-start.9 = (bf16[512,768]{1,0:T(8,128)(2,1)S(1)}, bf16[512,768]{1,0:T(8,128)(2,1)S(1)}, u32[]{:S(2)}, u32[]{:S(2)}) collective-permute-start(bf16[512,768]{1,0:T(8,128)(2,1)S(1)} %stacked.9.refs_0_), channel_id=1, source_target_pairs={{0,4},{12,8},{1,5},{13,9},{2,6},{14,10},{3,7},{15,11},{16,20},{28,... | collective-permute-start | bytes 2359304 | tf_op jit(solution)/shard_map/ppermute | solution.py:388
  59.8 1.8 collective-permute-start.8
  59.9 19.1 %collective-permute-start.10 = (bf16[512,768]{1,0:T(8,128)(2,1)S(1)}, bf16[512,768]{1,0:T(8,128)(2,1)S(1)}, u32[]{:S(2)}, u32[]{:S(2)}) collective-permute-start(bf16[512,768]{1,0:T(8,128)(2,1)S(1)} %added.8.refs_1_), channel_id=1, source_target_pairs={{4,8},{8,4},{5,9},{9,5},{6,10},{10,6},{7,11},{11,7},{20,24},{24,20... | collective-permute-start | bytes 2359304 | tf_op jit(solution)/shard_map/ppermute | solution.py:393
  67.1 29.5 %collective-permute-start.12 = (bf16[512,768]{1,0:T(8,128)(2,1)S(1)}, bf16[512,768]{1,0:T(8,128)(2,1)S(1)}, u32[]{:S(2)}, u32[]{:S(2)}) collective-permute-start(bf16[512,768]{1,0:T(8,128)(2,1)S(1)} %stacked.10.refs_0_), channel_id=1, source_target_pairs={{0,4},{12,8},{1,5},{13,9},{2,6},{14,10},{3,7},{15,11},{16,20},{28,... | collective-permute-start | bytes 2359304 | tf_op jit(solution)/shard_map/ppermute | solution.py:388
  78.2 19.9 %collective-permute-start.13 = (bf16[512,768]{1,0:T(8,128)(2,1)S(1)}, bf16[512,768]{1,0:T(8,128)(2,1)S(1)}, u32[]{:S(2)}, u32[]{:S(2)}) collective-permute-start(bf16[512,768]{1,0:T(8,128)(2,1)S(1)} %added.9.refs_1_), channel_id=1, source_target_pairs={{4,8},{8,4},{5,9},{9,5},{6,10},{10,6},{7,11},{11,7},{20,24},{24,20... | collective-permute-start | bytes 2359304 | tf_op jit(solution)/shard_map/ppermute | solution.py:393
  78.9 2.4 collective-permute-start.11
  80.0 24.9 %collective-permute-start.14 = (bf16[512,768]{1,0:T(8,128)(2,1)S(1)}, bf16[512,768]{1,0:T(8,128)(2,1)S(1)}, u32[]{:S(2)}, u32[]{:S(2)}) collective-permute-start(bf16[512,768]{1,0:T(8,128)(2,1)S(1)} %activated.8.refs_1_), channel_id=1, source_target_pairs={{4,0},{8,12},{5,1},{9,13},{6,2},{10,14},{7,3},{11,15},{20,16},{24,... | collective-permute-start | bytes 2359304 | tf_op jit(solution)/shard_map/ppermute | solution.py:399
  89.4 25.5 %collective-permute-start.16 = (bf16[512,768]{1,0:T(8,128)(2,1)S(1)}, bf16[512,768]{1,0:T(8,128)(2,1)S(1)}, u32[]{:S(2)}, u32[]{:S(2)}) collective-permute-start(bf16[512,768]{1,0:T(8,128)(2,1)S(1)} %stacked.11.refs_0_), channel_id=1, source_target_pairs={{0,4},{12,8},{1,5},{13,9},{2,6},{14,10},{3,7},{15,11},{16,20},{28,... | collective-permute-start | bytes 2359304 | tf_op jit(solution)/shard_map/ppermute | solution.py:388
  97.1 8.2 %collective-permute-start.15 = (bf16[256,768]{1,0:T(8,128)(2,1)S(1)}, bf16[256,768]{1,0:T(8,128)(2,1)S(1)}, u32[]{:S(2)}, u32[]{:S(2)}) collective-permute-start(bf16[256,768]{1,0:T(8,128)(2,1)S(1)} %get-tuple-element.216), channel_id=1, source_target_pairs={{0,16},{16,0},{1,17},{17,1},{2,18},{18,2},{3,19},{19,3},{4,20},{20... | collective-permute-start | bytes 1179656 | tf_op jit(solution)/shard_map/ppermute | solution.py:321
  97.3 18.7 %collective-permute-start.17 = (bf16[512,768]{1,0:T(8,128)(2,1)S(1)}, bf16[512,768]{1,0:T(8,128)(2,1)S(1)}, u32[]{:S(2)}, u32[]{:S(2)}) collective-permute-start(bf16[512,768]{1,0:T(8,128)(2,1)S(1)} %added.10.refs_1_), channel_id=1, source_target_pairs={{4,8},{8,4},{5,9},{9,5},{6,10},{10,6},{7,11},{11,7},{20,24},{24,20... | collective-permute-start | bytes 2359304 | tf_op jit(solution)/shard_map/ppermute | solution.py:393
  99.1 22.5 %collective-permute-start.18 = (bf16[512,768]{1,0:T(8,128)(2,1)S(1)}, bf16[512,768]{1,0:T(8,128)(2,1)S(1)}, u32[]{:S(2)}, u32[]{:S(2)}) collective-permute-start(bf16[512,768]{1,0:T(8,128)(2,1)S(1)} %activated.9.refs_1_), channel_id=1, source_target_pairs={{4,0},{8,12},{5,1},{9,13},{6,2},{10,14},{7,3},{11,15},{20,16},{24,... | collective-permute-start | bytes 2359304 | tf_op jit(solution)/shard_map/ppermute | solution.py:399
  113.3 8.6 %collective-permute-start.19 = (bf16[256,768]{1,0:T(8,128)(2,1)S(1)}, bf16[256,768]{1,0:T(8,128)(2,1)S(1)}, u32[]{:S(2)}, u32[]{:S(2)}) collective-permute-start(bf16[256,768]{1,0:T(8,128)(2,1)S(1)} %get-tuple-element.233), channel_id=1, source_target_pairs={{0,16},{16,0},{1,17},{17,1},{2,18},{18,2},{3,19},{19,3},{4,20},{20... | collective-permute-start | bytes 1179656 | tf_op jit(solution)/shard_map/ppermute | solution.py:321
  113.4 20.7 %collective-permute-start.22 = (bf16[512,768]{1,0:T(8,128)(2,1)S(1)}, bf16[512,768]{1,0:T(8,128)(2,1)S(1)}, u32[]{:S(2)}, u32[]{:S(2)}) collective-permute-start(bf16[512,768]{1,0:T(8,128)(2,1)S(1)} %stacked.12.refs_0_), channel_id=1, source_target_pairs={{0,4},{12,8},{1,5},{13,9},{2,6},{14,10},{3,7},{15,11},{16,20},{28,... | collective-permute-start | bytes 2359304 | tf_op jit(solution)/shard_map/ppermute | solution.py:388
  115.3 20.0 %collective-permute-start.23 = (bf16[512,768]{1,0:T(8,128)(2,1)S(1)}, bf16[512,768]{1,0:T(8,128)(2,1)S(1)}, u32[]{:S(2)}, u32[]{:S(2)}) collective-permute-start(bf16[512,768]{1,0:T(8,128)(2,1)S(1)} %added.11.refs_1_), channel_id=1, source_target_pairs={{4,8},{8,4},{5,9},{9,5},{6,10},{10,6},{7,11},{11,7},{20,24},{24,20... | collective-permute-start | bytes 2359304 | tf_op jit(solution)/shard_map/ppermute | solution.py:393
  117.1 21.7 %collective-permute-start.24 = (bf16[512,768]{1,0:T(8,128)(2,1)S(1)}, bf16[512,768]{1,0:T(8,128)(2,1)S(1)}, u32[]{:S(2)}, u32[]{:S(2)}) collective-permute-start(bf16[512,768]{1,0:T(8,128)(2,1)S(1)} %activated.10.refs_1_), channel_id=1, source_target_pairs={{4,0},{8,12},{5,1},{9,13},{6,2},{10,14},{7,3},{11,15},{20,16},{24,... | collective-permute-start | bytes 2359304 | tf_op jit(solution)/shard_map/ppermute | solution.py:399
  121.6 2.6 collective-permute-start.21
  121.9 4.4 %collective-permute-start.20 = (bf16[256,768]{1,0:T(8,128)(2,1)S(1)}, bf16[256,768]{1,0:T(8,128)(2,1)S(1)}, u32[]{:S(2)}, u32[]{:S(2)}) collective-permute-start(bf16[256,768]{1,0:T(8,128)(2,1)S(1)} %get-tuple-element.237), channel_id=1, source_target_pairs={{0,16},{16,0},{1,17},{17,1},{2,18},{18,2},{3,19},{19,3},{4,20},{20... | collective-permute-start | bytes 1179656 | tf_op jit(solution)/shard_map/ppermute | solution.py:321
  124.2 26.6 %collective-permute-start.27 = (bf16[512,768]{1,0:T(8,128)(2,1)S(1)}, bf16[512,768]{1,0:T(8,128)(2,1)S(1)}, u32[]{:S(2)}, u32[]{:S(2)}) collective-permute-start(bf16[512,768]{1,0:T(8,128)(2,1)S(1)} %stacked.13.refs_0_), channel_id=1, source_target_pairs={{0,4},{12,8},{1,5},{13,9},{2,6},{14,10},{3,7},{15,11},{16,20},{28,... | collective-permute-start | bytes 2359304 | tf_op jit(solution)/shard_map/ppermute | solution.py:388
  134.5 17.3 %collective-permute-start.28 = (bf16[512,768]{1,0:T(8,128)(2,1)S(1)}, bf16[512,768]{1,0:T(8,128)(2,1)S(1)}, u32[]{:S(2)}, u32[]{:S(2)}) collective-permute-start(bf16[512,768]{1,0:T(8,128)(2,1)S(1)} %added.12.refs_1_), channel_id=1, source_target_pairs={{4,8},{8,4},{5,9},{9,5},{6,10},{10,6},{7,11},{11,7},{20,24},{24,20... | collective-permute-start | bytes 2359304 | tf_op jit(solution)/shard_map/ppermute | solution.py:393
  135.3 3.9 %collective-permute-start.25 = (bf16[256,768]{1,0:T(8,128)(2,1)S(1)}, bf16[256,768]{1,0:T(8,128)(2,1)S(1)}, u32[]{:S(2)}, u32[]{:S(2)}) collective-permute-start(bf16[256,768]{1,0:T(8,128)(2,1)S(1)} %get-tuple-element.249), channel_id=1, source_target_pairs={{0,16},{16,0},{1,17},{17,1},{2,18},{18,2},{3,19},{19,3},{4,20},{20... | collective-permute-start | bytes 1179656 | tf_op jit(solution)/shard_map/ppermute | solution.py:321
  136.4 22.2 %collective-permute-start.29 = (bf16[512,768]{1,0:T(8,128)(2,1)S(1)}, bf16[512,768]{1,0:T(8,128)(2,1)S(1)}, u32[]{:S(2)}, u32[]{:S(2)}) collective-permute-start(bf16[512,768]{1,0:T(8,128)(2,1)S(1)} %activated.11.refs_1_), channel_id=1, source_target_pairs={{4,0},{8,12},{5,1},{9,13},{6,2},{10,14},{7,3},{11,15},{20,16},{24,... | collective-permute-start | bytes 2359304 | tf_op jit(solution)/shard_map/ppermute | solution.py:399
  139.1 4.4 %collective-permute-start.26 = (bf16[256,768]{1,0:T(8,128)(2,1)S(1)}, bf16[256,768]{1,0:T(8,128)(2,1)S(1)}, u32[]{:S(2)}, u32[]{:S(2)}) collective-permute-start(bf16[256,768]{1,0:T(8,128)(2,1)S(1)} %get-tuple-element.251), channel_id=1, source_target_pairs={{0,16},{16,0},{1,17},{17,1},{2,18},{18,2},{3,19},{19,3},{4,20},{20... | collective-permute-start | bytes 1179656 | tf_op jit(solution)/shard_map/ppermute | solution.py:321
  139.4 31.3 %collective-permute-start.32 = (bf16[512,768]{1,0:T(8,128)(2,1)S(1)}, bf16[512,768]{1,0:T(8,128)(2,1)S(1)}, u32[]{:S(2)}, u32[]{:S(2)}) collective-permute-start(bf16[512,768]{1,0:T(8,128)(2,1)S(1)} %stacked.14.refs_0_), channel_id=1, source_target_pairs={{0,4},{12,8},{1,5},{13,9},{2,6},{14,10},{3,7},{15,11},{16,20},{28,... | collective-permute-start | bytes 2359304 | tf_op jit(solution)/shard_map/ppermute | solution.py:388
  151.1 20.0 %collective-permute-start.33 = (bf16[512,768]{1,0:T(8,128)(2,1)S(1)}, bf16[512,768]{1,0:T(8,128)(2,1)S(1)}, u32[]{:S(2)}, u32[]{:S(2)}) collective-permute-start(bf16[512,768]{1,0:T(8,128)(2,1)S(1)} %added.13.refs_1_), channel_id=1, source_target_pairs={{4,8},{8,4},{5,9},{9,5},{6,10},{10,6},{7,11},{11,7},{20,24},{24,20... | collective-permute-start | bytes 2359304 | tf_op jit(solution)/shard_map/ppermute | solution.py:393
  152.9 22.5 %collective-permute-start.34 = (bf16[512,768]{1,0:T(8,128)(2,1)S(1)}, bf16[512,768]{1,0:T(8,128)(2,1)S(1)}, u32[]{:S(2)}, u32[]{:S(2)}) collective-permute-start(bf16[512,768]{1,0:T(8,128)(2,1)S(1)} %activated.12.refs_1_), channel_id=1, source_target_pairs={{4,0},{8,12},{5,1},{9,13},{6,2},{10,14},{7,3},{11,15},{20,16},{24,... | collective-permute-start | bytes 2359304 | tf_op jit(solution)/shard_map/ppermute | solution.py:399
  154.2 4.8 %collective-permute-start.30 = (bf16[256,768]{1,0:T(8,128)(2,1)S(1)}, bf16[256,768]{1,0:T(8,128)(2,1)S(1)}, u32[]{:S(2)}, u32[]{:S(2)}) collective-permute-start(bf16[256,768]{1,0:T(8,128)(2,1)S(1)} %get-tuple-element.264), channel_id=1, source_target_pairs={{0,16},{16,0},{1,17},{17,1},{2,18},{18,2},{3,19},{19,3},{4,20},{20... | collective-permute-start | bytes 1179656 | tf_op jit(solution)/shard_map/ppermute | solution.py:321
  158.9 3.9 %collective-permute-start.31 = (bf16[256,768]{1,0:T(8,128)(2,1)S(1)}, bf16[256,768]{1,0:T(8,128)(2,1)S(1)}, u32[]{:S(2)}, u32[]{:S(2)}) collective-permute-start(bf16[256,768]{1,0:T(8,128)(2,1)S(1)} %get-tuple-element.267), channel_id=1, source_target_pairs={{0,16},{16,0},{1,17},{17,1},{2,18},{18,2},{3,19},{19,3},{4,20},{20... | collective-permute-start | bytes 1179656 | tf_op jit(solution)/shard_map/ppermute | solution.py:321
  159.3 31.4 %collective-permute-start.36 = (bf16[512,768]{1,0:T(8,128)(2,1)S(1)}, bf16[512,768]{1,0:T(8,128)(2,1)S(1)}, u32[]{:S(2)}, u32[]{:S(2)}) collective-permute-start(bf16[512,768]{1,0:T(8,128)(2,1)S(1)} %stacked.15.refs_0_), channel_id=1, source_target_pairs={{0,4},{12,8},{1,5},{13,9},{2,6},{14,10},{3,7},{15,11},{16,20},{28,... | collective-permute-start | bytes 2359304 | tf_op jit(solution)/shard_map/ppermute | solution.py:388
  172.2 19.7 %collective-permute-start.37 = (bf16[512,768]{1,0:T(8,128)(2,1)S(1)}, bf16[512,768]{1,0:T(8,128)(2,1)S(1)}, u32[]{:S(2)}, u32[]{:S(2)}) collective-permute-start(bf16[512,768]{1,0:T(8,128)(2,1)S(1)} %added.14.refs_1_), channel_id=1, source_target_pairs={{4,8},{8,4},{5,9},{9,5},{6,10},{10,6},{7,11},{11,7},{20,24},{24,20... | collective-permute-start | bytes 2359304 | tf_op jit(solution)/shard_map/ppermute | solution.py:393
  175.7 1.8 collective-permute-start.35
  175.8 21.8 %collective-permute-start.38 = (bf16[512,768]{1,0:T(8,128)(2,1)S(1)}, bf16[512,768]{1,0:T(8,128)(2,1)S(1)}, u32[]{:S(2)}, u32[]{:S(2)}) collective-permute-start(bf16[512,768]{1,0:T(8,128)(2,1)S(1)} %activated.13.refs_1_), channel_id=1, source_target_pairs={{4,0},{8,12},{5,1},{9,13},{6,2},{10,14},{7,3},{11,15},{20,16},{24,... | collective-permute-start | bytes 2359304 | tf_op jit(solution)/shard_map/ppermute | solution.py:399
  191.1 16.9 %collective-permute-start.40 = (bf16[512,768]{1,0:T(8,128)(2,1)S(1)}, bf16[512,768]{1,0:T(8,128)(2,1)S(1)}, u32[]{:S(2)}, u32[]{:S(2)}) collective-permute-start(bf16[512,768]{1,0:T(8,128)(2,1)S(1)} %added.15.refs_1_), channel_id=1, source_target_pairs={{4,8},{8,4},{5,9},{9,5},{6,10},{10,6},{7,11},{11,7},{20,24},{24,20... | collective-permute-start | bytes 2359304 | tf_op jit(solution)/shard_map/ppermute | solution.py:393
  192.9 24.2 %collective-permute-start.41 = (bf16[512,768]{1,0:T(8,128)(2,1)S(1)}, bf16[512,768]{1,0:T(8,128)(2,1)S(1)}, u32[]{:S(2)}, u32[]{:S(2)}) collective-permute-start(bf16[512,768]{1,0:T(8,128)(2,1)S(1)} %activated.14.refs_1_), channel_id=1, source_target_pairs={{4,0},{8,12},{5,1},{9,13},{6,2},{10,14},{7,3},{11,15},{20,16},{24,... | collective-permute-start | bytes 2359304 | tf_op jit(solution)/shard_map/ppermute | solution.py:399
  197.9 1.8 collective-permute-start.39
  205.9 26.5 %collective-permute-start.43 = (bf16[128,3072]{1,0:T(8,128)(2,1)S(1)}, bf16[128,3072]{1,0:T(8,128)(2,1)S(1)}, u32[]{:S(2)}, u32[]{:S(2)}) collective-permute-start(bf16[128,3072]{1,0:T(8,128)(2,1)S(1)} %get-tuple-element.292), channel_id=1, source_target_pairs={{0,2},{1,3},{2,0},{3,1},{4,6},{5,7},{6,4},{7,5},{8,10},{9,11},{10,... | collective-permute-start | bytes 2359304 | tf_op jit(solution)/shard_map/ppermute | solution.py:317
  206.5 35.9 %collective-permute-start.44 = (bf16[128,3072]{1,0:T(8,128)(2,1)S(1)}, bf16[128,3072]{1,0:T(8,128)(2,1)S(1)}, u32[]{:S(2)}, u32[]{:S(2)}) collective-permute-start(bf16[128,3072]{1,0:T(8,128)(2,1)S(1)} %get-tuple-element.293), channel_id=1, source_target_pairs={{0,2},{1,3},{2,0},{3,1},{4,6},{5,7},{6,4},{7,5},{8,10},{9,11},{10,... | collective-permute-start | bytes 2359304 | tf_op jit(solution)/shard_map/ppermute | solution.py:317
  209.1 33.4 %collective-permute-start.45 = (bf16[512,768]{1,0:T(8,128)(2,1)S(1)}, bf16[512,768]{1,0:T(8,128)(2,1)S(1)}, u32[]{:S(2)}, u32[]{:S(2)}) collective-permute-start(bf16[512,768]{1,0:T(8,128)(2,1)S(1)} %activated.15.refs_1_), channel_id=1, source_target_pairs={{4,0},{8,12},{5,1},{9,13},{6,2},{10,14},{7,3},{11,15},{20,16},{24,... | collective-permute-start | bytes 2359304 | tf_op jit(solution)/shard_map/ppermute | solution.py:399
  217.4 1.8 collective-permute-start.42
  242.8 1.8 collective-permute-start.46
  250.8 19.6 %collective-permute-start.47 = (bf16[128,3072]{1,0:T(8,128)(2,1)S(1)}, bf16[128,3072]{1,0:T(8,128)(2,1)S(1)}, u32[]{:S(2)}, u32[]{:S(2)}) collective-permute-start(bf16[128,3072]{1,0:T(8,128)(2,1)S(1)} %get-tuple-element.315), channel_id=1, source_target_pairs={{0,1},{1,0},{2,3},{3,2},{4,5},{5,4},{6,7},{7,6},{8,9},{9,8},{10,11... | collective-permute-start | bytes 2359304 | tf_op jit(solution)/shard_map/ppermute | solution.py:317

commit v8 on v7

--- a/solution.py
+++ b/solution.py
@@ -8,7 +8,7 @@
 D = 12288
 MATMUL_VMEM = 22 * 1024 * 1024
 SMALL_VMEM = 8 * 1024 * 1024
-FAR, NEAR = 0, 1
+FAR, NEAR, PEER, OWN = (0, 2), (2, 2), (2, 1), (3, 1)
 
 
 epsilon = 1e-05
@@ -70,7 +70,7 @@
         [pl.BlockSpec((1, tile), column), fixed((count, 2), (0, 0))]
         + [pl.BlockSpec((rows, tile), column)] * len(blocks)
         + [pl.BlockSpec(memory_space=pl.ANY)] * len(extra),
-        pl.BlockSpec((count, tile), lambda i, _: (group, i)),
+        pl.BlockSpec((count, tile), lambda i, _: (group[0] // group[1], i)),
         jax.ShapeDtypeStruct((2 * count, width), jnp.bfloat16),
         aliases={3 + len(blocks): 0} if extra else {},
         vmem=SMALL_VMEM,
@@ -79,20 +79,21 @@
 
 def up_product(section, rows, weight, part, parts, groups):
     pieces = len(groups)
-    count, width = rows.shape[0] // 2 * pieces, rows.shape[1]
-    at = groups[0]
+    quarter, width = rows.shape[0] // 4, rows.shape[1]
+    total = sum(group[1] for group in groups)
+    count, at = quarter * total, groups[0][0] // total
+    places = [((g[0] - groups[0][0]) * quarter, g[1] * quarter) for g in groups]
     columns = weight.shape[1] // parts
     tile = tile_of(columns // 2, 768)
     steps = columns // tile
     mine = steps // 2
-    piece = count // pieces
 
     def kernel(section_ref, rows_ref, weight_ref, *results):
         product = dot_f32(rows_ref[...], weight_ref[...], (1, 0)).astype(jnp.bfloat16)
 
         def store(refs):
-            for i, result in enumerate(refs):
-                result[...] = product[i * piece : (i + 1) * piece]
+            for (first, size), result in zip(places, refs):
+                result[...] = product[first : first + size]
 
         pl.when(pl.program_id(0) < mine)(lambda: store(results[:pieces]))
         pl.when(pl.program_id(0) >= mine)(lambda: store(results[pieces:]))
@@ -107,9 +108,9 @@
             fixed((count, width), (at, 0)),
             pl.BlockSpec((width, tile), lambda i, s: (0, part * steps + lax.rem(i + s[0] * mine, steps))),
         ],
-        [pl.BlockSpec((piece, tile), lambda i, s: (0, jnp.minimum(i, mine - 1)))] * pieces
-        + [pl.BlockSpec((piece, tile), lambda i, s: (0, jnp.maximum(i - mine, 0)))] * pieces,
-        [jax.ShapeDtypeStruct((piece, columns // 2), jnp.bfloat16)] * (2 * pieces),
+        [pl.BlockSpec((size, tile), lambda i, s: (0, jnp.minimum(i, mine - 1))) for _, size in places]
+        + [pl.BlockSpec((size, tile), lambda i, s: (0, jnp.maximum(i - mine, 0))) for _, size in places],
+        [jax.ShapeDtypeStruct((size, columns // 2), jnp.bfloat16) for _, size in places] * 2,
     )
 
 
@@ -409,22 +410,31 @@
                 chunks[part, g]["came"] = across_sections(chunks[part, g]["halves"]["value"][1])
         return kept, [chunks[part, g]["came"] for g in groups]
 
-    both = (FAR, NEAR)
-    order = [(part, g) for part in (0, 1) for g in (NEAR, FAR)]
-    order += [(part, g) for g in (FAR, NEAR) for part in range(2, parts)]
+    def groups_of(part):
+        return (FAR, NEAR) if part < parts - 1 else (FAR, PEER, OWN)
+
+    order = [(part, g) for g in (NEAR, FAR) for part in (0, 1)]
+    order += [(part, FAR) for part in range(2, parts)] + [(part, NEAR) for part in range(2, parts - 1)]
+    order += [(parts - 1, PEER), (parts - 1, OWN)]
     count = len(order)
     held = {"gradient": None}
 
     def need(c):
         if c < count and order[c] not in chunks:
             part, group = order[c]
-            multiply(x_all, part, [group] if part < 2 else both)
+            multiply(x_all, part, [group] if part < 2 else groups_of(part))
 
     def tick(t):
-        if 0 <= t - 1 < count:
+        if 0 < t < count - 1:
+            inward(chunks[order[t]])
+        if 0 <= t - 1 < count - 2:
             middle(chunks[order[t - 1]])
         if 0 <= t - 2 < count:
             outward(chunks[order[t - 2]])
+        if t == count - 1:
+            inward(chunks[order[t]])
+        if count - 2 <= t - 1 < count:
+            middle(chunks[order[t - 1]])
         if 2 <= t + 2 < count:
             stack(chunks[order[t + 2]])
 
@@ -437,7 +447,7 @@
         )
 
     def go_gradient(part):
-        kept, came = hidden(part, both)
+        kept, came = hidden(part, groups_of(part))
         into = None if held["gradient"] is None else held["gradient"]["value"]
         held["gradient"] = run(
             lambda k: weight_gradient(section, turned, [k] + kept[1:], came, part, parts, into), kept[0]
@@ -447,44 +457,38 @@
     multiply(x_near, 0, [NEAR])
     stack(chunks[order[0]])
     multiply(x_near, 1, [NEAR])
+    stack(chunks[order[1]])
     x_all = prepare(far, far_scale, FAR, x_near)
     multiply(x_all, 0, [FAR])
     inward(chunks[order[0]])
-    stack(chunks[order[1]])
     for t in range(count + 2):
-        if 0 < t < count:
-            inward(chunks[order[t]])
         tick(t)
         need(t + 3)
         far_part, near_part = t - 4, t - 2 - parts
         if t == 3:
             turned = run(transposed, x_all)["value"]
-            near_sum = go_down(0, both, None, 0)
         elif t == 4:
-            hidden(1, [NEAR])
-            kept = chunks[0, NEAR]["halves"]
-            waited = chunks[1, NEAR]
-            kept["value"], waited["came"] = lax.optimization_barrier((kept["value"], waited["came"]))
-            go_gradient(0)
+            near_sum = go_down(0, (FAR, NEAR), None, 0)
         elif t == 5:
-            near_sum = far_sum = go_down(1, both, near_sum, 0)
+            near_sum = far_sum = go_down(1, (FAR, NEAR), near_sum, 0)
         if 2 <= far_part < parts - 1:
-            far_sum = go_down(far_part, [FAR], far_sum, FAR if far_part == 2 else 0)
+            far_sum = go_down(far_part, [FAR], far_sum, 0)
         elif far_part == parts - 1:
-            sent_far = go_down(far_part, [FAR], far_sum, FAR if far_part == 2 else 0, [jnp.bfloat16] * 2)
+            sent_far = go_down(far_part, [FAR], far_sum, 0, [jnp.bfloat16] * 2)
             arrived = [from_peer(value, across) for value in sent_far["value"]]
-        if t == 6:
-            go_gradient(1)
+        if t in (6, 7):
+            go_gradient(t - 6)
         if 2 <= near_part < parts - 1:
             go_gradient(near_part)
-            near_sum = go_down(near_part, [NEAR], near_sum, NEAR if near_part == 2 else 0)
-            near_sum["value"], arrived = lax.optimization_barrier((near_sum["value"], arrived))
-    column = NEAR if parts == 3 else 0
-    sent_near = go_down(parts - 1, [NEAR], near_sum, column, [jnp.bfloat16, jnp.float32], arrived)
+            near_sum = go_down(near_part, [NEAR], near_sum, 1 if near_part == 2 else 0)
+        if t == count:
+            first_column = 2 if parts == 3 else 0
+            peer_sum = go_down(parts - 1, [PEER], near_sum, first_column, [jnp.bfloat16], arrived[:1])
     go_gradient(parts - 1)
-
-    own = sent_near["value"][1]
-    blocks = {0: own.astype(jnp.bfloat16), 1: sent_near["value"][0]}
+    own_sum = go_down(parts - 1, [OWN], near_sum, first_column + 1, [jnp.float32], arrived[1:])
+
+    own = own_sum["value"][0]
+    blocks = {0: own.astype(jnp.bfloat16), 1: peer_sum["value"][0]}
     result = own[:rows]
     for by in range(1, across):
         at = (by % each) * rows

time: 272 us -> 278 us (1.022)
  waiting for transfers between devices: 71.1 us -> 60.7 us
  starting transfers between devices: 57.7 us -> 66.9 us
  Pallas kernels: 125 us -> 132 us
    ppermute x8, waiting for transfers between devices: 26.8 us -> 13.5 us  [from_peer(): return lax.ppermute(value, 'mp', [(i, i ^ by) for i in range(peers)])]
    pallas_call x51 -> x56, Pallas kernels: 125 us -> 132 us  [call(): pl.pallas_call(kernel, grid_spec=pltpu.PrefetchScalarGridSpec(num_scalar_...]
    ppermute x8 -> x9, starting transfers between devices: 29.5 us -> 34.1 us  [inward(): lax.ppermute(value, 'dp', [(hop, hop + 1), (line - 1 - hop, line - 2 - ho...]
    ppermute x8 -> x9, waiting for transfers between devices: 25.6 us -> 29.1 us  [outward(): lax.ppermute(value, 'dp', [(hop + 1, hop), (line - 2 - hop, line - 1 - ho...]
    ppermute x16 -> x18, waiting for transfers between devices: 8.04 us -> 5.03 us  [across_sections(): return lax.ppermute(value, 'section', [(0, 1), (1, 0)])]
    ppermute x8 -> x9, waiting for transfers between devices: 10.7 us -> 13.1 us  [inward(): lax.ppermute(value, 'dp', [(hop, hop + 1), (line - 1 - hop, line - 2 - ho...]
    ppermute x8 -> x9, starting transfers between devices: 10.7 us -> 12.1 us  [outward(): lax.ppermute(value, 'dp', [(hop + 1, hop), (line - 2 - hop, line - 1 - ho...]
    ppermute x8 -> x9, starting transfers between devices: 5.68 us -> 6.35 us  [middle(): arrived = lax.ppermute(value, 'dp', [(half - 1, half), (half, half - 1)])]
  transfers between devices with their start and end apart: 48 -> 53, of which waited for: 20 -> 17; matrix products, arithmetic and copies ran while one was open for 1% -> 1% of each run, Pallas kernels for 44% -> 45%
where the time goes in v8:
time: 278 us; the launch traced here: 277 us
  Pallas kernels  132 us (47%)
  starting transfers between devices  66.9 us (24%)
  waiting for transfers between devices  60.7 us (22%)
  blocking collectives  12 us (4%)
  other arithmetic  3.71 us (1%)
    pallas_call x56, Pallas kernels, call(): pl.pallas_call(kernel, grid_spec=pltpu.PrefetchScalarGridSpec(num_scalar_...  132 us
    ppermute x9, starting transfers between devices, inward(): lax.ppermute(value, 'dp', [(hop, hop + 1), (line - 1 - hop, line - 2 - ho...  34.1 us
    ppermute x9, waiting for transfers between devices, outward(): lax.ppermute(value, 'dp', [(hop + 1, hop), (line - 2 - hop, line - 1 - ho...  29.1 us
    ppermute x8, waiting for transfers between devices, from_peer(): return lax.ppermute(value, 'mp', [(i, i ^ by) for i in range(peers)])  13.5 us
    ppermute x9, waiting for transfers between devices, inward(): lax.ppermute(value, 'dp', [(hop, hop + 1), (line - 1 - hop, line - 2 - ho...  13.1 us
    ppermute x9, starting transfers between devices, outward(): lax.ppermute(value, 'dp', [(hop + 1, hop), (line - 2 - hop, line - 1 - ho...  12.1 us
    psum x1, blocking collectives, local(): lax.psum((jnp.sum(values, 1), jnp.sum(values * values, 1)), 'dp')  12 us
    ppermute x8, starting transfers between devices, from_peer(): return lax.ppermute(value, 'mp', [(i, i ^ by) for i in range(peers)])  11.5 us
  transfers between devices with their start and end apart: 53, of which 17 were waited for; matrix products, arithmetic and copies ran while one was open for 1% of the time, Pallas kernels for 45%

profile of v8, /device:TPU:0, one launch (start us, length us, event | category | flops | bytes accessed | tf_op | source)
XLA Modules:
  0.0 276.8 jit_solution(18439455576818337605)
XLA Ops:
  0.7 1.2 broadcast_select_fusion.refs_1_
  1.9 3.0 %collective-permute-start = (bf16[128,3072]{1,0:T(8,128)(2,1)S(1)}, bf16[128,3072]{1,0:T(8,128)(2,1)S(1)}, u32[]{:S(2)}, u32[]{:S(2)}) collective-permute-start(bf16[128,3072]{1,0:T(8,128)(2,1)S(1)} %broadcast_select_fusion.refs_1_), channel_id=1, source_target_pairs={{0,1},{1,0},{2,3},{3,2},{4,5},{5,4},{6,7},{7,6},{8,9},{9,8},{10,11... | collective-permute-start | bytes 2359304 | tf_op jit(solution)/shard_map/ppermute | solution.py:318
  4.9 1.5 collective-permute-start.1
  6.4 1.4 convert_reduce_fusion
  7.8 12.0 %all-reduce = (f32[128]{0:T(128)S(1)}, f32[128]{0:T(128)S(1)}) all-reduce(f32[128]{0:T(128)S(1)} %get-tuple-element.337, f32[128]{0:T(128)S(1)} %get-tuple-element.336), channel_id=1, replica_groups=mesh['section'=2,'dp'=4,'mp'=4] {'dp'}, use_global_device_ids=true, to_apply=%region_3.4 | all-reduce | flops 256 | bytes 2048 | tf_op jit(solution)/shard_map/psum | solution.py:360
  20.4 3.0 %collective-permute-done.2 = f32[128,2]{0,1:T(2,128)S(1)} collective-permute-done((f32[128,2]{0,1:T(2,128)S(1)}, f32[128,2]{0,1:T(2,128)S(1)}, u32[]{:S(2)}, u32[]{:S(2)}) %collective-permute-start.2) | collective-permute-done | bytes 1056 | tf_op jit(solution)/shard_map/ppermute | solution.py:318
  24.0 1.2 normalize.2.rows_ref.refs_2_
  25.3 5.3 %up_product.6 = (bf16[256,768]{1,0:T(8,128)(2,1)S(1)}, bf16[256,768]{1,0:T(8,128)(2,1)S(1)}) custom-call(s32[1]{0:T(128)} %bitcast.section_ref, bf16[512,3072]{1,0:T(8,128)(2,1)S(1)} %normalize.2.rows_ref.refs_2_, bf16[3072,6144]{1,0:T(8,128)(2,1)} %bitcast.15), custom_call_target="tpu_custom_call" | custom-call | tf_op jit(solution)/shard_map/up_product/pallas_call | solution.py:32
  30.6 1.6 collective-permute-start.6
  32.6 3.5 %collective-permute-start.7 = (bf16[512,768]{1,0:T(8,128)(2,1)S(1)}, bf16[512,768]{1,0:T(8,128)(2,1)S(1)}, u32[]{:S(2)}, u32[]{:S(2)}) collective-permute-start(bf16[512,768]{1,0:T(8,128)(2,1)S(1)} %stacked.9.refs_0_), channel_id=1, source_target_pairs={{0,4},{12,8},{1,5},{13,9},{2,6},{14,10},{3,7},{15,11},{16,20},{28,... | collective-permute-start | bytes 2359304 | tf_op jit(solution)/shard_map/ppermute | solution.py:389
  36.1 5.3 %up_product.7 = (bf16[256,768]{1,0:T(8,128)(2,1)S(1)}, bf16[256,768]{1,0:T(8,128)(2,1)S(1)}) custom-call(s32[1]{0:T(128)} %bitcast.section_ref, bf16[512,3072]{1,0:T(8,128)(2,1)S(1)} %normalize.2.rows_ref.refs_2_, bf16[3072,6144]{1,0:T(8,128)(2,1)} %bitcast.16), custom_call_target="tpu_custom_call" | custom-call | tf_op jit(solution)/shard_map/up_product/pallas_call | solution.py:32
  41.5 1.6 collective-permute-start.5
  43.4 10.0 %collective-permute-done.5.scale_ref = f32[256,2]{1,0:T(8,128)S(1)} collective-permute-done((f32[256,2]{1,0:T(8,128)S(1)}, f32[256,2]{1,0:T(8,128)S(1)}, u32[]{:S(2)}, u32[]{:S(2)}) %collective-permute-start.5) | collective-permute-done | bytes 2080 | tf_op jit(solution)/shard_map/ppermute | solution.py:318
  53.4 1.2 normalize.3.rows_ref.value_ref
  54.6 5.3 %up_product.8 = (bf16[256,768]{1,0:T(8,128)(2,1)S(1)}, bf16[256,768]{1,0:T(8,128)(2,1)S(1)}) custom-call(s32[1]{0:T(128)} %bitcast.section_ref, bf16[512,3072]{1,0:T(8,128)(2,1)S(1)} %normalize.3.rows_ref.value_ref, bf16[3072,6144]{1,0:T(8,128)(2,1)} %bitcast.17), custom_call_target="tpu_custom_call" | custom-call | tf_op jit(solution)/shard_map/up_product/pallas_call | solution.py:32
  60.0 3.5 %collective-permute-start.9 = (bf16[512,768]{1,0:T(8,128)(2,1)S(1)}, bf16[512,768]{1,0:T(8,128)(2,1)S(1)}, u32[]{:S(2)}, u32[]{:S(2)}) collective-permute-start(bf16[512,768]{1,0:T(8,128)(2,1)S(1)} %stacked.10.refs_0_), channel_id=1, source_target_pairs={{0,4},{12,8},{1,5},{13,9},{2,6},{14,10},{3,7},{15,11},{16,20},{28,... | collective-permute-start | bytes 2359304 | tf_op jit(solution)/shard_map/ppermute | solution.py:389
  64.9 4.1 %collective-permute-start.12 = (bf16[512,768]{1,0:T(8,128)(2,1)S(1)}, bf16[512,768]{1,0:T(8,128)(2,1)S(1)}, u32[]{:S(2)}, u32[]{:S(2)}) collective-permute-start(bf16[512,768]{1,0:T(8,128)(2,1)S(1)} %stacked.11.refs_0_), channel_id=1, source_target_pairs={{0,4},{12,8},{1,5},{13,9},{2,6},{14,10},{3,7},{15,11},{16,20},{28,... | collective-permute-start | bytes 2359304 | tf_op jit(solution)/shard_map/ppermute | solution.py:389
  69.0 5.3 %up_product.9 = (bf16[256,768]{1,0:T(8,128)(2,1)S(1)}, bf16[256,768]{1,0:T(8,128)(2,1)S(1)}) custom-call(s32[1]{0:T(128)} %bitcast.section_ref, bf16[512,3072]{1,0:T(8,128)(2,1)S(1)} %normalize.3.rows_ref.value_ref, bf16[3072,6144]{1,0:T(8,128)(2,1)} %bitcast.18), custom_call_target="tpu_custom_call" | custom-call | tf_op jit(solution)/shard_map/up_product/pallas_call | solution.py:32
  74.4 6.9 %collective-permute-done.9.refs_1_ = bf16[512,768]{1,0:T(8,128)(2,1)S(1)} collective-permute-done((bf16[512,768]{1,0:T(8,128)(2,1)S(1)}, bf16[512,768]{1,0:T(8,128)(2,1)S(1)}, u32[]{:S(2)}, u32[]{:S(2)}) %collective-permute-start.9) | collective-permute-done | bytes 786464 | tf_op jit(solution)/shard_map/ppermute | solution.py:389
  82.4 1.0 activated.9.refs_1_
  83.5 1.3 collective-permute-start.14
  85.0 7.3 %collective-permute-start.16 = (bf16[512,768]{1,0:T(8,128)(2,1)S(1)}, bf16[512,768]{1,0:T(8,128)(2,1)S(1)}, u32[]{:S(2)}, u32[]{:S(2)}) collective-permute-start(bf16[512,768]{1,0:T(8,128)(2,1)S(1)} %stacked.12.refs_0_), channel_id=1, source_target_pairs={{0,4},{12,8},{1,5},{13,9},{2,6},{14,10},{3,7},{15,11},{16,20},{28,... | collective-permute-start | bytes 2359304 | tf_op jit(solution)/shard_map/ppermute | solution.py:389
  92.3 7.8 %up_product.10 = (bf16[256,768]{1,0:T(8,128)(2,1)S(1)}, bf16[256,768]{1,0:T(8,128)(2,1)S(1)}, bf16[256,768]{1,0:T(8,128)(2,1)S(1)}, bf16[256,768]{1,0:T(8,128)(2,1)S(1)}) custom-call(s32[1]{0:T(128)} %bitcast.section_ref, bf16[512,3072]{1,0:T(8,128)(2,1)S(1)} %normalize.3.rows_ref.value_ref, bf16[3072,6144]{1,0:T(8,128)(2,1)} %bitcast.19), custom_call_target="tpu_custom_call" | custom-call | tf_op jit(solution)/shard_map/up_product/pallas_call | solution.py:32
  101.3 1.0 activated.10.refs_1_
  102.4 1.5 collective-permute-start.18
  103.8 2.9 %collective-permute-done.14.refs_2_ = bf16[512,768]{1,0:T(8,128)(2,1)S(1)} collective-permute-done((bf16[512,768]{1,0:T(8,128)(2,1)S(1)}, bf16[512,768]{1,0:T(8,128)(2,1)S(1)}, u32[]{:S(2)}, u32[]{:S(2)}) %collective-permute-start.14) | collective-permute-done | bytes 786464 | tf_op jit(solution)/shard_map/ppermute | solution.py:400
  107.3 7.8 %up_product.11 = (bf16[256,768]{1,0:T(8,128)(2,1)S(1)}, bf16[128,768]{1,0:T(8,128)(2,1)S(1)}, bf16[128,768]{1,0:T(8,128)(2,1)S(1)}, bf16[256,768]{1,0:T(8,128)(2...) custom-call(s32[1]{0:T(128)} %bitcast.section_ref, ...), custom_call_target="tpu_custom_call" | custom-call | tf_op jit(solution)/shard_map/up_product/pallas_call | solution.py:32
  115.1 2.6 collective-permute-start.20
  118.9 1.0 activated.11.refs_1_
  119.9 1.3 collective-permute-start.22
  121.3 4.1 %collective-permute-done.18.refs_2_ = bf16[512,768]{1,0:T(8,128)(2,1)S(1)} collective-permute-done((bf16[512,768]{1,0:T(8,128)(2,1)S(1)}, bf16[512,768]{1,0:T(8,128)(2,1)S(1)}, u32[]{:S(2)}, u32[]{:S(2)}) %collective-permute-start.18) | collective-permute-done | bytes 786464 | tf_op jit(solution)/shard_map/ppermute | solution.py:400
  126.0 2.0 collective-permute-start.26
  128.0 1.4 transposed.1.turned_ref
  129.5 6.1 %collective-permute-done.20.refs_1_ = bf16[512,768]{1,0:T(8,128)(2,1)S(1)} collective-permute-done((bf16[512,768]{1,0:T(8,128)(2,1)S(1)}, bf16[512,768]{1,0:T(8,128)(2,1)S(1)}, u32[]{:S(2)}, u32[]{:S(2)}) %collective-permute-start.20) | collective-permute-done | bytes 786464 | tf_op jit(solution)/shard_map/ppermute | solution.py:389
  136.7 1.0 activated.12.refs_1_
  137.7 1.3 collective-permute-start.28
  139.0 2.9 %collective-permute-done.22.refs_2_ = bf16[512,768]{1,0:T(8,128)(2,1)S(1)} collective-permute-done((bf16[512,768]{1,0:T(8,128)(2,1)S(1)}, bf16[512,768]{1,0:T(8,128)(2,1)S(1)}, u32[]{:S(2)}, u32[]{:S(2)}) %collective-permute-start.22) | collective-permute-done | bytes 786464 | tf_op jit(solution)/shard_map/ppermute | solution.py:400
  143.7 4.5 %collective-permute-start.32 = (bf16[512,768]{1,0:T(8,128)(2,1)S(1)}, bf16[512,768]{1,0:T(8,128)(2,1)S(1)}, u32[]{:S(2)}, u32[]{:S(2)}) collective-permute-start(bf16[512,768]{1,0:T(8,128)(2,1)S(1)} %stacked.15.refs_0_), channel_id=1, source_target_pairs={{0,4},{12,8},{1,5},{13,9},{2,6},{14,10},{3,7},{15,11},{16,20},{28,... | collective-permute-start | bytes 2359304 | tf_op jit(solution)/shard_map/ppermute | solution.py:389
  148.3 7.8 %down_product.7.refs_5_ = f32[3072,512]{1,0:T(8,128)S(1)} custom-call(s32[1]{0:T(128)} %bitcast.section_ref, bf16[256,768]{1,0:T(8,128)(2,1)S(1)} %get-tuple-element.290.refs_0_, bf16[256,768]{1,0:T(8,128)(2,1)S(1)} %get-tuple-element.255.refs_1_, bf16[256,768]{1,0:T(8,128)(2,1)S(1)} %collective-permute-done.24.refs_2_, ...), custom_call_target="tpu_custom_call" | custom-call | tf_op jit(solution)/shard_map/down_product/pallas_call | solution.py:32
  157.3 1.0 activated.13.refs_1_
  158.3 1.3 collective-permute-start.34
  162.3 7.8 %down_product.8.refs_3_ = f32[3072,512]{1,0:T(8,128)S(1)} custom-call(s32[1]{0:T(128)} %bitcast.section_ref, bf16[256,768]{1,0:T(8,128)(2,1)S(1)} %get-tuple-element.304.refs_0_, bf16[256,768]{1,0:T(8,128)(2,1)S(1)} %get-tuple-element.271.refs_1_, bf16[256,768]{1,0:T(8,128)(2,1)S(1)} %collective-permute-done.30.refs_2_, ...), custom_call_target="tpu_custom_call" | custom-call | tf_op jit(solution)/shard_map/down_product/pallas_call | solution.py:32
  171.3 1.0 activated.14.refs_1_
  172.3 1.3 collective-permute-start.39
  173.6 6.5 %collective-permute-done.34.refs_2_ = bf16[512,768]{1,0:T(8,128)(2,1)S(1)} collective-permute-done((bf16[512,768]{1,0:T(8,128)(2,1)S(1)}, bf16[512,768]{1,0:T(8,128)(2,1)S(1)}, u32[]{:S(2)}, u32[]{:S(2)}) %collective-permute-start.34) | collective-permute-done | bytes 786464 | tf_op jit(solution)/shard_map/ppermute | solution.py:400
  180.6 2.1 collective-permute-start.37
  183.0 1.2 collective-permute-done.35.refs_1_
  184.4 6.0 %down_product.9.refs_3_ = f32[3072,256]{1,0:T(8,128)S(1)} custom-call(s32[1]{0:T(128)} %bitcast.section_ref, bf16[256,768]{1,0:T(8,128)(2,1)S(1)} %get-tuple-element.314.refs_0_, bf16[256,768]{1,0:T(8,128)(2,1)S(1)} %collective-permute-done.36.refs_1_.refs_2_, bf16[3072,6144]{1,0:T(8,128)(2,1)} %bitcast.23, f32[3072,512]{1,0:T(8,128)S(1)} %down_product.8.refs_3_), custom_call_target="tpu_custom_call" | custom-call | tf_op jit(solution)/shard_map/down_product/pallas_call | solution.py:32
  190.4 7.2 %weight_gradient.4.refs_4_ = bf16[3072,6144]{1,0:T(8,128)(2,1)} custom-call(s32[1]{0:T(128)} %bitcast.section_ref, bf16[3072,512]{1,0:T(8,128)(2,1)S(1)} %transposed.1.turned_ref, bf16[256,768]{1,0:T(8,128)(2,1)S(1)} %get-tuple-element.290.refs_0_, bf16[256,768]{1,0:T(8,128)(2,1)S(1)} %get-tuple-element.255.refs_1_, ...), custom_call_target="tpu_custom_call" | custom-call | tf_op jit(solution)/shard_map/weight_gradient/pallas_call | solution.py:32
  198.9 1.3 collective-permute-start.41
  200.9 4.4 %collective-permute-start.42 = (bf16[256,768]{1,0:T(8,128)(2,1)S(1)}, bf16[256,768]{1,0:T(8,128)(2,1)S(1)}, u32[]{:S(2)}, u32[]{:S(2)}) collective-permute-start(bf16[256,768]{1,0:T(8,128)(2,1)S(1)} %stacked.17.refs_0_), channel_id=1, source_target_pairs={{0,4},{12,8},{1,5},{13,9},{2,6},{14,10},{3,7},{15,11},{16,20},{28,... | collective-permute-start | bytes 1179656 | tf_op jit(solution)/shard_map/ppermute | solution.py:389
  206.0 6.2 %down_product.10 = (bf16[128,3072]{1,0:T(8,128)(2,1)S(1)}, bf16[128,3072]{1,0:T(8,128)(2,1)S(1)}) custom-call(s32[1]{0:T(128)} %bitcast.section_ref, bf16[256,768]{1,0:T(8,128)(2,1)S(1)} %get-tuple-element.331.refs_0_, bf16[256,768]{1,0:T(8,128)(2,1)S(1)} %collective-permute-done.40.refs_1_.refs_3_, bf16[3072,6144]{1,0:T(8,128)(2,1)} %bitcast.24, ...), custom_call_target="tpu_custom_call" | custom-call | tf_op jit(solution)/shard_map/down_product/pallas_call | solution.py:32
  212.2 1.6 collective-permute-start.48
  213.8 7.2 %weight_gradient.5.refs_4_ = bf16[3072,6144]{1,0:T(8,128)(2,1)} custom-call(s32[1]{0:T(128)} %bitcast.section_ref, bf16[3072,512]{1,0:T(8,128)(2,1)S(1)} %transposed.1.turned_ref, bf16[256,768]{1,0:T(8,128)(2,1)S(1)} %get-tuple-element.304.refs_0_, bf16[256,768]{1,0:T(8,128)(2,1)S(1)} %get-tuple-element.271.refs_1_, ...), custom_call_target="tpu_custom_call", output_to_operand_aliasing={{}: (6, {})} | custom-call | tf_op jit(solution)/shard_map/weight_gradient/pallas_call | solution.py:32
  222.3 1.3 collective-permute-start.45
  224.3 7.2 %weight_gradient.6.refs_6_ = bf16[3072,6144]{1,0:T(8,128)(2,1)} custom-call(s32[1]{0:T(128)} %bitcast.section_ref, bf16[3072,512]{1,0:T(8,128)(2,1)S(1)} %transposed.1.turned_ref, bf16[256,768]{1,0:T(8,128)(2,1)S(1)} %get-tuple-element.314.refs_0_, bf16[256,768]{1,0:T(8,128)(2,1)S(1)} %get-tuple-element.317.refs_1_.refs_0_, ...), custom_call_target="tpu_custom_call", output_to_operand_aliasing={{}: (6, {})} | custom-call | tf_op jit(solution)/shard_map/weight_gradient/pallas_call | solution.py:32
  231.5 6.0 %down_product.11.refs_3_ = f32[3072,256]{1,0:T(8,128)S(1)} custom-call(s32[1]{0:T(128)} %bitcast.section_ref, bf16[256,768]{1,0:T(8,128)(2,1)S(1)} %get-tuple-element.317.refs_1_.refs_0_, bf16[256,768]{1,0:T(8,128)(2,1)S(1)} %collective-permute-done.44.refs_3_.refs_1_, bf16[3072,6144]{1,0:T(8,128)(2,1)} %bitcast.25, f32[3072,512]{1,0:T(8,128)S(1)} %down_product.8.refs_3_), custom_call_target="tpu_custom_call" | custom-call | tf_op jit(solution)/shard_map/down_product/pallas_call | solution.py:32
  239.8 6.1 %down_product.12 = bf16[128,3072]{1,0:T(8,128)(2,1)S(1)} custom-call(s32[1]{0:T(128)} %bitcast.section_ref, bf16[128,768]{1,0:T(8,128)(2,1)S(1)} %get-tuple-element.324.refs_0_.refs_1_, bf16[128,768]{1,0:T(8,128)(2,1)S(1)} %collective-permute-done.47.refs_1_.refs_4_, bf16[3072,6144]{1,0:T(8,128)(2,1)} %bitcast.26, f32[3072,256]{1,0:T(8,128)S(1)} %down_product.11.refs_3_, ...), custom_call_target="tpu_custom_call" | custom-call | tf_op jit(solution)/shard_map/down_product/pallas_call | solution.py:32
  246.6 1.5 collective-permute-start.49
  248.1 12.7 %collective-permute-done.49.refs_2_ = bf16[256,768]{1,0:T(8,128)(2,1)S(1)} collective-permute-done((bf16[256,768]{1,0:T(8,128)(2,1)S(1)}, bf16[256,768]{1,0:T(8,128)(2,1)S(1)}, u32[]{:S(2)}, u32[]{:S(2)}) %collective-permute-start.49) | collective-permute-done | bytes 393248 | tf_op jit(solution)/shard_map/ppermute | solution.py:400
  261.1 1.4 collective-permute-done.50.refs_5_.refs_1_
  262.5 7.2 %weight_gradient.7 = bf16[3072,6144]{1,0:T(8,128)(2,1)} custom-call(s32[1]{0:T(128)} %bitcast.section_ref, bf16[3072,512]{1,0:T(8,128)(2,1)S(1)} %transposed.1.turned_ref, bf16[256,768]{1,0:T(8,128)(2,1)S(1)} %get-tuple-element.331.refs_0_, bf16[128,768]{1,0:T(8,128)(2,1)S(1)} %get-tuple-element.324.refs_0_.refs_1_, ...), custom_call_target="tpu_custom_call", output_to_operand_aliasing={{}: (8, {})} | custom-call | tf_op jit(solution)/shard_map/weight_gradient/pallas_call | solution.py:32
  269.7 6.1 %down_product.13 = f32[128,3072]{1,0:T(8,128)S(1)} custom-call(s32[1]{0:T(128)} %bitcast.section_ref, bf16[128,768]{1,0:T(8,128)(2,1)S(1)} %get-tuple-element.333.refs_2_.refs_0_, bf16[128,768]{1,0:T(8,128)(2,1)S(1)} %collective-permute-done.50.refs_5_.refs_1_, bf16[3072,6144]{1,0:T(8,128)(2,1)} %bitcast.27, f32[3072,256]{1,0:T(8,128)S(1)} %down_product.11.refs_3_, ...), custom_call_target="tpu_custom_call" | custom-call | tf_op jit(solution)/shard_map/down_product/pallas_call | solution.py:32
  275.8 1.0 fusion.1
  (108 shorter events, 24.7 us)
Async XLA Ops:
  0.6 23.4 %copy-start = (f32[3072]{0:T(1024)S(1)}, f32[3072]{0:T(1024)}, u32[]{:S(2)}) copy-start(f32[3072]{0:T(1024)} %param.6) | copy-start | bytes 36868
  1.9 21.6 %collective-permute-start = (bf16[128,3072]{1,0:T(8,128)(2,1)S(1)}, bf16[128,3072]{1,0:T(8,128)(2,1)S(1)}, u32[]{:S(2)}, u32[]{:S(2)}) collective-permute-start(bf16[128,3072]{1,0:T(8,128)(2,1)S(1)} %broadcast_select_fusion.refs_1_), channel_id=1, source_target_pairs={{0,1},{1,0},{2,3},{3,2},{4,5},{5,4},{6,7},{7,6},{8,9},{9,8},{10,11... | collective-permute-start | bytes 2359304 | tf_op jit(solution)/shard_map/ppermute | solution.py:318
  4.9 19.0 %collective-permute-start.1 = (bf16[128,3072]{1,0:T(8,128)(2,1)S(1)}, bf16[128,3072]{1,0:T(8,128)(2,1)S(1)}, u32[]{:S(2)}, u32[]{:S(2)}) collective-permute-start(bf16[128,3072]{1,0:T(8,128)(2,1)S(1)} %broadcast_select_fusion.refs_1_), channel_id=1, source_target_pairs={{0,2},{1,3},{2,0},{3,1},{4,6},{5,7},{6,4},{7,5},{8,10},{9,11},{10,... | collective-permute-start | bytes 2359304 | tf_op jit(solution)/shard_map/ppermute | solution.py:318
  19.8 3.6 %collective-permute-start.2 = (f32[128,2]{0,1:T(2,128)S(1)}, f32[128,2]{0,1:T(2,128)S(1)}, u32[]{:S(2)}, u32[]{:S(2)}) collective-permute-start(f32[128,2]{0,1:T(2,128)S(1)} %pad_maximum_fusion), channel_id=1, source_target_pairs={{0,1},{1,0},{2,3},{3,2},{4,5},{5,4},{6,7},{7,6},{8,9},{9,8},{10,11... | collective-permute-start | bytes 3080 | tf_op jit(solution)/shard_map/ppermute | solution.py:318
  30.5 1.8 collective-permute-start.3
  30.6 22.8 %collective-permute-start.6 = (bf16[128,3072]{1,0:T(8,128)(2,1)S(1)}, bf16[128,3072]{1,0:T(8,128)(2,1)S(1)}, u32[]{:S(2)}, u32[]{:S(2)}) collective-permute-start(bf16[128,3072]{1,0:T(8,128)(2,1)S(1)} %collective-permute-done.refs_0_), channel_id=1, source_target_pairs={{0,2},{1,3},{2,0},{3,1},{4,6},{5,7},{6,4},{7,5},{8,10},{9,11},{10,... | collective-permute-start | bytes 2359304 | tf_op jit(solution)/shard_map/ppermute | solution.py:318
  32.6 30.9 %collective-permute-start.7 = (bf16[512,768]{1,0:T(8,128)(2,1)S(1)}, bf16[512,768]{1,0:T(8,128)(2,1)S(1)}, u32[]{:S(2)}, u32[]{:S(2)}) collective-permute-start(bf16[512,768]{1,0:T(8,128)(2,1)S(1)} %stacked.9.refs_0_), channel_id=1, source_target_pairs={{0,4},{12,8},{1,5},{13,9},{2,6},{14,10},{3,7},{15,11},{16,20},{28,... | collective-permute-start | bytes 2359304 | tf_op jit(solution)/shard_map/ppermute | solution.py:389
  41.4 1.8 collective-permute-start.4
  41.5 11.9 %collective-permute-start.5 = (f32[256,2]{1,0:T(8,128)S(1)}, f32[256,2]{1,0:T(8,128)S(1)}, u32[]{:S(2)}, u32[]{:S(2)}) collective-permute-start(f32[256,2]{1,0:T(8,128)S(1)} %copy.12.scale_ref), channel_id=1, source_target_pairs={{0,2},{1,3},{2,0},{3,1},{4,6},{5,7},{6,4},{7,5},{8,10},{9,11},{10,... | collective-permute-start | bytes 6152 | tf_op jit(solution)/shard_map/ppermute | solution.py:318
  59.9 4.8 %collective-permute-start.8 = (bf16[256,768]{1,0:T(8,128)(2,1)S(1)}, bf16[256,768]{1,0:T(8,128)(2,1)S(1)}, u32[]{:S(2)}, u32[]{:S(2)}) collective-permute-start(bf16[256,768]{1,0:T(8,128)(2,1)S(1)} %get-tuple-element.194), channel_id=1, source_target_pairs={{0,16},{16,0},{1,17},{17,1},{2,18},{18,2},{3,19},{19,3},{4,20},{20... | collective-permute-start | bytes 1179656 | tf_op jit(solution)/shard_map/ppermute | solution.py:322
  60.0 21.3 %collective-permute-start.9 = (bf16[512,768]{1,0:T(8,128)(2,1)S(1)}, bf16[512,768]{1,0:T(8,128)(2,1)S(1)}, u32[]{:S(2)}, u32[]{:S(2)}) collective-permute-start(bf16[512,768]{1,0:T(8,128)(2,1)S(1)} %stacked.10.refs_0_), channel_id=1, source_target_pairs={{0,4},{12,8},{1,5},{13,9},{2,6},{14,10},{3,7},{15,11},{16,20},{28,... | collective-permute-start | bytes 2359304 | tf_op jit(solution)/shard_map/ppermute | solution.py:389
  63.9 18.5 %collective-permute-start.10 = (bf16[512,768]{1,0:T(8,128)(2,1)S(1)}, bf16[512,768]{1,0:T(8,128)(2,1)S(1)}, u32[]{:S(2)}, u32[]{:S(2)}) collective-permute-start(bf16[512,768]{1,0:T(8,128)(2,1)S(1)} %added.9.refs_1_), channel_id=1, source_target_pairs={{4,8},{8,4},{5,9},{9,5},{6,10},{10,6},{7,11},{11,7},{20,24},{24,20... | collective-permute-start | bytes 2359304 | tf_op jit(solution)/shard_map/ppermute | solution.py:394
  64.9 35.2 %collective-permute-start.12 = (bf16[512,768]{1,0:T(8,128)(2,1)S(1)}, bf16[512,768]{1,0:T(8,128)(2,1)S(1)}, u32[]{:S(2)}, u32[]{:S(2)}) collective-permute-start(bf16[512,768]{1,0:T(8,128)(2,1)S(1)} %stacked.11.refs_0_), channel_id=1, source_target_pairs={{0,4},{12,8},{1,5},{13,9},{2,6},{14,10},{3,7},{15,11},{16,20},{28,... | collective-permute-start | bytes 2359304 | tf_op jit(solution)/shard_map/ppermute | solution.py:389
  74.3 10.5 %collective-permute-start.11 = (bf16[256,768]{1,0:T(8,128)(2,1)S(1)}, bf16[256,768]{1,0:T(8,128)(2,1)S(1)}, u32[]{:S(2)}, u32[]{:S(2)}) collective-permute-start(bf16[256,768]{1,0:T(8,128)(2,1)S(1)} %get-tuple-element.206), channel_id=1, source_target_pairs={{0,16},{16,0},{1,17},{17,1},{2,18},{18,2},{3,19},{19,3},{4,20},{20... | collective-permute-start | bytes 1179656 | tf_op jit(solution)/shard_map/ppermute | solution.py:322
  81.7 19.6 %collective-permute-start.13 = (bf16[512,768]{1,0:T(8,128)(2,1)S(1)}, bf16[512,768]{1,0:T(8,128)(2,1)S(1)}, u32[]{:S(2)}, u32[]{:S(2)}) collective-permute-start(bf16[512,768]{1,0:T(8,128)(2,1)S(1)} %added.10.refs_1_), channel_id=1, source_target_pairs={{4,8},{8,4},{5,9},{9,5},{6,10},{10,6},{7,11},{11,7},{20,24},{24,20... | collective-permute-start | bytes 2359304 | tf_op jit(solution)/shard_map/ppermute | solution.py:394
  83.5 23.3 %collective-permute-start.14 = (bf16[512,768]{1,0:T(8,128)(2,1)S(1)}, bf16[512,768]{1,0:T(8,128)(2,1)S(1)}, u32[]{:S(2)}, u32[]{:S(2)}) collective-permute-start(bf16[512,768]{1,0:T(8,128)(2,1)S(1)} %activated.9.refs_1_), channel_id=1, source_target_pairs={{4,0},{8,12},{5,1},{9,13},{6,2},{10,14},{7,3},{11,15},{20,16},{24,... | collective-permute-start | bytes 2359304 | tf_op jit(solution)/shard_map/ppermute | solution.py:400
  85.0 32.7 %collective-permute-start.16 = (bf16[512,768]{1,0:T(8,128)(2,1)S(1)}, bf16[512,768]{1,0:T(8,128)(2,1)S(1)}, u32[]{:S(2)}, u32[]{:S(2)}) collective-permute-start(bf16[512,768]{1,0:T(8,128)(2,1)S(1)} %stacked.12.refs_0_), channel_id=1, source_target_pairs={{0,4},{12,8},{1,5},{13,9},{2,6},{14,10},{3,7},{15,11},{16,20},{28,... | collective-permute-start | bytes 2359304 | tf_op jit(solution)/shard_map/ppermute | solution.py:389
  100.5 18.4 %collective-permute-start.17 = (bf16[512,768]{1,0:T(8,128)(2,1)S(1)}, bf16[512,768]{1,0:T(8,128)(2,1)S(1)}, u32[]{:S(2)}, u32[]{:S(2)}) collective-permute-start(bf16[512,768]{1,0:T(8,128)(2,1)S(1)} %added.11.refs_1_), channel_id=1, source_target_pairs={{4,8},{8,4},{5,9},{9,5},{6,10},{10,6},{7,11},{11,7},{20,24},{24,20... | collective-permute-start | bytes 2359304 | tf_op jit(solution)/shard_map/ppermute | solution.py:394
  101.2 5.8 %collective-permute-start.15 = (bf16[256,768]{1,0:T(8,128)(2,1)S(1)}, bf16[256,768]{1,0:T(8,128)(2,1)S(1)}, u32[]{:S(2)}, u32[]{:S(2)}) collective-permute-start(bf16[256,768]{1,0:T(8,128)(2,1)S(1)} %get-tuple-element.222), channel_id=1, source_target_pairs={{0,16},{16,0},{1,17},{17,1},{2,18},{18,2},{3,19},{19,3},{4,20},{20... | collective-permute-start | bytes 1179656 | tf_op jit(solution)/shard_map/ppermute | solution.py:322
  102.4 23.1 %collective-permute-start.18 = (bf16[512,768]{1,0:T(8,128)(2,1)S(1)}, bf16[512,768]{1,0:T(8,128)(2,1)S(1)}, u32[]{:S(2)}, u32[]{:S(2)}) collective-permute-start(bf16[512,768]{1,0:T(8,128)(2,1)S(1)} %activated.10.refs_1_), channel_id=1, source_target_pairs={{4,0},{8,12},{5,1},{9,13},{6,2},{10,14},{7,3},{11,15},{20,16},{24,... | collective-permute-start | bytes 2359304 | tf_op jit(solution)/shard_map/ppermute | solution.py:400
  115.1 20.4 %collective-permute-start.20 = (bf16[512,768]{1,0:T(8,128)(2,1)S(1)}, bf16[512,768]{1,0:T(8,128)(2,1)S(1)}, u32[]{:S(2)}, u32[]{:S(2)}) collective-permute-start(bf16[512,768]{1,0:T(8,128)(2,1)S(1)} %stacked.13.refs_0_), channel_id=1, source_target_pairs={{0,4},{12,8},{1,5},{13,9},{2,6},{14,10},{3,7},{15,11},{16,20},{28,... | collective-permute-start | bytes 2359304 | tf_op jit(solution)/shard_map/ppermute | solution.py:389
  118.2 18.5 %collective-permute-start.21 = (bf16[512,768]{1,0:T(8,128)(2,1)S(1)}, bf16[512,768]{1,0:T(8,128)(2,1)S(1)}, u32[]{:S(2)}, u32[]{:S(2)}) collective-permute-start(bf16[512,768]{1,0:T(8,128)(2,1)S(1)} %added.12.refs_1_), channel_id=1, source_target_pairs={{4,8},{8,4},{5,9},{9,5},{6,10},{10,6},{7,11},{11,7},{20,24},{24,20... | collective-permute-start | bytes 2359304 | tf_op jit(solution)/shard_map/ppermute | solution.py:394
  119.9 22.0 %collective-permute-start.22 = (bf16[512,768]{1,0:T(8,128)(2,1)S(1)}, bf16[512,768]{1,0:T(8,128)(2,1)S(1)}, u32[]{:S(2)}, u32[]{:S(2)}) collective-permute-start(bf16[512,768]{1,0:T(8,128)(2,1)S(1)} %activated.11.refs_1_), channel_id=1, source_target_pairs={{4,0},{8,12},{5,1},{9,13},{6,2},{10,14},{7,3},{11,15},{20,16},{24,... | collective-permute-start | bytes 2359304 | tf_op jit(solution)/shard_map/ppermute | solution.py:400
  121.2 4.5 %collective-permute-start.19 = (bf16[256,768]{1,0:T(8,128)(2,1)S(1)}, bf16[256,768]{1,0:T(8,128)(2,1)S(1)}, u32[]{:S(2)}, u32[]{:S(2)}) collective-permute-start(bf16[256,768]{1,0:T(8,128)(2,1)S(1)} %get-tuple-element.240), channel_id=1, source_target_pairs={{0,16},{16,0},{1,17},{17,1},{2,18},{18,2},{3,19},{19,3},{4,20},{20... | collective-permute-start | bytes 1179656 | tf_op jit(solution)/shard_map/ppermute | solution.py:322
  125.4 16.9 %collective-permute-start.23 = (bf16[256,768]{1,0:T(8,128)(2,1)S(1)}, bf16[256,768]{1,0:T(8,128)(2,1)S(1)}, u32[]{:S(2)}, u32[]{:S(2)}) collective-permute-start(bf16[256,768]{1,0:T(8,128)(2,1)S(1)} %get-tuple-element.253), channel_id=1, source_target_pairs={{0,16},{16,0},{1,17},{17,1},{2,18},{18,2},{3,19},{19,3},{4,20},{20... | collective-permute-start | bytes 1179656 | tf_op jit(solution)/shard_map/ppermute | solution.py:322
  126.0 30.1 %collective-permute-start.26 = (bf16[512,768]{1,0:T(8,128)(2,1)S(1)}, bf16[512,768]{1,0:T(8,128)(2,1)S(1)}, u32[]{:S(2)}, u32[]{:S(2)}) collective-permute-start(bf16[512,768]{1,0:T(8,128)(2,1)S(1)} %stacked.14.refs_0_), channel_id=1, source_target_pairs={{0,4},{12,8},{1,5},{13,9},{2,6},{14,10},{3,7},{15,11},{16,20},{28,... | collective-permute-start | bytes 2359304 | tf_op jit(solution)/shard_map/ppermute | solution.py:389
  136.0 21.3 %collective-permute-start.27 = (bf16[512,768]{1,0:T(8,128)(2,1)S(1)}, bf16[512,768]{1,0:T(8,128)(2,1)S(1)}, u32[]{:S(2)}, u32[]{:S(2)}) collective-permute-start(bf16[512,768]{1,0:T(8,128)(2,1)S(1)} %added.13.refs_1_), channel_id=1, source_target_pairs={{4,8},{8,4},{5,9},{9,5},{6,10},{10,6},{7,11},{11,7},{20,24},{24,20... | collective-permute-start | bytes 2359304 | tf_op jit(solution)/shard_map/ppermute | solution.py:394
  137.7 21.9 %collective-permute-start.28 = (bf16[512,768]{1,0:T(8,128)(2,1)S(1)}, bf16[512,768]{1,0:T(8,128)(2,1)S(1)}, u32[]{:S(2)}, u32[]{:S(2)}) collective-permute-start(bf16[512,768]{1,0:T(8,128)(2,1)S(1)} %activated.12.refs_1_), channel_id=1, source_target_pairs={{4,0},{8,12},{5,1},{9,13},{6,2},{10,14},{7,3},{11,15},{20,16},{24,... | collective-permute-start | bytes 2359304 | tf_op jit(solution)/shard_map/ppermute | solution.py:400
  142.0 1.7 collective-permute-start.25
  142.3 5.9 %collective-permute-start.24 = (bf16[256,768]{1,0:T(8,128)(2,1)S(1)}, bf16[256,768]{1,0:T(8,128)(2,1)S(1)}, u32[]{:S(2)}, u32[]{:S(2)}) collective-permute-start(bf16[256,768]{1,0:T(8,128)(2,1)S(1)} %get-tuple-element.256), channel_id=1, source_target_pairs={{0,16},{16,0},{1,17},{17,1},{2,18},{18,2},{3,19},{19,3},{4,20},{20... | collective-permute-start | bytes 1179656 | tf_op jit(solution)/shard_map/ppermute | solution.py:322
  143.7 26.5 %collective-permute-start.32 = (bf16[512,768]{1,0:T(8,128)(2,1)S(1)}, bf16[512,768]{1,0:T(8,128)(2,1)S(1)}, u32[]{:S(2)}, u32[]{:S(2)}) collective-permute-start(bf16[512,768]{1,0:T(8,128)(2,1)S(1)} %stacked.15.refs_0_), channel_id=1, source_target_pairs={{0,4},{12,8},{1,5},{13,9},{2,6},{14,10},{3,7},{15,11},{16,20},{28,... | collective-permute-start | bytes 2359304 | tf_op jit(solution)/shard_map/ppermute | solution.py:389
  148.2 12.3 %collective-permute-start.29 = (bf16[128,768]{1,0:T(8,128)(2,1)S(1)}, bf16[128,768]{1,0:T(8,128)(2,1)S(1)}, u32[]{:S(2)}, u32[]{:S(2)}) collective-permute-start(bf16[128,768]{1,0:T(8,128)(2,1)S(1)} %get-tuple-element.269), channel_id=1, source_target_pairs={{0,16},{16,0},{1,17},{17,1},{2,18},{18,2},{3,19},{19,3},{4,20},{20... | collective-permute-start | bytes 589832 | tf_op jit(solution)/shard_map/ppermute | solution.py:322
  156.6 14.7 %collective-permute-start.33 = (bf16[512,768]{1,0:T(8,128)(2,1)S(1)}, bf16[512,768]{1,0:T(8,128)(2,1)S(1)}, u32[]{:S(2)}, u32[]{:S(2)}) collective-permute-start(bf16[512,768]{1,0:T(8,128)(2,1)S(1)} %added.14.refs_1_), channel_id=1, source_target_pairs={{4,8},{8,4},{5,9},{9,5},{6,10},{10,6},{7,11},{11,7},{20,24},{24,20... | collective-permute-start | bytes 2359304 | tf_op jit(solution)/shard_map/ppermute | solution.py:394
  158.3 21.8 %collective-permute-start.34 = (bf16[512,768]{1,0:T(8,128)(2,1)S(1)}, bf16[512,768]{1,0:T(8,128)(2,1)S(1)}, u32[]{:S(2)}, u32[]{:S(2)}) collective-permute-start(bf16[512,768]{1,0:T(8,128)(2,1)S(1)} %activated.13.refs_1_), channel_id=1, source_target_pairs={{4,0},{8,12},{5,1},{9,13},{6,2},{10,14},{7,3},{11,15},{20,16},{24,... | collective-permute-start | bytes 2359304 | tf_op jit(solution)/shard_map/ppermute | solution.py:400
  159.7 1.9 collective-permute-start.31
  160.5 1.8 collective-permute-start.30
  170.6 27.3 %collective-permute-start.38 = (bf16[512,768]{1,0:T(8,128)(2,1)S(1)}, bf16[512,768]{1,0:T(8,128)(2,1)S(1)}, u32[]{:S(2)}, u32[]{:S(2)}) collective-permute-start(bf16[512,768]{1,0:T(8,128)(2,1)S(1)} %added.15.refs_1_), channel_id=1, source_target_pairs={{4,8},{8,4},{5,9},{9,5},{6,10},{10,6},{7,11},{11,7},{20,24},{24,20... | collective-permute-start | bytes 2359304 | tf_op jit(solution)/shard_map/ppermute | solution.py:394
  172.3 27.9 %collective-permute-start.39 = (bf16[512,768]{1,0:T(8,128)(2,1)S(1)}, bf16[512,768]{1,0:T(8,128)(2,1)S(1)}, u32[]{:S(2)}, u32[]{:S(2)}) collective-permute-start(bf16[512,768]{1,0:T(8,128)(2,1)S(1)} %activated.14.refs_1_), channel_id=1, source_target_pairs={{4,0},{8,12},{5,1},{9,13},{6,2},{10,14},{7,3},{11,15},{20,16},{24,... | collective-permute-start | bytes 2359304 | tf_op jit(solution)/shard_map/ppermute | solution.py:400
  180.5 3.9 %collective-permute-start.36 = (bf16[256,768]{1,0:T(8,128)(2,1)S(1)}, bf16[256,768]{1,0:T(8,128)(2,1)S(1)}, u32[]{:S(2)}, u32[]{:S(2)}) collective-permute-start(bf16[256,768]{1,0:T(8,128)(2,1)S(1)} %get-tuple-element.288), channel_id=1, source_target_pairs={{0,16},{16,0},{1,17},{17,1},{2,18},{18,2},{3,19},{19,3},{4,20},{20... | collective-permute-start | bytes 1179656 | tf_op jit(solution)/shard_map/ppermute | solution.py:322
  180.6 17.1 %collective-permute-start.37 = (bf16[256,768]{1,0:T(8,128)(2,1)S(1)}, bf16[256,768]{1,0:T(8,128)(2,1)S(1)}, u32[]{:S(2)}, u32[]{:S(2)}) collective-permute-start(bf16[256,768]{1,0:T(8,128)(2,1)S(1)} %stacked.16.refs_0_), channel_id=1, source_target_pairs={{0,4},{12,8},{1,5},{13,9},{2,6},{14,10},{3,7},{15,11},{16,20},{28,... | collective-permute-start | bytes 1179656 | tf_op jit(solution)/shard_map/ppermute | solution.py:389
  182.7 1.5 collective-permute-start.35
  198.9 22.1 %collective-permute-start.41 = (bf16[512,768]{1,0:T(8,128)(2,1)S(1)}, bf16[512,768]{1,0:T(8,128)(2,1)S(1)}, u32[]{:S(2)}, u32[]{:S(2)}) collective-permute-start(bf16[512,768]{1,0:T(8,128)(2,1)S(1)} %activated.15.refs_1_), channel_id=1, source_target_pairs={{4,0},{8,12},{5,1},{9,13},{6,2},{10,14},{7,3},{11,15},{20,16},{24,... | collective-permute-start | bytes 2359304 | tf_op jit(solution)/shard_map/ppermute | solution.py:400
  200.6 5.4 %collective-permute-start.40 = (bf16[256,768]{1,0:T(8,128)(2,1)S(1)}, bf16[256,768]{1,0:T(8,128)(2,1)S(1)}, u32[]{:S(2)}, u32[]{:S(2)}) collective-permute-start(bf16[256,768]{1,0:T(8,128)(2,1)S(1)} %get-tuple-element.295), channel_id=1, source_target_pairs={{0,16},{16,0},{1,17},{17,1},{2,18},{18,2},{3,19},{19,3},{4,20},{20... | collective-permute-start | bytes 1179656 | tf_op jit(solution)/shard_map/ppermute | solution.py:322
  200.9 20.6 %collective-permute-start.42 = (bf16[256,768]{1,0:T(8,128)(2,1)S(1)}, bf16[256,768]{1,0:T(8,128)(2,1)S(1)}, u32[]{:S(2)}, u32[]{:S(2)}) collective-permute-start(bf16[256,768]{1,0:T(8,128)(2,1)S(1)} %stacked.17.refs_0_), channel_id=1, source_target_pairs={{0,4},{12,8},{1,5},{13,9},{2,6},{14,10},{3,7},{15,11},{16,20},{28,... | collective-permute-start | bytes 1179656 | tf_op jit(solution)/shard_map/ppermute | solution.py:389
  205.3 16.4 %collective-permute-start.43 = (bf16[256,768]{1,0:T(8,128)(2,1)S(1)}, bf16[256,768]{1,0:T(8,128)(2,1)S(1)}, u32[]{:S(2)}, u32[]{:S(2)}) collective-permute-start(bf16[256,768]{1,0:T(8,128)(2,1)S(1)} %added.16.refs_1_), channel_id=1, source_target_pairs={{4,8},{8,4},{5,9},{9,5},{6,10},{10,6},{7,11},{11,7},{20,24},{24,20... | collective-permute-start | bytes 1179656 | tf_op jit(solution)/shard_map/ppermute | solution.py:394
  212.2 27.6 %collective-permute-start.48 = (bf16[128,3072]{1,0:T(8,128)(2,1)S(1)}, bf16[128,3072]{1,0:T(8,128)(2,1)S(1)}, u32[]{:S(2)}, u32[]{:S(2)}) collective-permute-start(bf16[128,3072]{1,0:T(8,128)(2,1)S(1)} %get-tuple-element.302), channel_id=1, source_target_pairs={{0,2},{1,3},{2,0},{3,1},{4,6},{5,7},{6,4},{7,5},{8,10},{9,11},{10,... | collective-permute-start | bytes 2359304 | tf_op jit(solution)/shard_map/ppermute | solution.py:318
  221.3 2.9 %collective-permute-start.44 = (bf16[256,768]{1,0:T(8,128)(2,1)S(1)}, bf16[256,768]{1,0:T(8,128)(2,1)S(1)}, u32[]{:S(2)}, u32[]{:S(2)}) collective-permute-start(bf16[256,768]{1,0:T(8,128)(2,1)S(1)} %get-tuple-element.315), channel_id=1, source_target_pairs={{0,16},{16,0},{1,17},{17,1},{2,18},{18,2},{3,19},{19,3},{4,20},{20... | collective-permute-start | bytes 1179656 | tf_op jit(solution)/shard_map/ppermute | solution.py:322
  222.3 15.3 %collective-permute-start.45 = (bf16[256,768]{1,0:T(8,128)(2,1)S(1)}, bf16[256,768]{1,0:T(8,128)(2,1)S(1)}, u32[]{:S(2)}, u32[]{:S(2)}) collective-permute-start(bf16[256,768]{1,0:T(8,128)(2,1)S(1)} %activated.16.refs_1_), channel_id=1, source_target_pairs={{4,0},{8,12},{5,1},{9,13},{6,2},{10,14},{7,3},{11,15},{20,16},{24,... | collective-permute-start | bytes 1179656 | tf_op jit(solution)/shard_map/ppermute | solution.py:400
  223.6 15.7 %collective-permute-start.46 = (bf16[256,768]{1,0:T(8,128)(2,1)S(1)}, bf16[256,768]{1,0:T(8,128)(2,1)S(1)}, u32[]{:S(2)}, u32[]{:S(2)}) collective-permute-start(bf16[256,768]{1,0:T(8,128)(2,1)S(1)} %added.17.refs_1_), channel_id=1, source_target_pairs={{4,8},{8,4},{5,9},{9,5},{6,10},{10,6},{7,11},{11,7},{20,24},{24,20... | collective-permute-start | bytes 1179656 | tf_op jit(solution)/shard_map/ppermute | solution.py:394
  237.8 2.1 collective-permute-start.47
  238.3 31.4 %collective-permute-start.51 = (bf16[128,3072]{1,0:T(8,128)(2,1)S(1)}, bf16[128,3072]{1,0:T(8,128)(2,1)S(1)}, u32[]{:S(2)}, u32[]{:S(2)}) collective-permute-start(bf16[128,3072]{1,0:T(8,128)(2,1)S(1)} %get-tuple-element.303), channel_id=1, source_target_pairs={{0,2},{1,3},{2,0},{3,1},{4,6},{5,7},{6,4},{7,5},{8,10},{9,11},{10,... | collective-permute-start | bytes 2359304 | tf_op jit(solution)/shard_map/ppermute | solution.py:318
  245.9 29.9 %collective-permute-start.52 = (bf16[128,3072]{1,0:T(8,128)(2,1)S(1)}, bf16[128,3072]{1,0:T(8,128)(2,1)S(1)}, u32[]{:S(2)}, u32[]{:S(2)}) collective-permute-start(bf16[128,3072]{1,0:T(8,128)(2,1)S(1)} %down_product.12), channel_id=1, source_target_pairs={{0,1},{1,0},{2,3},{3,2},{4,5},{5,4},{6,7},{7,6},{8,9},{9,8},{10,11... | collective-permute-start | bytes 2359304 | tf_op jit(solution)/shard_map/ppermute | solution.py:318
  246.6 14.2 %collective-permute-start.49 = (bf16[256,768]{1,0:T(8,128)(2,1)S(1)}, bf16[256,768]{1,0:T(8,128)(2,1)S(1)}, u32[]{:S(2)}, u32[]{:S(2)}) collective-permute-start(bf16[256,768]{1,0:T(8,128)(2,1)S(1)} %activated.17.refs_1_), channel_id=1, source_target_pairs={{4,0},{8,12},{5,1},{9,13},{6,2},{10,14},{7,3},{11,15},{20,16},{24,... | collective-permute-start | bytes 1179656 | tf_op jit(solution)/shard_map/ppermute | solution.py:400
  261.0 1.5 collective-permute-start.50

commit v9 on v7

--- a/solution.py
+++ b/solution.py
@@ -473,15 +473,15 @@
         elif far_part == parts - 1:
             sent_far = go_down(far_part, [FAR], far_sum, FAR if far_part == 2 else 0, [jnp.bfloat16] * 2)
             arrived = [from_peer(value, across) for value in sent_far["value"]]
-        if t == 6:
+        if t == count - 1:
             go_gradient(1)
         if 2 <= near_part < parts - 1:
-            go_gradient(near_part)
             near_sum = go_down(near_part, [NEAR], near_sum, NEAR if near_part == 2 else 0)
             near_sum["value"], arrived = lax.optimization_barrier((near_sum["value"], arrived))
     column = NEAR if parts == 3 else 0
     sent_near = go_down(parts - 1, [NEAR], near_sum, column, [jnp.bfloat16, jnp.float32], arrived)
-    go_gradient(parts - 1)
+    for part in range(2, parts):
+        go_gradient(part)
 
     own = sent_near["value"][1]
     blocks = {0: own.astype(jnp.bfloat16), 1: sent_near["value"][0]}

time: 272 us -> 268 us (0.985)
  waiting for transfers between devices: 71.1 us -> 66.2 us
    ppermute x8, waiting for transfers between devices: 26.8 us -> 23.2 us  [from_peer(): return lax.ppermute(value, 'mp', [(i, i ^ by) for i in range(peers)])]
  transfers between devices with their start and end apart: 48 -> 48, of which waited for: 20 -> 19; matrix products, arithmetic and copies ran while one was open for 1% -> 1% of each run, Pallas kernels for 44% -> 44%
where the time goes in v9:
time: 268 us; the launch traced here: 267 us
  Pallas kernels  125 us (47%)
  waiting for transfers between devices  66.2 us (25%)
  starting transfers between devices  57.9 us (22%)
  blocking collectives  12 us (4%)
  other arithmetic  3.71 us (1%)
    pallas_call x51, Pallas kernels, call(): pl.pallas_call(kernel, grid_spec=pltpu.PrefetchScalarGridSpec(num_scalar_...  125 us
    ppermute x8, starting transfers between devices, inward(): lax.ppermute(value, 'dp', [(hop, hop + 1), (line - 1 - hop, line - 2 - ho...  29 us
    ppermute x8, waiting for transfers between devices, outward(): lax.ppermute(value, 'dp', [(hop + 1, hop), (line - 2 - hop, line - 1 - ho...  25.1 us
    ppermute x8, waiting for transfers between devices, from_peer(): return lax.ppermute(value, 'mp', [(i, i ^ by) for i in range(peers)])  23.2 us
    psum x1, blocking collectives, local(): lax.psum((jnp.sum(values, 1), jnp.sum(values * values, 1)), 'dp')  12 us
    ppermute x8, starting transfers between devices, from_peer(): return lax.ppermute(value, 'mp', [(i, i ^ by) for i in range(peers)])  10.8 us
    ppermute x8, starting transfers between devices, outward(): lax.ppermute(value, 'dp', [(hop + 1, hop), (line - 2 - hop, line - 1 - ho...  10.7 us
    ppermute x8, waiting for transfers between devices, inward(): lax.ppermute(value, 'dp', [(hop, hop + 1), (line - 1 - hop, line - 2 - ho...  9.7 us
  transfers between devices with their start and end apart: 48, of which 19 were waited for; matrix products, arithmetic and copies ran while one was open for 1% of the time, Pallas kernels for 44%

profile of v9, /device:TPU:0, one launch (start us, length us, event | category | flops | bytes accessed | tf_op | source)
XLA Modules:
  0.0 266.9 jit_solution(14990514993409872241)
XLA Ops:
  0.7 1.2 broadcast_select_fusion.refs_1_
  1.9 3.0 %collective-permute-start.1 = (bf16[128,3072]{1,0:T(8,128)(2,1)S(1)}, bf16[128,3072]{1,0:T(8,128)(2,1)S(1)}, u32[]{:S(2)}, u32[]{:S(2)}) collective-permute-start(bf16[128,3072]{1,0:T(8,128)(2,1)S(1)} %broadcast_select_fusion.refs_1_), channel_id=1, source_target_pairs={{0,2},{1,3},{2,0},{3,1},{4,6},{5,7},{6,4},{7,5},{8,10},{9,11},{10,... | collective-permute-start | bytes 2359304 | tf_op jit(solution)/shard_map/ppermute | solution.py:317
  4.9 1.5 collective-permute-start
  6.4 1.4 convert_reduce_fusion
  7.8 12.0 %all-reduce = (f32[128]{0:T(128)S(1)}, f32[128]{0:T(128)S(1)}) all-reduce(f32[128]{0:T(128)S(1)} %get-tuple-element.318, f32[128]{0:T(128)S(1)} %get-tuple-element.317), channel_id=1, replica_groups=mesh['section'=2,'dp'=4,'mp'=4] {'dp'}, use_global_device_ids=true, to_apply=%region_3.4 | all-reduce | flops 256 | bytes 2048 | tf_op jit(solution)/shard_map/psum | solution.py:359
  20.4 3.6 %collective-permute-done.2 = f32[128,2]{0,1:T(2,128)S(1)} collective-permute-done((f32[128,2]{0,1:T(2,128)S(1)}, f32[128,2]{0,1:T(2,128)S(1)}, u32[]{:S(2)}, u32[]{:S(2)}) %collective-permute-start.2) | collective-permute-done | bytes 1056 | tf_op jit(solution)/shard_map/ppermute | solution.py:317
  24.6 1.2 normalize.2.rows_ref.refs_2_
  25.8 5.3 %up_product.6 = (bf16[256,768]{1,0:T(8,128)(2,1)S(1)}, bf16[256,768]{1,0:T(8,128)(2,1)S(1)}) custom-call(s32[1]{0:T(128)} %bitcast.section_ref, bf16[512,3072]{1,0:T(8,128)(2,1)S(1)} %normalize.2.rows_ref.refs_2_, bf16[3072,6144]{1,0:T(8,128)(2,1)} %bitcast.15), custom_call_target="tpu_custom_call" | custom-call | tf_op jit(solution)/shard_map/up_product/pallas_call | solution.py:32
  31.1 1.7 collective-permute-done.3.refs_1_
  33.1 3.7 %collective-permute-start.6 = (bf16[512,768]{1,0:T(8,128)(2,1)S(1)}, bf16[512,768]{1,0:T(8,128)(2,1)S(1)}, u32[]{:S(2)}, u32[]{:S(2)}) collective-permute-start(bf16[512,768]{1,0:T(8,128)(2,1)S(1)} %stacked.8.refs_0_), channel_id=1, source_target_pairs={{0,4},{12,8},{1,5},{13,9},{2,6},{14,10},{3,7},{15,11},{16,20},{28,... | collective-permute-start | bytes 2359304 | tf_op jit(solution)/shard_map/ppermute | solution.py:388
  36.8 1.6 collective-permute-start.4
  38.4 5.2 %up_product.7 = (bf16[256,768]{1,0:T(8,128)(2,1)S(1)}, bf16[256,768]{1,0:T(8,128)(2,1)S(1)}) custom-call(s32[1]{0:T(128)} %bitcast.section_ref, bf16[512,3072]{1,0:T(8,128)(2,1)S(1)} %normalize.2.rows_ref.refs_2_, bf16[3072,6144]{1,0:T(8,128)(2,1)} %bitcast.16), custom_call_target="tpu_custom_call" | custom-call | tf_op jit(solution)/shard_map/up_product/pallas_call | solution.py:32
  43.6 1.5 collective-permute-done.4.scale_ref
  45.1 1.2 normalize.3.rows_ref.value_ref
  46.3 5.3 %up_product.8 = (bf16[256,768]{1,0:T(8,128)(2,1)S(1)}, bf16[256,768]{1,0:T(8,128)(2,1)S(1)}) custom-call(s32[1]{0:T(128)} %bitcast.section_ref, bf16[512,3072]{1,0:T(8,128)(2,1)S(1)} %normalize.3.rows_ref.value_ref, bf16[3072,6144]{1,0:T(8,128)(2,1)} %bitcast.17), custom_call_target="tpu_custom_call" | custom-call | tf_op jit(solution)/shard_map/up_product/pallas_call | solution.py:32
  51.6 2.2 collective-permute-done.6.refs_1_
  54.5 4.4 %collective-permute-start.9 = (bf16[512,768]{1,0:T(8,128)(2,1)S(1)}, bf16[512,768]{1,0:T(8,128)(2,1)S(1)}, u32[]{:S(2)}, u32[]{:S(2)}) collective-permute-start(bf16[512,768]{1,0:T(8,128)(2,1)S(1)} %stacked.9.refs_0_), channel_id=1, source_target_pairs={{0,4},{12,8},{1,5},{13,9},{2,6},{14,10},{3,7},{15,11},{16,20},{28,... | collective-permute-start | bytes 2359304 | tf_op jit(solution)/shard_map/ppermute | solution.py:388
  61.0 5.3 %up_product.9 = (bf16[256,768]{1,0:T(8,128)(2,1)S(1)}, bf16[256,768]{1,0:T(8,128)(2,1)S(1)}) custom-call(s32[1]{0:T(128)} %bitcast.section_ref, bf16[512,3072]{1,0:T(8,128)(2,1)S(1)} %normalize.3.rows_ref.value_ref, bf16[3072,6144]{1,0:T(8,128)(2,1)} %bitcast.18), custom_call_target="tpu_custom_call" | custom-call | tf_op jit(solution)/shard_map/up_product/pallas_call | solution.py:32
  66.2 3.1 %collective-permute-start.12 = (bf16[512,768]{1,0:T(8,128)(2,1)S(1)}, bf16[512,768]{1,0:T(8,128)(2,1)S(1)}, u32[]{:S(2)}, u32[]{:S(2)}) collective-permute-start(bf16[512,768]{1,0:T(8,128)(2,1)S(1)} %stacked.10.refs_0_), channel_id=1, source_target_pairs={{0,4},{12,8},{1,5},{13,9},{2,6},{14,10},{3,7},{15,11},{16,20},{28,... | collective-permute-start | bytes 2359304 | tf_op jit(solution)/shard_map/ppermute | solution.py:388
  69.3 7.5 %collective-permute-done.9.refs_1_ = bf16[512,768]{1,0:T(8,128)(2,1)S(1)} collective-permute-done((bf16[512,768]{1,0:T(8,128)(2,1)S(1)}, bf16[512,768]{1,0:T(8,128)(2,1)S(1)}, u32[]{:S(2)}, u32[]{:S(2)}) %collective-permute-start.9) | collective-permute-done | bytes 786464 | tf_op jit(solution)/shard_map/ppermute | solution.py:388
  78.1 1.0 activated.8.refs_1_
  79.1 1.3 collective-permute-start.14
  80.7 7.3 %collective-permute-start.16 = (bf16[512,768]{1,0:T(8,128)(2,1)S(1)}, bf16[512,768]{1,0:T(8,128)(2,1)S(1)}, u32[]{:S(2)}, u32[]{:S(2)}) collective-permute-start(bf16[512,768]{1,0:T(8,128)(2,1)S(1)} %stacked.11.refs_0_), channel_id=1, source_target_pairs={{0,4},{12,8},{1,5},{13,9},{2,6},{14,10},{3,7},{15,11},{16,20},{28,... | collective-permute-start | bytes 2359304 | tf_op jit(solution)/shard_map/ppermute | solution.py:388
  87.9 7.8 %up_product.10 = (bf16[256,768]{1,0:T(8,128)(2,1)S(1)}, bf16[256,768]{1,0:T(8,128)(2,1)S(1)}, bf16[256,768]{1,0:T(8,128)(2,1)S(1)}, bf16[256,768]{1,0:T(8,128)(2,1)S(1)}) custom-call(s32[1]{0:T(128)} %bitcast.section_ref, bf16[512,3072]{1,0:T(8,128)(2,1)S(1)} %normalize.3.rows_ref.value_ref, bf16[3072,6144]{1,0:T(8,128)(2,1)} %bitcast.19), custom_call_target="tpu_custom_call" | custom-call | tf_op jit(solution)/shard_map/up_product/pallas_call | solution.py:32
  98.2 1.5 collective-permute-start.18
  99.6 4.2 %collective-permute-done.14.refs_2_ = bf16[512,768]{1,0:T(8,128)(2,1)S(1)} collective-permute-done((bf16[512,768]{1,0:T(8,128)(2,1)S(1)}, bf16[512,768]{1,0:T(8,128)(2,1)S(1)}, u32[]{:S(2)}, u32[]{:S(2)}) %collective-permute-start.14) | collective-permute-done | bytes 786464 | tf_op jit(solution)/shard_map/ppermute | solution.py:399
  104.4 7.8 %up_product.11 = (bf16[256,768]{1,0:T(8,128)(2,1)S(1)}, bf16[256,768]{1,0:T(8,128)(2,1)S(1)}, bf16[256,768]{1,0:T(8,128)(2,1)S(1)}, bf16[256,768]{1,0:T(8,128)(2,1)S(1)}) custom-call(s32[1]{0:T(128)} %bitcast.section_ref, bf16[512,3072]{1,0:T(8,128)(2,1)S(1)} %normalize.3.rows_ref.value_ref, bf16[3072,6144]{1,0:T(8,128)(2,1)} %bitcast.20), custom_call_target="tpu_custom_call" | custom-call | tf_op jit(solution)/shard_map/up_product/pallas_call | solution.py:32
  112.3 1.5 collective-permute-start.22
  114.9 1.0 activated.10.refs_1_
  116.0 1.3 collective-permute-start.24
  117.3 3.4 %collective-permute-done.18.refs_2_ = bf16[512,768]{1,0:T(8,128)(2,1)S(1)} collective-permute-done((bf16[512,768]{1,0:T(8,128)(2,1)S(1)}, bf16[512,768]{1,0:T(8,128)(2,1)S(1)}, u32[]{:S(2)}, u32[]{:S(2)}) %collective-permute-start.18) | collective-permute-done | bytes 786464 | tf_op jit(solution)/shard_map/ppermute | solution.py:399
  121.8 1.4 transposed.1.turned_ref
  123.3 1.5 collective-permute-start.27
  124.8 7.8 %down_product.6.refs_5_ = f32[3072,512]{1,0:T(8,128)S(1)} custom-call(s32[1]{0:T(128)} %bitcast.section_ref, bf16[256,768]{1,0:T(8,128)(2,1)S(1)} %get-tuple-element.249.refs_0_, bf16[256,768]{1,0:T(8,128)(2,1)S(1)} %get-tuple-element.251.refs_1_, bf16[256,768]{1,0:T(8,128)(2,1)S(1)} %collective-permute-done.20.refs_2_, ...), custom_call_target="tpu_custom_call" | custom-call | tf_op jit(solution)/shard_map/down_product/pallas_call | solution.py:32
  133.9 1.0 activated.11.refs_1_
  134.9 1.3 collective-permute-start.29
  136.2 1.4 collective-permute-done.24.refs_2_
  138.3 4.1 %collective-permute-start.32 = (bf16[512,768]{1,0:T(8,128)(2,1)S(1)}, bf16[512,768]{1,0:T(8,128)(2,1)S(1)}, u32[]{:S(2)}, u32[]{:S(2)}) collective-permute-start(bf16[512,768]{1,0:T(8,128)(2,1)S(1)} %stacked.14.refs_0_), channel_id=1, source_target_pairs={{0,4},{12,8},{1,5},{13,9},{2,6},{14,10},{3,7},{15,11},{16,20},{28,... | collective-permute-start | bytes 2359304 | tf_op jit(solution)/shard_map/ppermute | solution.py:388
  142.4 7.2 %weight_gradient.4.refs_4_ = bf16[3072,6144]{1,0:T(8,128)(2,1)} custom-call(s32[1]{0:T(128)} %bitcast.section_ref, bf16[3072,512]{1,0:T(8,128)(2,1)S(1)} %transposed.1.turned_ref, bf16[256,768]{1,0:T(8,128)(2,1)S(1)} %get-tuple-element.249.refs_0_, bf16[256,768]{1,0:T(8,128)(2,1)S(1)} %get-tuple-element.251.refs_1_, ...), custom_call_target="tpu_custom_call" | custom-call | tf_op jit(solution)/shard_map/weight_gradient/pallas_call | solution.py:32
  151.8 1.3 collective-permute-start.34
  153.2 4.4 %collective-permute-done.29.refs_2_ = bf16[512,768]{1,0:T(8,128)(2,1)S(1)} collective-permute-done((bf16[512,768]{1,0:T(8,128)(2,1)S(1)}, bf16[512,768]{1,0:T(8,128)(2,1)S(1)}, u32[]{:S(2)}, u32[]{:S(2)}) %collective-permute-start.29) | collective-permute-done | bytes 786464 | tf_op jit(solution)/shard_map/ppermute | solution.py:399
  158.3 3.4 %collective-permute-start.36 = (bf16[512,768]{1,0:T(8,128)(2,1)S(1)}, bf16[512,768]{1,0:T(8,128)(2,1)S(1)}, u32[]{:S(2)}, u32[]{:S(2)}) collective-permute-start(bf16[512,768]{1,0:T(8,128)(2,1)S(1)} %stacked.15.refs_0_), channel_id=1, source_target_pairs={{0,4},{12,8},{1,5},{13,9},{2,6},{14,10},{3,7},{15,11},{16,20},{28,... | collective-permute-start | bytes 2359304 | tf_op jit(solution)/shard_map/ppermute | solution.py:388
  161.7 7.8 %down_product.7.refs_3_ = f32[3072,512]{1,0:T(8,128)S(1)} custom-call(s32[1]{0:T(128)} %bitcast.section_ref, bf16[256,768]{1,0:T(8,128)(2,1)S(1)} %get-tuple-element.291.refs_0_, bf16[256,768]{1,0:T(8,128)(2,1)S(1)} %get-tuple-element.265.refs_1_, bf16[256,768]{1,0:T(8,128)(2,1)S(1)} %collective-permute-done.31.refs_2_, ...), custom_call_target="tpu_custom_call" | custom-call | tf_op jit(solution)/shard_map/down_product/pallas_call | solution.py:32
  170.7 1.0 activated.13.refs_1_
  171.8 1.5 collective-permute-start.38
  174.6 1.7 collective-permute-done.35.refs_1_.refs_2_
  176.3 6.0 %down_product.8.refs_3_ = f32[3072,256]{1,0:T(8,128)S(1)} custom-call(s32[1]{0:T(128)} %bitcast.section_ref, bf16[256,768]{1,0:T(8,128)(2,1)S(1)} %get-tuple-element.312.refs_0_, bf16[256,768]{1,0:T(8,128)(2,1)S(1)} %collective-permute-done.35.refs_1_.refs_2_, bf16[3072,6144]{1,0:T(8,128)(2,1)} %bitcast.23, f32[3072,512]{1,0:T(8,128)S(1)} %down_product.7.refs_3_), custom_call_target="tpu_custom_call" | custom-call | tf_op jit(solution)/shard_map/down_product/pallas_call | solution.py:32
  184.6 8.4 %collective-permute-done.38.refs_2_ = bf16[512,768]{1,0:T(8,128)(2,1)S(1)} collective-permute-done((bf16[512,768]{1,0:T(8,128)(2,1)S(1)}, bf16[512,768]{1,0:T(8,128)(2,1)S(1)}, u32[]{:S(2)}, u32[]{:S(2)}) %collective-permute-start.38) | collective-permute-done | bytes 786464 | tf_op jit(solution)/shard_map/ppermute | solution.py:399
  193.4 1.3 collective-permute-start.41
  195.1 6.2 %down_product.9 = (bf16[128,3072]{1,0:T(8,128)(2,1)S(1)}, bf16[128,3072]{1,0:T(8,128)(2,1)S(1)}) custom-call(s32[1]{0:T(128)} %bitcast.section_ref, bf16[256,768]{1,0:T(8,128)(2,1)S(1)} %get-tuple-element.315.refs_0_, bf16[256,768]{1,0:T(8,128)(2,1)S(1)} %collective-permute-done.39.refs_1_.refs_2_, bf16[3072,6144]{1,0:T(8,128)(2,1)} %bitcast.24, ...), custom_call_target="tpu_custom_call" | custom-call | tf_op jit(solution)/shard_map/down_product/pallas_call | solution.py:32
  201.3 1.6 collective-permute-start.43
  203.4 7.2 %weight_gradient.5.refs_4_ = bf16[3072,6144]{1,0:T(8,128)(2,1)} custom-call(s32[1]{0:T(128)} %bitcast.section_ref, bf16[3072,512]{1,0:T(8,128)(2,1)S(1)} %transposed.1.turned_ref, bf16[256,768]{1,0:T(8,128)(2,1)S(1)} %get-tuple-element.291.refs_0_, bf16[256,768]{1,0:T(8,128)(2,1)S(1)} %get-tuple-element.265.refs_1_, ...), custom_call_target="tpu_custom_call", output_to_operand_aliasing={{}: (6, {})} | custom-call | tf_op jit(solution)/shard_map/weight_gradient/pallas_call | solution.py:32
  211.6 1.3 collective-permute-start.45
  212.9 2.3 collective-permute-done.41.refs_2_
  215.6 1.7 collective-permute-done.42.refs_1_.refs_3_
  217.3 6.0 %down_product.10.refs_3_ = f32[3072,256]{1,0:T(8,128)S(1)} custom-call(s32[1]{0:T(128)} %bitcast.section_ref, bf16[256,768]{1,0:T(8,128)(2,1)S(1)} %get-tuple-element.313.refs_0_.refs_1_, bf16[256,768]{1,0:T(8,128)(2,1)S(1)} %collective-permute-done.42.refs_1_.refs_3_, bf16[3072,6144]{1,0:T(8,128)(2,1)} %bitcast.25, f32[3072,512]{1,0:T(8,128)S(1)} %down_product.7.refs_3_), custom_call_target="tpu_custom_call" | custom-call | tf_op jit(solution)/shard_map/down_product/pallas_call | solution.py:32
  223.3 14.5 %collective-permute-done.44.refs_5_ = bf16[128,3072]{1,0:T(8,128)(2,1)S(1)} collective-permute-done((bf16[128,3072]{1,0:T(8,128)(2,1)S(1)}, bf16[128,3072]{1,0:T(8,128)(2,1)S(1)}, u32[]{:S(2)}, u32[]{:S(2)}) %collective-permute-start.44) | collective-permute-done | bytes 786464 | tf_op jit(solution)/shard_map/ppermute | solution.py:317
  238.2 1.7 collective-permute-done.46.refs_1_.refs_3_
  239.9 6.3 %down_product.11 = (bf16[128,3072]{1,0:T(8,128)(2,1)S(1)}, f32[128,3072]{1,0:T(8,128)S(1)}) custom-call(s32[1]{0:T(128)} %bitcast.section_ref, bf16[256,768]{1,0:T(8,128)(2,1)S(1)} %get-tuple-element.316.refs_0_.refs_1_, bf16[256,768]{1,0:T(8,128)(2,1)S(1)} %collective-permute-done.46.refs_1_.refs_3_, bf16[3072,6144]{1,0:T(8,128)(2,1)} %bitcast.26, ...), custom_call_target="tpu_custom_call" | custom-call | tf_op jit(solution)/shard_map/down_product/pallas_call | solution.py:32
  246.2 1.6 collective-permute-start.47
  247.8 7.2 %weight_gradient.6.refs_4_ = bf16[3072,6144]{1,0:T(8,128)(2,1)} custom-call(s32[1]{0:T(128)} %bitcast.section_ref, bf16[3072,512]{1,0:T(8,128)(2,1)S(1)} %transposed.1.turned_ref, bf16[256,768]{1,0:T(8,128)(2,1)S(1)} %get-tuple-element.312.refs_0_, bf16[256,768]{1,0:T(8,128)(2,1)S(1)} %get-tuple-element.313.refs_0_.refs_1_, ...), custom_call_target="tpu_custom_call", output_to_operand_aliasing={{}: (6, {})} | custom-call | tf_op jit(solution)/shard_map/weight_gradient/pallas_call | solution.py:32
  255.0 7.2 %weight_gradient.7 = bf16[3072,6144]{1,0:T(8,128)(2,1)} custom-call(s32[1]{0:T(128)} %bitcast.section_ref, bf16[3072,512]{1,0:T(8,128)(2,1)S(1)} %transposed.1.turned_ref, bf16[256,768]{1,0:T(8,128)(2,1)S(1)} %get-tuple-element.315.refs_0_, bf16[256,768]{1,0:T(8,128)(2,1)S(1)} %get-tuple-element.316.refs_0_.refs_1_, ...), custom_call_target="tpu_custom_call", output_to_operand_aliasing={{}: (6, {})} | custom-call | tf_op jit(solution)/shard_map/weight_gradient/pallas_call | solution.py:32
  262.2 3.7 %collective-permute-done.47 = bf16[128,3072]{1,0:T(8,128)(2,1)S(1)} collective-permute-done((bf16[128,3072]{1,0:T(8,128)(2,1)S(1)}, bf16[128,3072]{1,0:T(8,128)(2,1)S(1)}, u32[]{:S(2)}, u32[]{:S(2)}) %collective-permute-start.47) | collective-permute-done | bytes 786464 | tf_op jit(solution)/shard_map/ppermute | solution.py:317
  265.9 1.0 fusion.1
  (93 shorter events, 23.4 us)
Async XLA Ops:
  0.6 23.9 %copy-start = (f32[3072]{0:T(1024)S(1)}, f32[3072]{0:T(1024)}, u32[]{:S(2)}) copy-start(f32[3072]{0:T(1024)} %param.6) | copy-start | bytes 36868
  1.9 22.1 %collective-permute-start.1 = (bf16[128,3072]{1,0:T(8,128)(2,1)S(1)}, bf16[128,3072]{1,0:T(8,128)(2,1)S(1)}, u32[]{:S(2)}, u32[]{:S(2)}) collective-permute-start(bf16[128,3072]{1,0:T(8,128)(2,1)S(1)} %broadcast_select_fusion.refs_1_), channel_id=1, source_target_pairs={{0,2},{1,3},{2,0},{3,1},{4,6},{5,7},{6,4},{7,5},{8,10},{9,11},{10,... | collective-permute-start | bytes 2359304 | tf_op jit(solution)/shard_map/ppermute | solution.py:317
  4.9 19.1 %collective-permute-start = (bf16[128,3072]{1,0:T(8,128)(2,1)S(1)}, bf16[128,3072]{1,0:T(8,128)(2,1)S(1)}, u32[]{:S(2)}, u32[]{:S(2)}) collective-permute-start(bf16[128,3072]{1,0:T(8,128)(2,1)S(1)} %broadcast_select_fusion.refs_1_), channel_id=1, source_target_pairs={{0,1},{1,0},{2,3},{3,2},{4,5},{5,4},{6,7},{7,6},{8,9},{9,8},{10,11... | collective-permute-start | bytes 2359304 | tf_op jit(solution)/shard_map/ppermute | solution.py:317
  19.8 4.2 %collective-permute-start.2 = (f32[128,2]{0,1:T(2,128)S(1)}, f32[128,2]{0,1:T(2,128)S(1)}, u32[]{:S(2)}, u32[]{:S(2)}) collective-permute-start(f32[128,2]{0,1:T(2,128)S(1)} %pad_maximum_fusion), channel_id=1, source_target_pairs={{0,1},{1,0},{2,3},{3,2},{4,5},{5,4},{6,7},{7,6},{8,9},{9,8},{10,11... | collective-permute-start | bytes 3080 | tf_op jit(solution)/shard_map/ppermute | solution.py:317
  24.1 20.9 %collective-permute-start.5 = (bf16[128,3072]{1,0:T(8,128)(2,1)S(1)}, bf16[128,3072]{1,0:T(8,128)(2,1)S(1)}, u32[]{:S(2)}, u32[]{:S(2)}) collective-permute-start(bf16[128,3072]{1,0:T(8,128)(2,1)S(1)} %collective-permute-done.refs_0_), channel_id=1, source_target_pairs={{0,2},{1,3},{2,0},{3,1},{4,6},{5,7},{6,4},{7,5},{8,10},{9,11},{10,... | collective-permute-start | bytes 2359304 | tf_op jit(solution)/shard_map/ppermute | solution.py:317
  31.1 1.8 collective-permute-start.3
  33.1 20.7 %collective-permute-start.6 = (bf16[512,768]{1,0:T(8,128)(2,1)S(1)}, bf16[512,768]{1,0:T(8,128)(2,1)S(1)}, u32[]{:S(2)}, u32[]{:S(2)}) collective-permute-start(bf16[512,768]{1,0:T(8,128)(2,1)S(1)} %stacked.8.refs_0_), channel_id=1, source_target_pairs={{0,4},{12,8},{1,5},{13,9},{2,6},{14,10},{3,7},{15,11},{16,20},{28,... | collective-permute-start | bytes 2359304 | tf_op jit(solution)/shard_map/ppermute | solution.py:388
  36.8 8.3 %collective-permute-start.4 = (f32[256,2]{1,0:T(8,128)S(1)}, f32[256,2]{1,0:T(8,128)S(1)}, u32[]{:S(2)}, u32[]{:S(2)}) collective-permute-start(f32[256,2]{1,0:T(8,128)S(1)} %copy.12.scale_ref), channel_id=1, source_target_pairs={{0,2},{1,3},{2,0},{3,1},{4,6},{5,7},{6,4},{7,5},{8,10},{9,11},{10,... | collective-permute-start | bytes 6152 | tf_op jit(solution)/shard_map/ppermute | solution.py:317
  51.6 2.6 collective-permute-start.7
  54.5 22.4 %collective-permute-start.9 = (bf16[512,768]{1,0:T(8,128)(2,1)S(1)}, bf16[512,768]{1,0:T(8,128)(2,1)S(1)}, u32[]{:S(2)}, u32[]{:S(2)}) collective-permute-start(bf16[512,768]{1,0:T(8,128)(2,1)S(1)} %stacked.9.refs_0_), channel_id=1, source_target_pairs={{0,4},{12,8},{1,5},{13,9},{2,6},{14,10},{3,7},{15,11},{16,20},{28,... | collective-permute-start | bytes 2359304 | tf_op jit(solution)/shard_map/ppermute | solution.py:388
  58.9 1.8 collective-permute-start.8
  59.0 19.1 %collective-permute-start.10 = (bf16[512,768]{1,0:T(8,128)(2,1)S(1)}, bf16[512,768]{1,0:T(8,128)(2,1)S(1)}, u32[]{:S(2)}, u32[]{:S(2)}) collective-permute-start(bf16[512,768]{1,0:T(8,128)(2,1)S(1)} %added.8.refs_1_), channel_id=1, source_target_pairs={{4,8},{8,4},{5,9},{9,5},{6,10},{10,6},{7,11},{11,7},{20,24},{24,20... | collective-permute-start | bytes 2359304 | tf_op jit(solution)/shard_map/ppermute | solution.py:393
  66.2 29.5 %collective-permute-start.12 = (bf16[512,768]{1,0:T(8,128)(2,1)S(1)}, bf16[512,768]{1,0:T(8,128)(2,1)S(1)}, u32[]{:S(2)}, u32[]{:S(2)}) collective-permute-start(bf16[512,768]{1,0:T(8,128)(2,1)S(1)} %stacked.10.refs_0_), channel_id=1, source_target_pairs={{0,4},{12,8},{1,5},{13,9},{2,6},{14,10},{3,7},{15,11},{16,20},{28,... | collective-permute-start | bytes 2359304 | tf_op jit(solution)/shard_map/ppermute | solution.py:388
  77.3 19.9 %collective-permute-start.13 = (bf16[512,768]{1,0:T(8,128)(2,1)S(1)}, bf16[512,768]{1,0:T(8,128)(2,1)S(1)}, u32[]{:S(2)}, u32[]{:S(2)}) collective-permute-start(bf16[512,768]{1,0:T(8,128)(2,1)S(1)} %added.9.refs_1_), channel_id=1, source_target_pairs={{4,8},{8,4},{5,9},{9,5},{6,10},{10,6},{7,11},{11,7},{20,24},{24,20... | collective-permute-start | bytes 2359304 | tf_op jit(solution)/shard_map/ppermute | solution.py:393
  78.0 2.4 collective-permute-start.11
  79.1 24.7 %collective-permute-start.14 = (bf16[512,768]{1,0:T(8,128)(2,1)S(1)}, bf16[512,768]{1,0:T(8,128)(2,1)S(1)}, u32[]{:S(2)}, u32[]{:S(2)}) collective-permute-start(bf16[512,768]{1,0:T(8,128)(2,1)S(1)} %activated.8.refs_1_), channel_id=1, source_target_pairs={{4,0},{8,12},{5,1},{9,13},{6,2},{10,14},{7,3},{11,15},{20,16},{24,... | collective-permute-start | bytes 2359304 | tf_op jit(solution)/shard_map/ppermute | solution.py:399
  80.7 33.1 %collective-permute-start.16 = (bf16[512,768]{1,0:T(8,128)(2,1)S(1)}, bf16[512,768]{1,0:T(8,128)(2,1)S(1)}, u32[]{:S(2)}, u32[]{:S(2)}) collective-permute-start(bf16[512,768]{1,0:T(8,128)(2,1)S(1)} %stacked.11.refs_0_), channel_id=1, source_target_pairs={{0,4},{12,8},{1,5},{13,9},{2,6},{14,10},{3,7},{15,11},{16,20},{28,... | collective-permute-start | bytes 2359304 | tf_op jit(solution)/shard_map/ppermute | solution.py:388
  96.2 18.8 %collective-permute-start.17 = (bf16[512,768]{1,0:T(8,128)(2,1)S(1)}, bf16[512,768]{1,0:T(8,128)(2,1)S(1)}, u32[]{:S(2)}, u32[]{:S(2)}) collective-permute-start(bf16[512,768]{1,0:T(8,128)(2,1)S(1)} %added.10.refs_1_), channel_id=1, source_target_pairs={{4,8},{8,4},{5,9},{9,5},{6,10},{10,6},{7,11},{11,7},{20,24},{24,20... | collective-permute-start | bytes 2359304 | tf_op jit(solution)/shard_map/ppermute | solution.py:393
  96.9 7.3 %collective-permute-start.15 = (bf16[256,768]{1,0:T(8,128)(2,1)S(1)}, bf16[256,768]{1,0:T(8,128)(2,1)S(1)}, u32[]{:S(2)}, u32[]{:S(2)}) collective-permute-start(bf16[256,768]{1,0:T(8,128)(2,1)S(1)} %get-tuple-element.215), channel_id=1, source_target_pairs={{0,16},{16,0},{1,17},{17,1},{2,18},{18,2},{3,19},{19,3},{4,20},{20... | collective-permute-start | bytes 1179656 | tf_op jit(solution)/shard_map/ppermute | solution.py:321
  98.2 22.5 %collective-permute-start.18 = (bf16[512,768]{1,0:T(8,128)(2,1)S(1)}, bf16[512,768]{1,0:T(8,128)(2,1)S(1)}, u32[]{:S(2)}, u32[]{:S(2)}) collective-permute-start(bf16[512,768]{1,0:T(8,128)(2,1)S(1)} %activated.9.refs_1_), channel_id=1, source_target_pairs={{4,0},{8,12},{5,1},{9,13},{6,2},{10,14},{7,3},{11,15},{20,16},{24,... | collective-permute-start | bytes 2359304 | tf_op jit(solution)/shard_map/ppermute | solution.py:399
  112.2 8.8 %collective-permute-start.19 = (bf16[256,768]{1,0:T(8,128)(2,1)S(1)}, bf16[256,768]{1,0:T(8,128)(2,1)S(1)}, u32[]{:S(2)}, u32[]{:S(2)}) collective-permute-start(bf16[256,768]{1,0:T(8,128)(2,1)S(1)} %get-tuple-element.232), channel_id=1, source_target_pairs={{0,16},{16,0},{1,17},{17,1},{2,18},{18,2},{3,19},{19,3},{4,20},{20... | collective-permute-start | bytes 1179656 | tf_op jit(solution)/shard_map/ppermute | solution.py:321
  112.3 20.3 %collective-permute-start.22 = (bf16[512,768]{1,0:T(8,128)(2,1)S(1)}, bf16[512,768]{1,0:T(8,128)(2,1)S(1)}, u32[]{:S(2)}, u32[]{:S(2)}) collective-permute-start(bf16[512,768]{1,0:T(8,128)(2,1)S(1)} %stacked.12.refs_0_), channel_id=1, source_target_pairs={{0,4},{12,8},{1,5},{13,9},{2,6},{14,10},{3,7},{15,11},{16,20},{28,... | collective-permute-start | bytes 2359304 | tf_op jit(solution)/shard_map/ppermute | solution.py:388
  114.2 19.6 %collective-permute-start.23 = (bf16[512,768]{1,0:T(8,128)(2,1)S(1)}, bf16[512,768]{1,0:T(8,128)(2,1)S(1)}, u32[]{:S(2)}, u32[]{:S(2)}) collective-permute-start(bf16[512,768]{1,0:T(8,128)(2,1)S(1)} %added.11.refs_1_), channel_id=1, source_target_pairs={{4,8},{8,4},{5,9},{9,5},{6,10},{10,6},{7,11},{11,7},{20,24},{24,20... | collective-permute-start | bytes 2359304 | tf_op jit(solution)/shard_map/ppermute | solution.py:393
  116.0 21.7 %collective-permute-start.24 = (bf16[512,768]{1,0:T(8,128)(2,1)S(1)}, bf16[512,768]{1,0:T(8,128)(2,1)S(1)}, u32[]{:S(2)}, u32[]{:S(2)}) collective-permute-start(bf16[512,768]{1,0:T(8,128)(2,1)S(1)} %activated.10.refs_1_), channel_id=1, source_target_pairs={{4,0},{8,12},{5,1},{9,13},{6,2},{10,14},{7,3},{11,15},{20,16},{24,... | collective-permute-start | bytes 2359304 | tf_op jit(solution)/shard_map/ppermute | solution.py:399
  120.7 2.6 collective-permute-start.21
  121.0 3.8 %collective-permute-start.20 = (bf16[256,768]{1,0:T(8,128)(2,1)S(1)}, bf16[256,768]{1,0:T(8,128)(2,1)S(1)}, u32[]{:S(2)}, u32[]{:S(2)}) collective-permute-start(bf16[256,768]{1,0:T(8,128)(2,1)S(1)} %get-tuple-element.236), channel_id=1, source_target_pairs={{0,16},{16,0},{1,17},{17,1},{2,18},{18,2},{3,19},{19,3},{4,20},{20... | collective-permute-start | bytes 1179656 | tf_op jit(solution)/shard_map/ppermute | solution.py:321
  123.3 26.4 %collective-permute-start.27 = (bf16[512,768]{1,0:T(8,128)(2,1)S(1)}, bf16[512,768]{1,0:T(8,128)(2,1)S(1)}, u32[]{:S(2)}, u32[]{:S(2)}) collective-permute-start(bf16[512,768]{1,0:T(8,128)(2,1)S(1)} %stacked.13.refs_0_), channel_id=1, source_target_pairs={{0,4},{12,8},{1,5},{13,9},{2,6},{14,10},{3,7},{15,11},{16,20},{28,... | collective-permute-start | bytes 2359304 | tf_op jit(solution)/shard_map/ppermute | solution.py:388
  133.1 17.7 %collective-permute-start.28 = (bf16[512,768]{1,0:T(8,128)(2,1)S(1)}, bf16[512,768]{1,0:T(8,128)(2,1)S(1)}, u32[]{:S(2)}, u32[]{:S(2)}) collective-permute-start(bf16[512,768]{1,0:T(8,128)(2,1)S(1)} %added.12.refs_1_), channel_id=1, source_target_pairs={{4,8},{8,4},{5,9},{9,5},{6,10},{10,6},{7,11},{11,7},{20,24},{24,20... | collective-permute-start | bytes 2359304 | tf_op jit(solution)/shard_map/ppermute | solution.py:393
  133.8 4.3 %collective-permute-start.25 = (bf16[256,768]{1,0:T(8,128)(2,1)S(1)}, bf16[256,768]{1,0:T(8,128)(2,1)S(1)}, u32[]{:S(2)}, u32[]{:S(2)}) collective-permute-start(bf16[256,768]{1,0:T(8,128)(2,1)S(1)} %get-tuple-element.248), channel_id=1, source_target_pairs={{0,16},{16,0},{1,17},{17,1},{2,18},{18,2},{3,19},{19,3},{4,20},{20... | collective-permute-start | bytes 1179656 | tf_op jit(solution)/shard_map/ppermute | solution.py:321
  134.9 22.7 %collective-permute-start.29 = (bf16[512,768]{1,0:T(8,128)(2,1)S(1)}, bf16[512,768]{1,0:T(8,128)(2,1)S(1)}, u32[]{:S(2)}, u32[]{:S(2)}) collective-permute-start(bf16[512,768]{1,0:T(8,128)(2,1)S(1)} %activated.11.refs_1_), channel_id=1, source_target_pairs={{4,0},{8,12},{5,1},{9,13},{6,2},{10,14},{7,3},{11,15},{20,16},{24,... | collective-permute-start | bytes 2359304 | tf_op jit(solution)/shard_map/ppermute | solution.py:399
  138.0 4.4 %collective-permute-start.26 = (bf16[256,768]{1,0:T(8,128)(2,1)S(1)}, bf16[256,768]{1,0:T(8,128)(2,1)S(1)}, u32[]{:S(2)}, u32[]{:S(2)}) collective-permute-start(bf16[256,768]{1,0:T(8,128)(2,1)S(1)} %get-tuple-element.250), channel_id=1, source_target_pairs={{0,16},{16,0},{1,17},{17,1},{2,18},{18,2},{3,19},{19,3},{4,20},{20... | collective-permute-start | bytes 1179656 | tf_op jit(solution)/shard_map/ppermute | solution.py:321
  138.3 31.3 %collective-permute-start.32 = (bf16[512,768]{1,0:T(8,128)(2,1)S(1)}, bf16[512,768]{1,0:T(8,128)(2,1)S(1)}, u32[]{:S(2)}, u32[]{:S(2)}) collective-permute-start(bf16[512,768]{1,0:T(8,128)(2,1)S(1)} %stacked.14.refs_0_), channel_id=1, source_target_pairs={{0,4},{12,8},{1,5},{13,9},{2,6},{14,10},{3,7},{15,11},{16,20},{28,... | collective-permute-start | bytes 2359304 | tf_op jit(solution)/shard_map/ppermute | solution.py:388
  150.0 20.7 %collective-permute-start.33 = (bf16[512,768]{1,0:T(8,128)(2,1)S(1)}, bf16[512,768]{1,0:T(8,128)(2,1)S(1)}, u32[]{:S(2)}, u32[]{:S(2)}) collective-permute-start(bf16[512,768]{1,0:T(8,128)(2,1)S(1)} %added.13.refs_1_), channel_id=1, source_target_pairs={{4,8},{8,4},{5,9},{9,5},{6,10},{10,6},{7,11},{11,7},{20,24},{24,20... | collective-permute-start | bytes 2359304 | tf_op jit(solution)/shard_map/ppermute | solution.py:393
  151.8 22.4 %collective-permute-start.34 = (bf16[512,768]{1,0:T(8,128)(2,1)S(1)}, bf16[512,768]{1,0:T(8,128)(2,1)S(1)}, u32[]{:S(2)}, u32[]{:S(2)}) collective-permute-start(bf16[512,768]{1,0:T(8,128)(2,1)S(1)} %activated.12.refs_1_), channel_id=1, source_target_pairs={{4,0},{8,12},{5,1},{9,13},{6,2},{10,14},{7,3},{11,15},{20,16},{24,... | collective-permute-start | bytes 2359304 | tf_op jit(solution)/shard_map/ppermute | solution.py:399
  153.1 4.9 %collective-permute-start.30 = (bf16[256,768]{1,0:T(8,128)(2,1)S(1)}, bf16[256,768]{1,0:T(8,128)(2,1)S(1)}, u32[]{:S(2)}, u32[]{:S(2)}) collective-permute-start(bf16[256,768]{1,0:T(8,128)(2,1)S(1)} %get-tuple-element.263), channel_id=1, source_target_pairs={{0,16},{16,0},{1,17},{17,1},{2,18},{18,2},{3,19},{19,3},{4,20},{20... | collective-permute-start | bytes 1179656 | tf_op jit(solution)/shard_map/ppermute | solution.py:321
  157.9 3.8 %collective-permute-start.31 = (bf16[256,768]{1,0:T(8,128)(2,1)S(1)}, bf16[256,768]{1,0:T(8,128)(2,1)S(1)}, u32[]{:S(2)}, u32[]{:S(2)}) collective-permute-start(bf16[256,768]{1,0:T(8,128)(2,1)S(1)} %get-tuple-element.266), channel_id=1, source_target_pairs={{0,16},{16,0},{1,17},{17,1},{2,18},{18,2},{3,19},{19,3},{4,20},{20... | collective-permute-start | bytes 1179656 | tf_op jit(solution)/shard_map/ppermute | solution.py:321
  158.3 24.1 %collective-permute-start.36 = (bf16[512,768]{1,0:T(8,128)(2,1)S(1)}, bf16[512,768]{1,0:T(8,128)(2,1)S(1)}, u32[]{:S(2)}, u32[]{:S(2)}) collective-permute-start(bf16[512,768]{1,0:T(8,128)(2,1)S(1)} %stacked.15.refs_0_), channel_id=1, source_target_pairs={{0,4},{12,8},{1,5},{13,9},{2,6},{14,10},{3,7},{15,11},{16,20},{28,... | collective-permute-start | bytes 2359304 | tf_op jit(solution)/shard_map/ppermute | solution.py:388
  170.0 13.5 %collective-permute-start.37 = (bf16[512,768]{1,0:T(8,128)(2,1)S(1)}, bf16[512,768]{1,0:T(8,128)(2,1)S(1)}, u32[]{:S(2)}, u32[]{:S(2)}) collective-permute-start(bf16[512,768]{1,0:T(8,128)(2,1)S(1)} %added.14.refs_1_), channel_id=1, source_target_pairs={{4,8},{8,4},{5,9},{9,5},{6,10},{10,6},{7,11},{11,7},{20,24},{24,20... | collective-permute-start | bytes 2359304 | tf_op jit(solution)/shard_map/ppermute | solution.py:393
  171.8 21.2 %collective-permute-start.38 = (bf16[512,768]{1,0:T(8,128)(2,1)S(1)}, bf16[512,768]{1,0:T(8,128)(2,1)S(1)}, u32[]{:S(2)}, u32[]{:S(2)}) collective-permute-start(bf16[512,768]{1,0:T(8,128)(2,1)S(1)} %activated.13.refs_1_), channel_id=1, source_target_pairs={{4,0},{8,12},{5,1},{9,13},{6,2},{10,14},{7,3},{11,15},{20,16},{24,... | collective-permute-start | bytes 2359304 | tf_op jit(solution)/shard_map/ppermute | solution.py:399
  174.6 1.8 collective-permute-start.35
  182.8 27.8 %collective-permute-start.40 = (bf16[512,768]{1,0:T(8,128)(2,1)S(1)}, bf16[512,768]{1,0:T(8,128)(2,1)S(1)}, u32[]{:S(2)}, u32[]{:S(2)}) collective-permute-start(bf16[512,768]{1,0:T(8,128)(2,1)S(1)} %added.15.refs_1_), channel_id=1, source_target_pairs={{4,8},{8,4},{5,9},{9,5},{6,10},{10,6},{7,11},{11,7},{20,24},{24,20... | collective-permute-start | bytes 2359304 | tf_op jit(solution)/shard_map/ppermute | solution.py:393
  193.3 1.8 collective-permute-start.39
  193.4 21.8 %collective-permute-start.41 = (bf16[512,768]{1,0:T(8,128)(2,1)S(1)}, bf16[512,768]{1,0:T(8,128)(2,1)S(1)}, u32[]{:S(2)}, u32[]{:S(2)}) collective-permute-start(bf16[512,768]{1,0:T(8,128)(2,1)S(1)} %activated.14.refs_1_), channel_id=1, source_target_pairs={{4,0},{8,12},{5,1},{9,13},{6,2},{10,14},{7,3},{11,15},{20,16},{24,... | collective-permute-start | bytes 2359304 | tf_op jit(solution)/shard_map/ppermute | solution.py:399
  201.3 22.0 %collective-permute-start.43 = (bf16[128,3072]{1,0:T(8,128)(2,1)S(1)}, bf16[128,3072]{1,0:T(8,128)(2,1)S(1)}, u32[]{:S(2)}, u32[]{:S(2)}) collective-permute-start(bf16[128,3072]{1,0:T(8,128)(2,1)S(1)} %get-tuple-element.289), channel_id=1, source_target_pairs={{0,2},{1,3},{2,0},{3,1},{4,6},{5,7},{6,4},{7,5},{8,10},{9,11},{10,... | collective-permute-start | bytes 2359304 | tf_op jit(solution)/shard_map/ppermute | solution.py:317
  202.9 34.9 %collective-permute-start.44 = (bf16[128,3072]{1,0:T(8,128)(2,1)S(1)}, bf16[128,3072]{1,0:T(8,128)(2,1)S(1)}, u32[]{:S(2)}, u32[]{:S(2)}) collective-permute-start(bf16[128,3072]{1,0:T(8,128)(2,1)S(1)} %get-tuple-element.290), channel_id=1, source_target_pairs={{0,2},{1,3},{2,0},{3,1},{4,6},{5,7},{6,4},{7,5},{8,10},{9,11},{10,... | collective-permute-start | bytes 2359304 | tf_op jit(solution)/shard_map/ppermute | solution.py:317
  211.6 26.2 %collective-permute-start.45 = (bf16[512,768]{1,0:T(8,128)(2,1)S(1)}, bf16[512,768]{1,0:T(8,128)(2,1)S(1)}, u32[]{:S(2)}, u32[]{:S(2)}) collective-permute-start(bf16[512,768]{1,0:T(8,128)(2,1)S(1)} %activated.15.refs_1_), channel_id=1, source_target_pairs={{4,0},{8,12},{5,1},{9,13},{6,2},{10,14},{7,3},{11,15},{20,16},{24,... | collective-permute-start | bytes 2359304 | tf_op jit(solution)/shard_map/ppermute | solution.py:399
  215.5 1.8 collective-permute-start.42
  238.1 1.8 collective-permute-start.46
  246.2 19.6 %collective-permute-start.47 = (bf16[128,3072]{1,0:T(8,128)(2,1)S(1)}, bf16[128,3072]{1,0:T(8,128)(2,1)S(1)}, u32[]{:S(2)}, u32[]{:S(2)}) collective-permute-start(bf16[128,3072]{1,0:T(8,128)(2,1)S(1)} %get-tuple-element.310), channel_id=1, source_target_pairs={{0,1},{1,0},{2,3},{3,2},{4,5},{5,4},{6,7},{7,6},{8,9},{9,8},{10,11... | collective-permute-start | bytes 2359304 | tf_op jit(solution)/shard_map/ppermute | solution.py:317

commit v10 on v9

--- a/solution.py
+++ b/solution.py
@@ -410,8 +410,7 @@
         return kept, [chunks[part, g]["came"] for g in groups]
 
     both = (FAR, NEAR)
-    order = [(part, g) for part in (0, 1) for g in (NEAR, FAR)]
-    order += [(part, g) for g in (FAR, NEAR) for part in range(2, parts)]
+    order = [(0, NEAR)] + [(part, FAR) for part in range(parts)] + [(part, NEAR) for part in range(1, parts)]
     count = len(order)
     held = {"gradient": None}
 
@@ -451,35 +450,30 @@
     multiply(x_all, 0, [FAR])
     inward(chunks[order[0]])
     stack(chunks[order[1]])
+    need(2)
     for t in range(count + 2):
         if 0 < t < count:
             inward(chunks[order[t]])
         tick(t)
         need(t + 3)
-        far_part, near_part = t - 4, t - 2 - parts
-        if t == 3:
+        far_part, near_part = t - 3, t - 2 - parts
+        if far_part == 0:
             turned = run(transposed, x_all)["value"]
-            near_sum = go_down(0, both, None, 0)
-        elif t == 4:
-            hidden(1, [NEAR])
-            kept = chunks[0, NEAR]["halves"]
-            waited = chunks[1, NEAR]
-            kept["value"], waited["came"] = lax.optimization_barrier((kept["value"], waited["came"]))
+            near_sum = far_sum = go_down(0, both, None, 0)
+        elif 0 < far_part < parts - 1:
+            far_sum = go_down(far_part, [FAR], far_sum, FAR if far_part == 1 else 0)
+        elif far_part == parts - 1:
+            sent_far = go_down(far_part, [FAR], far_sum, 0, [jnp.bfloat16] * 2)
+            arrived = [from_peer(value, across) for value in sent_far["value"]]
             go_gradient(0)
-        elif t == 5:
-            near_sum = far_sum = go_down(1, both, near_sum, 0)
-        if 2 <= far_part < parts - 1:
-            far_sum = go_down(far_part, [FAR], far_sum, FAR if far_part == 2 else 0)
-        elif far_part == parts - 1:
-            sent_far = go_down(far_part, [FAR], far_sum, FAR if far_part == 2 else 0, [jnp.bfloat16] * 2)
-            arrived = [from_peer(value, across) for value in sent_far["value"]]
-        if t == count - 1:
+        elif 0 < near_part < parts - 1:
+            near_sum = go_down(near_part, [NEAR], near_sum, NEAR if near_part == 1 else 0)
+        if t == count:
             go_gradient(1)
-        if 2 <= near_part < parts - 1:
-            near_sum = go_down(near_part, [NEAR], near_sum, NEAR if near_part == 2 else 0)
-            near_sum["value"], arrived = lax.optimization_barrier((near_sum["value"], arrived))
-    column = NEAR if parts == 3 else 0
-    sent_near = go_down(parts - 1, [NEAR], near_sum, column, [jnp.bfloat16, jnp.float32], arrived)
+        if t >= count - 1 and t <= count:
+            k = t - count + 1
+            last[-1]["value"], arrived[k] = lax.optimization_barrier((last[-1]["value"], arrived[k]))
+    sent_near = go_down(parts - 1, [NEAR], near_sum, 0, [jnp.bfloat16, jnp.float32], arrived)
     for part in range(2, parts):
         go_gradient(part)
 

time: 268 us -> 270 us (level)
  waiting for transfers between devices: 66.2 us -> 55.6 us
  starting transfers between devices: 57.9 us -> 66 us
  Pallas kernels: 125 us -> 130 us
    ppermute x8, waiting for transfers between devices: 23.2 us -> 8.72 us  [from_peer(): return lax.ppermute(value, 'mp', [(i, i ^ by) for i in range(peers)])]
    ppermute x8, waiting for transfers between devices: 25.1 us -> 38.2 us  [outward(): lax.ppermute(value, 'dp', [(hop + 1, hop), (line - 2 - hop, line - 1 - ho...]
    ppermute x8, waiting for transfers between devices: 9.7 us -> 2.18 us  [inward(): lax.ppermute(value, 'dp', [(hop, hop + 1), (line - 1 - hop, line - 2 - ho...]
    ppermute x8, starting transfers between devices: 29 us -> 36.4 us  [inward(): lax.ppermute(value, 'dp', [(hop, hop + 1), (line - 1 - hop, line - 2 - ho...]
    pallas_call x51 -> x52, Pallas kernels: 125 us -> 130 us  [call(): pl.pallas_call(kernel, grid_spec=pltpu.PrefetchScalarGridSpec(num_scalar_...]
  transfers between devices with their start and end apart: 48 -> 48, of which waited for: 19 -> 18; matrix products, arithmetic and copies ran while one was open for 1% -> 1% of each run, Pallas kernels for 44% -> 46%
where the time goes in v10:
time: 270 us; the launch traced here: 269 us
  Pallas kernels  130 us (48%)
  starting transfers between devices  66 us (24%)
  waiting for transfers between devices  55.6 us (21%)
  blocking collectives  12 us (4%)
  other arithmetic  3.71 us (1%)
    pallas_call x52, Pallas kernels, call(): pl.pallas_call(kernel, grid_spec=pltpu.PrefetchScalarGridSpec(num_scalar_...  130 us
    ppermute x8, waiting for transfers between devices, outward(): lax.ppermute(value, 'dp', [(hop + 1, hop), (line - 2 - hop, line - 1 - ho...  38.2 us
    ppermute x8, starting transfers between devices, inward(): lax.ppermute(value, 'dp', [(hop, hop + 1), (line - 1 - hop, line - 2 - ho...  36.4 us
    psum x1, blocking collectives, local(): lax.psum((jnp.sum(values, 1), jnp.sum(values * values, 1)), 'dp')  12 us
    ppermute x8, starting transfers between devices, from_peer(): return lax.ppermute(value, 'mp', [(i, i ^ by) for i in range(peers)])  11.9 us
    ppermute x8, starting transfers between devices, outward(): lax.ppermute(value, 'dp', [(hop + 1, hop), (line - 2 - hop, line - 1 - ho...  10.5 us
    ppermute x8, waiting for transfers between devices, from_peer(): return lax.ppermute(value, 'mp', [(i, i ^ by) for i in range(peers)])  8.72 us
    ppermute x16, waiting for transfers between devices, across_sections(): return lax.ppermute(value, 'section', [(0, 1), (1, 0)])  6.46 us
  transfers between devices with their start and end apart: 48, of which 18 were waited for; matrix products, arithmetic and copies ran while one was open for 1% of the time, Pallas kernels for 46%

profile of v10, /device:TPU:0, one launch (start us, length us, event | category | flops | bytes accessed | tf_op | source)
XLA Modules:
  0.0 268.7 jit_solution(16779588217894961269)
XLA Ops:
  0.7 1.2 broadcast_select_fusion.refs_1_
  1.9 3.0 %collective-permute-start.1 = (bf16[128,3072]{1,0:T(8,128)(2,1)S(1)}, bf16[128,3072]{1,0:T(8,128)(2,1)S(1)}, u32[]{:S(2)}, u32[]{:S(2)}) collective-permute-start(bf16[128,3072]{1,0:T(8,128)(2,1)S(1)} %broadcast_select_fusion.refs_1_), channel_id=1, source_target_pairs={{0,2},{1,3},{2,0},{3,1},{4,6},{5,7},{6,4},{7,5},{8,10},{9,11},{10,... | collective-permute-start | bytes 2359304 | tf_op jit(solution)/shard_map/ppermute | solution.py:317
  4.9 1.5 collective-permute-start
  6.4 1.4 convert_reduce_fusion
  7.8 12.0 %all-reduce = (f32[128]{0:T(128)S(1)}, f32[128]{0:T(128)S(1)}) all-reduce(f32[128]{0:T(128)S(1)} %get-tuple-element.315, f32[128]{0:T(128)S(1)} %get-tuple-element.314), channel_id=1, replica_groups=mesh['section'=2,'dp'=4,'mp'=4] {'dp'}, use_global_device_ids=true, to_apply=%region_3.4 | all-reduce | flops 256 | bytes 2048 | tf_op jit(solution)/shard_map/psum | solution.py:359
  20.4 3.6 %collective-permute-done.2 = f32[128,2]{0,1:T(2,128)S(1)} collective-permute-done((f32[128,2]{0,1:T(2,128)S(1)}, f32[128,2]{0,1:T(2,128)S(1)}, u32[]{:S(2)}, u32[]{:S(2)}) %collective-permute-start.2) | collective-permute-done | bytes 1056 | tf_op jit(solution)/shard_map/ppermute | solution.py:317
  24.6 1.2 normalize.2.rows_ref.refs_2_
  25.8 5.3 %up_product.6 = (bf16[256,768]{1,0:T(8,128)(2,1)S(1)}, bf16[256,768]{1,0:T(8,128)(2,1)S(1)}) custom-call(s32[1]{0:T(128)} %bitcast.section_ref, bf16[512,3072]{1,0:T(8,128)(2,1)S(1)} %normalize.2.rows_ref.refs_2_, bf16[3072,6144]{1,0:T(8,128)(2,1)} %bitcast.15), custom_call_target="tpu_custom_call" | custom-call | tf_op jit(solution)/shard_map/up_product/pallas_call | solution.py:32
  31.1 1.7 collective-permute-done.3.refs_1_
  33.1 3.7 %collective-permute-start.6 = (bf16[512,768]{1,0:T(8,128)(2,1)S(1)}, bf16[512,768]{1,0:T(8,128)(2,1)S(1)}, u32[]{:S(2)}, u32[]{:S(2)}) collective-permute-start(bf16[512,768]{1,0:T(8,128)(2,1)S(1)} %stacked.8.refs_0_), channel_id=1, source_target_pairs={{0,4},{12,8},{1,5},{13,9},{2,6},{14,10},{3,7},{15,11},{16,20},{28,... | collective-permute-start | bytes 2359304 | tf_op jit(solution)/shard_map/ppermute | solution.py:388
  36.8 1.6 collective-permute-start.4
  38.4 5.2 %up_product.7 = (bf16[256,768]{1,0:T(8,128)(2,1)S(1)}, bf16[256,768]{1,0:T(8,128)(2,1)S(1)}) custom-call(s32[1]{0:T(128)} %bitcast.section_ref, bf16[512,3072]{1,0:T(8,128)(2,1)S(1)} %normalize.2.rows_ref.refs_2_, bf16[3072,6144]{1,0:T(8,128)(2,1)} %bitcast.16), custom_call_target="tpu_custom_call" | custom-call | tf_op jit(solution)/shard_map/up_product/pallas_call | solution.py:32
  43.6 1.5 collective-permute-done.4.scale_ref
  45.1 1.2 normalize.3.rows_ref.value_ref
  46.3 5.3 %up_product.8 = (bf16[256,768]{1,0:T(8,128)(2,1)S(1)}, bf16[256,768]{1,0:T(8,128)(2,1)S(1)}) custom-call(s32[1]{0:T(128)} %bitcast.section_ref, bf16[512,3072]{1,0:T(8,128)(2,1)S(1)} %normalize.3.rows_ref.value_ref, bf16[3072,6144]{1,0:T(8,128)(2,1)} %bitcast.17), custom_call_target="tpu_custom_call" | custom-call | tf_op jit(solution)/shard_map/up_product/pallas_call | solution.py:32
  51.6 2.2 collective-permute-done.6.refs_1_
  54.5 4.4 %collective-permute-start.9 = (bf16[512,768]{1,0:T(8,128)(2,1)S(1)}, bf16[512,768]{1,0:T(8,128)(2,1)S(1)}, u32[]{:S(2)}, u32[]{:S(2)}) collective-permute-start(bf16[512,768]{1,0:T(8,128)(2,1)S(1)} %stacked.9.refs_0_), channel_id=1, source_target_pairs={{0,4},{12,8},{1,5},{13,9},{2,6},{14,10},{3,7},{15,11},{16,20},{28,... | collective-permute-start | bytes 2359304 | tf_op jit(solution)/shard_map/ppermute | solution.py:388
  58.9 5.3 %up_product.9 = (bf16[256,768]{1,0:T(8,128)(2,1)S(1)}, bf16[256,768]{1,0:T(8,128)(2,1)S(1)}) custom-call(s32[1]{0:T(128)} %bitcast.section_ref, bf16[512,3072]{1,0:T(8,128)(2,1)S(1)} %normalize.3.rows_ref.value_ref, bf16[3072,6144]{1,0:T(8,128)(2,1)} %bitcast.18), custom_call_target="tpu_custom_call" | custom-call | tf_op jit(solution)/shard_map/up_product/pallas_call | solution.py:32
  66.2 3.1 %collective-permute-start.12 = (bf16[512,768]{1,0:T(8,128)(2,1)S(1)}, bf16[512,768]{1,0:T(8,128)(2,1)S(1)}, u32[]{:S(2)}, u32[]{:S(2)}) collective-permute-start(bf16[512,768]{1,0:T(8,128)(2,1)S(1)} %stacked.10.refs_0_), channel_id=1, source_target_pairs={{0,4},{12,8},{1,5},{13,9},{2,6},{14,10},{3,7},{15,11},{16,20},{28,... | collective-permute-start | bytes 2359304 | tf_op jit(solution)/shard_map/ppermute | solution.py:388
  69.3 7.8 %up_product.10 = (bf16[256,768]{1,0:T(8,128)(2,1)S(1)}, bf16[256,768]{1,0:T(8,128)(2,1)S(1)}, bf16[256,768]{1,0:T(8,128)(2,1)S(1)}, bf16[256,768]{1,0:T(8,128)(2,1)S(1)}) custom-call(s32[1]{0:T(128)} %bitcast.section_ref, bf16[512,3072]{1,0:T(8,128)(2,1)S(1)} %normalize.3.rows_ref.value_ref, bf16[3072,6144]{1,0:T(8,128)(2,1)} %bitcast.19), custom_call_target="tpu_custom_call" | custom-call | tf_op jit(solution)/shard_map/up_product/pallas_call | solution.py:32
  78.4 1.0 activated.8.refs_1_
  79.4 1.3 collective-permute-start.14
  81.0 9.6 %collective-permute-start.16 = (bf16[512,768]{1,0:T(8,128)(2,1)S(1)}, bf16[512,768]{1,0:T(8,128)(2,1)S(1)}, u32[]{:S(2)}, u32[]{:S(2)}) collective-permute-start(bf16[512,768]{1,0:T(8,128)(2,1)S(1)} %stacked.11.refs_0_), channel_id=1, source_target_pairs={{0,4},{12,8},{1,5},{13,9},{2,6},{14,10},{3,7},{15,11},{16,20},{28,... | collective-permute-start | bytes 2359304 | tf_op jit(solution)/shard_map/ppermute | solution.py:388
  90.6 7.8 %up_product.11 = (bf16[256,768]{1,0:T(8,128)(2,1)S(1)}, bf16[256,768]{1,0:T(8,128)(2,1)S(1)}, bf16[256,768]{1,0:T(8,128)(2,1)S(1)}, bf16[256,768]{1,0:T(8,128)(2,1)S(1)}) custom-call(s32[1]{0:T(128)} %bitcast.section_ref, bf16[512,3072]{1,0:T(8,128)(2,1)S(1)} %normalize.3.rows_ref.value_ref, bf16[3072,6144]{1,0:T(8,128)(2,1)} %bitcast.20), custom_call_target="tpu_custom_call" | custom-call | tf_op jit(solution)/shard_map/up_product/pallas_call | solution.py:32
  100.6 1.3 collective-permute-start.18
  102.0 3.2 %collective-permute-done.14.refs_2_ = bf16[512,768]{1,0:T(8,128)(2,1)S(1)} collective-permute-done((bf16[512,768]{1,0:T(8,128)(2,1)S(1)}, bf16[512,768]{1,0:T(8,128)(2,1)S(1)}, u32[]{:S(2)}, u32[]{:S(2)}) %collective-permute-start.14) | collective-permute-done | bytes 786464 | tf_op jit(solution)/shard_map/ppermute | solution.py:399
  105.7 3.2 %collective-permute-start.22 = (bf16[512,768]{1,0:T(8,128)(2,1)S(1)}, bf16[512,768]{1,0:T(8,128)(2,1)S(1)}, u32[]{:S(2)}, u32[]{:S(2)}) collective-permute-start(bf16[512,768]{1,0:T(8,128)(2,1)S(1)} %stacked.12.refs_0_), channel_id=1, source_target_pairs={{0,4},{12,8},{1,5},{13,9},{2,6},{14,10},{3,7},{15,11},{16,20},{28,... | collective-permute-start | bytes 2359304 | tf_op jit(solution)/shard_map/ppermute | solution.py:388
  110.2 1.0 activated.10.refs_1_
  111.2 10.8 %collective-permute-done.18.refs_2_ = bf16[512,768]{1,0:T(8,128)(2,1)S(1)} collective-permute-done((bf16[512,768]{1,0:T(8,128)(2,1)S(1)}, bf16[512,768]{1,0:T(8,128)(2,1)S(1)}, u32[]{:S(2)}, u32[]{:S(2)}) %collective-permute-start.18) | collective-permute-done | bytes 786464 | tf_op jit(solution)/shard_map/ppermute | solution.py:399
  122.0 1.3 collective-permute-start.24
  124.0 1.4 transposed.1.turned_ref
  125.4 4.6 %collective-permute-start.27 = (bf16[512,768]{1,0:T(8,128)(2,1)S(1)}, bf16[512,768]{1,0:T(8,128)(2,1)S(1)}, u32[]{:S(2)}, u32[]{:S(2)}) collective-permute-start(bf16[512,768]{1,0:T(8,128)(2,1)S(1)} %stacked.13.refs_0_), channel_id=1, source_target_pairs={{0,4},{12,8},{1,5},{13,9},{2,6},{14,10},{3,7},{15,11},{16,20},{28,... | collective-permute-start | bytes 2359304 | tf_op jit(solution)/shard_map/ppermute | solution.py:388
  130.1 7.8 %down_product.7.refs_3_ = f32[3072,512]{1,0:T(8,128)S(1)} custom-call(s32[1]{0:T(128)} %bitcast.section_ref, bf16[256,768]{1,0:T(8,128)(2,1)S(1)} %get-tuple-element.276.refs_0_, bf16[256,768]{1,0:T(8,128)(2,1)S(1)} %get-tuple-element.232.refs_1_, bf16[256,768]{1,0:T(8,128)(2,1)S(1)} %collective-permute-done.20.refs_2_, ...), custom_call_target="tpu_custom_call" | custom-call | tf_op jit(solution)/shard_map/down_product/pallas_call | solution.py:32
  140.3 1.3 collective-permute-start.29
  142.8 4.2 %collective-permute-start.32 = (bf16[512,768]{1,0:T(8,128)(2,1)S(1)}, bf16[512,768]{1,0:T(8,128)(2,1)S(1)}, u32[]{:S(2)}, u32[]{:S(2)}) collective-permute-start(bf16[512,768]{1,0:T(8,128)(2,1)S(1)} %stacked.14.refs_0_), channel_id=1, source_target_pairs={{0,4},{12,8},{1,5},{13,9},{2,6},{14,10},{3,7},{15,11},{16,20},{28,... | collective-permute-start | bytes 2359304 | tf_op jit(solution)/shard_map/ppermute | solution.py:388
  147.0 6.0 %down_product.8.refs_3_ = f32[3072,256]{1,0:T(8,128)S(1)} custom-call(s32[1]{0:T(128)} %bitcast.section_ref, bf16[256,768]{1,0:T(8,128)(2,1)S(1)} %get-tuple-element.293.refs_0_, bf16[256,768]{1,0:T(8,128)(2,1)S(1)} %collective-permute-done.26.refs_1_.refs_2_, bf16[3072,6144]{1,0:T(8,128)(2,1)} %bitcast.22, f32[3072,512]{1,0:T(8,128)S(1)} %down_product.7.refs_3_), custom_call_target="tpu_custom_call" | custom-call | tf_op jit(solution)/shard_map/down_product/pallas_call | solution.py:32
  154.2 1.0 activated.12.refs_1_
  155.2 1.3 collective-permute-start.34
  156.8 5.2 %collective-permute-done.29.refs_2_ = bf16[512,768]{1,0:T(8,128)(2,1)S(1)} collective-permute-done((bf16[512,768]{1,0:T(8,128)(2,1)S(1)}, bf16[512,768]{1,0:T(8,128)(2,1)S(1)}, u32[]{:S(2)}, u32[]{:S(2)}) %collective-permute-start.29) | collective-permute-done | bytes 786464 | tf_op jit(solution)/shard_map/ppermute | solution.py:399
  162.7 3.6 %collective-permute-start.36 = (bf16[512,768]{1,0:T(8,128)(2,1)S(1)}, bf16[512,768]{1,0:T(8,128)(2,1)S(1)}, u32[]{:S(2)}, u32[]{:S(2)}) collective-permute-start(bf16[512,768]{1,0:T(8,128)(2,1)S(1)} %stacked.15.refs_0_), channel_id=1, source_target_pairs={{0,4},{12,8},{1,5},{13,9},{2,6},{14,10},{3,7},{15,11},{16,20},{28,... | collective-permute-start | bytes 2359304 | tf_op jit(solution)/shard_map/ppermute | solution.py:388
  166.3 6.0 %down_product.9.refs_3_ = f32[3072,256]{1,0:T(8,128)S(1)} custom-call(s32[1]{0:T(128)} %bitcast.section_ref, bf16[256,768]{1,0:T(8,128)(2,1)S(1)} %get-tuple-element.309.refs_0_, bf16[256,768]{1,0:T(8,128)(2,1)S(1)} %collective-permute-done.31.refs_1_.refs_2_, bf16[3072,6144]{1,0:T(8,128)(2,1)} %bitcast.23, f32[3072,256]{1,0:T(8,128)S(1)} %down_product.8.refs_3_), custom_call_target="tpu_custom_call" | custom-call | tf_op jit(solution)/shard_map/down_product/pallas_call | solution.py:32
  174.5 4.7 %collective-permute-done.34.refs_2_ = bf16[512,768]{1,0:T(8,128)(2,1)S(1)} collective-permute-done((bf16[512,768]{1,0:T(8,128)(2,1)S(1)}, bf16[512,768]{1,0:T(8,128)(2,1)S(1)}, u32[]{:S(2)}, u32[]{:S(2)}) %collective-permute-start.34) | collective-permute-done | bytes 786464 | tf_op jit(solution)/shard_map/ppermute | solution.py:399
  179.6 1.5 collective-permute-start.38
  181.3 6.2 %down_product.10 = (bf16[128,3072]{1,0:T(8,128)(2,1)S(1)}, bf16[128,3072]{1,0:T(8,128)(2,1)S(1)}) custom-call(s32[1]{0:T(128)} %bitcast.section_ref, bf16[256,768]{1,0:T(8,128)(2,1)S(1)} %get-tuple-element.312.refs_0_, bf16[256,768]{1,0:T(8,128)(2,1)S(1)} %collective-permute-done.35.refs_1_.refs_2_, bf16[3072,6144]{1,0:T(8,128)(2,1)} %bitcast.24, ...), custom_call_target="tpu_custom_call" | custom-call | tf_op jit(solution)/shard_map/down_product/pallas_call | solution.py:32
  187.5 1.6 collective-permute-start.40
  189.1 7.2 %weight_gradient.4.refs_4_ = bf16[3072,6144]{1,0:T(8,128)(2,1)} custom-call(s32[1]{0:T(128)} %bitcast.section_ref, bf16[3072,512]{1,0:T(8,128)(2,1)S(1)} %transposed.1.turned_ref, bf16[256,768]{1,0:T(8,128)(2,1)S(1)} %get-tuple-element.276.refs_0_, bf16[256,768]{1,0:T(8,128)(2,1)S(1)} %get-tuple-element.232.refs_1_, ...), custom_call_target="tpu_custom_call" | custom-call | tf_op jit(solution)/shard_map/weight_gradient/pallas_call | solution.py:32
  198.5 1.3 collective-permute-start.42
  199.8 1.6 collective-permute-done.38.refs_2_
  201.8 1.6 collective-permute-start.44
  203.5 6.0 %down_product.11.refs_3_ = f32[3072,256]{1,0:T(8,128)S(1)} custom-call(s32[1]{0:T(128)} %bitcast.section_ref, bf16[256,768]{1,0:T(8,128)(2,1)S(1)} %get-tuple-element.294.refs_0_.refs_1_, bf16[256,768]{1,0:T(8,128)(2,1)S(1)} %collective-permute-done.39.refs_1_.refs_3_, bf16[3072,6144]{1,0:T(8,128)(2,1)} %bitcast.25, f32[3072,512]{1,0:T(8,128)S(1)} %down_product.7.refs_3_), custom_call_target="tpu_custom_call" | custom-call | tf_op jit(solution)/shard_map/down_product/pallas_call | solution.py:32
  209.6 1.0 activated.15.refs_1_
  210.6 1.3 collective-permute-start.45
  211.9 10.5 %collective-permute-done.42.refs_2_ = bf16[512,768]{1,0:T(8,128)(2,1)S(1)} collective-permute-done((bf16[512,768]{1,0:T(8,128)(2,1)S(1)}, bf16[512,768]{1,0:T(8,128)(2,1)S(1)}, u32[]{:S(2)}, u32[]{:S(2)}) %collective-permute-start.42) | collective-permute-done | bytes 786464 | tf_op jit(solution)/shard_map/ppermute | solution.py:399
  222.8 1.7 collective-permute-done.43.refs_1_.refs_3_
  224.5 6.0 %down_product.12.refs_3_ = f32[3072,256]{1,0:T(8,128)S(1)} custom-call(s32[1]{0:T(128)} %bitcast.section_ref, bf16[256,768]{1,0:T(8,128)(2,1)S(1)} %get-tuple-element.310.refs_0_.refs_1_, bf16[256,768]{1,0:T(8,128)(2,1)S(1)} %collective-permute-done.43.refs_1_.refs_3_, bf16[3072,6144]{1,0:T(8,128)(2,1)} %bitcast.26, f32[3072,256]{1,0:T(8,128)S(1)} %down_product.11.refs_3_), custom_call_target="tpu_custom_call" | custom-call | tf_op jit(solution)/shard_map/down_product/pallas_call | solution.py:32
  230.6 7.2 %weight_gradient.5.refs_4_ = bf16[3072,6144]{1,0:T(8,128)(2,1)} custom-call(s32[1]{0:T(128)} %bitcast.section_ref, bf16[3072,512]{1,0:T(8,128)(2,1)S(1)} %transposed.1.turned_ref, bf16[256,768]{1,0:T(8,128)(2,1)S(1)} %get-tuple-element.293.refs_0_, bf16[256,768]{1,0:T(8,128)(2,1)S(1)} %get-tuple-element.294.refs_0_.refs_1_, ...), custom_call_target="tpu_custom_call", output_to_operand_aliasing={{}: (6, {})} | custom-call | tf_op jit(solution)/shard_map/weight_gradient/pallas_call | solution.py:32
  237.8 1.8 collective-permute-done.45.refs_2_
  240.0 1.7 collective-permute-done.46.refs_1_.refs_3_
  241.7 6.3 %down_product.13 = (bf16[128,3072]{1,0:T(8,128)(2,1)S(1)}, f32[128,3072]{1,0:T(8,128)S(1)}) custom-call(s32[1]{0:T(128)} %bitcast.section_ref, bf16[256,768]{1,0:T(8,128)(2,1)S(1)} %get-tuple-element.313.refs_0_.refs_1_, bf16[256,768]{1,0:T(8,128)(2,1)S(1)} %collective-permute-done.46.refs_1_.refs_3_, bf16[3072,6144]{1,0:T(8,128)(2,1)} %bitcast.27, ...), custom_call_target="tpu_custom_call" | custom-call | tf_op jit(solution)/shard_map/down_product/pallas_call | solution.py:32
  248.0 1.6 collective-permute-start.47
  249.6 7.2 %weight_gradient.6.refs_4_ = bf16[3072,6144]{1,0:T(8,128)(2,1)} custom-call(s32[1]{0:T(128)} %bitcast.section_ref, bf16[3072,512]{1,0:T(8,128)(2,1)S(1)} %transposed.1.turned_ref, bf16[256,768]{1,0:T(8,128)(2,1)S(1)} %get-tuple-element.309.refs_0_, bf16[256,768]{1,0:T(8,128)(2,1)S(1)} %get-tuple-element.310.refs_0_.refs_1_, ...), custom_call_target="tpu_custom_call", output_to_operand_aliasing={{}: (6, {})} | custom-call | tf_op jit(solution)/shard_map/weight_gradient/pallas_call | solution.py:32
  256.8 7.2 %weight_gradient.7 = bf16[3072,6144]{1,0:T(8,128)(2,1)} custom-call(s32[1]{0:T(128)} %bitcast.section_ref, bf16[3072,512]{1,0:T(8,128)(2,1)S(1)} %transposed.1.turned_ref, bf16[256,768]{1,0:T(8,128)(2,1)S(1)} %get-tuple-element.312.refs_0_, bf16[256,768]{1,0:T(8,128)(2,1)S(1)} %get-tuple-element.313.refs_0_.refs_1_, ...), custom_call_target="tpu_custom_call", output_to_operand_aliasing={{}: (6, {})} | custom-call | tf_op jit(solution)/shard_map/weight_gradient/pallas_call | solution.py:32
  264.0 3.7 %collective-permute-done.47 = bf16[128,3072]{1,0:T(8,128)(2,1)S(1)} collective-permute-done((bf16[128,3072]{1,0:T(8,128)(2,1)S(1)}, bf16[128,3072]{1,0:T(8,128)(2,1)S(1)}, u32[]{:S(2)}, u32[]{:S(2)}) %collective-permute-start.47) | collective-permute-done | bytes 786464 | tf_op jit(solution)/shard_map/ppermute | solution.py:317
  267.6 1.0 fusion.1
  (94 shorter events, 22.1 us)
Async XLA Ops:
  0.6 23.9 %copy-start = (f32[3072]{0:T(1024)S(1)}, f32[3072]{0:T(1024)}, u32[]{:S(2)}) copy-start(f32[3072]{0:T(1024)} %param.6) | copy-start | bytes 36868
  1.9 22.1 %collective-permute-start.1 = (bf16[128,3072]{1,0:T(8,128)(2,1)S(1)}, bf16[128,3072]{1,0:T(8,128)(2,1)S(1)}, u32[]{:S(2)}, u32[]{:S(2)}) collective-permute-start(bf16[128,3072]{1,0:T(8,128)(2,1)S(1)} %broadcast_select_fusion.refs_1_), channel_id=1, source_target_pairs={{0,2},{1,3},{2,0},{3,1},{4,6},{5,7},{6,4},{7,5},{8,10},{9,11},{10,... | collective-permute-start | bytes 2359304 | tf_op jit(solution)/shard_map/ppermute | solution.py:317
  4.9 19.1 %collective-permute-start = (bf16[128,3072]{1,0:T(8,128)(2,1)S(1)}, bf16[128,3072]{1,0:T(8,128)(2,1)S(1)}, u32[]{:S(2)}, u32[]{:S(2)}) collective-permute-start(bf16[128,3072]{1,0:T(8,128)(2,1)S(1)} %broadcast_select_fusion.refs_1_), channel_id=1, source_target_pairs={{0,1},{1,0},{2,3},{3,2},{4,5},{5,4},{6,7},{7,6},{8,9},{9,8},{10,11... | collective-permute-start | bytes 2359304 | tf_op jit(solution)/shard_map/ppermute | solution.py:317
  19.8 4.2 %collective-permute-start.2 = (f32[128,2]{0,1:T(2,128)S(1)}, f32[128,2]{0,1:T(2,128)S(1)}, u32[]{:S(2)}, u32[]{:S(2)}) collective-permute-start(f32[128,2]{0,1:T(2,128)S(1)} %pad_maximum_fusion), channel_id=1, source_target_pairs={{0,1},{1,0},{2,3},{3,2},{4,5},{5,4},{6,7},{7,6},{8,9},{9,8},{10,11... | collective-permute-start | bytes 3080 | tf_op jit(solution)/shard_map/ppermute | solution.py:317
  24.1 20.9 %collective-permute-start.5 = (bf16[128,3072]{1,0:T(8,128)(2,1)S(1)}, bf16[128,3072]{1,0:T(8,128)(2,1)S(1)}, u32[]{:S(2)}, u32[]{:S(2)}) collective-permute-start(bf16[128,3072]{1,0:T(8,128)(2,1)S(1)} %collective-permute-done.refs_0_), channel_id=1, source_target_pairs={{0,2},{1,3},{2,0},{3,1},{4,6},{5,7},{6,4},{7,5},{8,10},{9,11},{10,... | collective-permute-start | bytes 2359304 | tf_op jit(solution)/shard_map/ppermute | solution.py:317
  31.1 1.8 collective-permute-start.3
  33.1 20.7 %collective-permute-start.6 = (bf16[512,768]{1,0:T(8,128)(2,1)S(1)}, bf16[512,768]{1,0:T(8,128)(2,1)S(1)}, u32[]{:S(2)}, u32[]{:S(2)}) collective-permute-start(bf16[512,768]{1,0:T(8,128)(2,1)S(1)} %stacked.8.refs_0_), channel_id=1, source_target_pairs={{0,4},{12,8},{1,5},{13,9},{2,6},{14,10},{3,7},{15,11},{16,20},{28,... | collective-permute-start | bytes 2359304 | tf_op jit(solution)/shard_map/ppermute | solution.py:388
  36.8 8.3 %collective-permute-start.4 = (f32[256,2]{1,0:T(8,128)S(1)}, f32[256,2]{1,0:T(8,128)S(1)}, u32[]{:S(2)}, u32[]{:S(2)}) collective-permute-start(f32[256,2]{1,0:T(8,128)S(1)} %copy.12.scale_ref), channel_id=1, source_target_pairs={{0,2},{1,3},{2,0},{3,1},{4,6},{5,7},{6,4},{7,5},{8,10},{9,11},{10,... | collective-permute-start | bytes 6152 | tf_op jit(solution)/shard_map/ppermute | solution.py:317
  51.6 2.6 collective-permute-start.7
  54.5 22.6 %collective-permute-start.9 = (bf16[512,768]{1,0:T(8,128)(2,1)S(1)}, bf16[512,768]{1,0:T(8,128)(2,1)S(1)}, u32[]{:S(2)}, u32[]{:S(2)}) collective-permute-start(bf16[512,768]{1,0:T(8,128)(2,1)S(1)} %stacked.9.refs_0_), channel_id=1, source_target_pairs={{0,4},{12,8},{1,5},{13,9},{2,6},{14,10},{3,7},{15,11},{16,20},{28,... | collective-permute-start | bytes 2359304 | tf_op jit(solution)/shard_map/ppermute | solution.py:388
  64.2 1.8 collective-permute-start.8
  64.3 14.1 %collective-permute-start.10 = (bf16[512,768]{1,0:T(8,128)(2,1)S(1)}, bf16[512,768]{1,0:T(8,128)(2,1)S(1)}, u32[]{:S(2)}, u32[]{:S(2)}) collective-permute-start(bf16[512,768]{1,0:T(8,128)(2,1)S(1)} %added.8.refs_1_), channel_id=1, source_target_pairs={{4,8},{8,4},{5,9},{9,5},{6,10},{10,6},{7,11},{11,7},{20,24},{24,20... | collective-permute-start | bytes 2359304 | tf_op jit(solution)/shard_map/ppermute | solution.py:393
  66.2 32.2 %collective-permute-start.12 = (bf16[512,768]{1,0:T(8,128)(2,1)S(1)}, bf16[512,768]{1,0:T(8,128)(2,1)S(1)}, u32[]{:S(2)}, u32[]{:S(2)}) collective-permute-start(bf16[512,768]{1,0:T(8,128)(2,1)S(1)} %stacked.10.refs_0_), channel_id=1, source_target_pairs={{0,4},{12,8},{1,5},{13,9},{2,6},{14,10},{3,7},{15,11},{16,20},{28,... | collective-permute-start | bytes 2359304 | tf_op jit(solution)/shard_map/ppermute | solution.py:388
  77.6 22.0 %collective-permute-start.13 = (bf16[512,768]{1,0:T(8,128)(2,1)S(1)}, bf16[512,768]{1,0:T(8,128)(2,1)S(1)}, u32[]{:S(2)}, u32[]{:S(2)}) collective-permute-start(bf16[512,768]{1,0:T(8,128)(2,1)S(1)} %added.9.refs_1_), channel_id=1, source_target_pairs={{4,8},{8,4},{5,9},{9,5},{6,10},{10,6},{7,11},{11,7},{20,24},{24,20... | collective-permute-start | bytes 2359304 | tf_op jit(solution)/shard_map/ppermute | solution.py:393
  78.3 2.4 collective-permute-start.11
  79.4 25.7 %collective-permute-start.14 = (bf16[512,768]{1,0:T(8,128)(2,1)S(1)}, bf16[512,768]{1,0:T(8,128)(2,1)S(1)}, u32[]{:S(2)}, u32[]{:S(2)}) collective-permute-start(bf16[512,768]{1,0:T(8,128)(2,1)S(1)} %activated.8.refs_1_), channel_id=1, source_target_pairs={{4,0},{8,12},{5,1},{9,13},{6,2},{10,14},{7,3},{11,15},{20,16},{24,... | collective-permute-start | bytes 2359304 | tf_op jit(solution)/shard_map/ppermute | solution.py:399
  81.0 28.0 %collective-permute-start.16 = (bf16[512,768]{1,0:T(8,128)(2,1)S(1)}, bf16[512,768]{1,0:T(8,128)(2,1)S(1)}, u32[]{:S(2)}, u32[]{:S(2)}) collective-permute-start(bf16[512,768]{1,0:T(8,128)(2,1)S(1)} %stacked.11.refs_0_), channel_id=1, source_target_pairs={{0,4},{12,8},{1,5},{13,9},{2,6},{14,10},{3,7},{15,11},{16,20},{28,... | collective-permute-start | bytes 2359304 | tf_op jit(solution)/shard_map/ppermute | solution.py:388
  98.8 10.6 %collective-permute-start.17 = (bf16[512,768]{1,0:T(8,128)(2,1)S(1)}, bf16[512,768]{1,0:T(8,128)(2,1)S(1)}, u32[]{:S(2)}, u32[]{:S(2)}) collective-permute-start(bf16[512,768]{1,0:T(8,128)(2,1)S(1)} %added.10.refs_1_), channel_id=1, source_target_pairs={{4,8},{8,4},{5,9},{9,5},{6,10},{10,6},{7,11},{11,7},{20,24},{24,20... | collective-permute-start | bytes 2359304 | tf_op jit(solution)/shard_map/ppermute | solution.py:393
  100.6 21.4 %collective-permute-start.18 = (bf16[512,768]{1,0:T(8,128)(2,1)S(1)}, bf16[512,768]{1,0:T(8,128)(2,1)S(1)}, u32[]{:S(2)}, u32[]{:S(2)}) collective-permute-start(bf16[512,768]{1,0:T(8,128)(2,1)S(1)} %activated.9.refs_1_), channel_id=1, source_target_pairs={{4,0},{8,12},{5,1},{9,13},{6,2},{10,14},{7,3},{11,15},{20,16},{24,... | collective-permute-start | bytes 2359304 | tf_op jit(solution)/shard_map/ppermute | solution.py:399
  101.9 3.6 %collective-permute-start.15 = (bf16[256,768]{1,0:T(8,128)(2,1)S(1)}, bf16[256,768]{1,0:T(8,128)(2,1)S(1)}, u32[]{:S(2)}, u32[]{:S(2)}) collective-permute-start(bf16[256,768]{1,0:T(8,128)(2,1)S(1)} %get-tuple-element.217), channel_id=1, source_target_pairs={{0,16},{16,0},{1,17},{17,1},{2,18},{18,2},{3,19},{19,3},{4,20},{20... | collective-permute-start | bytes 1179656 | tf_op jit(solution)/shard_map/ppermute | solution.py:321
  105.1 18.5 %collective-permute-start.19 = (bf16[256,768]{1,0:T(8,128)(2,1)S(1)}, bf16[256,768]{1,0:T(8,128)(2,1)S(1)}, u32[]{:S(2)}, u32[]{:S(2)}) collective-permute-start(bf16[256,768]{1,0:T(8,128)(2,1)S(1)} %get-tuple-element.229), channel_id=1, source_target_pairs={{0,16},{16,0},{1,17},{17,1},{2,18},{18,2},{3,19},{19,3},{4,20},{20... | collective-permute-start | bytes 1179656 | tf_op jit(solution)/shard_map/ppermute | solution.py:321
  105.7 32.2 %collective-permute-start.22 = (bf16[512,768]{1,0:T(8,128)(2,1)S(1)}, bf16[512,768]{1,0:T(8,128)(2,1)S(1)}, u32[]{:S(2)}, u32[]{:S(2)}) collective-permute-start(bf16[512,768]{1,0:T(8,128)(2,1)S(1)} %stacked.12.refs_0_), channel_id=1, source_target_pairs={{0,4},{12,8},{1,5},{13,9},{2,6},{14,10},{3,7},{15,11},{16,20},{28,... | collective-permute-start | bytes 2359304 | tf_op jit(solution)/shard_map/ppermute | solution.py:388
  108.9 16.5 %collective-permute-start.21 = (bf16[256,768]{1,0:T(8,128)(2,1)S(1)}, bf16[256,768]{1,0:T(8,128)(2,1)S(1)}, u32[]{:S(2)}, u32[]{:S(2)}) collective-permute-start(bf16[256,768]{1,0:T(8,128)(2,1)S(1)} %get-tuple-element.234), channel_id=1, source_target_pairs={{0,16},{16,0},{1,17},{17,1},{2,18},{18,2},{3,19},{19,3},{4,20},{20... | collective-permute-start | bytes 1179656 | tf_op jit(solution)/shard_map/ppermute | solution.py:321
  109.4 29.9 %collective-permute-start.23 = (bf16[512,768]{1,0:T(8,128)(2,1)S(1)}, bf16[512,768]{1,0:T(8,128)(2,1)S(1)}, u32[]{:S(2)}, u32[]{:S(2)}) collective-permute-start(bf16[512,768]{1,0:T(8,128)(2,1)S(1)} %added.11.refs_1_), channel_id=1, source_target_pairs={{4,8},{8,4},{5,9},{9,5},{6,10},{10,6},{7,11},{11,7},{20,24},{24,20... | collective-permute-start | bytes 2359304 | tf_op jit(solution)/shard_map/ppermute | solution.py:393
  122.0 20.2 %collective-permute-start.24 = (bf16[512,768]{1,0:T(8,128)(2,1)S(1)}, bf16[512,768]{1,0:T(8,128)(2,1)S(1)}, u32[]{:S(2)}, u32[]{:S(2)}) collective-permute-start(bf16[512,768]{1,0:T(8,128)(2,1)S(1)} %activated.10.refs_1_), channel_id=1, source_target_pairs={{4,0},{8,12},{5,1},{9,13},{6,2},{10,14},{7,3},{11,15},{20,16},{24,... | collective-permute-start | bytes 2359304 | tf_op jit(solution)/shard_map/ppermute | solution.py:399
  123.6 6.4 %collective-permute-start.20 = (bf16[256,768]{1,0:T(8,128)(2,1)S(1)}, bf16[256,768]{1,0:T(8,128)(2,1)S(1)}, u32[]{:S(2)}, u32[]{:S(2)}) collective-permute-start(bf16[256,768]{1,0:T(8,128)(2,1)S(1)} %get-tuple-element.233), channel_id=1, source_target_pairs={{0,16},{16,0},{1,17},{17,1},{2,18},{18,2},{3,19},{19,3},{4,20},{20... | collective-permute-start | bytes 1179656 | tf_op jit(solution)/shard_map/ppermute | solution.py:321
  125.4 27.6 %collective-permute-start.27 = (bf16[512,768]{1,0:T(8,128)(2,1)S(1)}, bf16[512,768]{1,0:T(8,128)(2,1)S(1)}, u32[]{:S(2)}, u32[]{:S(2)}) collective-permute-start(bf16[512,768]{1,0:T(8,128)(2,1)S(1)} %stacked.13.refs_0_), channel_id=1, source_target_pairs={{0,4},{12,8},{1,5},{13,9},{2,6},{14,10},{3,7},{15,11},{16,20},{28,... | collective-permute-start | bytes 2359304 | tf_op jit(solution)/shard_map/ppermute | solution.py:388
  138.3 15.9 %collective-permute-start.28 = (bf16[512,768]{1,0:T(8,128)(2,1)S(1)}, bf16[512,768]{1,0:T(8,128)(2,1)S(1)}, u32[]{:S(2)}, u32[]{:S(2)}) collective-permute-start(bf16[512,768]{1,0:T(8,128)(2,1)S(1)} %added.12.refs_1_), channel_id=1, source_target_pairs={{4,8},{8,4},{5,9},{9,5},{6,10},{10,6},{7,11},{11,7},{20,24},{24,20... | collective-permute-start | bytes 2359304 | tf_op jit(solution)/shard_map/ppermute | solution.py:393
  139.1 3.5 %collective-permute-start.25 = (bf16[256,768]{1,0:T(8,128)(2,1)S(1)}, bf16[256,768]{1,0:T(8,128)(2,1)S(1)}, u32[]{:S(2)}, u32[]{:S(2)}) collective-permute-start(bf16[256,768]{1,0:T(8,128)(2,1)S(1)} %get-tuple-element.246), channel_id=1, source_target_pairs={{0,16},{16,0},{1,17},{17,1},{2,18},{18,2},{3,19},{19,3},{4,20},{20... | collective-permute-start | bytes 1179656 | tf_op jit(solution)/shard_map/ppermute | solution.py:321
  140.3 21.7 %collective-permute-start.29 = (bf16[512,768]{1,0:T(8,128)(2,1)S(1)}, bf16[512,768]{1,0:T(8,128)(2,1)S(1)}, u32[]{:S(2)}, u32[]{:S(2)}) collective-permute-start(bf16[512,768]{1,0:T(8,128)(2,1)S(1)} %activated.11.refs_1_), channel_id=1, source_target_pairs={{4,0},{8,12},{5,1},{9,13},{6,2},{10,14},{7,3},{11,15},{20,16},{24,... | collective-permute-start | bytes 2359304 | tf_op jit(solution)/shard_map/ppermute | solution.py:399
  142.5 4.5 %collective-permute-start.26 = (bf16[256,768]{1,0:T(8,128)(2,1)S(1)}, bf16[256,768]{1,0:T(8,128)(2,1)S(1)}, u32[]{:S(2)}, u32[]{:S(2)}) collective-permute-start(bf16[256,768]{1,0:T(8,128)(2,1)S(1)} %get-tuple-element.248), channel_id=1, source_target_pairs={{0,16},{16,0},{1,17},{17,1},{2,18},{18,2},{3,19},{19,3},{4,20},{20... | collective-permute-start | bytes 1179656 | tf_op jit(solution)/shard_map/ppermute | solution.py:321
  142.8 29.5 %collective-permute-start.32 = (bf16[512,768]{1,0:T(8,128)(2,1)S(1)}, bf16[512,768]{1,0:T(8,128)(2,1)S(1)}, u32[]{:S(2)}, u32[]{:S(2)}) collective-permute-start(bf16[512,768]{1,0:T(8,128)(2,1)S(1)} %stacked.14.refs_0_), channel_id=1, source_target_pairs={{0,4},{12,8},{1,5},{13,9},{2,6},{14,10},{3,7},{15,11},{16,20},{28,... | collective-permute-start | bytes 2359304 | tf_op jit(solution)/shard_map/ppermute | solution.py:388
  153.5 20.0 %collective-permute-start.33 = (bf16[512,768]{1,0:T(8,128)(2,1)S(1)}, bf16[512,768]{1,0:T(8,128)(2,1)S(1)}, u32[]{:S(2)}, u32[]{:S(2)}) collective-permute-start(bf16[512,768]{1,0:T(8,128)(2,1)S(1)} %added.13.refs_1_), channel_id=1, source_target_pairs={{4,8},{8,4},{5,9},{9,5},{6,10},{10,6},{7,11},{11,7},{20,24},{24,20... | collective-permute-start | bytes 2359304 | tf_op jit(solution)/shard_map/ppermute | solution.py:393
  155.2 23.9 %collective-permute-start.34 = (bf16[512,768]{1,0:T(8,128)(2,1)S(1)}, bf16[512,768]{1,0:T(8,128)(2,1)S(1)}, u32[]{:S(2)}, u32[]{:S(2)}) collective-permute-start(bf16[512,768]{1,0:T(8,128)(2,1)S(1)} %activated.12.refs_1_), channel_id=1, source_target_pairs={{4,0},{8,12},{5,1},{9,13},{6,2},{10,14},{7,3},{11,15},{20,16},{24,... | collective-permute-start | bytes 2359304 | tf_op jit(solution)/shard_map/ppermute | solution.py:399
  156.5 5.9 %collective-permute-start.30 = (bf16[256,768]{1,0:T(8,128)(2,1)S(1)}, bf16[256,768]{1,0:T(8,128)(2,1)S(1)}, u32[]{:S(2)}, u32[]{:S(2)}) collective-permute-start(bf16[256,768]{1,0:T(8,128)(2,1)S(1)} %get-tuple-element.260), channel_id=1, source_target_pairs={{0,16},{16,0},{1,17},{17,1},{2,18},{18,2},{3,19},{19,3},{4,20},{20... | collective-permute-start | bytes 1179656 | tf_op jit(solution)/shard_map/ppermute | solution.py:321
  162.3 4.0 %collective-permute-start.31 = (bf16[256,768]{1,0:T(8,128)(2,1)S(1)}, bf16[256,768]{1,0:T(8,128)(2,1)S(1)}, u32[]{:S(2)}, u32[]{:S(2)}) collective-permute-start(bf16[256,768]{1,0:T(8,128)(2,1)S(1)} %get-tuple-element.262), channel_id=1, source_target_pairs={{0,16},{16,0},{1,17},{17,1},{2,18},{18,2},{3,19},{19,3},{4,20},{20... | collective-permute-start | bytes 1179656 | tf_op jit(solution)/shard_map/ppermute | solution.py:321
  162.7 33.6 %collective-permute-start.36 = (bf16[512,768]{1,0:T(8,128)(2,1)S(1)}, bf16[512,768]{1,0:T(8,128)(2,1)S(1)}, u32[]{:S(2)}, u32[]{:S(2)}) collective-permute-start(bf16[512,768]{1,0:T(8,128)(2,1)S(1)} %stacked.15.refs_0_), channel_id=1, source_target_pairs={{0,4},{12,8},{1,5},{13,9},{2,6},{14,10},{3,7},{15,11},{16,20},{28,... | collective-permute-start | bytes 2359304 | tf_op jit(solution)/shard_map/ppermute | solution.py:388
  172.8 24.7 %collective-permute-start.37 = (bf16[512,768]{1,0:T(8,128)(2,1)S(1)}, bf16[512,768]{1,0:T(8,128)(2,1)S(1)}, u32[]{:S(2)}, u32[]{:S(2)}) collective-permute-start(bf16[512,768]{1,0:T(8,128)(2,1)S(1)} %added.14.refs_1_), channel_id=1, source_target_pairs={{4,8},{8,4},{5,9},{9,5},{6,10},{10,6},{7,11},{11,7},{20,24},{24,20... | collective-permute-start | bytes 2359304 | tf_op jit(solution)/shard_map/ppermute | solution.py:393
  179.5 1.8 collective-permute-start.35
  179.6 21.8 %collective-permute-start.38 = (bf16[512,768]{1,0:T(8,128)(2,1)S(1)}, bf16[512,768]{1,0:T(8,128)(2,1)S(1)}, u32[]{:S(2)}, u32[]{:S(2)}) collective-permute-start(bf16[512,768]{1,0:T(8,128)(2,1)S(1)} %activated.13.refs_1_), channel_id=1, source_target_pairs={{4,0},{8,12},{5,1},{9,13},{6,2},{10,14},{7,3},{11,15},{20,16},{24,... | collective-permute-start | bytes 2359304 | tf_op jit(solution)/shard_map/ppermute | solution.py:399
  187.5 22.0 %collective-permute-start.40 = (bf16[128,3072]{1,0:T(8,128)(2,1)S(1)}, bf16[128,3072]{1,0:T(8,128)(2,1)S(1)}, u32[]{:S(2)}, u32[]{:S(2)}) collective-permute-start(bf16[128,3072]{1,0:T(8,128)(2,1)S(1)} %get-tuple-element.274), channel_id=1, source_target_pairs={{0,2},{1,3},{2,0},{3,1},{4,6},{5,7},{6,4},{7,5},{8,10},{9,11},{10,... | collective-permute-start | bytes 2359304 | tf_op jit(solution)/shard_map/ppermute | solution.py:317
  196.7 12.8 %collective-permute-start.41 = (bf16[512,768]{1,0:T(8,128)(2,1)S(1)}, bf16[512,768]{1,0:T(8,128)(2,1)S(1)}, u32[]{:S(2)}, u32[]{:S(2)}) collective-permute-start(bf16[512,768]{1,0:T(8,128)(2,1)S(1)} %added.15.refs_1_), channel_id=1, source_target_pairs={{4,8},{8,4},{5,9},{9,5},{6,10},{10,6},{7,11},{11,7},{20,24},{24,20... | collective-permute-start | bytes 2359304 | tf_op jit(solution)/shard_map/ppermute | solution.py:393
  198.5 23.9 %collective-permute-start.42 = (bf16[512,768]{1,0:T(8,128)(2,1)S(1)}, bf16[512,768]{1,0:T(8,128)(2,1)S(1)}, u32[]{:S(2)}, u32[]{:S(2)}) collective-permute-start(bf16[512,768]{1,0:T(8,128)(2,1)S(1)} %activated.14.refs_1_), channel_id=1, source_target_pairs={{4,0},{8,12},{5,1},{9,13},{6,2},{10,14},{7,3},{11,15},{20,16},{24,... | collective-permute-start | bytes 2359304 | tf_op jit(solution)/shard_map/ppermute | solution.py:399
  201.7 1.8 collective-permute-start.39
  201.8 36.0 %collective-permute-start.44 = (bf16[128,3072]{1,0:T(8,128)(2,1)S(1)}, bf16[128,3072]{1,0:T(8,128)(2,1)S(1)}, u32[]{:S(2)}, u32[]{:S(2)}) collective-permute-start(bf16[128,3072]{1,0:T(8,128)(2,1)S(1)} %get-tuple-element.275), channel_id=1, source_target_pairs={{0,2},{1,3},{2,0},{3,1},{4,6},{5,7},{6,4},{7,5},{8,10},{9,11},{10,... | collective-permute-start | bytes 2359304 | tf_op jit(solution)/shard_map/ppermute | solution.py:317
  210.6 29.0 %collective-permute-start.45 = (bf16[512,768]{1,0:T(8,128)(2,1)S(1)}, bf16[512,768]{1,0:T(8,128)(2,1)S(1)}, u32[]{:S(2)}, u32[]{:S(2)}) collective-permute-start(bf16[512,768]{1,0:T(8,128)(2,1)S(1)} %activated.15.refs_1_), channel_id=1, source_target_pairs={{4,0},{8,12},{5,1},{9,13},{6,2},{10,14},{7,3},{11,15},{20,16},{24,... | collective-permute-start | bytes 2359304 | tf_op jit(solution)/shard_map/ppermute | solution.py:399
  222.8 1.8 collective-permute-start.43
  239.9 1.8 collective-permute-start.46
  248.0 19.6 %collective-permute-start.47 = (bf16[128,3072]{1,0:T(8,128)(2,1)S(1)}, bf16[128,3072]{1,0:T(8,128)(2,1)S(1)}, u32[]{:S(2)}, u32[]{:S(2)}) collective-permute-start(bf16[128,3072]{1,0:T(8,128)(2,1)S(1)} %get-tuple-element.307), channel_id=1, source_target_pairs={{0,1},{1,0},{2,3},{3,2},{4,5},{5,4},{6,7},{7,6},{8,9},{9,8},{10,11... | collective-permute-start | bytes 2359304 | tf_op jit(solution)/shard_map/ppermute | solution.py:317

commit v11 on v10

--- a/solution.py
+++ b/solution.py
@@ -457,19 +457,19 @@
         tick(t)
         need(t + 3)
         far_part, near_part = t - 3, t - 2 - parts
+        if t == 1:
+            turned = run(transposed, x_all)["value"]
         if far_part == 0:
-            turned = run(transposed, x_all)["value"]
             near_sum = far_sum = go_down(0, both, None, 0)
         elif 0 < far_part < parts - 1:
             far_sum = go_down(far_part, [FAR], far_sum, FAR if far_part == 1 else 0)
         elif far_part == parts - 1:
             sent_far = go_down(far_part, [FAR], far_sum, 0, [jnp.bfloat16] * 2)
             arrived = [from_peer(value, across) for value in sent_far["value"]]
-            go_gradient(0)
         elif 0 < near_part < parts - 1:
             near_sum = go_down(near_part, [NEAR], near_sum, NEAR if near_part == 1 else 0)
-        if t == count:
-            go_gradient(1)
+        if t >= count - 1 and t <= count:
+            go_gradient(t - count + 1)
         if t >= count - 1 and t <= count:
             k = t - count + 1
             last[-1]["value"], arrived[k] = lax.optimization_barrier((last[-1]["value"], arrived[k]))

time: 270 us -> 263 us (0.974)
  waiting for transfers between devices: 55.6 us -> 48.1 us
    ppermute x8, waiting for transfers between devices: 38.2 us -> 29.3 us  [outward(): lax.ppermute(value, 'dp', [(hop + 1, hop), (line - 2 - hop, line - 1 - ho...]
  transfers between devices with their start and end apart: 48 -> 48, of which waited for: 18 -> 17; matrix products, arithmetic and copies ran while one was open for 1% -> 1% of each run, Pallas kernels for 46% -> 47%
where the time goes in v11:
time: 263 us; the launch traced here: 262 us
  Pallas kernels  130 us (49%)
  starting transfers between devices  66.6 us (25%)
  waiting for transfers between devices  48.1 us (18%)
  blocking collectives  12 us (5%)
  other arithmetic  3.71 us (1%)
    pallas_call x52, Pallas kernels, call(): pl.pallas_call(kernel, grid_spec=pltpu.PrefetchScalarGridSpec(num_scalar_...  130 us
    ppermute x8, starting transfers between devices, inward(): lax.ppermute(value, 'dp', [(hop, hop + 1), (line - 1 - hop, line - 2 - ho...  36.9 us
    ppermute x8, waiting for transfers between devices, outward(): lax.ppermute(value, 'dp', [(hop + 1, hop), (line - 2 - hop, line - 1 - ho...  29.3 us
    psum x1, blocking collectives, local(): lax.psum((jnp.sum(values, 1), jnp.sum(values * values, 1)), 'dp')  12 us
    ppermute x8, starting transfers between devices, from_peer(): return lax.ppermute(value, 'mp', [(i, i ^ by) for i in range(peers)])  11.9 us
    ppermute x8, starting transfers between devices, outward(): lax.ppermute(value, 'dp', [(hop + 1, hop), (line - 2 - hop, line - 1 - ho...  10.5 us
    ppermute x8, waiting for transfers between devices, from_peer(): return lax.ppermute(value, 'mp', [(i, i ^ by) for i in range(peers)])  8.74 us
    ppermute x16, waiting for transfers between devices, across_sections(): return lax.ppermute(value, 'section', [(0, 1), (1, 0)])  7.86 us
  transfers between devices with their start and end apart: 48, of which 17 were waited for; matrix products, arithmetic and copies ran while one was open for 1% of the time, Pallas kernels for 47%

profile of v11, /device:TPU:0, one launch (start us, length us, event | category | flops | bytes accessed | tf_op | source)
XLA Modules:
  0.0 261.8 jit_solution(14956499931581551527)
XLA Ops:
  0.7 1.2 broadcast_select_fusion.refs_1_
  1.9 3.0 %collective-permute-start.1 = (bf16[128,3072]{1,0:T(8,128)(2,1)S(1)}, bf16[128,3072]{1,0:T(8,128)(2,1)S(1)}, u32[]{:S(2)}, u32[]{:S(2)}) collective-permute-start(bf16[128,3072]{1,0:T(8,128)(2,1)S(1)} %broadcast_select_fusion.refs_1_), channel_id=1, source_target_pairs={{0,2},{1,3},{2,0},{3,1},{4,6},{5,7},{6,4},{7,5},{8,10},{9,11},{10,... | collective-permute-start | bytes 2359304 | tf_op jit(solution)/shard_map/ppermute | solution.py:317
  4.9 1.5 collective-permute-start
  6.4 1.4 convert_reduce_fusion
  7.8 12.0 %all-reduce = (f32[128]{0:T(128)S(1)}, f32[128]{0:T(128)S(1)}) all-reduce(f32[128]{0:T(128)S(1)} %get-tuple-element.315, f32[128]{0:T(128)S(1)} %get-tuple-element.314), channel_id=1, replica_groups=mesh['section'=2,'dp'=4,'mp'=4] {'dp'}, use_global_device_ids=true, to_apply=%region_3.4 | all-reduce | flops 256 | bytes 2048 | tf_op jit(solution)/shard_map/psum | solution.py:359
  20.4 3.6 %collective-permute-done.2 = f32[128,2]{0,1:T(2,128)S(1)} collective-permute-done((f32[128,2]{0,1:T(2,128)S(1)}, f32[128,2]{0,1:T(2,128)S(1)}, u32[]{:S(2)}, u32[]{:S(2)}) %collective-permute-start.2) | collective-permute-done | bytes 1056 | tf_op jit(solution)/shard_map/ppermute | solution.py:317
  24.6 1.2 normalize.2.rows_ref.refs_2_
  25.8 5.3 %up_product.6 = (bf16[256,768]{1,0:T(8,128)(2,1)S(1)}, bf16[256,768]{1,0:T(8,128)(2,1)S(1)}) custom-call(s32[1]{0:T(128)} %bitcast.section_ref, bf16[512,3072]{1,0:T(8,128)(2,1)S(1)} %normalize.2.rows_ref.refs_2_, bf16[3072,6144]{1,0:T(8,128)(2,1)} %bitcast.15), custom_call_target="tpu_custom_call" | custom-call | tf_op jit(solution)/shard_map/up_product/pallas_call | solution.py:32
  31.1 1.7 collective-permute-done.3.refs_1_
  33.1 3.7 %collective-permute-start.6 = (bf16[512,768]{1,0:T(8,128)(2,1)S(1)}, bf16[512,768]{1,0:T(8,128)(2,1)S(1)}, u32[]{:S(2)}, u32[]{:S(2)}) collective-permute-start(bf16[512,768]{1,0:T(8,128)(2,1)S(1)} %stacked.8.refs_0_), channel_id=1, source_target_pairs={{0,4},{12,8},{1,5},{13,9},{2,6},{14,10},{3,7},{15,11},{16,20},{28,... | collective-permute-start | bytes 2359304 | tf_op jit(solution)/shard_map/ppermute | solution.py:388
  36.8 1.6 collective-permute-start.4
  38.4 5.2 %up_product.7 = (bf16[256,768]{1,0:T(8,128)(2,1)S(1)}, bf16[256,768]{1,0:T(8,128)(2,1)S(1)}) custom-call(s32[1]{0:T(128)} %bitcast.section_ref, bf16[512,3072]{1,0:T(8,128)(2,1)S(1)} %normalize.2.rows_ref.refs_2_, bf16[3072,6144]{1,0:T(8,128)(2,1)} %bitcast.16), custom_call_target="tpu_custom_call" | custom-call | tf_op jit(solution)/shard_map/up_product/pallas_call | solution.py:32
  43.6 1.5 collective-permute-done.4.scale_ref
  45.1 1.2 normalize.3.rows_ref.value_ref
  46.3 5.3 %up_product.8 = (bf16[256,768]{1,0:T(8,128)(2,1)S(1)}, bf16[256,768]{1,0:T(8,128)(2,1)S(1)}) custom-call(s32[1]{0:T(128)} %bitcast.section_ref, bf16[512,3072]{1,0:T(8,128)(2,1)S(1)} %normalize.3.rows_ref.value_ref, bf16[3072,6144]{1,0:T(8,128)(2,1)} %bitcast.17), custom_call_target="tpu_custom_call" | custom-call | tf_op jit(solution)/shard_map/up_product/pallas_call | solution.py:32
  51.6 2.2 collective-permute-done.6.refs_1_
  54.5 4.4 %collective-permute-start.9 = (bf16[512,768]{1,0:T(8,128)(2,1)S(1)}, bf16[512,768]{1,0:T(8,128)(2,1)S(1)}, u32[]{:S(2)}, u32[]{:S(2)}) collective-permute-start(bf16[512,768]{1,0:T(8,128)(2,1)S(1)} %stacked.9.refs_0_), channel_id=1, source_target_pairs={{0,4},{12,8},{1,5},{13,9},{2,6},{14,10},{3,7},{15,11},{16,20},{28,... | collective-permute-start | bytes 2359304 | tf_op jit(solution)/shard_map/ppermute | solution.py:388
  58.9 5.3 %up_product.9 = (bf16[256,768]{1,0:T(8,128)(2,1)S(1)}, bf16[256,768]{1,0:T(8,128)(2,1)S(1)}) custom-call(s32[1]{0:T(128)} %bitcast.section_ref, bf16[512,3072]{1,0:T(8,128)(2,1)S(1)} %normalize.3.rows_ref.value_ref, bf16[3072,6144]{1,0:T(8,128)(2,1)} %bitcast.18), custom_call_target="tpu_custom_call" | custom-call | tf_op jit(solution)/shard_map/up_product/pallas_call | solution.py:32
  66.2 3.1 %collective-permute-start.12 = (bf16[512,768]{1,0:T(8,128)(2,1)S(1)}, bf16[512,768]{1,0:T(8,128)(2,1)S(1)}, u32[]{:S(2)}, u32[]{:S(2)}) collective-permute-start(bf16[512,768]{1,0:T(8,128)(2,1)S(1)} %stacked.10.refs_0_), channel_id=1, source_target_pairs={{0,4},{12,8},{1,5},{13,9},{2,6},{14,10},{3,7},{15,11},{16,20},{28,... | collective-permute-start | bytes 2359304 | tf_op jit(solution)/shard_map/ppermute | solution.py:388
  69.3 7.8 %up_product.10 = (bf16[256,768]{1,0:T(8,128)(2,1)S(1)}, bf16[256,768]{1,0:T(8,128)(2,1)S(1)}, bf16[256,768]{1,0:T(8,128)(2,1)S(1)}, bf16[256,768]{1,0:T(8,128)(2,1)S(1)}) custom-call(s32[1]{0:T(128)} %bitcast.section_ref, bf16[512,3072]{1,0:T(8,128)(2,1)S(1)} %normalize.3.rows_ref.value_ref, bf16[3072,6144]{1,0:T(8,128)(2,1)} %bitcast.19), custom_call_target="tpu_custom_call" | custom-call | tf_op jit(solution)/shard_map/up_product/pallas_call | solution.py:32
  79.4 1.3 collective-permute-start.14
  81.0 9.6 %collective-permute-start.16 = (bf16[512,768]{1,0:T(8,128)(2,1)S(1)}, bf16[512,768]{1,0:T(8,128)(2,1)S(1)}, u32[]{:S(2)}, u32[]{:S(2)}) collective-permute-start(bf16[512,768]{1,0:T(8,128)(2,1)S(1)} %stacked.11.refs_0_), channel_id=1, source_target_pairs={{0,4},{12,8},{1,5},{13,9},{2,6},{14,10},{3,7},{15,11},{16,20},{28,... | collective-permute-start | bytes 2359304 | tf_op jit(solution)/shard_map/ppermute | solution.py:388
  90.6 7.8 %up_product.11 = (bf16[256,768]{1,0:T(8,128)(2,1)S(1)}, bf16[256,768]{1,0:T(8,128)(2,1)S(1)}, bf16[256,768]{1,0:T(8,128)(2,1)S(1)}, bf16[256,768]{1,0:T(8,128)(2,1)S(1)}) custom-call(s32[1]{0:T(128)} %bitcast.section_ref, bf16[512,3072]{1,0:T(8,128)(2,1)S(1)} %normalize.3.rows_ref.value_ref, bf16[3072,6144]{1,0:T(8,128)(2,1)} %bitcast.20), custom_call_target="tpu_custom_call" | custom-call | tf_op jit(solution)/shard_map/up_product/pallas_call | solution.py:32
  98.4 1.4 transposed.1.turned_ref
  102.0 1.3 collective-permute-start.18
  103.4 1.7 collective-permute-done.14.refs_2_
  105.7 4.3 %collective-permute-start.22 = (bf16[512,768]{1,0:T(8,128)(2,1)S(1)}, bf16[512,768]{1,0:T(8,128)(2,1)S(1)}, u32[]{:S(2)}, u32[]{:S(2)}) collective-permute-start(bf16[512,768]{1,0:T(8,128)(2,1)S(1)} %stacked.12.refs_0_), channel_id=1, source_target_pairs={{0,4},{12,8},{1,5},{13,9},{2,6},{14,10},{3,7},{15,11},{16,20},{28,... | collective-permute-start | bytes 2359304 | tf_op jit(solution)/shard_map/ppermute | solution.py:388
  111.2 1.0 activated.10.refs_1_
  112.3 10.1 %collective-permute-done.18.refs_2_ = bf16[512,768]{1,0:T(8,128)(2,1)S(1)} collective-permute-done((bf16[512,768]{1,0:T(8,128)(2,1)S(1)}, bf16[512,768]{1,0:T(8,128)(2,1)S(1)}, u32[]{:S(2)}, u32[]{:S(2)}) %collective-permute-start.18) | collective-permute-done | bytes 786464 | tf_op jit(solution)/shard_map/ppermute | solution.py:399
  122.4 1.3 collective-permute-start.24
  124.4 4.6 %collective-permute-start.27 = (bf16[512,768]{1,0:T(8,128)(2,1)S(1)}, bf16[512,768]{1,0:T(8,128)(2,1)S(1)}, u32[]{:S(2)}, u32[]{:S(2)}) collective-permute-start(bf16[512,768]{1,0:T(8,128)(2,1)S(1)} %stacked.13.refs_0_), channel_id=1, source_target_pairs={{0,4},{12,8},{1,5},{13,9},{2,6},{14,10},{3,7},{15,11},{16,20},{28,... | collective-permute-start | bytes 2359304 | tf_op jit(solution)/shard_map/ppermute | solution.py:388
  129.0 7.8 %down_product.7.refs_3_ = f32[3072,512]{1,0:T(8,128)S(1)} custom-call(s32[1]{0:T(128)} %bitcast.section_ref, bf16[256,768]{1,0:T(8,128)(2,1)S(1)} %get-tuple-element.284.refs_0_, bf16[256,768]{1,0:T(8,128)(2,1)S(1)} %get-tuple-element.232.refs_1_, bf16[256,768]{1,0:T(8,128)(2,1)S(1)} %collective-permute-done.20.refs_2_, ...), custom_call_target="tpu_custom_call" | custom-call | tf_op jit(solution)/shard_map/down_product/pallas_call | solution.py:32
  139.3 1.3 collective-permute-start.29
  140.6 1.2 collective-permute-done.24.refs_2_
  142.5 3.4 %collective-permute-start.32 = (bf16[512,768]{1,0:T(8,128)(2,1)S(1)}, bf16[512,768]{1,0:T(8,128)(2,1)S(1)}, u32[]{:S(2)}, u32[]{:S(2)}) collective-permute-start(bf16[512,768]{1,0:T(8,128)(2,1)S(1)} %stacked.14.refs_0_), channel_id=1, source_target_pairs={{0,4},{12,8},{1,5},{13,9},{2,6},{14,10},{3,7},{15,11},{16,20},{28,... | collective-permute-start | bytes 2359304 | tf_op jit(solution)/shard_map/ppermute | solution.py:388
  146.0 6.0 %down_product.8.refs_3_ = f32[3072,256]{1,0:T(8,128)S(1)} custom-call(s32[1]{0:T(128)} %bitcast.section_ref, bf16[256,768]{1,0:T(8,128)(2,1)S(1)} %get-tuple-element.293.refs_0_, bf16[256,768]{1,0:T(8,128)(2,1)S(1)} %collective-permute-done.26.refs_1_.refs_2_, bf16[3072,6144]{1,0:T(8,128)(2,1)} %bitcast.22, f32[3072,512]{1,0:T(8,128)S(1)} %down_product.7.refs_3_), custom_call_target="tpu_custom_call" | custom-call | tf_op jit(solution)/shard_map/down_product/pallas_call | solution.py:32
  154.2 1.3 collective-permute-start.34
  155.8 5.2 %collective-permute-done.29.refs_2_ = bf16[512,768]{1,0:T(8,128)(2,1)S(1)} collective-permute-done((bf16[512,768]{1,0:T(8,128)(2,1)S(1)}, bf16[512,768]{1,0:T(8,128)(2,1)S(1)}, u32[]{:S(2)}, u32[]{:S(2)}) %collective-permute-start.29) | collective-permute-done | bytes 786464 | tf_op jit(solution)/shard_map/ppermute | solution.py:399
  161.6 3.7 %collective-permute-start.36 = (bf16[512,768]{1,0:T(8,128)(2,1)S(1)}, bf16[512,768]{1,0:T(8,128)(2,1)S(1)}, u32[]{:S(2)}, u32[]{:S(2)}) collective-permute-start(bf16[512,768]{1,0:T(8,128)(2,1)S(1)} %stacked.15.refs_0_), channel_id=1, source_target_pairs={{0,4},{12,8},{1,5},{13,9},{2,6},{14,10},{3,7},{15,11},{16,20},{28,... | collective-permute-start | bytes 2359304 | tf_op jit(solution)/shard_map/ppermute | solution.py:388
  165.4 6.0 %down_product.9.refs_3_ = f32[3072,256]{1,0:T(8,128)S(1)} custom-call(s32[1]{0:T(128)} %bitcast.section_ref, bf16[256,768]{1,0:T(8,128)(2,1)S(1)} %get-tuple-element.309.refs_0_, bf16[256,768]{1,0:T(8,128)(2,1)S(1)} %collective-permute-done.31.refs_1_.refs_2_, bf16[3072,6144]{1,0:T(8,128)(2,1)} %bitcast.23, f32[3072,256]{1,0:T(8,128)S(1)} %down_product.8.refs_3_), custom_call_target="tpu_custom_call" | custom-call | tf_op jit(solution)/shard_map/down_product/pallas_call | solution.py:32
  172.6 1.0 activated.13.refs_1_
  173.6 1.5 collective-permute-start.38
  175.1 2.9 %collective-permute-done.34.refs_2_ = bf16[512,768]{1,0:T(8,128)(2,1)S(1)} collective-permute-done((bf16[512,768]{1,0:T(8,128)(2,1)S(1)}, bf16[512,768]{1,0:T(8,128)(2,1)S(1)}, u32[]{:S(2)}, u32[]{:S(2)}) %collective-permute-start.34) | collective-permute-done | bytes 786464 | tf_op jit(solution)/shard_map/ppermute | solution.py:399
  178.4 1.7 collective-permute-done.35.refs_1_.refs_2_
  180.1 6.2 %down_product.10 = (bf16[128,3072]{1,0:T(8,128)(2,1)S(1)}, bf16[128,3072]{1,0:T(8,128)(2,1)S(1)}) custom-call(s32[1]{0:T(128)} %bitcast.section_ref, bf16[256,768]{1,0:T(8,128)(2,1)S(1)} %get-tuple-element.312.refs_0_, bf16[256,768]{1,0:T(8,128)(2,1)S(1)} %collective-permute-done.35.refs_1_.refs_2_, bf16[3072,6144]{1,0:T(8,128)(2,1)} %bitcast.24, ...), custom_call_target="tpu_custom_call" | custom-call | tf_op jit(solution)/shard_map/down_product/pallas_call | solution.py:32
  186.4 1.6 collective-permute-start.40
  189.1 1.0 activated.14.refs_1_
  190.1 1.3 collective-permute-start.42
  191.4 3.4 %collective-permute-done.38.refs_2_ = bf16[512,768]{1,0:T(8,128)(2,1)S(1)} collective-permute-done((bf16[512,768]{1,0:T(8,128)(2,1)S(1)}, bf16[512,768]{1,0:T(8,128)(2,1)S(1)}, u32[]{:S(2)}, u32[]{:S(2)}) %collective-permute-start.38) | collective-permute-done | bytes 786464 | tf_op jit(solution)/shard_map/ppermute | solution.py:399
  195.3 1.6 collective-permute-start.44
  197.0 6.0 %down_product.11.refs_3_ = f32[3072,256]{1,0:T(8,128)S(1)} custom-call(s32[1]{0:T(128)} %bitcast.section_ref, bf16[256,768]{1,0:T(8,128)(2,1)S(1)} %get-tuple-element.294.refs_0_.refs_1_, bf16[256,768]{1,0:T(8,128)(2,1)S(1)} %collective-permute-done.39.refs_1_.refs_3_, bf16[3072,6144]{1,0:T(8,128)(2,1)} %bitcast.25, f32[3072,512]{1,0:T(8,128)S(1)} %down_product.7.refs_3_), custom_call_target="tpu_custom_call" | custom-call | tf_op jit(solution)/shard_map/down_product/pallas_call | solution.py:32
  203.0 7.2 %weight_gradient.4.refs_4_ = bf16[3072,6144]{1,0:T(8,128)(2,1)} custom-call(s32[1]{0:T(128)} %bitcast.section_ref, bf16[3072,512]{1,0:T(8,128)(2,1)S(1)} %transposed.1.turned_ref, bf16[256,768]{1,0:T(8,128)(2,1)S(1)} %get-tuple-element.284.refs_0_, bf16[256,768]{1,0:T(8,128)(2,1)S(1)} %get-tuple-element.232.refs_1_, ...), custom_call_target="tpu_custom_call" | custom-call | tf_op jit(solution)/shard_map/weight_gradient/pallas_call | solution.py:32
  211.3 1.3 collective-permute-start.45
  213.1 1.6 collective-permute-done.43.refs_1_.refs_3_
  214.7 6.0 %down_product.12.refs_3_ = f32[3072,256]{1,0:T(8,128)S(1)} custom-call(s32[1]{0:T(128)} %bitcast.section_ref, bf16[256,768]{1,0:T(8,128)(2,1)S(1)} %get-tuple-element.310.refs_0_.refs_1_, bf16[256,768]{1,0:T(8,128)(2,1)S(1)} %collective-permute-done.43.refs_1_.refs_3_, bf16[3072,6144]{1,0:T(8,128)(2,1)} %bitcast.26, f32[3072,256]{1,0:T(8,128)S(1)} %down_product.11.refs_3_), custom_call_target="tpu_custom_call" | custom-call | tf_op jit(solution)/shard_map/down_product/pallas_call | solution.py:32
  220.7 7.2 %weight_gradient.5.refs_4_ = bf16[3072,6144]{1,0:T(8,128)(2,1)} custom-call(s32[1]{0:T(128)} %bitcast.section_ref, bf16[3072,512]{1,0:T(8,128)(2,1)S(1)} %transposed.1.turned_ref, bf16[256,768]{1,0:T(8,128)(2,1)S(1)} %get-tuple-element.293.refs_0_, bf16[256,768]{1,0:T(8,128)(2,1)S(1)} %get-tuple-element.294.refs_0_.refs_1_, ...), custom_call_target="tpu_custom_call", output_to_operand_aliasing={{}: (6, {})} | custom-call | tf_op jit(solution)/shard_map/weight_gradient/pallas_call | solution.py:32
  228.0 4.8 %collective-permute-done.45.refs_2_ = bf16[512,768]{1,0:T(8,128)(2,1)S(1)} collective-permute-done((bf16[512,768]{1,0:T(8,128)(2,1)S(1)}, bf16[512,768]{1,0:T(8,128)(2,1)S(1)}, u32[]{:S(2)}, u32[]{:S(2)}) %collective-permute-start.45) | collective-permute-done | bytes 786464 | tf_op jit(solution)/shard_map/ppermute | solution.py:399
  233.1 1.7 collective-permute-done.46.refs_1_.refs_3_
  234.9 6.3 %down_product.13 = (bf16[128,3072]{1,0:T(8,128)(2,1)S(1)}, f32[128,3072]{1,0:T(8,128)S(1)}) custom-call(s32[1]{0:T(128)} %bitcast.section_ref, bf16[256,768]{1,0:T(8,128)(2,1)S(1)} %get-tuple-element.313.refs_0_.refs_1_, bf16[256,768]{1,0:T(8,128)(2,1)S(1)} %collective-permute-done.46.refs_1_.refs_3_, bf16[3072,6144]{1,0:T(8,128)(2,1)} %bitcast.27, ...), custom_call_target="tpu_custom_call" | custom-call | tf_op jit(solution)/shard_map/down_product/pallas_call | solution.py:32
  241.1 1.6 collective-permute-start.47
  242.7 7.2 %weight_gradient.6.refs_4_ = bf16[3072,6144]{1,0:T(8,128)(2,1)} custom-call(s32[1]{0:T(128)} %bitcast.section_ref, bf16[3072,512]{1,0:T(8,128)(2,1)S(1)} %transposed.1.turned_ref, bf16[256,768]{1,0:T(8,128)(2,1)S(1)} %get-tuple-element.309.refs_0_, bf16[256,768]{1,0:T(8,128)(2,1)S(1)} %get-tuple-element.310.refs_0_.refs_1_, ...), custom_call_target="tpu_custom_call", output_to_operand_aliasing={{}: (6, {})} | custom-call | tf_op jit(solution)/shard_map/weight_gradient/pallas_call | solution.py:32
  249.9 7.2 %weight_gradient.7 = bf16[3072,6144]{1,0:T(8,128)(2,1)} custom-call(s32[1]{0:T(128)} %bitcast.section_ref, bf16[3072,512]{1,0:T(8,128)(2,1)S(1)} %transposed.1.turned_ref, bf16[256,768]{1,0:T(8,128)(2,1)S(1)} %get-tuple-element.312.refs_0_, bf16[256,768]{1,0:T(8,128)(2,1)S(1)} %get-tuple-element.313.refs_0_.refs_1_, ...), custom_call_target="tpu_custom_call", output_to_operand_aliasing={{}: (6, {})} | custom-call | tf_op jit(solution)/shard_map/weight_gradient/pallas_call | solution.py:32
  257.1 3.7 %collective-permute-done.47 = bf16[128,3072]{1,0:T(8,128)(2,1)S(1)} collective-permute-done((bf16[128,3072]{1,0:T(8,128)(2,1)S(1)}, bf16[128,3072]{1,0:T(8,128)(2,1)S(1)}, u32[]{:S(2)}, u32[]{:S(2)}) %collective-permute-start.47) | collective-permute-done | bytes 786464 | tf_op jit(solution)/shard_map/ppermute | solution.py:317
  260.8 1.0 fusion.1
  (94 shorter events, 22.6 us)
Async XLA Ops:
  0.6 23.9 %copy-start = (f32[3072]{0:T(1024)S(1)}, f32[3072]{0:T(1024)}, u32[]{:S(2)}) copy-start(f32[3072]{0:T(1024)} %param.6) | copy-start | bytes 36868
  1.9 22.1 %collective-permute-start.1 = (bf16[128,3072]{1,0:T(8,128)(2,1)S(1)}, bf16[128,3072]{1,0:T(8,128)(2,1)S(1)}, u32[]{:S(2)}, u32[]{:S(2)}) collective-permute-start(bf16[128,3072]{1,0:T(8,128)(2,1)S(1)} %broadcast_select_fusion.refs_1_), channel_id=1, source_target_pairs={{0,2},{1,3},{2,0},{3,1},{4,6},{5,7},{6,4},{7,5},{8,10},{9,11},{10,... | collective-permute-start | bytes 2359304 | tf_op jit(solution)/shard_map/ppermute | solution.py:317
  4.9 19.1 %collective-permute-start = (bf16[128,3072]{1,0:T(8,128)(2,1)S(1)}, bf16[128,3072]{1,0:T(8,128)(2,1)S(1)}, u32[]{:S(2)}, u32[]{:S(2)}) collective-permute-start(bf16[128,3072]{1,0:T(8,128)(2,1)S(1)} %broadcast_select_fusion.refs_1_), channel_id=1, source_target_pairs={{0,1},{1,0},{2,3},{3,2},{4,5},{5,4},{6,7},{7,6},{8,9},{9,8},{10,11... | collective-permute-start | bytes 2359304 | tf_op jit(solution)/shard_map/ppermute | solution.py:317
  19.8 4.2 %collective-permute-start.2 = (f32[128,2]{0,1:T(2,128)S(1)}, f32[128,2]{0,1:T(2,128)S(1)}, u32[]{:S(2)}, u32[]{:S(2)}) collective-permute-start(f32[128,2]{0,1:T(2,128)S(1)} %pad_maximum_fusion), channel_id=1, source_target_pairs={{0,1},{1,0},{2,3},{3,2},{4,5},{5,4},{6,7},{7,6},{8,9},{9,8},{10,11... | collective-permute-start | bytes 3080 | tf_op jit(solution)/shard_map/ppermute | solution.py:317
  24.1 20.9 %collective-permute-start.5 = (bf16[128,3072]{1,0:T(8,128)(2,1)S(1)}, bf16[128,3072]{1,0:T(8,128)(2,1)S(1)}, u32[]{:S(2)}, u32[]{:S(2)}) collective-permute-start(bf16[128,3072]{1,0:T(8,128)(2,1)S(1)} %collective-permute-done.refs_0_), channel_id=1, source_target_pairs={{0,2},{1,3},{2,0},{3,1},{4,6},{5,7},{6,4},{7,5},{8,10},{9,11},{10,... | collective-permute-start | bytes 2359304 | tf_op jit(solution)/shard_map/ppermute | solution.py:317
  31.1 1.8 collective-permute-start.3
  33.1 20.7 %collective-permute-start.6 = (bf16[512,768]{1,0:T(8,128)(2,1)S(1)}, bf16[512,768]{1,0:T(8,128)(2,1)S(1)}, u32[]{:S(2)}, u32[]{:S(2)}) collective-permute-start(bf16[512,768]{1,0:T(8,128)(2,1)S(1)} %stacked.8.refs_0_), channel_id=1, source_target_pairs={{0,4},{12,8},{1,5},{13,9},{2,6},{14,10},{3,7},{15,11},{16,20},{28,... | collective-permute-start | bytes 2359304 | tf_op jit(solution)/shard_map/ppermute | solution.py:388
  36.8 8.3 %collective-permute-start.4 = (f32[256,2]{1,0:T(8,128)S(1)}, f32[256,2]{1,0:T(8,128)S(1)}, u32[]{:S(2)}, u32[]{:S(2)}) collective-permute-start(f32[256,2]{1,0:T(8,128)S(1)} %copy.12.scale_ref), channel_id=1, source_target_pairs={{0,2},{1,3},{2,0},{3,1},{4,6},{5,7},{6,4},{7,5},{8,10},{9,11},{10,... | collective-permute-start | bytes 6152 | tf_op jit(solution)/shard_map/ppermute | solution.py:317
  51.6 2.6 %collective-permute-start.7 = (bf16[256,768]{1,0:T(8,128)(2,1)S(1)}, bf16[256,768]{1,0:T(8,128)(2,1)S(1)}, u32[]{:S(2)}, u32[]{:S(2)}) collective-permute-start(bf16[256,768]{1,0:T(8,128)(2,1)S(1)} %get-tuple-element.181), channel_id=1, source_target_pairs={{0,16},{16,0},{1,17},{17,1},{2,18},{18,2},{3,19},{19,3},{4,20},{20... | collective-permute-start | bytes 1179656 | tf_op jit(solution)/shard_map/ppermute | solution.py:321
  54.5 22.6 %collective-permute-start.9 = (bf16[512,768]{1,0:T(8,128)(2,1)S(1)}, bf16[512,768]{1,0:T(8,128)(2,1)S(1)}, u32[]{:S(2)}, u32[]{:S(2)}) collective-permute-start(bf16[512,768]{1,0:T(8,128)(2,1)S(1)} %stacked.9.refs_0_), channel_id=1, source_target_pairs={{0,4},{12,8},{1,5},{13,9},{2,6},{14,10},{3,7},{15,11},{16,20},{28,... | collective-permute-start | bytes 2359304 | tf_op jit(solution)/shard_map/ppermute | solution.py:388
  64.2 1.8 collective-permute-start.8
  64.3 14.1 %collective-permute-start.10 = (bf16[512,768]{1,0:T(8,128)(2,1)S(1)}, bf16[512,768]{1,0:T(8,128)(2,1)S(1)}, u32[]{:S(2)}, u32[]{:S(2)}) collective-permute-start(bf16[512,768]{1,0:T(8,128)(2,1)S(1)} %added.8.refs_1_), channel_id=1, source_target_pairs={{4,8},{8,4},{5,9},{9,5},{6,10},{10,6},{7,11},{11,7},{20,24},{24,20... | collective-permute-start | bytes 2359304 | tf_op jit(solution)/shard_map/ppermute | solution.py:393
  66.2 33.6 %collective-permute-start.12 = (bf16[512,768]{1,0:T(8,128)(2,1)S(1)}, bf16[512,768]{1,0:T(8,128)(2,1)S(1)}, u32[]{:S(2)}, u32[]{:S(2)}) collective-permute-start(bf16[512,768]{1,0:T(8,128)(2,1)S(1)} %stacked.10.refs_0_), channel_id=1, source_target_pairs={{0,4},{12,8},{1,5},{13,9},{2,6},{14,10},{3,7},{15,11},{16,20},{28,... | collective-permute-start | bytes 2359304 | tf_op jit(solution)/shard_map/ppermute | solution.py:388
  77.6 23.4 %collective-permute-start.13 = (bf16[512,768]{1,0:T(8,128)(2,1)S(1)}, bf16[512,768]{1,0:T(8,128)(2,1)S(1)}, u32[]{:S(2)}, u32[]{:S(2)}) collective-permute-start(bf16[512,768]{1,0:T(8,128)(2,1)S(1)} %added.9.refs_1_), channel_id=1, source_target_pairs={{4,8},{8,4},{5,9},{9,5},{6,10},{10,6},{7,11},{11,7},{20,24},{24,20... | collective-permute-start | bytes 2359304 | tf_op jit(solution)/shard_map/ppermute | solution.py:393
  78.3 2.4 collective-permute-start.11
  79.4 25.7 %collective-permute-start.14 = (bf16[512,768]{1,0:T(8,128)(2,1)S(1)}, bf16[512,768]{1,0:T(8,128)(2,1)S(1)}, u32[]{:S(2)}, u32[]{:S(2)}) collective-permute-start(bf16[512,768]{1,0:T(8,128)(2,1)S(1)} %activated.8.refs_1_), channel_id=1, source_target_pairs={{4,0},{8,12},{5,1},{9,13},{6,2},{10,14},{7,3},{11,15},{20,16},{24,... | collective-permute-start | bytes 2359304 | tf_op jit(solution)/shard_map/ppermute | solution.py:399
  81.0 29.0 %collective-permute-start.16 = (bf16[512,768]{1,0:T(8,128)(2,1)S(1)}, bf16[512,768]{1,0:T(8,128)(2,1)S(1)}, u32[]{:S(2)}, u32[]{:S(2)}) collective-permute-start(bf16[512,768]{1,0:T(8,128)(2,1)S(1)} %stacked.11.refs_0_), channel_id=1, source_target_pairs={{0,4},{12,8},{1,5},{13,9},{2,6},{14,10},{3,7},{15,11},{16,20},{28,... | collective-permute-start | bytes 2359304 | tf_op jit(solution)/shard_map/ppermute | solution.py:388
  100.3 10.3 %collective-permute-start.17 = (bf16[512,768]{1,0:T(8,128)(2,1)S(1)}, bf16[512,768]{1,0:T(8,128)(2,1)S(1)}, u32[]{:S(2)}, u32[]{:S(2)}) collective-permute-start(bf16[512,768]{1,0:T(8,128)(2,1)S(1)} %added.10.refs_1_), channel_id=1, source_target_pairs={{4,8},{8,4},{5,9},{9,5},{6,10},{10,6},{7,11},{11,7},{20,24},{24,20... | collective-permute-start | bytes 2359304 | tf_op jit(solution)/shard_map/ppermute | solution.py:393
  102.0 20.4 %collective-permute-start.18 = (bf16[512,768]{1,0:T(8,128)(2,1)S(1)}, bf16[512,768]{1,0:T(8,128)(2,1)S(1)}, u32[]{:S(2)}, u32[]{:S(2)}) collective-permute-start(bf16[512,768]{1,0:T(8,128)(2,1)S(1)} %activated.9.refs_1_), channel_id=1, source_target_pairs={{4,0},{8,12},{5,1},{9,13},{6,2},{10,14},{7,3},{11,15},{20,16},{24,... | collective-permute-start | bytes 2359304 | tf_op jit(solution)/shard_map/ppermute | solution.py:399
  103.3 2.2 collective-permute-start.15
  105.1 18.9 %collective-permute-start.19 = (bf16[256,768]{1,0:T(8,128)(2,1)S(1)}, bf16[256,768]{1,0:T(8,128)(2,1)S(1)}, u32[]{:S(2)}, u32[]{:S(2)}) collective-permute-start(bf16[256,768]{1,0:T(8,128)(2,1)S(1)} %get-tuple-element.230), channel_id=1, source_target_pairs={{0,16},{16,0},{1,17},{17,1},{2,18},{18,2},{3,19},{19,3},{4,20},{20... | collective-permute-start | bytes 1179656 | tf_op jit(solution)/shard_map/ppermute | solution.py:321
  105.7 31.1 %collective-permute-start.22 = (bf16[512,768]{1,0:T(8,128)(2,1)S(1)}, bf16[512,768]{1,0:T(8,128)(2,1)S(1)}, u32[]{:S(2)}, u32[]{:S(2)}) collective-permute-start(bf16[512,768]{1,0:T(8,128)(2,1)S(1)} %stacked.12.refs_0_), channel_id=1, source_target_pairs={{0,4},{12,8},{1,5},{13,9},{2,6},{14,10},{3,7},{15,11},{16,20},{28,... | collective-permute-start | bytes 2359304 | tf_op jit(solution)/shard_map/ppermute | solution.py:388
  110.4 13.9 %collective-permute-start.21 = (bf16[256,768]{1,0:T(8,128)(2,1)S(1)}, bf16[256,768]{1,0:T(8,128)(2,1)S(1)}, u32[]{:S(2)}, u32[]{:S(2)}) collective-permute-start(bf16[256,768]{1,0:T(8,128)(2,1)S(1)} %get-tuple-element.234), channel_id=1, source_target_pairs={{0,16},{16,0},{1,17},{17,1},{2,18},{18,2},{3,19},{19,3},{4,20},{20... | collective-permute-start | bytes 1179656 | tf_op jit(solution)/shard_map/ppermute | solution.py:321
  110.5 27.8 %collective-permute-start.23 = (bf16[512,768]{1,0:T(8,128)(2,1)S(1)}, bf16[512,768]{1,0:T(8,128)(2,1)S(1)}, u32[]{:S(2)}, u32[]{:S(2)}) collective-permute-start(bf16[512,768]{1,0:T(8,128)(2,1)S(1)} %added.11.refs_1_), channel_id=1, source_target_pairs={{4,8},{8,4},{5,9},{9,5},{6,10},{10,6},{7,11},{11,7},{20,24},{24,20... | collective-permute-start | bytes 2359304 | tf_op jit(solution)/shard_map/ppermute | solution.py:393
  122.4 19.5 %collective-permute-start.24 = (bf16[512,768]{1,0:T(8,128)(2,1)S(1)}, bf16[512,768]{1,0:T(8,128)(2,1)S(1)}, u32[]{:S(2)}, u32[]{:S(2)}) collective-permute-start(bf16[512,768]{1,0:T(8,128)(2,1)S(1)} %activated.10.refs_1_), channel_id=1, source_target_pairs={{4,0},{8,12},{5,1},{9,13},{6,2},{10,14},{7,3},{11,15},{20,16},{24,... | collective-permute-start | bytes 2359304 | tf_op jit(solution)/shard_map/ppermute | solution.py:399
  124.0 5.0 %collective-permute-start.20 = (bf16[256,768]{1,0:T(8,128)(2,1)S(1)}, bf16[256,768]{1,0:T(8,128)(2,1)S(1)}, u32[]{:S(2)}, u32[]{:S(2)}) collective-permute-start(bf16[256,768]{1,0:T(8,128)(2,1)S(1)} %get-tuple-element.233), channel_id=1, source_target_pairs={{0,16},{16,0},{1,17},{17,1},{2,18},{18,2},{3,19},{19,3},{4,20},{20... | collective-permute-start | bytes 1179656 | tf_op jit(solution)/shard_map/ppermute | solution.py:321
  124.4 27.6 %collective-permute-start.27 = (bf16[512,768]{1,0:T(8,128)(2,1)S(1)}, bf16[512,768]{1,0:T(8,128)(2,1)S(1)}, u32[]{:S(2)}, u32[]{:S(2)}) collective-permute-start(bf16[512,768]{1,0:T(8,128)(2,1)S(1)} %stacked.13.refs_0_), channel_id=1, source_target_pairs={{0,4},{12,8},{1,5},{13,9},{2,6},{14,10},{3,7},{15,11},{16,20},{28,... | collective-permute-start | bytes 2359304 | tf_op jit(solution)/shard_map/ppermute | solution.py:388
  137.3 15.9 %collective-permute-start.28 = (bf16[512,768]{1,0:T(8,128)(2,1)S(1)}, bf16[512,768]{1,0:T(8,128)(2,1)S(1)}, u32[]{:S(2)}, u32[]{:S(2)}) collective-permute-start(bf16[512,768]{1,0:T(8,128)(2,1)S(1)} %added.12.refs_1_), channel_id=1, source_target_pairs={{4,8},{8,4},{5,9},{9,5},{6,10},{10,6},{7,11},{11,7},{20,24},{24,20... | collective-permute-start | bytes 2359304 | tf_op jit(solution)/shard_map/ppermute | solution.py:393
  138.0 4.2 %collective-permute-start.25 = (bf16[256,768]{1,0:T(8,128)(2,1)S(1)}, bf16[256,768]{1,0:T(8,128)(2,1)S(1)}, u32[]{:S(2)}, u32[]{:S(2)}) collective-permute-start(bf16[256,768]{1,0:T(8,128)(2,1)S(1)} %get-tuple-element.246), channel_id=1, source_target_pairs={{0,16},{16,0},{1,17},{17,1},{2,18},{18,2},{3,19},{19,3},{4,20},{20... | collective-permute-start | bytes 1179656 | tf_op jit(solution)/shard_map/ppermute | solution.py:321
  139.3 21.7 %collective-permute-start.29 = (bf16[512,768]{1,0:T(8,128)(2,1)S(1)}, bf16[512,768]{1,0:T(8,128)(2,1)S(1)}, u32[]{:S(2)}, u32[]{:S(2)}) collective-permute-start(bf16[512,768]{1,0:T(8,128)(2,1)S(1)} %activated.11.refs_1_), channel_id=1, source_target_pairs={{4,0},{8,12},{5,1},{9,13},{6,2},{10,14},{7,3},{11,15},{20,16},{24,... | collective-permute-start | bytes 2359304 | tf_op jit(solution)/shard_map/ppermute | solution.py:399
  142.2 3.8 %collective-permute-start.26 = (bf16[256,768]{1,0:T(8,128)(2,1)S(1)}, bf16[256,768]{1,0:T(8,128)(2,1)S(1)}, u32[]{:S(2)}, u32[]{:S(2)}) collective-permute-start(bf16[256,768]{1,0:T(8,128)(2,1)S(1)} %get-tuple-element.248), channel_id=1, source_target_pairs={{0,16},{16,0},{1,17},{17,1},{2,18},{18,2},{3,19},{19,3},{4,20},{20... | collective-permute-start | bytes 1179656 | tf_op jit(solution)/shard_map/ppermute | solution.py:321
  142.5 28.9 %collective-permute-start.32 = (bf16[512,768]{1,0:T(8,128)(2,1)S(1)}, bf16[512,768]{1,0:T(8,128)(2,1)S(1)}, u32[]{:S(2)}, u32[]{:S(2)}) collective-permute-start(bf16[512,768]{1,0:T(8,128)(2,1)S(1)} %stacked.14.refs_0_), channel_id=1, source_target_pairs={{0,4},{12,8},{1,5},{13,9},{2,6},{14,10},{3,7},{15,11},{16,20},{28,... | collective-permute-start | bytes 2359304 | tf_op jit(solution)/shard_map/ppermute | solution.py:388
  152.4 20.1 %collective-permute-start.33 = (bf16[512,768]{1,0:T(8,128)(2,1)S(1)}, bf16[512,768]{1,0:T(8,128)(2,1)S(1)}, u32[]{:S(2)}, u32[]{:S(2)}) collective-permute-start(bf16[512,768]{1,0:T(8,128)(2,1)S(1)} %added.13.refs_1_), channel_id=1, source_target_pairs={{4,8},{8,4},{5,9},{9,5},{6,10},{10,6},{7,11},{11,7},{20,24},{24,20... | collective-permute-start | bytes 2359304 | tf_op jit(solution)/shard_map/ppermute | solution.py:393
  154.2 23.8 %collective-permute-start.34 = (bf16[512,768]{1,0:T(8,128)(2,1)S(1)}, bf16[512,768]{1,0:T(8,128)(2,1)S(1)}, u32[]{:S(2)}, u32[]{:S(2)}) collective-permute-start(bf16[512,768]{1,0:T(8,128)(2,1)S(1)} %activated.12.refs_1_), channel_id=1, source_target_pairs={{4,0},{8,12},{5,1},{9,13},{6,2},{10,14},{7,3},{11,15},{20,16},{24,... | collective-permute-start | bytes 2359304 | tf_op jit(solution)/shard_map/ppermute | solution.py:399
  155.5 5.9 %collective-permute-start.30 = (bf16[256,768]{1,0:T(8,128)(2,1)S(1)}, bf16[256,768]{1,0:T(8,128)(2,1)S(1)}, u32[]{:S(2)}, u32[]{:S(2)}) collective-permute-start(bf16[256,768]{1,0:T(8,128)(2,1)S(1)} %get-tuple-element.260), channel_id=1, source_target_pairs={{0,16},{16,0},{1,17},{17,1},{2,18},{18,2},{3,19},{19,3},{4,20},{20... | collective-permute-start | bytes 1179656 | tf_op jit(solution)/shard_map/ppermute | solution.py:321
  161.3 4.1 %collective-permute-start.31 = (bf16[256,768]{1,0:T(8,128)(2,1)S(1)}, bf16[256,768]{1,0:T(8,128)(2,1)S(1)}, u32[]{:S(2)}, u32[]{:S(2)}) collective-permute-start(bf16[256,768]{1,0:T(8,128)(2,1)S(1)} %get-tuple-element.262), channel_id=1, source_target_pairs={{0,16},{16,0},{1,17},{17,1},{2,18},{18,2},{3,19},{19,3},{4,20},{20... | collective-permute-start | bytes 1179656 | tf_op jit(solution)/shard_map/ppermute | solution.py:321
  161.6 26.3 %collective-permute-start.36 = (bf16[512,768]{1,0:T(8,128)(2,1)S(1)}, bf16[512,768]{1,0:T(8,128)(2,1)S(1)}, u32[]{:S(2)}, u32[]{:S(2)}) collective-permute-start(bf16[512,768]{1,0:T(8,128)(2,1)S(1)} %stacked.15.refs_0_), channel_id=1, source_target_pairs={{0,4},{12,8},{1,5},{13,9},{2,6},{14,10},{3,7},{15,11},{16,20},{28,... | collective-permute-start | bytes 2359304 | tf_op jit(solution)/shard_map/ppermute | solution.py:388
  171.9 17.2 %collective-permute-start.37 = (bf16[512,768]{1,0:T(8,128)(2,1)S(1)}, bf16[512,768]{1,0:T(8,128)(2,1)S(1)}, u32[]{:S(2)}, u32[]{:S(2)}) collective-permute-start(bf16[512,768]{1,0:T(8,128)(2,1)S(1)} %added.14.refs_1_), channel_id=1, source_target_pairs={{4,8},{8,4},{5,9},{9,5},{6,10},{10,6},{7,11},{11,7},{20,24},{24,20... | collective-permute-start | bytes 2359304 | tf_op jit(solution)/shard_map/ppermute | solution.py:393
  173.6 21.2 %collective-permute-start.38 = (bf16[512,768]{1,0:T(8,128)(2,1)S(1)}, bf16[512,768]{1,0:T(8,128)(2,1)S(1)}, u32[]{:S(2)}, u32[]{:S(2)}) collective-permute-start(bf16[512,768]{1,0:T(8,128)(2,1)S(1)} %activated.13.refs_1_), channel_id=1, source_target_pairs={{4,0},{8,12},{5,1},{9,13},{6,2},{10,14},{7,3},{11,15},{20,16},{24,... | collective-permute-start | bytes 2359304 | tf_op jit(solution)/shard_map/ppermute | solution.py:399
  178.3 1.8 collective-permute-start.35
  186.4 23.9 %collective-permute-start.40 = (bf16[128,3072]{1,0:T(8,128)(2,1)S(1)}, bf16[128,3072]{1,0:T(8,128)(2,1)S(1)}, u32[]{:S(2)}, u32[]{:S(2)}) collective-permute-start(bf16[128,3072]{1,0:T(8,128)(2,1)S(1)} %get-tuple-element.274), channel_id=1, source_target_pairs={{0,2},{1,3},{2,0},{3,1},{4,6},{5,7},{6,4},{7,5},{8,10},{9,11},{10,... | collective-permute-start | bytes 2359304 | tf_op jit(solution)/shard_map/ppermute | solution.py:317
  188.4 21.9 %collective-permute-start.41 = (bf16[512,768]{1,0:T(8,128)(2,1)S(1)}, bf16[512,768]{1,0:T(8,128)(2,1)S(1)}, u32[]{:S(2)}, u32[]{:S(2)}) collective-permute-start(bf16[512,768]{1,0:T(8,128)(2,1)S(1)} %added.15.refs_1_), channel_id=1, source_target_pairs={{4,8},{8,4},{5,9},{9,5},{6,10},{10,6},{7,11},{11,7},{20,24},{24,20... | collective-permute-start | bytes 2359304 | tf_op jit(solution)/shard_map/ppermute | solution.py:393
  190.1 22.4 %collective-permute-start.42 = (bf16[512,768]{1,0:T(8,128)(2,1)S(1)}, bf16[512,768]{1,0:T(8,128)(2,1)S(1)}, u32[]{:S(2)}, u32[]{:S(2)}) collective-permute-start(bf16[512,768]{1,0:T(8,128)(2,1)S(1)} %activated.14.refs_1_), channel_id=1, source_target_pairs={{4,0},{8,12},{5,1},{9,13},{6,2},{10,14},{7,3},{11,15},{20,16},{24,... | collective-permute-start | bytes 2359304 | tf_op jit(solution)/shard_map/ppermute | solution.py:399
  195.2 1.8 collective-permute-start.39
  195.3 32.7 %collective-permute-start.44 = (bf16[128,3072]{1,0:T(8,128)(2,1)S(1)}, bf16[128,3072]{1,0:T(8,128)(2,1)S(1)}, u32[]{:S(2)}, u32[]{:S(2)}) collective-permute-start(bf16[128,3072]{1,0:T(8,128)(2,1)S(1)} %get-tuple-element.275), channel_id=1, source_target_pairs={{0,2},{1,3},{2,0},{3,1},{4,6},{5,7},{6,4},{7,5},{8,10},{9,11},{10,... | collective-permute-start | bytes 2359304 | tf_op jit(solution)/shard_map/ppermute | solution.py:317
  211.3 21.5 %collective-permute-start.45 = (bf16[512,768]{1,0:T(8,128)(2,1)S(1)}, bf16[512,768]{1,0:T(8,128)(2,1)S(1)}, u32[]{:S(2)}, u32[]{:S(2)}) collective-permute-start(bf16[512,768]{1,0:T(8,128)(2,1)S(1)} %activated.15.refs_1_), channel_id=1, source_target_pairs={{4,0},{8,12},{5,1},{9,13},{6,2},{10,14},{7,3},{11,15},{20,16},{24,... | collective-permute-start | bytes 2359304 | tf_op jit(solution)/shard_map/ppermute | solution.py:399
  212.9 1.8 collective-permute-start.43
  233.1 1.8 collective-permute-start.46
  241.1 19.6 %collective-permute-start.47 = (bf16[128,3072]{1,0:T(8,128)(2,1)S(1)}, bf16[128,3072]{1,0:T(8,128)(2,1)S(1)}, u32[]{:S(2)}, u32[]{:S(2)}) collective-permute-start(bf16[128,3072]{1,0:T(8,128)(2,1)S(1)} %get-tuple-element.307), channel_id=1, source_target_pairs={{0,1},{1,0},{2,3},{3,2},{4,5},{5,4},{6,7},{7,6},{8,9},{9,8},{10,11... | collective-permute-start | bytes 2359304 | tf_op jit(solution)/shard_map/ppermute | solution.py:317

commit v12 on v10

--- a/solution.py
+++ b/solution.py
@@ -454,27 +454,27 @@
     for t in range(count + 2):
         if 0 < t < count:
             inward(chunks[order[t]])
+        if t == 3:
+            turned = run(transposed, x_all)["value"]
         tick(t)
         need(t + 3)
         far_part, near_part = t - 3, t - 2 - parts
         if far_part == 0:
-            turned = run(transposed, x_all)["value"]
             near_sum = far_sum = go_down(0, both, None, 0)
         elif 0 < far_part < parts - 1:
             far_sum = go_down(far_part, [FAR], far_sum, FAR if far_part == 1 else 0)
         elif far_part == parts - 1:
             sent_far = go_down(far_part, [FAR], far_sum, 0, [jnp.bfloat16] * 2)
             arrived = [from_peer(value, across) for value in sent_far["value"]]
-            go_gradient(0)
         elif 0 < near_part < parts - 1:
             near_sum = go_down(near_part, [NEAR], near_sum, NEAR if near_part == 1 else 0)
         if t == count:
-            go_gradient(1)
+            go_gradient(0)
         if t >= count - 1 and t <= count:
             k = t - count + 1
             last[-1]["value"], arrived[k] = lax.optimization_barrier((last[-1]["value"], arrived[k]))
     sent_near = go_down(parts - 1, [NEAR], near_sum, 0, [jnp.bfloat16, jnp.float32], arrived)
-    for part in range(2, parts):
+    for part in range(1, parts):
         go_gradient(part)
 
     own = sent_near["value"][1]

time: 270 us -> 269 us (level)
  starting transfers between devices: 66 us -> 62 us
  waiting for transfers between devices: 55.6 us -> 58.5 us
    ppermute x8, waiting for transfers between devices: 2.18 us -> 10.6 us  [inward(): lax.ppermute(value, 'dp', [(hop, hop + 1), (line - 1 - hop, line - 2 - ho...]
    ppermute x8, waiting for transfers between devices: 8.72 us -> 4.97 us  [from_peer(): return lax.ppermute(value, 'mp', [(i, i ^ by) for i in range(peers)])]
    ppermute x8, starting transfers between devices: 11.9 us -> 9.02 us  [from_peer(): return lax.ppermute(value, 'mp', [(i, i ^ by) for i in range(peers)])]
    ppermute x8, waiting for transfers between devices: 38.2 us -> 35.5 us  [outward(): lax.ppermute(value, 'dp', [(hop + 1, hop), (line - 2 - hop, line - 1 - ho...]
  transfers between devices with their start and end apart: 48 -> 48, of which waited for: 18 -> 19; matrix products, arithmetic and copies ran while one was open for 1% -> 1% of each run, Pallas kernels for 46% -> 46%
where the time goes in v12:
time: 269 us; the launch traced here: 268 us
  Pallas kernels  130 us (48%)
  starting transfers between devices  62 us (23%)
  waiting for transfers between devices  58.5 us (22%)
  blocking collectives  12 us (4%)
  other arithmetic  3.71 us (1%)
    pallas_call x52, Pallas kernels, call(): pl.pallas_call(kernel, grid_spec=pltpu.PrefetchScalarGridSpec(num_scalar_...  130 us
    ppermute x8, waiting for transfers between devices, outward(): lax.ppermute(value, 'dp', [(hop + 1, hop), (line - 2 - hop, line - 1 - ho...  35.5 us
    ppermute x8, starting transfers between devices, inward(): lax.ppermute(value, 'dp', [(hop, hop + 1), (line - 1 - hop, line - 2 - ho...  35.3 us
    psum x1, blocking collectives, local(): lax.psum((jnp.sum(values, 1), jnp.sum(values * values, 1)), 'dp')  12 us
    ppermute x8, starting transfers between devices, outward(): lax.ppermute(value, 'dp', [(hop + 1, hop), (line - 2 - hop, line - 1 - ho...  10.7 us
    ppermute x8, waiting for transfers between devices, inward(): lax.ppermute(value, 'dp', [(hop, hop + 1), (line - 1 - hop, line - 2 - ho...  10.6 us
    ppermute x8, starting transfers between devices, from_peer(): return lax.ppermute(value, 'mp', [(i, i ^ by) for i in range(peers)])  9.02 us
    ppermute x16, waiting for transfers between devices, across_sections(): return lax.ppermute(value, 'section', [(0, 1), (1, 0)])  7.47 us
  transfers between devices with their start and end apart: 48, of which 19 were waited for; matrix products, arithmetic and copies ran while one was open for 1% of the time, Pallas kernels for 46%

profile of v12, /device:TPU:0, one launch (start us, length us, event | category | flops | bytes accessed | tf_op | source)
XLA Modules:
  0.0 267.6 jit_solution(9251517516800208814)
XLA Ops:
  0.7 1.2 broadcast_select_fusion.refs_1_
  1.9 3.0 %collective-permute-start = (bf16[128,3072]{1,0:T(8,128)(2,1)S(1)}, bf16[128,3072]{1,0:T(8,128)(2,1)S(1)}, u32[]{:S(2)}, u32[]{:S(2)}) collective-permute-start(bf16[128,3072]{1,0:T(8,128)(2,1)S(1)} %broadcast_select_fusion.refs_1_), channel_id=1, source_target_pairs={{0,1},{1,0},{2,3},{3,2},{4,5},{5,4},{6,7},{7,6},{8,9},{9,8},{10,11... | collective-permute-start | bytes 2359304 | tf_op jit(solution)/shard_map/ppermute | solution.py:317
  4.9 1.5 collective-permute-start.1
  6.4 1.4 convert_reduce_fusion
  7.8 12.0 %all-reduce = (f32[128]{0:T(128)S(1)}, f32[128]{0:T(128)S(1)}) all-reduce(f32[128]{0:T(128)S(1)} %get-tuple-element.313, f32[128]{0:T(128)S(1)} %get-tuple-element.312), channel_id=1, replica_groups=mesh['section'=2,'dp'=4,'mp'=4] {'dp'}, use_global_device_ids=true, to_apply=%region_3.4 | all-reduce | flops 256 | bytes 2048 | tf_op jit(solution)/shard_map/psum | solution.py:359
  20.4 3.0 %collective-permute-done.2 = f32[128,2]{0,1:T(2,128)S(1)} collective-permute-done((f32[128,2]{0,1:T(2,128)S(1)}, f32[128,2]{0,1:T(2,128)S(1)}, u32[]{:S(2)}, u32[]{:S(2)}) %collective-permute-start.2) | collective-permute-done | bytes 1056 | tf_op jit(solution)/shard_map/ppermute | solution.py:317
  24.0 1.6 collective-permute-start.5
  25.6 1.2 normalize.2.rows_ref.refs_2_
  26.8 5.3 %up_product.6 = (bf16[256,768]{1,0:T(8,128)(2,1)S(1)}, bf16[256,768]{1,0:T(8,128)(2,1)S(1)}) custom-call(s32[1]{0:T(128)} %bitcast.section_ref, bf16[512,3072]{1,0:T(8,128)(2,1)S(1)} %normalize.2.rows_ref.refs_2_, bf16[3072,6144]{1,0:T(8,128)(2,1)} %bitcast.15), custom_call_target="tpu_custom_call" | custom-call | tf_op jit(solution)/shard_map/up_product/pallas_call | solution.py:32
  32.2 1.7 collective-permute-done.3.refs_1_
  34.1 3.5 %collective-permute-start.6 = (bf16[512,768]{1,0:T(8,128)(2,1)S(1)}, bf16[512,768]{1,0:T(8,128)(2,1)S(1)}, u32[]{:S(2)}, u32[]{:S(2)}) collective-permute-start(bf16[512,768]{1,0:T(8,128)(2,1)S(1)} %stacked.8.refs_0_), channel_id=1, source_target_pairs={{0,4},{12,8},{1,5},{13,9},{2,6},{14,10},{3,7},{15,11},{16,20},{28,... | collective-permute-start | bytes 2359304 | tf_op jit(solution)/shard_map/ppermute | solution.py:388
  38.2 5.2 %up_product.7 = (bf16[256,768]{1,0:T(8,128)(2,1)S(1)}, bf16[256,768]{1,0:T(8,128)(2,1)S(1)}) custom-call(s32[1]{0:T(128)} %bitcast.section_ref, bf16[512,3072]{1,0:T(8,128)(2,1)S(1)} %normalize.2.rows_ref.refs_2_, bf16[3072,6144]{1,0:T(8,128)(2,1)} %bitcast.16), custom_call_target="tpu_custom_call" | custom-call | tf_op jit(solution)/shard_map/up_product/pallas_call | solution.py:32
  43.5 1.5 collective-permute-done.4.scale_ref
  45.0 1.2 normalize.3.rows_ref.value_ref
  46.2 5.3 %up_product.8 = (bf16[256,768]{1,0:T(8,128)(2,1)S(1)}, bf16[256,768]{1,0:T(8,128)(2,1)S(1)}) custom-call(s32[1]{0:T(128)} %bitcast.section_ref, bf16[512,3072]{1,0:T(8,128)(2,1)S(1)} %normalize.3.rows_ref.value_ref, bf16[3072,6144]{1,0:T(8,128)(2,1)} %bitcast.17), custom_call_target="tpu_custom_call" | custom-call | tf_op jit(solution)/shard_map/up_product/pallas_call | solution.py:32
  51.6 3.1 %collective-permute-done.6.refs_1_ = bf16[512,768]{1,0:T(8,128)(2,1)S(1)} collective-permute-done((bf16[512,768]{1,0:T(8,128)(2,1)S(1)}, bf16[512,768]{1,0:T(8,128)(2,1)S(1)}, u32[]{:S(2)}, u32[]{:S(2)}) %collective-permute-start.6) | collective-permute-done | bytes 786464 | tf_op jit(solution)/shard_map/ppermute | solution.py:388
  55.4 4.4 %collective-permute-start.9 = (bf16[512,768]{1,0:T(8,128)(2,1)S(1)}, bf16[512,768]{1,0:T(8,128)(2,1)S(1)}, u32[]{:S(2)}, u32[]{:S(2)}) collective-permute-start(bf16[512,768]{1,0:T(8,128)(2,1)S(1)} %stacked.9.refs_0_), channel_id=1, source_target_pairs={{0,4},{12,8},{1,5},{13,9},{2,6},{14,10},{3,7},{15,11},{16,20},{28,... | collective-permute-start | bytes 2359304 | tf_op jit(solution)/shard_map/ppermute | solution.py:388
  59.8 5.3 %up_product.9 = (bf16[256,768]{1,0:T(8,128)(2,1)S(1)}, bf16[256,768]{1,0:T(8,128)(2,1)S(1)}) custom-call(s32[1]{0:T(128)} %bitcast.section_ref, bf16[512,3072]{1,0:T(8,128)(2,1)S(1)} %normalize.3.rows_ref.value_ref, bf16[3072,6144]{1,0:T(8,128)(2,1)} %bitcast.18), custom_call_target="tpu_custom_call" | custom-call | tf_op jit(solution)/shard_map/up_product/pallas_call | solution.py:32
  67.1 7.8 %up_product.10 = (bf16[256,768]{1,0:T(8,128)(2,1)S(1)}, bf16[256,768]{1,0:T(8,128)(2,1)S(1)}, bf16[256,768]{1,0:T(8,128)(2,1)S(1)}, bf16[256,768]{1,0:T(8,128)(2,1)S(1)}) custom-call(s32[1]{0:T(128)} %bitcast.section_ref, bf16[512,3072]{1,0:T(8,128)(2,1)S(1)} %normalize.3.rows_ref.value_ref, bf16[3072,6144]{1,0:T(8,128)(2,1)} %bitcast.19), custom_call_target="tpu_custom_call" | custom-call | tf_op jit(solution)/shard_map/up_product/pallas_call | solution.py:32
  74.9 3.1 %collective-permute-start.12 = (bf16[512,768]{1,0:T(8,128)(2,1)S(1)}, bf16[512,768]{1,0:T(8,128)(2,1)S(1)}, u32[]{:S(2)}, u32[]{:S(2)}) collective-permute-start(bf16[512,768]{1,0:T(8,128)(2,1)S(1)} %stacked.10.refs_0_), channel_id=1, source_target_pairs={{0,4},{12,8},{1,5},{13,9},{2,6},{14,10},{3,7},{15,11},{16,20},{28,... | collective-permute-start | bytes 2359304 | tf_op jit(solution)/shard_map/ppermute | solution.py:388
  79.3 1.0 activated.8.refs_1_
  80.3 1.5 collective-permute-start.14
  82.0 7.8 %up_product.11 = (bf16[256,768]{1,0:T(8,128)(2,1)S(1)}, bf16[256,768]{1,0:T(8,128)(2,1)S(1)}, bf16[256,768]{1,0:T(8,128)(2,1)S(1)}, bf16[256,768]{1,0:T(8,128)(2,1)S(1)}) custom-call(s32[1]{0:T(128)} %bitcast.section_ref, bf16[512,3072]{1,0:T(8,128)(2,1)S(1)} %normalize.3.rows_ref.value_ref, bf16[3072,6144]{1,0:T(8,128)(2,1)} %bitcast.20), custom_call_target="tpu_custom_call" | custom-call | tf_op jit(solution)/shard_map/up_product/pallas_call | solution.py:32
  89.8 9.5 %collective-permute-start.16 = (bf16[512,768]{1,0:T(8,128)(2,1)S(1)}, bf16[512,768]{1,0:T(8,128)(2,1)S(1)}, u32[]{:S(2)}, u32[]{:S(2)}) collective-permute-start(bf16[512,768]{1,0:T(8,128)(2,1)S(1)} %stacked.11.refs_0_), channel_id=1, source_target_pairs={{0,4},{12,8},{1,5},{13,9},{2,6},{14,10},{3,7},{15,11},{16,20},{28,... | collective-permute-start | bytes 2359304 | tf_op jit(solution)/shard_map/ppermute | solution.py:388
  100.5 1.0 activated.9.refs_1_
  101.5 1.3 collective-permute-start.18
  102.9 3.2 %collective-permute-done.14.refs_2_ = bf16[512,768]{1,0:T(8,128)(2,1)S(1)} collective-permute-done((bf16[512,768]{1,0:T(8,128)(2,1)S(1)}, bf16[512,768]{1,0:T(8,128)(2,1)S(1)}, u32[]{:S(2)}, u32[]{:S(2)}) %collective-permute-start.14) | collective-permute-done | bytes 786464 | tf_op jit(solution)/shard_map/ppermute | solution.py:399
  106.6 3.2 %collective-permute-start.22 = (bf16[512,768]{1,0:T(8,128)(2,1)S(1)}, bf16[512,768]{1,0:T(8,128)(2,1)S(1)}, u32[]{:S(2)}, u32[]{:S(2)}) collective-permute-start(bf16[512,768]{1,0:T(8,128)(2,1)S(1)} %stacked.12.refs_0_), channel_id=1, source_target_pairs={{0,4},{12,8},{1,5},{13,9},{2,6},{14,10},{3,7},{15,11},{16,20},{28,... | collective-permute-start | bytes 2359304 | tf_op jit(solution)/shard_map/ppermute | solution.py:388
  109.8 7.4 %collective-permute-done.16.refs_1_ = bf16[512,768]{1,0:T(8,128)(2,1)S(1)} collective-permute-done((bf16[512,768]{1,0:T(8,128)(2,1)S(1)}, bf16[512,768]{1,0:T(8,128)(2,1)S(1)}, u32[]{:S(2)}, u32[]{:S(2)}) %collective-permute-start.16) | collective-permute-done | bytes 786464 | tf_op jit(solution)/shard_map/ppermute | solution.py:388
  117.6 1.4 transposed.1.turned_ref
  119.9 1.0 activated.10.refs_1_
  120.9 2.0 collective-permute-done.18.refs_2_
  122.9 1.3 collective-permute-start.24
  124.9 5.5 %collective-permute-start.27 = (bf16[512,768]{1,0:T(8,128)(2,1)S(1)}, bf16[512,768]{1,0:T(8,128)(2,1)S(1)}, u32[]{:S(2)}, u32[]{:S(2)}) collective-permute-start(bf16[512,768]{1,0:T(8,128)(2,1)S(1)} %stacked.13.refs_0_), channel_id=1, source_target_pairs={{0,4},{12,8},{1,5},{13,9},{2,6},{14,10},{3,7},{15,11},{16,20},{28,... | collective-permute-start | bytes 2359304 | tf_op jit(solution)/shard_map/ppermute | solution.py:388
  130.4 7.8 %down_product.7.refs_3_ = f32[3072,512]{1,0:T(8,128)S(1)} custom-call(s32[1]{0:T(128)} %bitcast.section_ref, bf16[256,768]{1,0:T(8,128)(2,1)S(1)} %get-tuple-element.291.refs_0_, bf16[256,768]{1,0:T(8,128)(2,1)S(1)} %get-tuple-element.231.refs_1_, bf16[256,768]{1,0:T(8,128)(2,1)S(1)} %collective-permute-done.20.refs_2_, ...), custom_call_target="tpu_custom_call" | custom-call | tf_op jit(solution)/shard_map/down_product/pallas_call | solution.py:32
  140.5 1.3 collective-permute-start.29
  141.8 3.6 %collective-permute-done.24.refs_2_ = bf16[512,768]{1,0:T(8,128)(2,1)S(1)} collective-permute-done((bf16[512,768]{1,0:T(8,128)(2,1)S(1)}, bf16[512,768]{1,0:T(8,128)(2,1)S(1)}, u32[]{:S(2)}, u32[]{:S(2)}) %collective-permute-start.24) | collective-permute-done | bytes 786464 | tf_op jit(solution)/shard_map/ppermute | solution.py:399
  146.0 2.9 %collective-permute-start.32 = (bf16[512,768]{1,0:T(8,128)(2,1)S(1)}, bf16[512,768]{1,0:T(8,128)(2,1)S(1)}, u32[]{:S(2)}, u32[]{:S(2)}) collective-permute-start(bf16[512,768]{1,0:T(8,128)(2,1)S(1)} %stacked.14.refs_0_), channel_id=1, source_target_pairs={{0,4},{12,8},{1,5},{13,9},{2,6},{14,10},{3,7},{15,11},{16,20},{28,... | collective-permute-start | bytes 2359304 | tf_op jit(solution)/shard_map/ppermute | solution.py:388
  148.9 6.0 %down_product.8.refs_3_ = f32[3072,256]{1,0:T(8,128)S(1)} custom-call(s32[1]{0:T(128)} %bitcast.section_ref, bf16[256,768]{1,0:T(8,128)(2,1)S(1)} %get-tuple-element.305.refs_0_, bf16[256,768]{1,0:T(8,128)(2,1)S(1)} %collective-permute-done.26.refs_1_.refs_2_, bf16[3072,6144]{1,0:T(8,128)(2,1)} %bitcast.22, f32[3072,512]{1,0:T(8,128)S(1)} %down_product.7.refs_3_), custom_call_target="tpu_custom_call" | custom-call | tf_op jit(solution)/shard_map/down_product/pallas_call | solution.py:32
  156.1 1.0 activated.12.refs_1_
  157.2 1.3 collective-permute-start.34
  158.7 4.4 %collective-permute-done.29.refs_2_ = bf16[512,768]{1,0:T(8,128)(2,1)S(1)} collective-permute-done((bf16[512,768]{1,0:T(8,128)(2,1)S(1)}, bf16[512,768]{1,0:T(8,128)(2,1)S(1)}, u32[]{:S(2)}, u32[]{:S(2)}) %collective-permute-start.29) | collective-permute-done | bytes 786464 | tf_op jit(solution)/shard_map/ppermute | solution.py:399
  163.8 3.3 %collective-permute-start.36 = (bf16[512,768]{1,0:T(8,128)(2,1)S(1)}, bf16[512,768]{1,0:T(8,128)(2,1)S(1)}, u32[]{:S(2)}, u32[]{:S(2)}) collective-permute-start(bf16[512,768]{1,0:T(8,128)(2,1)S(1)} %stacked.15.refs_0_), channel_id=1, source_target_pairs={{0,4},{12,8},{1,5},{13,9},{2,6},{14,10},{3,7},{15,11},{16,20},{28,... | collective-permute-start | bytes 2359304 | tf_op jit(solution)/shard_map/ppermute | solution.py:388
  167.1 6.0 %down_product.9.refs_3_ = f32[3072,256]{1,0:T(8,128)S(1)} custom-call(s32[1]{0:T(128)} %bitcast.section_ref, bf16[256,768]{1,0:T(8,128)(2,1)S(1)} %get-tuple-element.308.refs_0_, bf16[256,768]{1,0:T(8,128)(2,1)S(1)} %collective-permute-done.31.refs_1_.refs_2_, bf16[3072,6144]{1,0:T(8,128)(2,1)} %bitcast.23, f32[3072,256]{1,0:T(8,128)S(1)} %down_product.8.refs_3_), custom_call_target="tpu_custom_call" | custom-call | tf_op jit(solution)/shard_map/down_product/pallas_call | solution.py:32
  173.6 1.0 activated.13.refs_1_
  175.3 4.7 %collective-permute-done.34.refs_2_ = bf16[512,768]{1,0:T(8,128)(2,1)S(1)} collective-permute-done((bf16[512,768]{1,0:T(8,128)(2,1)S(1)}, bf16[512,768]{1,0:T(8,128)(2,1)S(1)}, u32[]{:S(2)}, u32[]{:S(2)}) %collective-permute-start.34) | collective-permute-done | bytes 786464 | tf_op jit(solution)/shard_map/ppermute | solution.py:399
  180.4 1.5 collective-permute-start.38
  182.1 6.2 %down_product.10 = (bf16[128,3072]{1,0:T(8,128)(2,1)S(1)}, bf16[128,3072]{1,0:T(8,128)(2,1)S(1)}) custom-call(s32[1]{0:T(128)} %bitcast.section_ref, bf16[256,768]{1,0:T(8,128)(2,1)S(1)} %get-tuple-element.310.refs_0_, bf16[256,768]{1,0:T(8,128)(2,1)S(1)} %collective-permute-done.35.refs_1_.refs_2_, bf16[3072,6144]{1,0:T(8,128)(2,1)} %bitcast.24, ...), custom_call_target="tpu_custom_call" | custom-call | tf_op jit(solution)/shard_map/down_product/pallas_call | solution.py:32
  191.1 1.3 collective-permute-start.42
  192.4 10.2 %collective-permute-done.38.refs_2_ = bf16[512,768]{1,0:T(8,128)(2,1)S(1)} collective-permute-done((bf16[512,768]{1,0:T(8,128)(2,1)S(1)}, bf16[512,768]{1,0:T(8,128)(2,1)S(1)}, u32[]{:S(2)}, u32[]{:S(2)}) %collective-permute-start.38) | collective-permute-done | bytes 786464 | tf_op jit(solution)/shard_map/ppermute | solution.py:399
  203.6 1.1 collective-permute-done.39.refs_1_.refs_3_
  204.8 6.0 %down_product.11.refs_3_ = f32[3072,256]{1,0:T(8,128)S(1)} custom-call(s32[1]{0:T(128)} %bitcast.section_ref, bf16[256,768]{1,0:T(8,128)(2,1)S(1)} %get-tuple-element.306.refs_0_.refs_1_, bf16[256,768]{1,0:T(8,128)(2,1)S(1)} %collective-permute-done.39.refs_1_.refs_3_, bf16[3072,6144]{1,0:T(8,128)(2,1)} %bitcast.25, f32[3072,512]{1,0:T(8,128)S(1)} %down_product.7.refs_3_), custom_call_target="tpu_custom_call" | custom-call | tf_op jit(solution)/shard_map/down_product/pallas_call | solution.py:32
  210.8 1.0 activated.15.refs_1_
  211.8 1.3 collective-permute-start.45
  213.1 7.0 %collective-permute-done.42.refs_2_ = bf16[512,768]{1,0:T(8,128)(2,1)S(1)} collective-permute-done((bf16[512,768]{1,0:T(8,128)(2,1)S(1)}, bf16[512,768]{1,0:T(8,128)(2,1)S(1)}, u32[]{:S(2)}, u32[]{:S(2)}) %collective-permute-start.42) | collective-permute-done | bytes 786464 | tf_op jit(solution)/shard_map/ppermute | solution.py:399
  220.5 1.7 collective-permute-done.43.refs_1_.refs_3_
  222.2 6.0 %down_product.12.refs_3_ = f32[3072,256]{1,0:T(8,128)S(1)} custom-call(s32[1]{0:T(128)} %bitcast.section_ref, bf16[256,768]{1,0:T(8,128)(2,1)S(1)} %get-tuple-element.309.refs_0_.refs_1_, bf16[256,768]{1,0:T(8,128)(2,1)S(1)} %collective-permute-done.43.refs_1_.refs_3_, bf16[3072,6144]{1,0:T(8,128)(2,1)} %bitcast.26, f32[3072,256]{1,0:T(8,128)S(1)} %down_product.11.refs_3_), custom_call_target="tpu_custom_call" | custom-call | tf_op jit(solution)/shard_map/down_product/pallas_call | solution.py:32
  228.2 7.2 %weight_gradient.4.refs_4_ = bf16[3072,6144]{1,0:T(8,128)(2,1)} custom-call(s32[1]{0:T(128)} %bitcast.section_ref, bf16[3072,512]{1,0:T(8,128)(2,1)S(1)} %transposed.1.turned_ref, bf16[256,768]{1,0:T(8,128)(2,1)S(1)} %get-tuple-element.291.refs_0_, bf16[256,768]{1,0:T(8,128)(2,1)S(1)} %get-tuple-element.231.refs_1_, ...), custom_call_target="tpu_custom_call" | custom-call | tf_op jit(solution)/shard_map/weight_gradient/pallas_call | solution.py:32
  236.3 1.7 collective-permute-done.46.refs_1_.refs_3_
  238.1 6.3 %down_product.13 = (bf16[128,3072]{1,0:T(8,128)(2,1)S(1)}, f32[128,3072]{1,0:T(8,128)S(1)}) custom-call(s32[1]{0:T(128)} %bitcast.section_ref, bf16[256,768]{1,0:T(8,128)(2,1)S(1)} %get-tuple-element.311.refs_0_.refs_1_, bf16[256,768]{1,0:T(8,128)(2,1)S(1)} %collective-permute-done.46.refs_1_.refs_3_, bf16[3072,6144]{1,0:T(8,128)(2,1)} %bitcast.27, ...), custom_call_target="tpu_custom_call" | custom-call | tf_op jit(solution)/shard_map/down_product/pallas_call | solution.py:32
  244.9 7.2 %weight_gradient.5.refs_4_ = bf16[3072,6144]{1,0:T(8,128)(2,1)} custom-call(s32[1]{0:T(128)} %bitcast.section_ref, bf16[3072,512]{1,0:T(8,128)(2,1)S(1)} %transposed.1.turned_ref, bf16[256,768]{1,0:T(8,128)(2,1)S(1)} %get-tuple-element.305.refs_0_, bf16[256,768]{1,0:T(8,128)(2,1)S(1)} %get-tuple-element.306.refs_0_.refs_1_, ...), custom_call_target="tpu_custom_call", output_to_operand_aliasing={{}: (6, {})} | custom-call | tf_op jit(solution)/shard_map/weight_gradient/pallas_call | solution.py:32
  252.1 7.2 %weight_gradient.6.refs_4_ = bf16[3072,6144]{1,0:T(8,128)(2,1)} custom-call(s32[1]{0:T(128)} %bitcast.section_ref, bf16[3072,512]{1,0:T(8,128)(2,1)S(1)} %transposed.1.turned_ref, bf16[256,768]{1,0:T(8,128)(2,1)S(1)} %get-tuple-element.308.refs_0_, bf16[256,768]{1,0:T(8,128)(2,1)S(1)} %get-tuple-element.309.refs_0_.refs_1_, ...), custom_call_target="tpu_custom_call", output_to_operand_aliasing={{}: (6, {})} | custom-call | tf_op jit(solution)/shard_map/weight_gradient/pallas_call | solution.py:32
  259.3 7.2 %weight_gradient.7 = bf16[3072,6144]{1,0:T(8,128)(2,1)} custom-call(s32[1]{0:T(128)} %bitcast.section_ref, bf16[3072,512]{1,0:T(8,128)(2,1)S(1)} %transposed.1.turned_ref, bf16[256,768]{1,0:T(8,128)(2,1)S(1)} %get-tuple-element.310.refs_0_, bf16[256,768]{1,0:T(8,128)(2,1)S(1)} %get-tuple-element.311.refs_0_.refs_1_, ...), custom_call_target="tpu_custom_call", output_to_operand_aliasing={{}: (6, {})} | custom-call | tf_op jit(solution)/shard_map/weight_gradient/pallas_call | solution.py:32
  266.5 1.0 fusion.1
  (94 shorter events, 22.0 us)
Async XLA Ops:
  0.6 25.0 %copy-start = (f32[3072]{0:T(1024)S(1)}, f32[3072]{0:T(1024)}, u32[]{:S(2)}) copy-start(f32[3072]{0:T(1024)} %param.6) | copy-start | bytes 36868
  1.9 21.6 %collective-permute-start = (bf16[128,3072]{1,0:T(8,128)(2,1)S(1)}, bf16[128,3072]{1,0:T(8,128)(2,1)S(1)}, u32[]{:S(2)}, u32[]{:S(2)}) collective-permute-start(bf16[128,3072]{1,0:T(8,128)(2,1)S(1)} %broadcast_select_fusion.refs_1_), channel_id=1, source_target_pairs={{0,1},{1,0},{2,3},{3,2},{4,5},{5,4},{6,7},{7,6},{8,9},{9,8},{10,11... | collective-permute-start | bytes 2359304 | tf_op jit(solution)/shard_map/ppermute | solution.py:317
  4.9 19.0 %collective-permute-start.1 = (bf16[128,3072]{1,0:T(8,128)(2,1)S(1)}, bf16[128,3072]{1,0:T(8,128)(2,1)S(1)}, u32[]{:S(2)}, u32[]{:S(2)}) collective-permute-start(bf16[128,3072]{1,0:T(8,128)(2,1)S(1)} %broadcast_select_fusion.refs_1_), channel_id=1, source_target_pairs={{0,2},{1,3},{2,0},{3,1},{4,6},{5,7},{6,4},{7,5},{8,10},{9,11},{10,... | collective-permute-start | bytes 2359304 | tf_op jit(solution)/shard_map/ppermute | solution.py:317
  19.8 3.6 %collective-permute-start.2 = (f32[128,2]{0,1:T(2,128)S(1)}, f32[128,2]{0,1:T(2,128)S(1)}, u32[]{:S(2)}, u32[]{:S(2)}) collective-permute-start(f32[128,2]{0,1:T(2,128)S(1)} %pad_maximum_fusion), channel_id=1, source_target_pairs={{0,1},{1,0},{2,3},{3,2},{4,5},{5,4},{6,7},{7,6},{8,9},{9,8},{10,11... | collective-permute-start | bytes 3080 | tf_op jit(solution)/shard_map/ppermute | solution.py:317
  24.0 21.0 %collective-permute-start.5 = (bf16[128,3072]{1,0:T(8,128)(2,1)S(1)}, bf16[128,3072]{1,0:T(8,128)(2,1)S(1)}, u32[]{:S(2)}, u32[]{:S(2)}) collective-permute-start(bf16[128,3072]{1,0:T(8,128)(2,1)S(1)} %collective-permute-done.refs_0_), channel_id=1, source_target_pairs={{0,2},{1,3},{2,0},{3,1},{4,6},{5,7},{6,4},{7,5},{8,10},{9,11},{10,... | collective-permute-start | bytes 2359304 | tf_op jit(solution)/shard_map/ppermute | solution.py:317
  32.1 1.8 collective-permute-start.3
  34.1 20.6 %collective-permute-start.6 = (bf16[512,768]{1,0:T(8,128)(2,1)S(1)}, bf16[512,768]{1,0:T(8,128)(2,1)S(1)}, u32[]{:S(2)}, u32[]{:S(2)}) collective-permute-start(bf16[512,768]{1,0:T(8,128)(2,1)S(1)} %stacked.8.refs_0_), channel_id=1, source_target_pairs={{0,4},{12,8},{1,5},{13,9},{2,6},{14,10},{3,7},{15,11},{16,20},{28,... | collective-permute-start | bytes 2359304 | tf_op jit(solution)/shard_map/ppermute | solution.py:388
  37.7 7.3 %collective-permute-start.4 = (f32[256,2]{1,0:T(8,128)S(1)}, f32[256,2]{1,0:T(8,128)S(1)}, u32[]{:S(2)}, u32[]{:S(2)}) collective-permute-start(f32[256,2]{1,0:T(8,128)S(1)} %copy.12.scale_ref), channel_id=1, source_target_pairs={{0,2},{1,3},{2,0},{3,1},{4,6},{5,7},{6,4},{7,5},{8,10},{9,11},{10,... | collective-permute-start | bytes 6152 | tf_op jit(solution)/shard_map/ppermute | solution.py:317
  51.5 3.6 %collective-permute-start.7 = (bf16[256,768]{1,0:T(8,128)(2,1)S(1)}, bf16[256,768]{1,0:T(8,128)(2,1)S(1)}, u32[]{:S(2)}, u32[]{:S(2)}) collective-permute-start(bf16[256,768]{1,0:T(8,128)(2,1)S(1)} %get-tuple-element.180), channel_id=1, source_target_pairs={{0,16},{16,0},{1,17},{17,1},{2,18},{18,2},{3,19},{19,3},{4,20},{20... | collective-permute-start | bytes 1179656 | tf_op jit(solution)/shard_map/ppermute | solution.py:321
  55.4 22.6 %collective-permute-start.9 = (bf16[512,768]{1,0:T(8,128)(2,1)S(1)}, bf16[512,768]{1,0:T(8,128)(2,1)S(1)}, u32[]{:S(2)}, u32[]{:S(2)}) collective-permute-start(bf16[512,768]{1,0:T(8,128)(2,1)S(1)} %stacked.9.refs_0_), channel_id=1, source_target_pairs={{0,4},{12,8},{1,5},{13,9},{2,6},{14,10},{3,7},{15,11},{16,20},{28,... | collective-permute-start | bytes 2359304 | tf_op jit(solution)/shard_map/ppermute | solution.py:388
  65.1 1.8 collective-permute-start.8
  65.2 14.1 %collective-permute-start.10 = (bf16[512,768]{1,0:T(8,128)(2,1)S(1)}, bf16[512,768]{1,0:T(8,128)(2,1)S(1)}, u32[]{:S(2)}, u32[]{:S(2)}) collective-permute-start(bf16[512,768]{1,0:T(8,128)(2,1)S(1)} %added.8.refs_1_), channel_id=1, source_target_pairs={{4,8},{8,4},{5,9},{9,5},{6,10},{10,6},{7,11},{11,7},{20,24},{24,20... | collective-permute-start | bytes 2359304 | tf_op jit(solution)/shard_map/ppermute | solution.py:393
  74.9 24.4 %collective-permute-start.12 = (bf16[512,768]{1,0:T(8,128)(2,1)S(1)}, bf16[512,768]{1,0:T(8,128)(2,1)S(1)}, u32[]{:S(2)}, u32[]{:S(2)}) collective-permute-start(bf16[512,768]{1,0:T(8,128)(2,1)S(1)} %stacked.10.refs_0_), channel_id=1, source_target_pairs={{0,4},{12,8},{1,5},{13,9},{2,6},{14,10},{3,7},{15,11},{16,20},{28,... | collective-permute-start | bytes 2359304 | tf_op jit(solution)/shard_map/ppermute | solution.py:388
  78.5 22.0 %collective-permute-start.13 = (bf16[512,768]{1,0:T(8,128)(2,1)S(1)}, bf16[512,768]{1,0:T(8,128)(2,1)S(1)}, u32[]{:S(2)}, u32[]{:S(2)}) collective-permute-start(bf16[512,768]{1,0:T(8,128)(2,1)S(1)} %added.9.refs_1_), channel_id=1, source_target_pairs={{4,8},{8,4},{5,9},{9,5},{6,10},{10,6},{7,11},{11,7},{20,24},{24,20... | collective-permute-start | bytes 2359304 | tf_op jit(solution)/shard_map/ppermute | solution.py:393
  79.2 2.6 collective-permute-start.11
  80.3 25.7 %collective-permute-start.14 = (bf16[512,768]{1,0:T(8,128)(2,1)S(1)}, bf16[512,768]{1,0:T(8,128)(2,1)S(1)}, u32[]{:S(2)}, u32[]{:S(2)}) collective-permute-start(bf16[512,768]{1,0:T(8,128)(2,1)S(1)} %activated.8.refs_1_), channel_id=1, source_target_pairs={{4,0},{8,12},{5,1},{9,13},{6,2},{10,14},{7,3},{11,15},{20,16},{24,... | collective-permute-start | bytes 2359304 | tf_op jit(solution)/shard_map/ppermute | solution.py:399
  89.8 27.4 %collective-permute-start.16 = (bf16[512,768]{1,0:T(8,128)(2,1)S(1)}, bf16[512,768]{1,0:T(8,128)(2,1)S(1)}, u32[]{:S(2)}, u32[]{:S(2)}) collective-permute-start(bf16[512,768]{1,0:T(8,128)(2,1)S(1)} %stacked.11.refs_0_), channel_id=1, source_target_pairs={{0,4},{12,8},{1,5},{13,9},{2,6},{14,10},{3,7},{15,11},{16,20},{28,... | collective-permute-start | bytes 2359304 | tf_op jit(solution)/shard_map/ppermute | solution.py:388
  99.7 19.4 %collective-permute-start.17 = (bf16[512,768]{1,0:T(8,128)(2,1)S(1)}, bf16[512,768]{1,0:T(8,128)(2,1)S(1)}, u32[]{:S(2)}, u32[]{:S(2)}) collective-permute-start(bf16[512,768]{1,0:T(8,128)(2,1)S(1)} %added.10.refs_1_), channel_id=1, source_target_pairs={{4,8},{8,4},{5,9},{9,5},{6,10},{10,6},{7,11},{11,7},{20,24},{24,20... | collective-permute-start | bytes 2359304 | tf_op jit(solution)/shard_map/ppermute | solution.py:393
  101.5 21.4 %collective-permute-start.18 = (bf16[512,768]{1,0:T(8,128)(2,1)S(1)}, bf16[512,768]{1,0:T(8,128)(2,1)S(1)}, u32[]{:S(2)}, u32[]{:S(2)}) collective-permute-start(bf16[512,768]{1,0:T(8,128)(2,1)S(1)} %activated.9.refs_1_), channel_id=1, source_target_pairs={{4,0},{8,12},{5,1},{9,13},{6,2},{10,14},{7,3},{11,15},{20,16},{24,... | collective-permute-start | bytes 2359304 | tf_op jit(solution)/shard_map/ppermute | solution.py:399
  102.8 3.6 %collective-permute-start.15 = (bf16[256,768]{1,0:T(8,128)(2,1)S(1)}, bf16[256,768]{1,0:T(8,128)(2,1)S(1)}, u32[]{:S(2)}, u32[]{:S(2)}) collective-permute-start(bf16[256,768]{1,0:T(8,128)(2,1)S(1)} %get-tuple-element.216), channel_id=1, source_target_pairs={{0,16},{16,0},{1,17},{17,1},{2,18},{18,2},{3,19},{19,3},{4,20},{20... | collective-permute-start | bytes 1179656 | tf_op jit(solution)/shard_map/ppermute | solution.py:321
  106.0 18.5 %collective-permute-start.19 = (bf16[256,768]{1,0:T(8,128)(2,1)S(1)}, bf16[256,768]{1,0:T(8,128)(2,1)S(1)}, u32[]{:S(2)}, u32[]{:S(2)}) collective-permute-start(bf16[256,768]{1,0:T(8,128)(2,1)S(1)} %get-tuple-element.229), channel_id=1, source_target_pairs={{0,16},{16,0},{1,17},{17,1},{2,18},{18,2},{3,19},{19,3},{4,20},{20... | collective-permute-start | bytes 1179656 | tf_op jit(solution)/shard_map/ppermute | solution.py:321
  106.6 31.6 %collective-permute-start.22 = (bf16[512,768]{1,0:T(8,128)(2,1)S(1)}, bf16[512,768]{1,0:T(8,128)(2,1)S(1)}, u32[]{:S(2)}, u32[]{:S(2)}) collective-permute-start(bf16[512,768]{1,0:T(8,128)(2,1)S(1)} %stacked.12.refs_0_), channel_id=1, source_target_pairs={{0,4},{12,8},{1,5},{13,9},{2,6},{14,10},{3,7},{15,11},{16,20},{28,... | collective-permute-start | bytes 2359304 | tf_op jit(solution)/shard_map/ppermute | solution.py:388
  119.1 5.8 %collective-permute-start.21 = (bf16[256,768]{1,0:T(8,128)(2,1)S(1)}, bf16[256,768]{1,0:T(8,128)(2,1)S(1)}, u32[]{:S(2)}, u32[]{:S(2)}) collective-permute-start(bf16[256,768]{1,0:T(8,128)(2,1)S(1)} %get-tuple-element.233), channel_id=1, source_target_pairs={{0,16},{16,0},{1,17},{17,1},{2,18},{18,2},{3,19},{19,3},{4,20},{20... | collective-permute-start | bytes 1179656 | tf_op jit(solution)/shard_map/ppermute | solution.py:321
  119.2 20.3 %collective-permute-start.23 = (bf16[512,768]{1,0:T(8,128)(2,1)S(1)}, bf16[512,768]{1,0:T(8,128)(2,1)S(1)}, u32[]{:S(2)}, u32[]{:S(2)}) collective-permute-start(bf16[512,768]{1,0:T(8,128)(2,1)S(1)} %added.11.refs_1_), channel_id=1, source_target_pairs={{4,8},{8,4},{5,9},{9,5},{6,10},{10,6},{7,11},{11,7},{20,24},{24,20... | collective-permute-start | bytes 2359304 | tf_op jit(solution)/shard_map/ppermute | solution.py:393
  122.9 22.5 %collective-permute-start.24 = (bf16[512,768]{1,0:T(8,128)(2,1)S(1)}, bf16[512,768]{1,0:T(8,128)(2,1)S(1)}, u32[]{:S(2)}, u32[]{:S(2)}) collective-permute-start(bf16[512,768]{1,0:T(8,128)(2,1)S(1)} %activated.10.refs_1_), channel_id=1, source_target_pairs={{4,0},{8,12},{5,1},{9,13},{6,2},{10,14},{7,3},{11,15},{20,16},{24,... | collective-permute-start | bytes 2359304 | tf_op jit(solution)/shard_map/ppermute | solution.py:399
  124.5 5.8 %collective-permute-start.20 = (bf16[256,768]{1,0:T(8,128)(2,1)S(1)}, bf16[256,768]{1,0:T(8,128)(2,1)S(1)}, u32[]{:S(2)}, u32[]{:S(2)}) collective-permute-start(bf16[256,768]{1,0:T(8,128)(2,1)S(1)} %get-tuple-element.232), channel_id=1, source_target_pairs={{0,16},{16,0},{1,17},{17,1},{2,18},{18,2},{3,19},{19,3},{4,20},{20... | collective-permute-start | bytes 1179656 | tf_op jit(solution)/shard_map/ppermute | solution.py:321
  124.9 30.1 %collective-permute-start.27 = (bf16[512,768]{1,0:T(8,128)(2,1)S(1)}, bf16[512,768]{1,0:T(8,128)(2,1)S(1)}, u32[]{:S(2)}, u32[]{:S(2)}) collective-permute-start(bf16[512,768]{1,0:T(8,128)(2,1)S(1)} %stacked.13.refs_0_), channel_id=1, source_target_pairs={{0,4},{12,8},{1,5},{13,9},{2,6},{14,10},{3,7},{15,11},{16,20},{28,... | collective-permute-start | bytes 2359304 | tf_op jit(solution)/shard_map/ppermute | solution.py:388
  138.6 17.5 %collective-permute-start.28 = (bf16[512,768]{1,0:T(8,128)(2,1)S(1)}, bf16[512,768]{1,0:T(8,128)(2,1)S(1)}, u32[]{:S(2)}, u32[]{:S(2)}) collective-permute-start(bf16[512,768]{1,0:T(8,128)(2,1)S(1)} %added.12.refs_1_), channel_id=1, source_target_pairs={{4,8},{8,4},{5,9},{9,5},{6,10},{10,6},{7,11},{11,7},{20,24},{24,20... | collective-permute-start | bytes 2359304 | tf_op jit(solution)/shard_map/ppermute | solution.py:393
  139.4 6.4 %collective-permute-start.25 = (bf16[256,768]{1,0:T(8,128)(2,1)S(1)}, bf16[256,768]{1,0:T(8,128)(2,1)S(1)}, u32[]{:S(2)}, u32[]{:S(2)}) collective-permute-start(bf16[256,768]{1,0:T(8,128)(2,1)S(1)} %get-tuple-element.244), channel_id=1, source_target_pairs={{0,16},{16,0},{1,17},{17,1},{2,18},{18,2},{3,19},{19,3},{4,20},{20... | collective-permute-start | bytes 1179656 | tf_op jit(solution)/shard_map/ppermute | solution.py:321
  140.5 22.7 %collective-permute-start.29 = (bf16[512,768]{1,0:T(8,128)(2,1)S(1)}, bf16[512,768]{1,0:T(8,128)(2,1)S(1)}, u32[]{:S(2)}, u32[]{:S(2)}) collective-permute-start(bf16[512,768]{1,0:T(8,128)(2,1)S(1)} %activated.11.refs_1_), channel_id=1, source_target_pairs={{4,0},{8,12},{5,1},{9,13},{6,2},{10,14},{7,3},{11,15},{20,16},{24,... | collective-permute-start | bytes 2359304 | tf_op jit(solution)/shard_map/ppermute | solution.py:399
  145.7 3.2 %collective-permute-start.26 = (bf16[256,768]{1,0:T(8,128)(2,1)S(1)}, bf16[256,768]{1,0:T(8,128)(2,1)S(1)}, u32[]{:S(2)}, u32[]{:S(2)}) collective-permute-start(bf16[256,768]{1,0:T(8,128)(2,1)S(1)} %get-tuple-element.246), channel_id=1, source_target_pairs={{0,16},{16,0},{1,17},{17,1},{2,18},{18,2},{3,19},{19,3},{4,20},{20... | collective-permute-start | bytes 1179656 | tf_op jit(solution)/shard_map/ppermute | solution.py:321
  146.0 27.1 %collective-permute-start.32 = (bf16[512,768]{1,0:T(8,128)(2,1)S(1)}, bf16[512,768]{1,0:T(8,128)(2,1)S(1)}, u32[]{:S(2)}, u32[]{:S(2)}) collective-permute-start(bf16[512,768]{1,0:T(8,128)(2,1)S(1)} %stacked.14.refs_0_), channel_id=1, source_target_pairs={{0,4},{12,8},{1,5},{13,9},{2,6},{14,10},{3,7},{15,11},{16,20},{28,... | collective-permute-start | bytes 2359304 | tf_op jit(solution)/shard_map/ppermute | solution.py:388
  155.4 18.2 %collective-permute-start.33 = (bf16[512,768]{1,0:T(8,128)(2,1)S(1)}, bf16[512,768]{1,0:T(8,128)(2,1)S(1)}, u32[]{:S(2)}, u32[]{:S(2)}) collective-permute-start(bf16[512,768]{1,0:T(8,128)(2,1)S(1)} %added.13.refs_1_), channel_id=1, source_target_pairs={{4,8},{8,4},{5,9},{9,5},{6,10},{10,6},{7,11},{11,7},{20,24},{24,20... | collective-permute-start | bytes 2359304 | tf_op jit(solution)/shard_map/ppermute | solution.py:393
  157.2 22.9 %collective-permute-start.34 = (bf16[512,768]{1,0:T(8,128)(2,1)S(1)}, bf16[512,768]{1,0:T(8,128)(2,1)S(1)}, u32[]{:S(2)}, u32[]{:S(2)}) collective-permute-start(bf16[512,768]{1,0:T(8,128)(2,1)S(1)} %activated.12.refs_1_), channel_id=1, source_target_pairs={{4,0},{8,12},{5,1},{9,13},{6,2},{10,14},{7,3},{11,15},{20,16},{24,... | collective-permute-start | bytes 2359304 | tf_op jit(solution)/shard_map/ppermute | solution.py:399
  158.4 5.1 %collective-permute-start.30 = (bf16[256,768]{1,0:T(8,128)(2,1)S(1)}, bf16[256,768]{1,0:T(8,128)(2,1)S(1)}, u32[]{:S(2)}, u32[]{:S(2)}) collective-permute-start(bf16[256,768]{1,0:T(8,128)(2,1)S(1)} %get-tuple-element.259), channel_id=1, source_target_pairs={{0,16},{16,0},{1,17},{17,1},{2,18},{18,2},{3,19},{19,3},{4,20},{20... | collective-permute-start | bytes 1179656 | tf_op jit(solution)/shard_map/ppermute | solution.py:321
  163.5 3.6 %collective-permute-start.31 = (bf16[256,768]{1,0:T(8,128)(2,1)S(1)}, bf16[256,768]{1,0:T(8,128)(2,1)S(1)}, u32[]{:S(2)}, u32[]{:S(2)}) collective-permute-start(bf16[256,768]{1,0:T(8,128)(2,1)S(1)} %get-tuple-element.261), channel_id=1, source_target_pairs={{0,16},{16,0},{1,17},{17,1},{2,18},{18,2},{3,19},{19,3},{4,20},{20... | collective-permute-start | bytes 1179656 | tf_op jit(solution)/shard_map/ppermute | solution.py:321
  163.8 25.1 %collective-permute-start.36 = (bf16[512,768]{1,0:T(8,128)(2,1)S(1)}, bf16[512,768]{1,0:T(8,128)(2,1)S(1)}, u32[]{:S(2)}, u32[]{:S(2)}) collective-permute-start(bf16[512,768]{1,0:T(8,128)(2,1)S(1)} %stacked.15.refs_0_), channel_id=1, source_target_pairs={{0,4},{12,8},{1,5},{13,9},{2,6},{14,10},{3,7},{15,11},{16,20},{28,... | collective-permute-start | bytes 2359304 | tf_op jit(solution)/shard_map/ppermute | solution.py:388
  174.6 15.5 %collective-permute-start.37 = (bf16[512,768]{1,0:T(8,128)(2,1)S(1)}, bf16[512,768]{1,0:T(8,128)(2,1)S(1)}, u32[]{:S(2)}, u32[]{:S(2)}) collective-permute-start(bf16[512,768]{1,0:T(8,128)(2,1)S(1)} %added.14.refs_1_), channel_id=1, source_target_pairs={{4,8},{8,4},{5,9},{9,5},{6,10},{10,6},{7,11},{11,7},{20,24},{24,20... | collective-permute-start | bytes 2359304 | tf_op jit(solution)/shard_map/ppermute | solution.py:393
  180.3 1.8 collective-permute-start.35
  180.4 22.2 %collective-permute-start.38 = (bf16[512,768]{1,0:T(8,128)(2,1)S(1)}, bf16[512,768]{1,0:T(8,128)(2,1)S(1)}, u32[]{:S(2)}, u32[]{:S(2)}) collective-permute-start(bf16[512,768]{1,0:T(8,128)(2,1)S(1)} %activated.13.refs_1_), channel_id=1, source_target_pairs={{4,0},{8,12},{5,1},{9,13},{6,2},{10,14},{7,3},{11,15},{20,16},{24,... | collective-permute-start | bytes 2359304 | tf_op jit(solution)/shard_map/ppermute | solution.py:399
  188.4 22.4 %collective-permute-start.40 = (bf16[128,3072]{1,0:T(8,128)(2,1)S(1)}, bf16[128,3072]{1,0:T(8,128)(2,1)S(1)}, u32[]{:S(2)}, u32[]{:S(2)}) collective-permute-start(bf16[128,3072]{1,0:T(8,128)(2,1)S(1)} %get-tuple-element.273), channel_id=1, source_target_pairs={{0,2},{1,3},{2,0},{3,1},{4,6},{5,7},{6,4},{7,5},{8,10},{9,11},{10,... | collective-permute-start | bytes 2359304 | tf_op jit(solution)/shard_map/ppermute | solution.py:317
  189.3 21.5 %collective-permute-start.41 = (bf16[512,768]{1,0:T(8,128)(2,1)S(1)}, bf16[512,768]{1,0:T(8,128)(2,1)S(1)}, u32[]{:S(2)}, u32[]{:S(2)}) collective-permute-start(bf16[512,768]{1,0:T(8,128)(2,1)S(1)} %added.15.refs_1_), channel_id=1, source_target_pairs={{4,8},{8,4},{5,9},{9,5},{6,10},{10,6},{7,11},{11,7},{20,24},{24,20... | collective-permute-start | bytes 2359304 | tf_op jit(solution)/shard_map/ppermute | solution.py:393
  191.1 29.0 %collective-permute-start.42 = (bf16[512,768]{1,0:T(8,128)(2,1)S(1)}, bf16[512,768]{1,0:T(8,128)(2,1)S(1)}, u32[]{:S(2)}, u32[]{:S(2)}) collective-permute-start(bf16[512,768]{1,0:T(8,128)(2,1)S(1)} %activated.14.refs_1_), channel_id=1, source_target_pairs={{4,0},{8,12},{5,1},{9,13},{6,2},{10,14},{7,3},{11,15},{20,16},{24,... | collective-permute-start | bytes 2359304 | tf_op jit(solution)/shard_map/ppermute | solution.py:399
  203.0 1.8 collective-permute-start.39
  203.0 32.4 %collective-permute-start.44 = (bf16[128,3072]{1,0:T(8,128)(2,1)S(1)}, bf16[128,3072]{1,0:T(8,128)(2,1)S(1)}, u32[]{:S(2)}, u32[]{:S(2)}) collective-permute-start(bf16[128,3072]{1,0:T(8,128)(2,1)S(1)} %get-tuple-element.274), channel_id=1, source_target_pairs={{0,2},{1,3},{2,0},{3,1},{4,6},{5,7},{6,4},{7,5},{8,10},{9,11},{10,... | collective-permute-start | bytes 2359304 | tf_op jit(solution)/shard_map/ppermute | solution.py:317
  211.8 24.1 %collective-permute-start.45 = (bf16[512,768]{1,0:T(8,128)(2,1)S(1)}, bf16[512,768]{1,0:T(8,128)(2,1)S(1)}, u32[]{:S(2)}, u32[]{:S(2)}) collective-permute-start(bf16[512,768]{1,0:T(8,128)(2,1)S(1)} %activated.15.refs_1_), channel_id=1, source_target_pairs={{4,0},{8,12},{5,1},{9,13},{6,2},{10,14},{7,3},{11,15},{20,16},{24,... | collective-permute-start | bytes 2359304 | tf_op jit(solution)/shard_map/ppermute | solution.py:399
  220.4 1.8 collective-permute-start.43
  236.3 1.8 collective-permute-start.46
  244.3 22.2 %collective-permute-start.47 = (bf16[128,3072]{1,0:T(8,128)(2,1)S(1)}, bf16[128,3072]{1,0:T(8,128)(2,1)S(1)}, u32[]{:S(2)}, u32[]{:S(2)}) collective-permute-start(bf16[128,3072]{1,0:T(8,128)(2,1)S(1)} %get-tuple-element.303), channel_id=1, source_target_pairs={{0,1},{1,0},{2,3},{3,2},{4,5},{5,4},{6,7},{7,6},{8,9},{9,8},{10,11... | collective-permute-start | bytes 2359304 | tf_op jit(solution)/shard_map/ppermute | solution.py:317
